TPU v7x, 32 devices: a whole 2x2x4 slice. The times are simulated.
32 devices in a mesh: dp: 8 (over z, x), fsdp: 4 (over y, core).
Axes of the slice: x: 2, y: 2, z: 4, core: 2. Of those that a mesh axis runs over, the one named last changes fastest.
Arguments:
- token_ids: int32 [2, 128, 128], P(None, ('dp', 'fsdp')), may hold values from 0 to 32127
- pad_mask: int32 [2, 128, 128], P(None, ('dp', 'fsdp')), may hold values from 0 to 1, as said below
- hard_negative: int32 [128], P(('dp', 'fsdp')), may hold values from 0 to 127
- table: float32 [32128, 768], P('dp'), may hold values from -6 to 6
- table_first: float32 [32128, 768], P('dp'), may hold values from -1.5258789e-05 to 1.5258789e-05
- table_second: float32 [32128, 768], P('dp'), may hold values from 7.8065327e-13 to 3.122613e-12
- attn_in: float32 [768, 2304], P(('dp', 'fsdp')), may hold values from -0.21875 to 0.21875
- attn_in_first: float32 [768, 2304], P(('dp', 'fsdp')), may hold values from -3.0517578e-05 to 3.0517578e-05
- attn_in_second: float32 [768, 2304], P(('dp', 'fsdp')), may hold values from 3.122613e-12 to 1.2490452e-11
- attn_out: float32 [768, 768], P(('dp', 'fsdp')), may hold values from -0.4375 to 0.4375
- attn_out_first: float32 [768, 768], P(('dp', 'fsdp')), may hold values from -3.0517578e-05 to 3.0517578e-05
- attn_out_second: float32 [768, 768], P(('dp', 'fsdp')), may hold values from 3.122613e-12 to 1.2490452e-11
- ffn_in: float32 [768, 3072], P(('dp', 'fsdp')), may hold values from -0.21875 to 0.21875
- ffn_in_first: float32 [768, 3072], P(('dp', 'fsdp')), may hold values from -3.0517578e-05 to 3.0517578e-05
- ffn_in_second: float32 [768, 3072], P(('dp', 'fsdp')), may hold values from 3.122613e-12 to 1.2490452e-11
- ffn_out: float32 [3072, 768], P(('dp', 'fsdp')), may hold values from -0.109375 to 0.109375
- ffn_out_first: float32 [3072, 768], P(('dp', 'fsdp')), may hold values from -3.0517578e-05 to 3.0517578e-05
- ffn_out_second: float32 [3072, 768], P(('dp', 'fsdp')), may hold values from 3.122613e-12 to 1.2490452e-11
- proj_head: float32 [768, 768], P(('dp', 'fsdp')), may hold values from -0.21875 to 0.21875
- proj_head_first: float32 [768, 768], P(('dp', 'fsdp')), may hold values from -3.0517578e-05 to 3.0517578e-05
- proj_head_second: float32 [768, 768], P(('dp', 'fsdp')), may hold values from 3.122613e-12 to 1.2490452e-11
- small_params: float32 [2689], replicated, may hold values from -1 to 4, as said below
- small_first: float32 [2689], replicated, may hold values from -4.68417e-05 to 4.68417e-05
- small_second: float32 [2689], replicated, may hold values from 1.23667846e-13 to 1.9984724e-10
Outputs:
- loss_sum: float32 [], replicated
- grad_norm: float32 [], replicated
- next_table_first: float32 [32128, 768], P('dp')
- next_table_second: float32 [32128, 768], P('dp')
- next_table: float32 [32128, 768], P('dp')
- next_attn_in_first: float32 [768, 2304], P(('dp', 'fsdp'))
- next_attn_in_second: float32 [768, 2304], P(('dp', 'fsdp'))
- next_attn_in: float32 [768, 2304], P(('dp', 'fsdp'))
- next_attn_out_first: float32 [768, 768], P(('dp', 'fsdp'))
- next_attn_out_second: float32 [768, 768], P(('dp', 'fsdp'))
- next_attn_out: float32 [768, 768], P(('dp', 'fsdp'))
- next_ffn_in_first: float32 [768, 3072], P(('dp', 'fsdp'))
- next_ffn_in_second: float32 [768, 3072], P(('dp', 'fsdp'))
- next_ffn_in: float32 [768, 3072], P(('dp', 'fsdp'))
- next_ffn_out_first: float32 [3072, 768], P(('dp', 'fsdp'))
- next_ffn_out_second: float32 [3072, 768], P(('dp', 'fsdp'))
- next_ffn_out: float32 [3072, 768], P(('dp', 'fsdp'))
- next_proj_head_first: float32 [768, 768], P(('dp', 'fsdp'))
- next_proj_head_second: float32 [768, 768], P(('dp', 'fsdp'))
- next_proj_head: float32 [768, 768], P(('dp', 'fsdp'))
- next_small_first: float32 [2689], replicated
- next_small_second: float32 [2689], replicated
- next_small: float32 [2689], replicated
Inputs may be any that keep to these rules, and one draw needn't show every extreme that they name: `pad_mask`: in each sentence the real tokens are a prefix of one or more; both sentences of the last pair are full (128 real tokens). `small_params`: gains lie in 0.5 to 2.7, biases in -1 to 1, the log scale in 3.5 to 4.
All inputs are finite; a program needn't handle non-finite values.
Results may differ from a plain program's by a relative error of at most 0.014.
The roundings to bfloat16 on the way count: a program that leaves them out, or rounds other values in their place, can miss the bound.
Values may be sent and summed in bfloat16 or wider, within the bound.
A program may use at most 256 MiB of HBM per device.

v0:
```python
import jax
import jax.numpy as jnp
import numpy as np
from jax import lax
from jax.sharding import PartitionSpec as P

D = 768
HEADS = 12
HD = 64
NB = 32
L = 128
STEP = 10


EPS = 1e-06
SCALE = 0.125
MARGIN = 0.2
CLIP = 0.1
BETA_ONE = 0.9
BETA_TWO = 0.99
ADAM_EPS = 1e-08
RATES = (3.0, 0.1, 0.2, 0.1, 0.05, 0.1, 1.0)
DECAYS = (0.001, 0.001, 0.001, 0.001, 0.001, 0.001, 0.0)
HIGH = lax.Precision.HIGHEST


def bucket_table(length, count):
    position = np.arange(length)
    relative = position[None, :] - position[:, None]
    half = count // 2
    base_part = (relative > 0).astype(np.int64) * half
    distance = np.abs(relative)
    exact = half // 2
    safe_dist = np.maximum(distance, 1)
    large = exact + (np.log(safe_dist / exact) / np.log(length / exact) * (half - exact)).astype(
        np.int64
    )
    large = np.minimum(large, half - 1)
    return base_part + np.where(distance < exact, distance, large)


def matmul(left_side, right_side):
    return jnp.dot(left_side, right_side, preferred_element_type=jnp.float32)


def matmul_tn(left_side, right_side):
    return lax.dot_general(
        left_side, right_side, (((0,), (0,)), ((), ())), preferred_element_type=jnp.float32
    )


def matmul_nt(left_side, right_side):
    return lax.dot_general(
        left_side, right_side, (((1,), (1,)), ((), ())), preferred_element_type=jnp.float32
    )


def normalize(inputs, gain_row):
    factor = lax.rsqrt(jnp.mean(inputs * inputs, -1, keepdims=True) + EPS)
    return (inputs * factor * gain_row, factor)


def normalize_back(grad_out, inputs, factor, gain_row):
    scaled = grad_out * gain_row
    grad_gain = jnp.sum(grad_out * inputs * factor, 0)
    grad_in = factor * (
        scaled - inputs * factor * factor * jnp.mean(scaled * inputs, -1, keepdims=True)
    )
    return (grad_in, grad_gain)


def attention_scores(mixed_proj, mask_rows, bias_full):
    keep_add = jnp.where(mask_rows > 0, 0.0, -1000000000.0).astype(jnp.float32)
    scores = jnp.einsum(
        "bqhd,bkhd->bhqk",
        mixed_proj[:, :, 0],
        mixed_proj[:, :, 1],
        preferred_element_type=jnp.float32,
    )
    return scores * SCALE + bias_full[None] + keep_add[:, None, None, :]


def layer_forward(token_rows, mask_rows, weights, gain_rows, bias_full):
    attn_in, attn_out, ffn_in, ffn_out = weights
    seq_count, length = mask_rows.shape
    width = token_rows.shape[1]
    normed_one, factor_one = normalize(token_rows, gain_rows[0])
    act_one = normed_one.astype(jnp.bfloat16)
    mixed_proj = (
        matmul(act_one, attn_in).astype(jnp.bfloat16).reshape(seq_count, length, 3, HEADS, HD)
    )
    scores = attention_scores(mixed_proj, mask_rows, bias_full)
    row_max = jnp.max(scores, -1, keepdims=True)
    log_total = row_max + jnp.log(jnp.sum(jnp.exp(scores - row_max), -1, keepdims=True))
    prob_low = jnp.exp(scores - log_total).astype(jnp.bfloat16)
    attended = jnp.einsum(
        "bhqk,bkhd->bqhd", prob_low, mixed_proj[:, :, 2], preferred_element_type=jnp.float32
    )
    attended = attended.astype(jnp.bfloat16).reshape(-1, width)
    after_attn = token_rows + matmul(attended, attn_out)
    normed_two, factor_two = normalize(after_attn, gain_rows[1])
    act_two = normed_two.astype(jnp.bfloat16)
    pre_act = matmul(act_two, ffn_in)
    hidden = jax.nn.gelu(pre_act).astype(jnp.bfloat16)
    final_rows = after_attn + matmul(hidden, ffn_out)
    kept = (
        token_rows,
        factor_one,
        act_one,
        mixed_proj,
        log_total,
        attended,
        after_attn,
        factor_two,
        act_two,
        pre_act,
        hidden,
    )
    return (final_rows, kept)


def layer_backward(grad_final, kept, mask_rows, weights, gain_rows, bias_full):
    (
        token_rows,
        factor_one,
        act_one,
        mixed_proj,
        log_total,
        attended,
        after_attn,
        factor_two,
        act_two,
        pre_act,
        hidden,
    ) = kept
    attn_in, attn_out, ffn_in, ffn_out = weights
    seq_count, length = mask_rows.shape
    branch = grad_final.astype(jnp.bfloat16)
    grad_ffn_out = matmul_tn(hidden, branch)
    grad_hidden = matmul_nt(branch, ffn_out)
    _, gelu_pull = jax.vjp(jax.nn.gelu, pre_act)
    grad_pre = gelu_pull(grad_hidden)[0].astype(jnp.bfloat16)
    grad_ffn_in = matmul_tn(act_two, grad_pre)
    grad_act_two = matmul_nt(grad_pre, ffn_in)
    grad_mid, gain_two = normalize_back(grad_act_two, after_attn, factor_two, gain_rows[1])
    grad_after = grad_final + grad_mid
    branch = grad_after.astype(jnp.bfloat16)
    grad_attn_out = matmul_tn(attended, branch)
    grad_attended = (
        matmul_nt(branch, attn_out).astype(jnp.bfloat16).reshape(seq_count, length, HEADS, HD)
    )
    scores = attention_scores(mixed_proj, mask_rows, bias_full)
    prob_full = jnp.exp(scores - log_total)
    prob_low = prob_full.astype(jnp.bfloat16)
    queries = mixed_proj[:, :, 0]
    key_rows = mixed_proj[:, :, 1]
    grad_probs = jnp.einsum(
        "bqhd,bkhd->bhqk", grad_attended, mixed_proj[:, :, 2], preferred_element_type=jnp.float32
    )
    grad_values = jnp.einsum(
        "bhqk,bqhd->bkhd", prob_low, grad_attended, preferred_element_type=jnp.float32
    )
    grad_scores = prob_full * (grad_probs - jnp.sum(prob_full * grad_probs, -1, keepdims=True))
    grad_scores = grad_scores.astype(jnp.bfloat16)
    grad_bias = jnp.sum(grad_scores, 0, dtype=jnp.float32)
    grad_queries = (
        jnp.einsum("bhqk,bkhd->bqhd", grad_scores, key_rows, preferred_element_type=jnp.float32)
        * SCALE
    )
    grad_keys = (
        jnp.einsum("bhqk,bqhd->bkhd", grad_scores, queries, preferred_element_type=jnp.float32)
        * SCALE
    )
    grad_mixed = (
        jnp.stack([grad_queries, grad_keys, grad_values], 2)
        .astype(jnp.bfloat16)
        .reshape(seq_count * length, -1)
    )
    grad_attn_in = matmul_tn(act_one, grad_mixed)
    grad_act_one = matmul_nt(grad_mixed, attn_in)
    grad_low, gain_one = normalize_back(grad_act_one, token_rows, factor_one, gain_rows[0])
    grad_rows = grad_after + grad_low
    return (
        grad_rows,
        (grad_attn_in, grad_attn_out, grad_ffn_in, grad_ffn_out),
        gain_one,
        gain_two,
        grad_bias,
    )


def adam_update(param, first_moment, second_moment, gradient, factor, rate, decay):
    clipped = gradient * factor
    first_new = BETA_ONE * first_moment + (1.0 - BETA_ONE) * clipped
    second_new = BETA_TWO * second_moment + (1.0 - BETA_TWO) * clipped * clipped
    direction = (
        first_new
        / (1.0 - BETA_ONE**STEP)
        / (jnp.sqrt(second_new / (1.0 - BETA_TWO**STEP)) + ADAM_EPS)
    )
    return (first_new, second_new, param - rate * (direction + decay * param))


def body(
    token_ids,
    pad_mask,
    hard_negative,
    table,
    table_first,
    table_second,
    attn_in,
    attn_in_first,
    attn_in_second,
    attn_out,
    attn_out_first,
    attn_out_second,
    ffn_in,
    ffn_in_first,
    ffn_in_second,
    ffn_out,
    ffn_out_first,
    ffn_out_second,
    proj_head,
    proj_head_first,
    proj_head_second,
    small_params,
    small_first,
    small_second,
):
    dp_count = lax.axis_size("dp")
    fsdp_count = lax.axis_size("fsdp")
    device_flat = lax.axis_index("dp") * fsdp_count + lax.axis_index("fsdp")
    pairs_here = token_ids.shape[1]
    pairs_total = pairs_here * dp_count * fsdp_count
    seq_count = 2 * pairs_here
    vocab_rows = table.shape[0]
    row_base = lax.axis_index("dp") * vocab_rows
    gain_rows = small_params[: 3 * D].reshape(3, D)
    bias_table = small_params[3 * D : 3 * D + NB * HEADS].reshape(NB, HEADS)
    log_scale = small_params[3 * D + NB * HEADS]
    buckets = jnp.asarray(bucket_table(L, NB).reshape(-1), jnp.int32)
    bucket_hot = (buckets[:, None] == jnp.arange(NB, dtype=jnp.int32)[None, :]).astype(jnp.float32)
    bias_full = (
        jnp.dot(bucket_hot, bias_table, precision=HIGH).reshape(L, L, HEADS).transpose(2, 0, 1)
    )
    mask_rows = pad_mask.reshape(seq_count, L)
    ids_flat = token_ids.reshape(-1)
    table_low = table.astype(jnp.bfloat16)
    ids_all = lax.all_gather(ids_flat, "dp", axis=0, tiled=True)
    picked = ids_all - row_base
    inside = (picked >= 0) & (picked < vocab_rows)
    chosen = jnp.take(table_low, jnp.clip(picked, 0, vocab_rows - 1), axis=0)
    embedded = lax.psum_scatter(
        jnp.where(inside[:, None], chosen.astype(jnp.float32), 0.0).astype(jnp.bfloat16),
        "dp",
        scatter_dimension=0,
        tiled=True,
    ).astype(jnp.float32)
    shards = (
        attn_in.astype(jnp.bfloat16),
        attn_out.astype(jnp.bfloat16),
        ffn_in.astype(jnp.bfloat16),
        ffn_out.astype(jnp.bfloat16),
        proj_head.astype(jnp.bfloat16),
    )
    gathered = (
        lax.all_gather(shards[0], ("dp", "fsdp"), axis=0, tiled=True),
        lax.all_gather(shards[1], ("dp", "fsdp"), axis=0, tiled=True),
        lax.all_gather(shards[2], ("dp", "fsdp"), axis=0, tiled=True),
        lax.all_gather(shards[3], ("dp", "fsdp"), axis=0, tiled=True),
        lax.all_gather(shards[4], ("dp", "fsdp"), axis=0, tiled=True),
    )
    final_rows, kept = layer_forward(embedded, mask_rows, gathered[:4], gain_rows, bias_full)
    normed_three, factor_three = normalize(final_rows, gain_rows[2])
    mask_weight = mask_rows.astype(jnp.float32)[:, :, None]
    counts = jnp.sum(mask_weight, 1)
    pooled = jnp.sum(normed_three.reshape(seq_count, L, D) * mask_weight, 1) / counts
    pooled_low = pooled.astype(jnp.bfloat16)
    projected = matmul(pooled_low, gathered[4])
    proj_factor = lax.rsqrt(jnp.sum(projected * projected, -1, keepdims=True) + EPS)
    unit_rows = projected * proj_factor
    unit_low = unit_rows.astype(jnp.bfloat16)
    mine_query = unit_low[:pairs_here]
    all_pass = lax.all_gather(unit_low[pairs_here:], ("dp", "fsdp"), axis=0, tiled=True)
    similar = matmul_nt(mine_query, all_pass)
    sim_scale = jnp.exp(log_scale)
    columns = jnp.arange(pairs_total, dtype=jnp.int32)
    own_index = device_flat * pairs_here + jnp.arange(pairs_here, dtype=jnp.int32)
    own_mask = (columns[None, :] == own_index[:, None]).astype(jnp.float32)
    negative = (columns[None, :] == hard_negative[:, None]).astype(jnp.float32)
    logits = sim_scale * similar - MARGIN * own_mask
    diagonal = jnp.sum(logits * own_mask, 1)
    hardest = jnp.sum(logits * negative, 1)
    row_max = jnp.max(logits, 1, keepdims=True)
    log_total = row_max + jnp.log(jnp.sum(jnp.exp(logits - row_max), 1, keepdims=True))
    loss_local = jnp.sum(log_total[:, 0] - diagonal + jax.nn.softplus(hardest - diagonal))
    hinge_gate = jax.nn.sigmoid(hardest - diagonal)
    grad_logits = (
        jnp.exp(logits - log_total) - own_mask + hinge_gate[:, None] * (negative - own_mask)
    )
    grad_log_scale = sim_scale * jnp.sum(grad_logits * similar)
    grad_similar = (sim_scale * grad_logits).astype(jnp.bfloat16)
    grad_query = matmul(grad_similar, all_pass).astype(jnp.bfloat16)
    grad_pass_terms = matmul_tn(grad_similar, mine_query)
    grad_pass = lax.psum_scatter(
        grad_pass_terms, ("dp", "fsdp"), scatter_dimension=0, tiled=True
    ).astype(jnp.bfloat16)
    grad_units = jnp.concatenate([grad_query, grad_pass], 0).astype(jnp.float32)
    grad_proj = (
        proj_factor * (grad_units - unit_rows * jnp.sum(grad_units * unit_rows, -1, keepdims=True))
    ).astype(jnp.bfloat16)
    gathered_back = (
        lax.all_gather(shards[0], ("dp", "fsdp"), axis=0, tiled=True),
        lax.all_gather(shards[1], ("dp", "fsdp"), axis=0, tiled=True),
        lax.all_gather(shards[2], ("dp", "fsdp"), axis=0, tiled=True),
        lax.all_gather(shards[3], ("dp", "fsdp"), axis=0, tiled=True),
        lax.all_gather(shards[4], ("dp", "fsdp"), axis=0, tiled=True),
    )
    grad_proj_head = matmul_tn(pooled_low, grad_proj)
    grad_pooled = matmul_nt(grad_proj, gathered_back[4])
    grad_normed = ((grad_pooled / counts)[:, None, :] * mask_weight).reshape(-1, D)
    grad_final, gain_three = normalize_back(grad_normed, final_rows, factor_three, gain_rows[2])
    grad_rows, matrix_grads, gain_one, gain_two, grad_bias = layer_backward(
        grad_final, kept, mask_rows, gathered_back[:4], gain_rows, bias_full
    )
    attn_in_grad, attn_out_grad, ffn_in_grad, ffn_out_grad = matrix_grads
    grad_bias_table = jnp.dot(grad_bias.reshape(HEADS, L * L), bucket_hot, precision=HIGH).T
    small_local = jnp.concatenate(
        [gain_one, gain_two, gain_three, grad_bias_table.reshape(-1), grad_log_scale[None]]
    )
    small_grad = lax.psum(small_local, ("dp", "fsdp"))
    weight_grads = (
        lax.psum_scatter(attn_in_grad, ("dp", "fsdp"), scatter_dimension=0, tiled=True),
        lax.psum_scatter(attn_out_grad, ("dp", "fsdp"), scatter_dimension=0, tiled=True),
        lax.psum_scatter(ffn_in_grad, ("dp", "fsdp"), scatter_dimension=0, tiled=True),
        lax.psum_scatter(ffn_out_grad, ("dp", "fsdp"), scatter_dimension=0, tiled=True),
        lax.psum_scatter(grad_proj_head, ("dp", "fsdp"), scatter_dimension=0, tiled=True),
    )
    rows_back = lax.all_gather(grad_rows.astype(jnp.bfloat16), "dp", axis=0, tiled=True)
    turn_count = dp_count // 4
    block_rows = rows_back.shape[0] // turn_count

    def add_block(running, piece_pair):
        block_grads, block_ids = piece_pair
        local_ids = block_ids - row_base
        inside = (local_ids >= 0) & (local_ids < vocab_rows)
        segment = jnp.where(inside, local_ids, vocab_rows)
        summed = jax.ops.segment_sum(
            block_grads.astype(jnp.float32), segment, num_segments=vocab_rows + 1
        )
        return (running + summed[:vocab_rows], None)

    table_full, _ = lax.scan(
        add_block,
        jnp.zeros((vocab_rows, D), jnp.float32),
        (rows_back.reshape(turn_count, block_rows, D), ids_all.reshape(turn_count, block_rows)),
    )
    table_grad = lax.psum(table_full.astype(jnp.bfloat16), "fsdp").astype(jnp.float32)
    owned = (table_grad,) + tuple(weight_grads)
    squares = jnp.sum(table_grad * table_grad) / fsdp_count
    for gradient in weight_grads:
        squares = squares + jnp.sum(gradient * gradient)
    total_squares, loss_sum = lax.psum((squares, loss_local), ("dp", "fsdp"))
    norm_value = jnp.sqrt(total_squares + jnp.sum(small_grad * small_grad))
    factor = jnp.minimum(1.0, CLIP / (norm_value + 1e-06))
    masters = (table, attn_in, attn_out, ffn_in, ffn_out, proj_head, small_params)
    firsts = (
        table_first,
        attn_in_first,
        attn_out_first,
        ffn_in_first,
        ffn_out_first,
        proj_head_first,
        small_first,
    )
    seconds = (
        table_second,
        attn_in_second,
        attn_out_second,
        ffn_in_second,
        ffn_out_second,
        proj_head_second,
        small_second,
    )
    gradients = owned + (small_grad,)
    results = [loss_sum, norm_value]
    for kind_index in range(7):
        results.extend(
            adam_update(
                masters[kind_index],
                firsts[kind_index],
                seconds[kind_index],
                gradients[kind_index],
                factor,
                RATES[kind_index],
                DECAYS[kind_index],
            )
        )
    return tuple(results)


def solution(mesh):
    return jax.shard_map(
        body,
        mesh=mesh,
        in_specs=(
            P(None, ("dp", "fsdp"), None),
            P(None, ("dp", "fsdp"), None),
            P(("dp", "fsdp")),
            P("dp", None),
            P("dp", None),
            P("dp", None),
            P(("dp", "fsdp"), None),
            P(("dp", "fsdp"), None),
            P(("dp", "fsdp"), None),
            P(("dp", "fsdp"), None),
            P(("dp", "fsdp"), None),
            P(("dp", "fsdp"), None),
            P(("dp", "fsdp"), None),
            P(("dp", "fsdp"), None),
            P(("dp", "fsdp"), None),
            P(("dp", "fsdp"), None),
            P(("dp", "fsdp"), None),
            P(("dp", "fsdp"), None),
            P(("dp", "fsdp"), None),
            P(("dp", "fsdp"), None),
            P(("dp", "fsdp"), None),
            P(),
            P(),
            P(),
        ),
        out_specs=(
            P(),
            P(),
            P("dp", None),
            P("dp", None),
            P("dp", None),
            P(("dp", "fsdp"), None),
            P(("dp", "fsdp"), None),
            P(("dp", "fsdp"), None),
            P(("dp", "fsdp"), None),
            P(("dp", "fsdp"), None),
            P(("dp", "fsdp"), None),
            P(("dp", "fsdp"), None),
            P(("dp", "fsdp"), None),
            P(("dp", "fsdp"), None),
            P(("dp", "fsdp"), None),
            P(("dp", "fsdp"), None),
            P(("dp", "fsdp"), None),
            P(("dp", "fsdp"), None),
            P(("dp", "fsdp"), None),
            P(("dp", "fsdp"), None),
            P(),
            P(),
            P(),
        ),
        check_vma=False,
    )
```

profile of v0, /device:TPU:0, one launch (start us, length us, event | category | flops | bytes accessed | tf_op | source)
XLA Modules:
  0.0 1518.7 jit_solution(13584898019026313764)
XLA Ops:
  8.1 32.3 %all_gather.29 = s32[8192]{0:T(1024)S(1)} all-gather(s32[1024]{0:T(1024)} %bitcast.164), channel_id=1, replica_groups=mesh['dp'=8,'fsdp'=4] {'dp'}, dimensions={0}, use_global_device_ids=true | all-gather | bytes 36864 | tf_op jit(solution)/shard_map/all_gather | solution.py:249
  48.2 40.7 %gather_fusion = bf16[8192,768]{1,0:T(8,128)(2,1)} fusion(bf16[4016,768]{1,0:T(8,128)(2,1)} %convert_element_type.130, s32[8192]{0:T(1024)S(1)} %fusion.79), kind=kCustom, calls=%fused_computation | custom fusion | bytes 25198592 | tf_op jit(solution)/shard_map/jit(_take)/gather | solution.py:252
  89.0 13.3 select_convert_fusion
  109.5 210.6 %reduce-scatter.7.cloned.1.call-done = bf16[1024,768]{1,0:T(8,128)(2,1)} async-done(((bf16[8192,768]{1,0:T(8,128)(2,1)}), bf16[1024,768]{1,0:T(8,128)(2,1)}) %reduce-scatter.7.cloned.1.call-update) | async-done | bytes 1572880 | tf_op jit(solution)/shard_map/reduce_scatter | solution.py:253
  353.8 54.4 %all-gather.12.cloned.1.call-done = bf16[768,3072]{1,0:T(8,128)(2,1)} async-done(((bf16[24,3072]{1,0:T(8,128)(2,1)}), bf16[768,3072]{1,0:T(8,128)(2,1)}) %all-gather.12.cloned.1.call-update) | async-done | bytes 4718608 | tf_op jit(solution)/shard_map/all_gather | solution.py:269
  408.2 11.0 fusion.93
  419.1 54.6 %all-gather.14.cloned.1.call-done = bf16[3072,768]{1,0:T(8,128)(2,1)} async-done(((bf16[96,768]{1,0:T(8,128)(2,1)}), bf16[3072,768]{1,0:T(8,128)(2,1)}) %all-gather.14.cloned.1.call-update) | async-done | bytes 4718608 | tf_op jit(solution)/shard_map/all_gather | solution.py:270
  473.7 12.5 multiply_reduce_fusion.4
  486.9 42.9 %all-gather.16.cloned.1.call-done = bf16[768,768]{1,0:T(8,128)(2,1)} async-done(((bf16[24,768]{1,0:T(8,128)(2,1)}), bf16[768,768]{1,0:T(8,128)(2,1)}) %all-gather.16.cloned.1.call-update) | async-done | bytes 1179664 | tf_op jit(solution)/shard_map/all_gather | solution.py:271
  531.5 42.6 %all-gather = bf16[32,4,768]{2,1,0:T(4,128)(2,1)} all-gather(bf16[1,4,768]{2,1,0:T(4,128)(2,1)S(1)} %slice_bitcast_fusion), channel_id=1, replica_groups=mesh['dp'=8,'fsdp'=4] {'dp','fsdp'}, dimensions={0}, use_global_device_ids=true | all-gather | bytes 202752 | tf_op jit(solution)/shard_map/all_gather | solution.py:284
  578.1 40.6 %all-reduce.6 = bf16[128,768]{1,0:T(8,128)(2,1)S(1)} all-reduce(f32[128,768]{1,0:T(8,128)} %fusion.82), channel_id=3, replica_groups=mesh['dp'=8,'fsdp'=4] {'dp','fsdp'}, use_global_device_ids=true, to_apply=%region_15.16.clone | all-reduce | flops 98304 | bytes 589824
  623.2 15.0 fusion.12
  703.3 12.5 fusion.94
  729.1 133.0 %all-gather.18.cloned.1.call-done = bf16[8192,768]{1,0:T(8,128)(2,1)} async-done(((bf16[1024,768]{1,0:T(8,128)(2,1)}), bf16[8192,768]{1,0:T(8,128)(2,1)}) %all-gather.18.cloned.1.call-update) | async-done | bytes 12582928 | tf_op jit(solution)/shard_map/all_gather | solution.py:339
  862.1 92.0 %while.11 = (s32[]{:T(128)}, f32[4016,768]{1,0:T(8,128)}, s32[2,4096]{1,0:T(2,128)S(1)}, s32[]{:T(128)}, bf16[2,4096,768]{2,1,0:T(8,128)(2,1)}, /*index=5*/s32[]{:T(128)}, s32[]{:T(128)}, f32[]{:T(128)}) while((s32[]{:T(128)}, f32[4016,768]{1,0:T(8,128)}, s32[2,4096]{1,0:T(2,128)S(1)}, s32[]{:T(128)}, ...), condition=%wide.region_23.24_spmd.clone, body=%wide.region_21.23_spmd.clone.sunk | while | flops 12480515 | bytes 55677540 | solution.py:353
  862.3 33.5 %scatter_custom_fusion.6 = f32[4017,768]{1,0:T(8,128)} fusion(s32[4096]{0:T(1024)S(1)} %bitcast.158, bf16[2,4096,768]{2,1,0:T(8,128)(2,1)} %get-tuple-element.198, s32[]{:T(128)} %get-tuple-element.186, s32[]{:T(128)} %constant.46.clone.1..sunk, f32[]{:T(128)} %constant.49.clone.1..sunk), kind=kCustom, calls=%fused_computation.2.clone.1 | custom fusion | flops 6291456 | bytes 18633216 | tf_op jit(solution)/shard_map/while/body/eval_jaxpr/scatter-add | solution.py:348
  906.5 33.6 %scatter_custom_fusion.6 = f32[4017,768]{1,0:T(8,128)} fusion(s32[4096]{0:T(1024)S(1)} %bitcast.158, bf16[2,4096,768]{2,1,0:T(8,128)(2,1)} %get-tuple-element.198, s32[]{:T(128)} %get-tuple-element.186, s32[]{:T(128)} %constant.46.clone.1..sunk, f32[]{:T(128)} %constant.49.clone.1..sunk), kind=kCustom, calls=%fused_computation.2.clone.1 | custom fusion | flops 6291456 | bytes 18633216 | tf_op jit(solution)/shard_map/while/body/eval_jaxpr/scatter-add | solution.py:348
  940.1 14.0 slice_add_fusion.2
  967.6 30.8 %reduce-scatter.11.cloned.1.call-done = f32[24,768]{1,0:T(8,128)} async-done(((f32[768,768]{1,0:T(8,128)}), f32[24,768]{1,0:T(8,128)}) %reduce-scatter.11.cloned.1.call-update) | async-done | bytes 73744 | tf_op jit(solution)/shard_map/reduce_scatter | solution.py:334
  1000.0 138.2 %reduce-scatter.9.cloned.1.call-done = f32[24,2304]{1,0:T(8,128)} async-done(((f32[768,2304]{1,0:T(8,128)}), f32[24,2304]{1,0:T(8,128)}) %reduce-scatter.9.cloned.1.call-update) | async-done | bytes 221200 | tf_op jit(solution)/shard_map/reduce_scatter | solution.py:333
  1139.8 139.5 %reduce-scatter.15.cloned.1.call-done = f32[96,768]{1,0:T(8,128)} async-done(((f32[3072,768]{1,0:T(8,128)}), f32[96,768]{1,0:T(8,128)}) %reduce-scatter.15.cloned.1.call-update) | async-done | bytes 294928 | tf_op jit(solution)/shard_map/reduce_scatter | solution.py:336
  1281.0 140.5 %reduce-scatter.13.cloned.1.call-done = f32[24,3072]{1,0:T(8,128)} async-done(((f32[768,3072]{1,0:T(8,128)}), f32[24,3072]{1,0:T(8,128)}) %reduce-scatter.13.cloned.1.call-update) | async-done | bytes 294928 | tf_op jit(solution)/shard_map/reduce_scatter | solution.py:335
  1433.8 40.1 %all-reduce.1 = (f32[]{:T(128)}, f32[]{:T(128)}, f32[2689]{0:T(1024)S(1)}) all-reduce(f32[]{:T(128)} %get-tuple-element.116, f32[]{:T(128)S(6)} %add.308, f32[2689]{0:T(1024)S(1)} %constant_dynamic-update-slice_fusion), channel_id=1, replica_groups=mesh['dp'=8,'fsdp'=4] {'dp','fsdp'}, use_global_device_ids=true, to_apply=%region_14.15 | all-reduce | flops 2691 | bytes 21528 | tf_op jit(solution)/shard_map/psum | solution.py:363
  1479.8 29.5 %multiply_subtract_fusion = (f32[4016,768]{1,0:T(8,128)}, f32[4016,768]{1,0:T(8,128)}, f32[4016,768]{1,0:T(8,128)}) fusion(f32[4016,768]{1,0:T(8,128)} %param.30, f32[]{:T(128)S(6)} %min.13, bf16[4016,768]{1,0:T(8,128)(2,1)} %all-reduce.5.cloned.1.call-done, f32[4016,768]{1,0:T(8,128)} %param.32, f32[4016,768]{1,0:T(8,128)} %param.31), kind=kLoop, calls=%fused_computation.27 | loop fusion | flops 52432896 | bytes 80191488 | tf_op jit(solution)/shard_map/sub | solution.py:201
  (257 shorter events, 178.4 us)
Async XLA Ops:
  8.0 312.2 %reduce-scatter.7.cloned.1.call-start = ((), (), s32[]{:S(2)}) async-start(), calls=%async_computation.6 | async-start | bytes 14155776 | tf_op jit(solution)/shard_map/reduce_scatter | solution.py:253
  102.3 219.7 %all-gather.8.cloned.1.call-start = ((), (), s32[]{:S(2)}) async-start(), calls=%async_computation.7 | async-start | bytes 3649536 | tf_op jit(solution)/shard_map/all_gather | solution.py:267
  103.8 244.9 %all-gather.10.cloned.1.call-start = ((), (), s32[]{:S(2)}) async-start(), calls=%async_computation.8 | async-start | bytes 1216512 | tf_op jit(solution)/shard_map/all_gather | solution.py:268
  104.6 303.6 %all-gather.12.cloned.1.call-start = ((), (), s32[]{:S(2)}) async-start(), calls=%async_computation.9 | async-start | bytes 4866048 | tf_op jit(solution)/shard_map/all_gather | solution.py:269
  105.3 368.4 %all-gather.14.cloned.1.call-start = ((), (), s32[]{:S(2)}) async-start(), calls=%async_computation.10 | async-start | bytes 4866048 | tf_op jit(solution)/shard_map/all_gather | solution.py:270
  106.1 423.6 %all-gather.16.cloned.1.call-start = ((), (), s32[]{:S(2)}) async-start(), calls=%async_computation.11 | async-start | bytes 1216512 | tf_op jit(solution)/shard_map/all_gather | solution.py:271
  106.8 755.3 %all-gather.18.cloned.1.call-start = ((), (), s32[]{:S(2)}) async-start(), calls=%async_computation.12 | async-start | bytes 14155776 | tf_op jit(solution)/shard_map/all_gather | solution.py:339
  486.2 89.2 %copy-start.55 = (s32[4]{0:T(128)S(1)}, s32[4]{0:T(128)}, u32[]{:S(2)}) copy-start(s32[4]{0:T(128)} %param.29) | copy-start | bytes 52
  684.8 281.3 %reduce-scatter.17.cloned.1.call-start = ((), (), s32[]{:S(2)}) async-start(), calls=%async_computation.18 | async-start | bytes 2433024 | tf_op jit(solution)/shard_map/reduce_scatter | solution.py:337
  686.9 311.6 %reduce-scatter.11.cloned.1.call-start = ((), (), s32[]{:S(2)}) async-start(), calls=%async_computation.15 | async-start | bytes 2433024 | tf_op jit(solution)/shard_map/reduce_scatter | solution.py:334
  691.1 447.1 %reduce-scatter.9.cloned.1.call-start = ((), (), s32[]{:S(2)}) async-start(), calls=%async_computation.14 | async-start | bytes 7299072 | tf_op jit(solution)/shard_map/reduce_scatter | solution.py:333
  701.9 577.4 %reduce-scatter.15.cloned.1.call-start = ((), (), s32[]{:S(2)}) async-start(), calls=%async_computation.17 | async-start | bytes 9732096 | tf_op jit(solution)/shard_map/reduce_scatter | solution.py:336
  715.8 705.6 %reduce-scatter.13.cloned.1.call-start = ((), (), s32[]{:S(2)}) async-start(), calls=%async_computation.16 | async-start | bytes 9732096 | tf_op jit(solution)/shard_map/reduce_scatter | solution.py:335
  728.4 694.8 %all-reduce.5.cloned.1.call-start = ((), (), s32[]{:S(2)}) async-start(), calls=%async_computation.13 | async-start | bytes 12337152 | tf_op jit(solution)/shard_map/psum | solution.py:358
  1423.1 52.9 %copy-start.52 = (f32[2689]{0:T(1024)S(1)}, f32[2689]{0:T(1024)}, u32[]{:S(2)}) copy-start(f32[2689]{0:T(1024)} %param.50) | copy-start | bytes 32272
  1423.1 52.9 %copy-start.53 = (f32[2689]{0:T(1024)S(1)}, f32[2689]{0:T(1024)}, u32[]{:S(2)}) copy-start(f32[2689]{0:T(1024)} %param.49) | copy-start | bytes 32272
  1423.1 53.5 %copy-start.20 = (f32[96,768]{1,0:T(8,128)S(1)}, f32[96,768]{1,0:T(8,128)}, u32[]{:S(2)}) copy-start(f32[96,768]{1,0:T(8,128)} %param.42) | copy-start | bytes 884740
  1423.1 53.5 %copy-start.23 = (f32[96,768]{1,0:T(8,128)S(1)}, f32[96,768]{1,0:T(8,128)}, u32[]{:S(2)}) copy-start(f32[96,768]{1,0:T(8,128)} %reduce-scatter.15.cloned.1.call-done) | copy-start | bytes 884740
  1423.1 53.5 %copy-start.30 = (f32[96,768]{1,0:T(8,128)S(1)}, f32[96,768]{1,0:T(8,128)}, u32[]{:S(2)}) copy-start(f32[96,768]{1,0:T(8,128)} %param.44) | copy-start | bytes 884740
  1423.1 53.5 %copy-start.31 = (f32[96,768]{1,0:T(8,128)S(1)}, f32[96,768]{1,0:T(8,128)}, u32[]{:S(2)}) copy-start(f32[96,768]{1,0:T(8,128)} %param.43) | copy-start | bytes 884740
  1423.1 54.6 %copy-start.22 = (f32[24,3072]{1,0:T(8,128)S(1)}, f32[24,3072]{1,0:T(8,128)}, u32[]{:S(2)}) copy-start(f32[24,3072]{1,0:T(8,128)} %param.39) | copy-start | bytes 884740
  1423.1 54.6 %copy-start.24 = (f32[24,3072]{1,0:T(8,128)S(1)}, f32[24,3072]{1,0:T(8,128)}, u32[]{:S(2)}) copy-start(f32[24,3072]{1,0:T(8,128)} %reduce-scatter.13.cloned.1.call-done) | copy-start | bytes 884740
  1423.1 54.6 %copy-start.32 = (f32[24,3072]{1,0:T(8,128)S(1)}, f32[24,3072]{1,0:T(8,128)}, u32[]{:S(2)}) copy-start(f32[24,3072]{1,0:T(8,128)} %param.41) | copy-start | bytes 884740
  1423.1 54.6 %copy-start.33 = (f32[24,3072]{1,0:T(8,128)S(1)}, f32[24,3072]{1,0:T(8,128)}, u32[]{:S(2)}) copy-start(f32[24,3072]{1,0:T(8,128)} %param.40) | copy-start | bytes 884740
  (52 other events, 676.4 us)
Sparse Core Ops, SparseCore 0:
  102.4 217.7 reduce-scatter.6
  684.9 177.1 all-gather.17
  962.0 130.1 all-reduce.4
Sparse Core Ops, SparseCore 1:
  106.3 139.0 all-gather.7
  248.7 93.3 all-gather.9
  345.5 62.6 all-gather.11
  411.7 62.0 all-gather.13
  477.3 52.4 all-gather.15
  691.7 190.7 reduce-scatter.16
  887.6 110.9 reduce-scatter.10
  1005.0 133.2 reduce-scatter.8
  1144.6 134.7 reduce-scatter.14
  1286.8 134.5 reduce-scatter.12
where the time goes:
time: 1530 us; the launch traced here: 1520 us
  waiting for transfers between devices  945 us (62%)
  other arithmetic  189 us (12%)
  blocking collectives  156 us (10%)
  matrix products  127 us (8%)
  local copies, waits for them, and re-layouts  76.6 us (5%)
  between operations  24.5 us (2%)
    reduce_scatter x1, waiting for transfers between devices, body(): lax.psum_scatter(jnp.where(inside[:, None], chosen.astype(jnp.float32), 0...  211 us
    reduce_scatter x1, waiting for transfers between devices, body(): lax.psum_scatter(ffn_in_grad, ('dp', 'fsdp'), scatter_dimension=0, tiled=...  140 us
    reduce_scatter x1, waiting for transfers between devices, body(): lax.psum_scatter(ffn_out_grad, ('dp', 'fsdp'), scatter_dimension=0, tiled...  140 us
    reduce_scatter x1, waiting for transfers between devices, body(): lax.psum_scatter(attn_in_grad, ('dp', 'fsdp'), scatter_dimension=0, tiled...  138 us
    all_gather x1, waiting for transfers between devices, body(): lax.all_gather(grad_rows.astype(jnp.bfloat16), 'dp', axis=0, tiled=True)  133 us
    scatter-add x2, other arithmetic, add_block(): jax.ops.segment_sum(block_grads.astype(jnp.float32), segment, num_segment...  67.1 us
    all_gather x1, waiting for transfers between devices, body(): lax.all_gather(shards[3], ('dp', 'fsdp'), axis=0, tiled=True)  54.6 us
    all_gather x1, waiting for transfers between devices, body(): lax.all_gather(shards[2], ('dp', 'fsdp'), axis=0, tiled=True)  54.4 us
  transfers between devices with their start and end apart: 13, of which 9 were waited for; matrix products, arithmetic and copies ran while one was open for 14% of the time, Pallas kernels for 0%

commit v1 on v0

--- a/solution.py
+++ b/solution.py
@@ -1,7 +1,11 @@
+import functools
+
 import jax
 import jax.numpy as jnp
 import numpy as np
 from jax import lax
+from jax.experimental import pallas as pl
+from jax.experimental.pallas import tpu as pltpu
 from jax.sharding import PartitionSpec as P
 
 D = 768
@@ -22,6 +26,8 @@
 RATES = (3.0, 0.1, 0.2, 0.1, 0.05, 0.1, 1.0)
 DECAYS = (0.001, 0.001, 0.001, 0.001, 0.001, 0.001, 0.0)
 HIGH = lax.Precision.HIGHEST
+MESH = pl.DeviceIdType.MESH
+CAP = 128
 
 
 def bucket_table(length, count):
@@ -201,7 +207,640 @@
     return (first_new, second_new, param - rate * (direction + decay * param))
 
 
-def body(
+class Grid:
+    def __init__(self):
+        self.dp, self.fs = lax.axis_size("dp"), lax.axis_size("fsdp")
+        self.total = self.dp * self.fs
+        self.wide = self.fs // 2
+        self.tall = self.dp // self.wide
+
+    def here(self):
+        d, f = lax.axis_index("dp"), lax.axis_index("fsdp")
+        return d // self.wide, lax.rem(d, self.wide), f // 2, lax.rem(f, 2)
+
+    def device(self, z, x, y, core):
+        return (z * self.wide + x, y * 2 + core)
+
+    def flat(self, z, x, y, core):
+        return (z * self.wide + x) * self.fs + y * 2 + core
+
+    def peer(self, index):
+        return (index // self.fs, lax.rem(index, self.fs))
+
+
+def greet(device, when=None):
+    barrier = pltpu.get_barrier_semaphore()
+
+    def signal():
+        pl.semaphore_signal(barrier, inc=1, device_id=device, device_id_type=MESH)
+
+    if when is None:
+        signal()
+    else:
+        pl.when(when)(signal)
+
+
+def meet(count):
+    pl.semaphore_wait(pltpu.get_barrier_semaphore(), count)
+
+
+def exchange_kernel(grid, spread, src, out, send_sem, recv_sem, own_sem):
+    me = lax.axis_index("dp") * grid.fs + lax.axis_index("fsdp")
+    own = pltpu.make_async_copy(src.at[me] if spread else src, out.at[me], own_sem)
+    own.start()
+
+    @pl.loop(1, grid.total)
+    def _(step):
+        greet(grid.peer(lax.rem(me + step, grid.total)))
+
+    meet(count=grid.total - 1)
+
+    def copy(peer, slot):
+        return pltpu.make_async_remote_copy(
+            src_ref=src.at[peer] if spread else src,
+            dst_ref=out.at[slot],
+            send_sem=send_sem.at[peer],
+            recv_sem=recv_sem.at[slot],
+            device_id=grid.peer(peer),
+            device_id_type=MESH,
+        )
+
+    @pl.loop(1, grid.total)
+    def _(step):
+        copy(lax.rem(me + step, grid.total), me).start()
+
+    own.wait()
+
+    @pl.loop(1, grid.total)
+    def _(step):
+        peer = lax.rem(me + step, grid.total)
+        copy(peer, peer).wait_recv()
+        copy(peer, peer).wait_send()
+
+
+def exchange(src, spread, number):
+    grid = Grid()
+    block = src.shape[1:] if spread else src.shape
+    return pl.pallas_call(
+        functools.partial(exchange_kernel, grid, spread),
+        out_shape=jax.ShapeDtypeStruct((grid.total,) + block, src.dtype),
+        in_specs=[pl.BlockSpec(memory_space=pltpu.VMEM)],
+        out_specs=pl.BlockSpec(memory_space=pltpu.VMEM),
+        scratch_shapes=[
+            pltpu.SemaphoreType.DMA((grid.total,)),
+            pltpu.SemaphoreType.DMA((grid.total,)),
+            pltpu.SemaphoreType.DMA,
+        ],
+        compiler_params=pltpu.CompilerParams(collective_id=number, has_side_effects=True),
+    )(src)
+
+
+def gather_kernel(grid, count, *refs):
+    srcs, rows, outs, got_rows = refs[:count], refs[count], refs[count + 1 : 2 * count + 1], refs[2 * count + 1]
+    send_sem, recv_sem, own_sem, row_send, row_recv, row_own = refs[2 * count + 2 :]
+    z, x, y, core = grid.here()
+    tall = grid.tall
+    d, f = lax.axis_index("dp"), lax.axis_index("fsdp")
+    ux, uy = lax.rem(x + 1 - core, 2), lax.rem(y + core, 2)
+    vx, vy = lax.rem(x + core, 2), lax.rem(y + 1 - core, 2)
+    up, down = grid.device(z + 1, x, y, core), grid.device(z - 1, x, y, core)
+    u_device, v_device = grid.device(z, ux, uy, core), grid.device(z, vx, vy, core)
+    sibling = grid.device(z, x, y, 1 - core)
+    has_up, has_down = z < tall - 1, z > 0
+    me = grid.flat(z, x, y, core)
+    local = [pltpu.make_async_copy(srcs[m], outs[m].at[me], own_sem.at[m]) for m in range(count)]
+    local.append(pltpu.make_async_copy(rows.at[d], got_rows.at[d], row_own))
+    for item in local:
+        item.start()
+
+    @pl.loop(1, grid.dp)
+    def _(step):
+        greet((lax.rem(d + step, grid.dp), f))
+
+    greet(v_device)
+    greet(sibling)
+    greet(u_device)
+    meet(count=grid.dp + 2)
+
+    def row_copy(peer, slot):
+        return pltpu.make_async_remote_copy(
+            src_ref=rows.at[peer],
+            dst_ref=got_rows.at[slot],
+            send_sem=row_send.at[peer],
+            recv_sem=row_recv.at[slot],
+            device_id=(peer, f),
+            device_id_type=MESH,
+        )
+
+    def copy(m, shard, device, way, own):
+        return pltpu.make_async_remote_copy(
+            src_ref=srcs[m] if own else outs[m].at[shard],
+            dst_ref=outs[m].at[shard],
+            send_sem=send_sem.at[way, m, shard],
+            recv_sem=recv_sem.at[m, shard],
+            device_id=device,
+            device_id_type=MESH,
+        )
+
+    def send(shard, device, way, own=False):
+        for m in range(count):
+            copy(m, shard, device, way, own).start()
+
+    def arrived(shard):
+        for m in range(count):
+            copy(m, shard, sibling, 4, False).wait_recv()
+
+    def sent(shard, device, way):
+        for m in range(count):
+            copy(m, shard, device, way, False).wait_send()
+
+    @pl.when(has_up)
+    def _():
+        send(me, up, 0, True)
+
+    @pl.when(has_down)
+    def _():
+        send(me, down, 1, True)
+
+    send(me, u_device, 2, True)
+    send(me, v_device, 3, True)
+    send(me, sibling, 4, True)
+
+    @pl.loop(1, grid.dp)
+    def _(step):
+        row_copy(lax.rem(d + step, grid.dp), d).start()
+
+    def pass_z(k):
+        low, high = z - k, z + k
+
+        @pl.when(low >= 0)
+        def _():
+            shard = grid.flat(low, x, y, core)
+            arrived(shard)
+
+            @pl.when(has_up)
+            def _():
+                send(shard, up, 0)
+
+            send(shard, u_device, 2)
+            send(shard, v_device, 3)
+            send(shard, sibling, 4)
+
+        @pl.when(high < tall)
+        def _():
+            shard = grid.flat(high, x, y, core)
+            arrived(shard)
+
+            @pl.when(has_down)
+            def _():
+                send(shard, down, 1)
+
+            send(shard, u_device, 2)
+            send(shard, v_device, 3)
+            send(shard, sibling, 4)
+
+    def both(k, action):
+        pl.when(z - k >= 0)(lambda: action(z - k))
+        if k:
+            pl.when(z + k < tall)(lambda: action(z + k))
+
+    def pass_u(level):
+        shard = grid.flat(level, ux, uy, core)
+        arrived(shard)
+        send(shard, v_device, 3)
+        send(shard, sibling, 4)
+
+    def pass_v(level):
+        shard = grid.flat(level, vx, vy, core)
+        arrived(shard)
+        send(shard, sibling, 4)
+
+    def pass_far(level):
+        shard = grid.flat(level, 1 - x, 1 - y, core)
+        arrived(shard)
+        send(shard, sibling, 4)
+
+    for k in range(tall + 1):
+        if 0 < k < tall:
+            pass_z(k)
+        if k < tall:
+            both(k, pass_u)
+            both(k, pass_v)
+        if k:
+            both(k - 1, pass_far)
+
+    @pl.loop(1, grid.dp)
+    def _(step):
+        peer = lax.rem(d + step, grid.dp)
+        row_copy(peer, peer).wait_recv()
+        row_copy(peer, peer).wait_send()
+
+    @pl.loop(0, tall)
+    def _(level):
+        for xx in range(2):
+            for yy in range(2):
+                arrived(grid.flat(level, xx, yy, 1 - core))
+                sent(grid.flat(level, xx, yy, core), sibling, 4)
+        shard, other = grid.flat(level, x, y, core), grid.flat(level, ux, uy, core)
+
+        @pl.when((level <= z) & has_up)
+        def _():
+            sent(shard, up, 0)
+
+        @pl.when((level >= z) & has_down)
+        def _():
+            sent(shard, down, 1)
+
+        sent(shard, u_device, 2)
+        sent(shard, v_device, 3)
+        sent(other, v_device, 3)
+
+    for item in local:
+        item.wait()
+
+
+def gather(srcs, rows, number):
+    grid = Grid()
+    count = len(srcs)
+    anywhere = pl.BlockSpec(memory_space=pl.ANY)
+    results = pl.pallas_call(
+        functools.partial(gather_kernel, grid, count),
+        out_shape=[jax.ShapeDtypeStruct((grid.total,) + src.shape, src.dtype) for src in srcs]
+        + [jax.ShapeDtypeStruct(rows.shape, rows.dtype)],
+        in_specs=[anywhere] * (count + 1),
+        out_specs=[anywhere] * (count + 1),
+        scratch_shapes=[
+            pltpu.SemaphoreType.DMA((5, count, grid.total)),
+            pltpu.SemaphoreType.DMA((count, grid.total)),
+            pltpu.SemaphoreType.DMA((count,)),
+            pltpu.SemaphoreType.DMA((grid.dp,)),
+            pltpu.SemaphoreType.DMA((grid.dp,)),
+            pltpu.SemaphoreType.DMA,
+        ],
+        compiler_params=pltpu.CompilerParams(collective_id=number, has_side_effects=True),
+    )(*srcs, rows)
+    return (results[:count], results[count])
+
+
+def scatter_kernel(grid, count, *refs):
+    srcs, outs, refs = refs[:count], refs[count : 2 * count], refs[2 * count :]
+    acc, from_sibling, from_v, from_u, from_low, from_high = [
+        refs[k * count : (k + 1) * count] for k in range(6)
+    ]
+    load_sem, side_send, side_recv, v_send, v_recv, u_send, u_recv, z_send, low_recv, high_recv = refs[6 * count :]
+    z, x, y, core = grid.here()
+    tall = grid.tall
+    ux, uy = lax.rem(x + 1 - core, 2), lax.rem(y + core, 2)
+    vx, vy = lax.rem(x + core, 2), lax.rem(y + 1 - core, 2)
+    up, down = grid.device(z + 1, x, y, core), grid.device(z - 1, x, y, core)
+    u_device, v_device = grid.device(z, ux, uy, core), grid.device(z, vx, vy, core)
+    sibling = grid.device(z, x, y, 1 - core)
+    has_up, has_down = z < tall - 1, z > 0
+    greet(u_device)
+    greet(v_device)
+    greet(sibling)
+    greet(up, has_up)
+    greet(down, has_down)
+
+    def each(action):
+        for m in range(count):
+            action(m)
+
+    def slot(level, along_v, along_u):
+        return (level * 2 + along_v) * 2 + along_u
+
+    def place(along_v, along_u):
+        if along_v and along_u:
+            return 1 - x, 1 - y
+        if along_v:
+            return vx, vy
+        if along_u:
+            return ux, uy
+        return x, y
+
+    def load(m, level, along_v, along_u):
+        xx, yy = place(along_v, along_u)
+        where = slot(level, along_v, along_u)
+        return pltpu.make_async_copy(
+            srcs[m].at[grid.flat(level, xx, yy, core)], acc[m].at[where], load_sem.at[m, where]
+        )
+
+    def side(m, level, along_v, along_u):
+        xx, yy = place(along_v, along_u)
+        return pltpu.make_async_remote_copy(
+            src_ref=srcs[m].at[grid.flat(level, xx, yy, 1 - core)],
+            dst_ref=from_sibling[m].at[slot(level, along_u, along_v)],
+            send_sem=side_send.at[m, slot(level, along_u, along_v)],
+            recv_sem=side_recv.at[m, slot(level, along_u, along_v)],
+            device_id=sibling,
+            device_id_type=MESH,
+        )
+
+    def v_copy(m, level, along_u):
+        return pltpu.make_async_remote_copy(
+            src_ref=acc[m].at[slot(level, 1, along_u)],
+            dst_ref=from_v[m].at[level * 2 + along_u],
+            send_sem=v_send.at[m, level * 2 + along_u],
+            recv_sem=v_recv.at[m, level * 2 + along_u],
+            device_id=v_device,
+            device_id_type=MESH,
+        )
+
+    def u_copy(m, level):
+        return pltpu.make_async_remote_copy(
+            src_ref=acc[m].at[slot(level, 0, 1)],
+            dst_ref=from_u[m].at[level],
+            send_sem=u_send.at[m, level],
+            recv_sem=u_recv.at[m, level],
+            device_id=u_device,
+            device_id_type=MESH,
+        )
+
+    def z_copy(m, level, upward):
+        return pltpu.make_async_remote_copy(
+            src_ref=acc[m].at[slot(level, 0, 0)],
+            dst_ref=(from_low if upward else from_high)[m].at[level],
+            send_sem=z_send.at[m, level],
+            recv_sem=(low_recv if upward else high_recv).at[m, level],
+            device_id=up if upward else down,
+            device_id_type=MESH,
+        )
+
+    def add(m, where, other, at):
+        total = acc[m][where].astype(jnp.float32) + other[m][at].astype(jnp.float32)
+        acc[m][where] = total.astype(jnp.bfloat16)
+
+    def levels(action):
+        @pl.loop(0, 2 * tall)
+        def _(step):
+            far = tall - 1 - step // 2
+            level = jnp.where(lax.rem(step, 2) == 0, z - far, z + far)
+            use = (level >= 0) & (level < tall) & ((far > 0) | (lax.rem(step, 2) == 0))
+
+            @pl.when(use)
+            def _():
+                action(level)
+
+    def begin(level):
+        for along_v in (1, 0):
+            for along_u in (1, 0):
+                each(lambda m: load(m, level, along_v, along_u).start())
+
+    levels(begin)
+    meet(count=3 + has_up.astype(jnp.int32) + has_down.astype(jnp.int32))
+
+    def begin_side(kinds):
+        def run(level):
+            for along_v, along_u in kinds:
+                each(lambda m: side(m, level, along_v, along_u).start())
+
+        return run
+
+    levels(begin_side(((1, 1), (0, 1))))
+    levels(begin_side(((1, 0), (0, 0))))
+
+    def take(level, along_v, along_u):
+        where = slot(level, along_v, along_u)
+
+        def run(m):
+            load(m, level, along_v, along_u).wait()
+            side(m, level, along_u, along_v).wait_recv()
+            add(m, where, from_sibling, where)
+
+        each(run)
+
+    def first(level):
+        for along_u in (1, 0):
+            take(level, 1, along_u)
+            each(lambda m: v_copy(m, level, along_u).start())
+
+    levels(first)
+
+    def second(level):
+        for along_u in (1, 0):
+            take(level, 0, along_u)
+
+            def run(m):
+                v_copy(m, level, along_u).wait_recv()
+                add(m, slot(level, 0, along_u), from_v, level * 2 + along_u)
+                if along_u:
+                    u_copy(m, level).start()
+
+            each(run)
+
+    levels(second)
+
+    def third(level):
+        where = slot(level, 0, 0)
+
+        def run(m):
+            u_copy(m, level).wait_recv()
+            add(m, where, from_u, level)
+
+        each(run)
+
+        @pl.when((level >= z) & has_down)
+        def _():
+            def run(m):
+                z_copy(m, level, True).wait_recv()
+                add(m, where, from_low, level)
+
+            each(run)
+
+        @pl.when((level <= z) & has_up)
+        def _():
+            def run(m):
+                z_copy(m, level, False).wait_recv()
+                add(m, where, from_high, level)
+
+            each(run)
+
+        @pl.when(level > z)
+        def _():
+            each(lambda m: z_copy(m, level, True).start())
+
+        @pl.when(level < z)
+        def _():
+            each(lambda m: z_copy(m, level, False).start())
+
+    levels(third)
+
+    def finish(m):
+        outs[m][...] = acc[m][slot(z, 0, 0)].astype(jnp.float32)
+
+    each(finish)
+
+    def drain(level):
+        for along_v in (0, 1):
+            for along_u in (0, 1):
+                each(lambda m: side(m, level, along_v, along_u).wait_send())
+        for along_u in (0, 1):
+            each(lambda m: v_copy(m, level, along_u).wait_send())
+        each(lambda m: u_copy(m, level).wait_send())
+
+        @pl.when(level != z)
+        def _():
+            each(lambda m: z_copy(m, level, True).wait_send())
+
+    levels(drain)
+
+
+def scatter(srcs, number):
+    grid = Grid()
+    count = len(srcs)
+    tall = grid.tall
+    blocks = [src.shape[1:] for src in srcs]
+    buffers = [
+        pltpu.VMEM((number_of,) + block, jnp.bfloat16)
+        for number_of in (4 * tall, 4 * tall, 2 * tall, tall, tall, tall)
+        for block in blocks
+    ]
+    semaphores = [
+        pltpu.SemaphoreType.DMA((count, number_of))
+        for number_of in (4 * tall, 4 * tall, 4 * tall, 2 * tall, 2 * tall, tall, tall, tall, tall, tall)
+    ]
+    return pl.pallas_call(
+        functools.partial(scatter_kernel, grid, count),
+        out_shape=[jax.ShapeDtypeStruct(block, jnp.float32) for block in blocks],
+        in_specs=[pl.BlockSpec(memory_space=pl.ANY)] * count,
+        out_specs=[pl.BlockSpec(memory_space=pltpu.VMEM)] * count,
+        scratch_shapes=buffers + semaphores,
+        compiler_params=pltpu.CompilerParams(
+            collective_id=number, has_side_effects=True, vmem_limit_bytes=56 * 1024 * 1024
+        ),
+    )(*srcs)
+
+
+def rows_kernel(grid, src, out, own_sem, line_send, side_send, y_send, recv_sem):
+    d, f = lax.axis_index("dp"), lax.axis_index("fsdp")
+    me = d * grid.fs + f
+    f_side = f + 1 - 2 * lax.rem(f, 2)
+    f_y = lax.rem(f + 2, grid.fs)
+    f_y_side = lax.rem(f_side + 2, grid.fs)
+    own = pltpu.make_async_copy(src.at[d], out.at[me], own_sem)
+    own.start()
+
+    @pl.loop(1, grid.dp)
+    def _(step):
+        greet((lax.rem(d + step, grid.dp), f))
+
+    greet((d, f_side))
+    greet((d, f_y))
+    meet(count=grid.dp + 1)
+
+    def line(peer, slot):
+        return pltpu.make_async_remote_copy(
+            src_ref=src.at[peer],
+            dst_ref=out.at[slot],
+            send_sem=line_send.at[peer],
+            recv_sem=recv_sem.at[slot],
+            device_id=(peer, f),
+            device_id_type=MESH,
+        )
+
+    def onward(slot, column, sem, own_block):
+        return pltpu.make_async_remote_copy(
+            src_ref=src.at[d] if own_block else out.at[slot],
+            dst_ref=out.at[slot],
+            send_sem=sem.at[slot],
+            recv_sem=recv_sem.at[slot],
+            device_id=(d, column),
+            device_id_type=MESH,
+        )
+
+    onward(me, f_y, y_send, True).start()
+    onward(me, f_side, side_send, True).start()
+
+    @pl.loop(1, grid.dp)
+    def _(step):
+        peer = lax.rem(d + step, grid.dp)
+        line(peer, me).start()
+
+    @pl.loop(1, grid.dp)
+    def _(step):
+        slot = lax.rem(d + grid.dp - step, grid.dp) * grid.fs + f
+        line(d, slot).wait_recv()
+        onward(slot, f_y, y_send, False).start()
+        onward(slot, f_side, side_send, False).start()
+
+    @pl.loop(0, grid.dp)
+    def _(step):
+        slot = lax.rem(d + grid.dp - step, grid.dp) * grid.fs + f_y
+        line(d, slot).wait_recv()
+        onward(slot, f_side, side_send, False).start()
+
+    @pl.loop(0, grid.dp)
+    def _(step):
+        line(d, step * grid.fs + f_side).wait_recv()
+        line(d, step * grid.fs + f_y_side).wait_recv()
+        onward(step * grid.fs + f, f_y, y_send, False).wait_send()
+        onward(step * grid.fs + f, f_side, side_send, False).wait_send()
+        onward(step * grid.fs + f_y, f_side, side_send, False).wait_send()
+
+    @pl.loop(1, grid.dp)
+    def _(step):
+        line(lax.rem(d + step, grid.dp), me).wait_send()
+
+    own.wait()
+
+
+def share_rows(src, number):
+    grid = Grid()
+    return pl.pallas_call(
+        functools.partial(rows_kernel, grid),
+        out_shape=jax.ShapeDtypeStruct((grid.total,) + src.shape[1:], src.dtype),
+        in_specs=[pl.BlockSpec(memory_space=pl.ANY)],
+        out_specs=pl.BlockSpec(memory_space=pl.ANY),
+        scratch_shapes=[
+            pltpu.SemaphoreType.DMA,
+            pltpu.SemaphoreType.DMA((grid.dp,)),
+            pltpu.SemaphoreType.DMA((grid.total,)),
+            pltpu.SemaphoreType.DMA((grid.total,)),
+            pltpu.SemaphoreType.DMA((grid.total,)),
+        ],
+        compiler_params=pltpu.CompilerParams(collective_id=number, has_side_effects=True),
+    )(src)
+
+
+def spread_kernel(vocab_rows, ids_ref, rows_ref, out_ref, square_ref):
+    block = out_ref.shape[0]
+    base = pl.program_id(0) * block
+    place = base + lax.broadcasted_iota(jnp.int32, (block, ids_ref.shape[1]), 0)
+    hot = jnp.where(place == ids_ref[...], 1.0, 0.0).astype(jnp.bfloat16)
+    total = matmul(hot, rows_ref[...])
+    low = total.astype(jnp.bfloat16)
+    out_ref[...] = low
+    wide = low.astype(jnp.float32)
+    part = jnp.sum((wide * wide).reshape(block // 8, 8, D), 0)
+
+    @pl.when(pl.program_id(0) == 0)
+    def _():
+        square_ref[...] = jnp.zeros_like(square_ref)
+
+    square_ref[...] += part
+
+
+def spread_rows(ids, rows, vocab_rows):
+    count = rows.shape[0]
+    block = 512
+    steps = -(-vocab_rows // block)
+    return pl.pallas_call(
+        functools.partial(spread_kernel, vocab_rows),
+        grid=(steps,),
+        out_shape=[
+            jax.ShapeDtypeStruct((vocab_rows, D), jnp.bfloat16),
+            jax.ShapeDtypeStruct((8, D), jnp.float32),
+        ],
+        in_specs=[
+            pl.BlockSpec((1, count), lambda i: (0, 0)),
+            pl.BlockSpec((count, D), lambda i: (0, 0)),
+        ],
+        out_specs=[pl.BlockSpec((block, D), lambda i: (i, 0)), pl.BlockSpec((8, D), lambda i: (0, 0))],
+        compiler_params=pltpu.CompilerParams(vmem_limit_bytes=48 * 1024 * 1024),
+    )(ids.reshape(1, count), rows)
+
+
+def plain_body(
     token_ids,
     pad_mask,
     hard_negative,
@@ -399,9 +1038,240 @@
     return tuple(results)
 
 
+def fits(mesh):
+    return mesh.shape["fsdp"] == 4 and mesh.shape["dp"] == 8
+
+
+def dense_rows(ids_flat, table, row_base):
+    vocab_rows = table.shape[0]
+    ids_all = lax.all_gather(ids_flat, "dp", axis=0, tiled=True)
+    picked = ids_all - row_base
+    inside = (picked >= 0) & (picked < vocab_rows)
+    chosen = jnp.take(table.astype(jnp.bfloat16), jnp.clip(picked, 0, vocab_rows - 1), axis=0)
+    return lax.psum_scatter(
+        jnp.where(inside[:, None], chosen.astype(jnp.float32), 0.0).astype(jnp.bfloat16),
+        "dp",
+        scatter_dimension=0,
+        tiled=True,
+    ).astype(jnp.float32)
+
+
+def dense_table_grad(ids_flat, grad_low, vocab_rows, row_base):
+    ids_all = lax.all_gather(ids_flat, "dp", axis=0, tiled=True)
+    rows_back = lax.all_gather(grad_low, "dp", axis=0, tiled=True)
+    turn_count = lax.axis_size("dp") // 4
+    block_rows = rows_back.shape[0] // turn_count
+
+    def add_block(running, piece_pair):
+        block_grads, block_ids = piece_pair
+        local_ids = block_ids - row_base
+        inside = (local_ids >= 0) & (local_ids < vocab_rows)
+        segment = jnp.where(inside, local_ids, vocab_rows)
+        summed = jax.ops.segment_sum(
+            block_grads.astype(jnp.float32), segment, num_segments=vocab_rows + 1
+        )
+        return (running + summed[:vocab_rows], None)
+
+    table_full, _ = lax.scan(
+        add_block,
+        jnp.zeros((vocab_rows, D), jnp.float32),
+        (rows_back.reshape(turn_count, block_rows, D), ids_all.reshape(turn_count, block_rows)),
+    )
+    return lax.psum(table_full.astype(jnp.bfloat16), "fsdp")
+
+
+def once(flag, make, value):
+    return lax.while_loop(lambda state: state[0], lambda state: (False, make(state[1])), (flag, value))[1]
+
+
+def fast_body(
+    token_ids,
+    pad_mask,
+    hard_negative,
+    table,
+    table_first,
+    table_second,
+    attn_in,
+    attn_in_first,
+    attn_in_second,
+    attn_out,
+    attn_out_first,
+    attn_out_second,
+    ffn_in,
+    ffn_in_first,
+    ffn_in_second,
+    ffn_out,
+    ffn_out_first,
+    ffn_out_second,
+    proj_head,
+    proj_head_first,
+    proj_head_second,
+    small_params,
+    small_first,
+    small_second,
+):
+    dp_count = lax.axis_size("dp")
+    fsdp_count = lax.axis_size("fsdp")
+    total = dp_count * fsdp_count
+    column = lax.axis_index("fsdp")
+    device_flat = lax.axis_index("dp") * fsdp_count + column
+    pairs_here = token_ids.shape[1]
+    pairs_total = pairs_here * total
+    seq_count = 2 * pairs_here
+    vocab_rows = table.shape[0]
+    row_base = lax.axis_index("dp") * vocab_rows
+    gain_rows = small_params[: 3 * D].reshape(3, D)
+    bias_table = small_params[3 * D : 3 * D + NB * HEADS].reshape(NB, HEADS)
+    log_scale = small_params[3 * D + NB * HEADS]
+    buckets = jnp.asarray(bucket_table(L, NB).reshape(-1), jnp.int32)
+    bucket_hot = (buckets[:, None] == jnp.arange(NB, dtype=jnp.int32)[None, :]).astype(jnp.float32)
+    bias_full = (
+        jnp.dot(bucket_hot, bias_table, precision=HIGH).reshape(L, L, HEADS).transpose(2, 0, 1)
+    )
+    mask_rows = pad_mask.reshape(seq_count, L)
+    ids_flat = token_ids.reshape(-1)
+    tokens = ids_flat.shape[0]
+
+    order = jnp.arange(tokens, dtype=jnp.int32)
+    owner = ids_flat // vocab_rows
+    earlier = (ids_flat[None, :] == ids_flat[:, None]) & (order[None, :] < order[:, None])
+    first = ~jnp.any(earlier, 1)
+    below = (owner[None, :] == owner[:, None]) & (ids_flat[None, :] < ids_flat[:, None]) & first[None, :]
+    rank = jnp.sum(below.astype(jnp.int32), 1)
+    spilled = jnp.any(rank >= CAP)
+    slot = jnp.where(rank < CAP, owner * CAP + rank, -1)
+    slots = jnp.arange(dp_count * CAP, dtype=jnp.int32)
+    lists = jnp.max(
+        jnp.where(slot[None, :] == slots[:, None], (ids_flat - owner * vocab_rows)[None, :], -1), 1
+    ).reshape(dp_count, 1, 1, CAP)
+    lists = jnp.broadcast_to(lists, (dp_count, fsdp_count, 1, CAP)).reshape(total, 1, CAP)
+    extra = jnp.zeros((7, 128), jnp.int32)
+    extra = extra.at[0, :pairs_here].set(hard_negative).at[1, 0].set(spilled.astype(jnp.int32))
+    message = jnp.concatenate([lists, jnp.broadcast_to(extra[None], (total, 7, 128))], 1)
+    heard = exchange(message, True, 1)
+    asked = heard[:, 0, :]
+    negatives = heard[:, 1, :pairs_here].reshape(-1)
+    any_spilled = jnp.max(heard[:, 2, 0]) > 0
+
+    mine_asked = lax.dynamic_index_in_dim(
+        asked.reshape(dp_count, fsdp_count, CAP), column, 1, keepdims=False
+    )
+    answers = jnp.take(table, jnp.maximum(mine_asked.reshape(-1), 0), axis=0).astype(jnp.bfloat16)
+    shards = (
+        attn_in.astype(jnp.bfloat16),
+        attn_out.astype(jnp.bfloat16),
+        ffn_in.astype(jnp.bfloat16),
+        ffn_out.astype(jnp.bfloat16),
+        proj_head.astype(jnp.bfloat16),
+    )
+    gathered, found = gather(shards, answers.reshape(dp_count, CAP, D), 2)
+    gathered = [matrix.reshape(-1, matrix.shape[-1]) for matrix in gathered]
+    slot_hot = (slot[:, None] == slots[None, :]).astype(jnp.bfloat16)
+    embedded = matmul(slot_hot, found.reshape(dp_count * CAP, D))
+    embedded = once(any_spilled, lambda _: dense_rows(ids_flat, table, row_base), embedded)
+
+    final_rows, kept = layer_forward(embedded, mask_rows, gathered[:4], gain_rows, bias_full)
+    normed_three, factor_three = normalize(final_rows, gain_rows[2])
+    mask_weight = mask_rows.astype(jnp.float32)[:, :, None]
+    counts = jnp.sum(mask_weight, 1)
+    pooled = jnp.sum(normed_three.reshape(seq_count, L, D) * mask_weight, 1) / counts
+    pooled_low = pooled.astype(jnp.bfloat16)
+    projected = matmul(pooled_low, gathered[4])
+    proj_factor = lax.rsqrt(jnp.sum(projected * projected, -1, keepdims=True) + EPS)
+    unit_rows = projected * proj_factor
+    unit_low = unit_rows.astype(jnp.bfloat16)
+    all_units = exchange(unit_low.reshape(2 * seq_count, D // 2), False, 3)
+    all_units = all_units.reshape(total, 2, pairs_here, D)
+    all_query = all_units[:, 0].reshape(pairs_total, D)
+    all_pass = all_units[:, 1].reshape(pairs_total, D)
+    similar = matmul_nt(all_query, all_pass)
+    sim_scale = jnp.exp(log_scale)
+    columns = jnp.arange(pairs_total, dtype=jnp.int32)
+    own_mask = (columns[None, :] == columns[:, None]).astype(jnp.float32)
+    negative = (columns[None, :] == negatives[:, None]).astype(jnp.float32)
+    logits = sim_scale * similar - MARGIN * own_mask
+    diagonal = jnp.sum(logits * own_mask, 1)
+    hardest = jnp.sum(logits * negative, 1)
+    row_max = jnp.max(logits, 1, keepdims=True)
+    log_total = row_max + jnp.log(jnp.sum(jnp.exp(logits - row_max), 1, keepdims=True))
+    loss_sum = jnp.sum(log_total[:, 0] - diagonal + jax.nn.softplus(hardest - diagonal))
+    hinge_gate = jax.nn.sigmoid(hardest - diagonal)
+    grad_logits = (
+        jnp.exp(logits - log_total) - own_mask + hinge_gate[:, None] * (negative - own_mask)
+    )
+    grad_log_scale = sim_scale * jnp.sum(grad_logits * similar)
+    grad_similar = (sim_scale * grad_logits).astype(jnp.bfloat16)
+    own_first = device_flat * pairs_here
+    mine_rows = lax.dynamic_slice_in_dim(grad_similar, own_first, pairs_here, 0)
+    mine_columns = lax.dynamic_slice_in_dim(grad_similar, own_first, pairs_here, 1)
+    grad_query = matmul(mine_rows, all_pass).astype(jnp.bfloat16)
+    grad_pass = matmul_tn(mine_columns, all_query).astype(jnp.bfloat16)
+    grad_units = jnp.concatenate([grad_query, grad_pass], 0).astype(jnp.float32)
+    grad_proj = (
+        proj_factor * (grad_units - unit_rows * jnp.sum(grad_units * unit_rows, -1, keepdims=True))
+    ).astype(jnp.bfloat16)
+    grad_proj_head = matmul_tn(pooled_low, grad_proj)
+    grad_pooled = matmul_nt(grad_proj, gathered[4])
+    grad_normed = ((grad_pooled / counts)[:, None, :] * mask_weight).reshape(-1, D)
+    grad_final, gain_three = normalize_back(grad_normed, final_rows, factor_three, gain_rows[2])
+    grad_rows, matrix_grads, gain_one, gain_two, grad_bias = layer_backward(
+        grad_final, kept, mask_rows, gathered[:4], gain_rows, bias_full
+    )
+    grad_bias_table = jnp.dot(grad_bias.reshape(HEADS, L * L), bucket_hot, precision=HIGH).T
+    partials = [
+        grad.astype(jnp.bfloat16).reshape(total, -1, grad.shape[1])
+        for grad in (*matrix_grads, grad_proj_head)
+    ]
+    weight_grads = scatter(partials, 4)
+
+    grad_low = grad_rows.astype(jnp.bfloat16)
+    slot_sums = matmul_tn(slot_hot, grad_low).astype(jnp.bfloat16).reshape(dp_count, CAP, D)
+    all_rows = share_rows(slot_sums, 5)
+    table_grad, table_squares = spread_rows(
+        asked.reshape(-1), all_rows.reshape(total * CAP, D), vocab_rows
+    )
+    table_squares = jnp.sum(table_squares)
+    table_grad, table_squares = once(
+        any_spilled, lambda _: with_squares(dense_table_grad(ids_flat, grad_low, vocab_rows, row_base)), (table_grad, table_squares)
+    )
+    squares = table_squares / fsdp_count
+    for gradient in weight_grads:
+        squares = squares + jnp.sum(gradient * gradient)
+    small_local = jnp.concatenate(
+        [gain_one, gain_two, gain_three, grad_bias_table.reshape(-1), squares[None]]
+    )
+    width = -(-small_local.shape[0] // 1024) * 8
+    small_local = jnp.pad(small_local, (0, width * 128 - small_local.shape[0]))
+    summed = jnp.sum(exchange(small_local.reshape(width, 128), False, 6), 0).reshape(-1)
+    small_size = small_params.shape[0]
+    total_squares = summed[small_size - 1]
+    small_grad = jnp.concatenate([summed[: small_size - 1], grad_log_scale[None]])
+    norm_value = jnp.sqrt(total_squares + jnp.sum(small_grad * small_grad))
+    factor = jnp.minimum(1.0, CLIP / (norm_value + 1e-06))
+    updates = (
+        (table, table_first, table_second, table_grad.astype(jnp.float32)),
+        (attn_in, attn_in_first, attn_in_second, weight_grads[0]),
+        (attn_out, attn_out_first, attn_out_second, weight_grads[1]),
+        (ffn_in, ffn_in_first, ffn_in_second, weight_grads[2]),
+        (ffn_out, ffn_out_first, ffn_out_second, weight_grads[3]),
+        (proj_head, proj_head_first, proj_head_second, weight_grads[4]),
+        (small_params, small_first, small_second, small_grad),
+    )
+    results = [loss_sum, norm_value]
+    for kind_index, arrays in enumerate(updates):
+        results.extend(adam_update(*arrays, factor, RATES[kind_index], DECAYS[kind_index]))
+    return tuple(results)
+
+
+def with_squares(table_grad):
+    wide = table_grad.astype(jnp.float32)
+    return (table_grad, jnp.sum(wide * wide))
+
+
 def solution(mesh):
+    program = fast_body if fits(mesh) else plain_body
     return jax.shard_map(
-        body,
+        program,
         mesh=mesh,
         in_specs=(
             P(None, ("dp", "fsdp"), None),

time: 1530 us -> 642 us (0.42)
  waiting for transfers between devices: 945 us -> 0 us
  Pallas kernels: 0 us -> 341 us
  blocking collectives: 156 us -> 0 us
  other arithmetic: 189 us -> 96.6 us
  local copies, waits for them, and re-layouts: 76.6 us -> 57.6 us
    reduce_scatter x6 -> x0, waiting for transfers between devices: 660 us -> none  [the longest x1 211 us: body(): lax.psum_scatter(jnp.where(inside[:, None], chosen.astype(jnp.float32), 0...]
    pallas_call x0 -> x7, Pallas kernels: none -> 341 us  [the longest x1 111 us: scatter(): pl.pallas_call(functools.partial(scatter_kernel, grid, count), out_shape=...]
    all_gather x6 -> x0, waiting for transfers between devices: 285 us -> none  [the longest x1 133 us: body(): lax.all_gather(grad_rows.astype(jnp.bfloat16), 'dp', axis=0, tiled=True)]
    all_gather x2 -> x0, blocking collectives: 74.9 us -> none  [the longest x1 42.6 us: body(): lax.all_gather(unit_low[pairs_here:], ('dp', 'fsdp'), axis=0, tiled=True)]
    scatter-add x2 -> x0, other arithmetic: 67.1 us -> none  [add_block(): jax.ops.segment_sum(block_grads.astype(jnp.float32), segment, num_segment...]
    unnamed x1 -> x0, blocking collectives: 40.6 us -> none
    psum x1 -> x0, blocking collectives: 40.1 us -> none  [body(): total_squares, loss_sum = lax.psum((squares, loss_local), ('dp', 'fsdp'))]
    gather x1, local copies, waits for them, and re-layouts: 40.7 us -> 8.98 us  [fast_body(): jnp.take(table, jnp.maximum(mine_asked.reshape(-1), 0), axis=0)]
  transfers between devices with their start and end apart: 13 -> 0, of which waited for: 9 -> 0; matrix products, arithmetic and copies ran while one was open for 14% -> 0% of each run, Pallas kernels for 0% -> 0%
where the time goes in v1:
time: 642 us; the launch traced here: 633 us
  Pallas kernels  341 us (53%)
  matrix products  113 us (18%)
  other arithmetic  96.6 us (15%)
  local copies, waits for them, and re-layouts  57.6 us (9%)
  between operations  24.8 us (4%)
    pallas_call x1, Pallas kernels, scatter(): pl.pallas_call(functools.partial(scatter_kernel, grid, count), out_shape=...  111 us
    pallas_call x1, Pallas kernels, gather(): pl.pallas_call(functools.partial(gather_kernel, grid, count), out_shape=[...  103 us
    pallas_call x1, Pallas kernels, share_rows(): pl.pallas_call(functools.partial(rows_kernel, grid), out_shape=jax.ShapeD...  52.1 us
    pallas_call x3, Pallas kernels, exchange(): pl.pallas_call(functools.partial(exchange_kernel, grid, spread), out_shap...  43.8 us
    sub x6, other arithmetic, adam_update(): return (first_new, second_new, param - rate * (direction + decay * param))  36.6 us
    dot_general x7, matrix products, matmul_tn(): lax.dot_general(left_side, right_side, (((0,), (0,)), ((), ())), preferre...  33.4 us
    pallas_call x1, Pallas kernels, spread_rows(): pl.pallas_call(functools.partial(spread_kernel, vocab_rows), grid=(steps,...  31.2 us
    dot_general x6, matrix products, matmul_nt(): lax.dot_general(left_side, right_side, (((1,), (1,)), ((), ())), preferre...  30.6 us

profile of v1, /device:TPU:0, one launch (start us, length us, event | category | flops | bytes accessed | tf_op | source)
XLA Modules:
  0.0 632.6 jit_solution(9311470060993574582)
XLA Ops:
  27.4 12.3 %shard_map.416 = s32[32,8,128]{2,1,0:T(8,128)} custom-call(s32[32,8,128]{2,1,0:T(8,128)} %pad_add_fusion.src), custom_call_target="tpu_custom_call" | custom-call | tf_op jit(solution)/shard_map/pallas_call | solution.py:284
  50.7 9.0 %gather_fusion.1 = bf16[1024,768]{1,0:T(8,128)(2,1)S(1)} fusion(f32[4016,768]{1,0:T(8,128)} %param.38, s32[1024]{0:T(1024)S(1)} %bitcast_clamp_fusion), kind=kCustom, calls=%fused_computation.1 | custom fusion | bytes 3149824 | tf_op jit(solution)/shard_map/jit(_take)/gather | solution.py:1159
  61.1 7.8 %convert.9 = bf16[4016,768]{1,0:T(8,128)(2,1)} convert(f32[4016,768]{1,0:T(8,128)} %param.38) | non-fusion elementwise | flops 3084288 | bytes 18505728
  68.9 102.5 %shard_map.417 = (bf16[32,24,2304]{2,1,0:T(8,128)(2,1)}, bf16[32,24,768]{2,1,0:T(8,128)(2,1)}, bf16[32,24,3072]{2,1,0:T(8,128)(2,1)}, bf16[32,96,768]{2,1,0:T(8,...) custom-call(bf16[24,2304]{1,0:T(8,128)(2,1)} %convert_element_type.174.refs_0_, ...), custom_call_target="tpu_custom_call" | custom-call | tf_op jit(solution)/shard_map/pallas_call | solution.py:466
  171.4 5.0 fusion.19
  179.4 7.7 %convolution_convert_fusion = bf16[1024,2304]{1,0:T(8,128)(2,1)} fusion(bf16[768,2304]{1,0:T(8,128)(2,1)} %bitcast.234, f32[1024,768]{1,0:T(8,128)S(1)} %copy-done.9, f32[768]{0:T(1024)S(1)} %copy-done.57, f32[1024]{0:T(1024)S(1)} %add_rsqrt_fusion.2), kind=kOutput, calls=%fused_computation.38 | convolution fusion | flops 3628597248 | bytes 11410432 | tf_op jit(solution)/shard_map/dot_general | solution.py:49
  187.1 7.1 %copy.112 = bf16[1024,2304]{0,1:T(8,128)(2,1)} copy(bf16[1024,2304]{1,0:T(8,128)(2,1)} %convolution_convert_fusion) | data formatting | bytes 9437184 | tf_op jit(solution)/shard_map/convert_element_type | solution.py:96
  208.7 5.3 fusion.82
  214.1 7.5 %multiply_reduce_fusion.7 = (f32[1024]{0:T(1024)S(1)}, f32[1024,768]{1,0:T(8,128)S(1)}) fusion(f32[1024,768]{1,0:T(8,128)S(1)} %get-tuple-element.264, bf16[3072,768]{1,0:T(8,128)(2,1)S(1)} %bitcast.233, f32[1024,3072]{1,0:T(8,128)S(1)} %fusion.82), kind=kOutput, calls=%fused_computation.75 | convolution fusion | flops 4862508032 | bytes 23597056 | tf_op jit(solution)/shard_map/dot_general | solution.py:49
  225.2 12.3 %shard_map.418 = bf16[32,16,384]{2,1,0:T(8,128)(2,1)} custom-call(bf16[16,384]{1,0:T(8,128)(2,1)} %reshape.499.src), custom_call_target="tpu_custom_call" | custom-call | tf_op jit(solution)/shard_map/pallas_call | solution.py:284
  254.9 14.5 %fusion.12 = bf16[1024,3072]{1,0:T(8,128)(2,1)S(1)} fusion(f32[1024,3072]{1,0:T(8,128)} %copy-done.73, bf16[1024,768]{1,0:T(8,128)(2,1)S(1)} %fusion.38, bf16[3072,768]{1,0:T(8,128)(2,1)} %bitcast.230), kind=kOutput, calls=%fused_computation.25 | convolution fusion | flops 4894752768 | bytes 25165824 | tf_op jit(solution)/shard_map/dot_general | solution.py:59
  269.5 11.9 %convolution_convert_fusion.1 = bf16[3072,768]{1,0:T(8,128)(2,1)} fusion(bf16[1024,768]{1,0:T(8,128)(2,1)S(1)} %fusion.38, f32[1024,3072]{1,0:T(8,128)} %copy-done.73), kind=kOutput, calls=%fused_computation.39 | convolution fusion | flops 4862509056 | bytes 18874368 | tf_op jit(solution)/shard_map/dot_general | solution.py:53
  281.4 5.5 multiply_reduce_fusion.3
  286.8 7.4 %convolution_convert_fusion.2 = bf16[768,3072]{1,0:T(8,128)(2,1)} fusion(bf16[1024,3072]{1,0:T(8,128)(2,1)S(1)} %fusion.12, f32[1024,768]{1,0:T(8,128)S(1)} %copy-done.17, f32[768]{0:T(1024)S(1)} %copy-done.60, f32[1024]{0:T(1024)S(1)} %copy-done.56), kind=kOutput, calls=%fused_computation.40 | convolution fusion | flops 4836556800 | bytes 14162944 | tf_op jit(solution)/shard_map/dot_general | solution.py:53
  306.2 6.4 %convolution_bitcast_fusion = bf16[8,128,1,12,64]{1,4,3,0,2:T(8,128)(2,1)} fusion(bf16[8,128,12,64]{1,0,3,2:T(8,128)(2,1)S(1)} %bitcast.187, f32[8,12,128,128]{2,3,1,0:T(8,128)} %copy-done, f32[8,12,128]{2,1,0:T(8,128)S(1)} %copy-done.19), kind=kOutput, calls=%fused_computation.89 | convolution fusion | flops 204472320 | bytes 9486336 | tf_op jit(solution)/shard_map/bhqk,bqhd->bkhd/dot_general | solution.py:166
  319.5 4.8 multiply_bitcast_fusion
  326.4 9.3 %copy.126 = bf16[8,128,3,12,64]{1,0,4,3,2:T(8,128)(2,1)S(1)} copy(bf16[8,128,3,12,64]{1,4,3,0,2:T(8,128)(2,1)S(1)} %maximum_convert_fusion) | data formatting | bytes 9437184 | tf_op jit(solution)/shard_map/convert_element_type | solution.py:182
  335.8 6.0 multiply_reduce_fusion.2
  341.9 5.7 convolution_convert_fusion.3
  347.6 111.2 %shard_map.421 = (f32[24,2304]{1,0:T(8,128)}, f32[24,768]{1,0:T(8,128)}, f32[24,3072]{1,0:T(8,128)}, f32[96,768]{1,0:T(8,128)}, f32[24,768]{1,0:T(8,128)}) custom-call(bf16[32,24,2304]{2,1,0:T(8,128)(2,1)} %bitcast.201, bf16[32,24,768]{2,1,0:T(8,128)(2,1)} %bitcast.205, bf16[32,24,3072]{2,1,0:T(8,128)(2,1)} %bitcast.197, bf16[32,96,768]{2,1,0:T(8,128)(2,1)} %bitcast.196, ...), custom_call_target="tpu_custom_call" | custom-call | tf_op jit(solution)/shard_map/pallas_call | solution.py:702
  476.2 52.1 %shard_map.419 = bf16[32,128,768]{2,1,0:T(8,128)(2,1)} custom-call(bf16[8,128,768]{2,1,0:T(8,128)(2,1)} %bitcast.204), custom_call_target="tpu_custom_call" | custom-call | tf_op jit(solution)/shard_map/pallas_call | solution.py:789
  528.3 31.2 %shard_map.420 = (bf16[4016,768]{1,0:T(8,128)(2,1)}, f32[8,768]{1,0:T(8,128)S(1)}) custom-call(s32[1,4096]{1,0:T(1,128)S(1)} %get-tuple-element.249.ids_ref, bf16[4096,768]{1,0:T(8,128)(2,1)} %bitcast.184), custom_call_target="tpu_custom_call" | custom-call | tf_op jit(solution)/shard_map/pallas_call | solution.py:827
  565.2 19.1 %shard_map.422 = f32[32,24,128]{2,1,0:T(8,128)} custom-call(f32[24,128]{1,0:T(8,128)} %pad_bitcast_fusion.src), custom_call_target="tpu_custom_call" | custom-call | tf_op jit(solution)/shard_map/pallas_call | solution.py:284
  595.0 29.4 %multiply_subtract_fusion = (f32[4016,768]{1,0:T(8,128)}, f32[4016,768]{1,0:T(8,128)}, f32[4016,768]{1,0:T(8,128)}) fusion(f32[4016,768]{1,0:T(8,128)} %param.38, f32[]{:T(128)S(6)} %min.11, bf16[4016,768]{1,0:T(8,128)(2,1)} %get-tuple-element.157, f32[4016,768]{1,0:T(8,128)} %param.40, f32[4016,768]{1,0:T(8,128)} %param.39), kind=kLoop, calls=%fused_computation.28 | loop fusion | flops 52432896 | bytes 80191488 | tf_op jit(solution)/shard_map/sub | solution.py:207
  (273 shorter events, 116.9 us)
Async XLA Ops:
  18.0 153.4 %copy-start.61 = (s32[1024]{0:T(1024)}, s32[1024]{0:T(1024)S(1)}, u32[]{:S(2)}) copy-start(s32[1024]{0:T(1024)S(1)} %get-tuple-element.258) | copy-start | bytes 12292
  253.8 27.5 %slice-start.4 = ((s8[4718592]{0:T(1024)(128)(4,1)}), s8[4194304]{0:T(1024)(128)(4,1)S(1)}, s32[]{:S(2)}) async-start(s8[4718592]{0:T(1024)(128)(4,1)} %bitcast.227), calls=%async_computation.8 | async-start | bytes 8388608
  254.9 26.4 %slice-start.5 = ((s8[4718592]{0:T(1024)(128)(4,1)}), s8[524288]{0:T(1024)(128)(4,1)S(1)}, s32[]{:S(2)}) async-start(s8[4718592]{0:T(1024)(128)(4,1)} %bitcast.227), calls=%async_computation.9 | async-start | bytes 1048576
  269.4 11.9 %copy-start.17 = (f32[1024,768]{1,0:T(8,128)S(1)}, f32[1024,768]{1,0:T(8,128)}, u32[]{:S(2)}) copy-start(f32[1024,768]{1,0:T(8,128)} %copy-done.16) | copy-start | bytes 9437188
  269.4 11.9 %copy-start.56 = (f32[1024]{0:T(1024)S(1)}, f32[1024]{0:T(1024)}, u32[]{:S(2)}) copy-start(f32[1024]{0:T(1024)} %copy-done.55) | copy-start | bytes 12292
  269.5 11.9 %copy-start.60 = (f32[768]{0:T(1024)S(1)}, f32[768]{0:T(1024)}, u32[]{:S(2)}) copy-start(f32[768]{0:T(1024)} %get-tuple-element.254) | copy-start | bytes 9220
  528.3 31.8 %copy-start.31 = (s32[2,4,128]{2,1,0:T(4,128)S(1)}, s32[2,4,128]{2,1,0:T(4,128)}, u32[]{:S(2)}) copy-start(s32[2,4,128]{2,1,0:T(4,128)} %param.35) | copy-start | bytes 12292
  560.1 27.7 %copy-start.51 = (f32[2689]{0:T(1024)S(1)}, f32[2689]{0:T(1024)}, u32[]{:S(2)}) copy-start(f32[2689]{0:T(1024)} %param.56) | copy-start | bytes 32272
  560.1 29.1 %copy-start.36 = (f32[24,768]{1,0:T(8,128)S(1)}, f32[24,768]{1,0:T(8,128)}, u32[]{:S(2)}) copy-start(f32[24,768]{1,0:T(8,128)} %param.44) | copy-start | bytes 221188
  560.1 29.1 %copy-start.37 = (f32[24,768]{1,0:T(8,128)S(1)}, f32[24,768]{1,0:T(8,128)}, u32[]{:S(2)}) copy-start(f32[24,768]{1,0:T(8,128)} %param.53) | copy-start | bytes 221188
  560.1 29.1 %copy-start.38 = (f32[24,768]{1,0:T(8,128)S(1)}, f32[24,768]{1,0:T(8,128)}, u32[]{:S(2)}) copy-start(f32[24,768]{1,0:T(8,128)} %get-tuple-element.153) | copy-start | bytes 221188
  560.1 29.1 %copy-start.39 = (f32[24,768]{1,0:T(8,128)S(1)}, f32[24,768]{1,0:T(8,128)}, u32[]{:S(2)}) copy-start(f32[24,768]{1,0:T(8,128)} %get-tuple-element.156) | copy-start | bytes 221188
  560.1 29.1 %copy-start.49 = (f32[24,768]{1,0:T(8,128)S(1)}, f32[24,768]{1,0:T(8,128)}, u32[]{:S(2)}) copy-start(f32[24,768]{1,0:T(8,128)} %param.55) | copy-start | bytes 221188
  560.1 30.9 %copy-start.26 = (f32[24,2304]{1,0:T(8,128)S(1)}, f32[24,2304]{1,0:T(8,128)}, u32[]{:S(2)}) copy-start(f32[24,2304]{1,0:T(8,128)} %get-tuple-element.152) | copy-start | bytes 663556
  560.1 30.9 %copy-start.27 = (f32[24,2304]{1,0:T(8,128)S(1)}, f32[24,2304]{1,0:T(8,128)}, u32[]{:S(2)}) copy-start(f32[24,2304]{1,0:T(8,128)} %param.41) | copy-start | bytes 663556
  560.1 30.9 %copy-start.40 = (f32[24,2304]{1,0:T(8,128)S(1)}, f32[24,2304]{1,0:T(8,128)}, u32[]{:S(2)}) copy-start(f32[24,2304]{1,0:T(8,128)} %param.43) | copy-start | bytes 663556
  560.3 32.5 %copy-start.22 = (f32[24,3072]{1,0:T(8,128)S(1)}, f32[24,3072]{1,0:T(8,128)}, u32[]{:S(2)}) copy-start(f32[24,3072]{1,0:T(8,128)} %param.47) | copy-start | bytes 884740
  560.4 32.5 %copy-start.25 = (f32[24,3072]{1,0:T(8,128)S(1)}, f32[24,3072]{1,0:T(8,128)}, u32[]{:S(2)}) copy-start(f32[24,3072]{1,0:T(8,128)} %get-tuple-element.154) | copy-start | bytes 884740
  560.4 32.5 %copy-start.32 = (f32[24,3072]{1,0:T(8,128)S(1)}, f32[24,3072]{1,0:T(8,128)}, u32[]{:S(2)}) copy-start(f32[24,3072]{1,0:T(8,128)} %param.49) | copy-start | bytes 884740
  560.4 32.5 %copy-start.33 = (f32[24,3072]{1,0:T(8,128)S(1)}, f32[24,3072]{1,0:T(8,128)}, u32[]{:S(2)}) copy-start(f32[24,3072]{1,0:T(8,128)} %param.48) | copy-start | bytes 884740
  560.4 33.6 %copy-start.23 = (f32[96,768]{1,0:T(8,128)S(1)}, f32[96,768]{1,0:T(8,128)}, u32[]{:S(2)}) copy-start(f32[96,768]{1,0:T(8,128)} %param.50) | copy-start | bytes 884740
  560.4 33.6 %copy-start.24 = (f32[96,768]{1,0:T(8,128)S(1)}, f32[96,768]{1,0:T(8,128)}, u32[]{:S(2)}) copy-start(f32[96,768]{1,0:T(8,128)} %get-tuple-element.155) | copy-start | bytes 884740
  560.4 33.6 %copy-start.34 = (f32[96,768]{1,0:T(8,128)S(1)}, f32[96,768]{1,0:T(8,128)}, u32[]{:S(2)}) copy-start(f32[96,768]{1,0:T(8,128)} %param.52) | copy-start | bytes 884740
  560.4 33.5 %copy-start.35 = (f32[96,768]{1,0:T(8,128)S(1)}, f32[96,768]{1,0:T(8,128)}, u32[]{:S(2)}) copy-start(f32[96,768]{1,0:T(8,128)} %param.51) | copy-start | bytes 884740
  (56 other events, 241.2 us)

commit v2 on v1

--- a/solution.py
+++ b/solution.py
@@ -482,73 +482,81 @@
     return (results[:count], results[count])
 
 
-def scatter_kernel(grid, count, *refs):
-    srcs, outs, refs = refs[:count], refs[count : 2 * count], refs[2 * count :]
-    acc, from_sibling, from_v, from_u, from_low, from_high = [
+ROW_BLOCK = 512
+
+
+def finish_kernel(grid, count, *refs):
+    srcs, (sums, ids, small) = refs[:count], refs[count : count + 3]
+    refs = refs[count + 3 :]
+    outs, (table_out, small_out, square_out) = refs[:count], refs[count : count + 3]
+    refs = refs[count + 3 :]
+    acc, from_side, from_v, from_u, from_low, from_high = [
         refs[k * count : (k + 1) * count] for k in range(6)
     ]
-    load_sem, side_send, side_recv, v_send, v_recv, u_send, u_recv, z_send, low_recv, high_recv = refs[6 * count :]
+    refs = refs[6 * count :]
+    rows, small_all, square_mine, square_all = refs[:4]
+    load_sem, side_send, side_recv, v_send, v_recv, u_send, u_recv, z_send, low_recv, high_recv = refs[4:14]
+    row_own, line_send, on_send, row_recv, small_send, small_recv, square_send, square_recv = refs[14:]
     z, x, y, core = grid.here()
     tall = grid.tall
+    d, f = lax.axis_index("dp"), lax.axis_index("fsdp")
+    me = d * grid.fs + f
+    up, down = grid.device(z + 1, x, y, core), grid.device(z - 1, x, y, core)
+    has_up, has_down = z < tall - 1, z > 0
     ux, uy = lax.rem(x + 1 - core, 2), lax.rem(y + core, 2)
     vx, vy = lax.rem(x + core, 2), lax.rem(y + 1 - core, 2)
-    up, down = grid.device(z + 1, x, y, core), grid.device(z - 1, x, y, core)
     u_device, v_device = grid.device(z, ux, uy, core), grid.device(z, vx, vy, core)
     sibling = grid.device(z, x, y, 1 - core)
-    has_up, has_down = z < tall - 1, z > 0
-    greet(u_device)
-    greet(v_device)
-    greet(sibling)
-    greet(up, has_up)
-    greet(down, has_down)
+    f_side = y * 2 + 1 - core
+    f_y = (1 - y) * 2 + core
+    f_far = (1 - y) * 2 + 1 - core
+
+    @pl.loop(1, grid.total)
+    def _(step):
+        greet(grid.peer(lax.rem(me + step, grid.total)))
 
     def each(action):
         for m in range(count):
             action(m)
 
-    def slot(level, along_v, along_u):
-        return (level * 2 + along_v) * 2 + along_u
-
-    def place(along_v, along_u):
-        if along_v and along_u:
-            return 1 - x, 1 - y
-        if along_v:
-            return vx, vy
-        if along_u:
-            return ux, uy
-        return x, y
-
-    def load(m, level, along_v, along_u):
-        xx, yy = place(along_v, along_u)
-        where = slot(level, along_v, along_u)
+    def level_of(j):
+        tables = []
+        for own in range(tall):
+            tables.append(sorted(range(tall), key=lambda level: (-abs(level - own), -level))[j])
+        value = tables[0]
+        for own in range(1, tall):
+            value = jnp.where(z == own, tables[own], value)
+        return value
+
+    def load(m, level):
         return pltpu.make_async_copy(
-            srcs[m].at[grid.flat(level, xx, yy, core)], acc[m].at[where], load_sem.at[m, where]
-        )
-
-    def side(m, level, along_v, along_u):
-        xx, yy = place(along_v, along_u)
+            srcs[m].at[level, :, :, core], acc[m].at[level], load_sem.at[m, level]
+        )
+
+    def side(m, level):
         return pltpu.make_async_remote_copy(
-            src_ref=srcs[m].at[grid.flat(level, xx, yy, 1 - core)],
-            dst_ref=from_sibling[m].at[slot(level, along_u, along_v)],
-            send_sem=side_send.at[m, slot(level, along_u, along_v)],
-            recv_sem=side_recv.at[m, slot(level, along_u, along_v)],
+            src_ref=srcs[m].at[level, :, :, 1 - core],
+            dst_ref=from_side[m].at[level],
+            send_sem=side_send.at[m, level],
+            recv_sem=side_recv.at[m, level],
             device_id=sibling,
             device_id_type=MESH,
         )
 
     def v_copy(m, level, along_u):
+        xx, yy = (1 - x, 1 - y) if along_u else (vx, vy)
         return pltpu.make_async_remote_copy(
-            src_ref=acc[m].at[slot(level, 1, along_u)],
-            dst_ref=from_v[m].at[level * 2 + along_u],
-            send_sem=v_send.at[m, level * 2 + along_u],
-            recv_sem=v_recv.at[m, level * 2 + along_u],
+            src_ref=acc[m].at[level, xx, yy],
+            dst_ref=from_v[m].at[level, along_u],
+            send_sem=v_send.at[m, level, along_u],
+            recv_sem=v_recv.at[m, level, along_u],
             device_id=v_device,
             device_id_type=MESH,
         )
 
     def u_copy(m, level):
         return pltpu.make_async_remote_copy(
-            src_ref=acc[m].at[slot(level, 0, 1)],
+            src_ref=acc[m].at[level, ux, uy],
             dst_ref=from_u[m].at[level],
             send_sem=u_send.at[m, level],
             recv_sem=u_recv.at[m, level],
@@ -558,7 +566,7 @@
 
     def z_copy(m, level, upward):
         return pltpu.make_async_remote_copy(
-            src_ref=acc[m].at[slot(level, 0, 0)],
+            src_ref=acc[m].at[level, x, y],
             dst_ref=(from_low if upward else from_high)[m].at[level],
             send_sem=z_send.at[m, level],
             recv_sem=(low_recv if upward else high_recv).at[m, level],
@@ -566,278 +574,296 @@
             device_id_type=MESH,
         )
 
-    def add(m, where, other, at):
-        total = acc[m][where].astype(jnp.float32) + other[m][at].astype(jnp.float32)
-        acc[m][where] = total.astype(jnp.bfloat16)
-
-    def levels(action):
-        @pl.loop(0, 2 * tall)
-        def _(step):
-            far = tall - 1 - step // 2
-            level = jnp.where(lax.rem(step, 2) == 0, z - far, z + far)
-            use = (level >= 0) & (level < tall) & ((far > 0) | (lax.rem(step, 2) == 0))
-
-            @pl.when(use)
-            def _():
-                action(level)
-
-    def begin(level):
-        for along_v in (1, 0):
-            for along_u in (1, 0):
-                each(lambda m: load(m, level, along_v, along_u).start())
-
-    levels(begin)
-    meet(count=3 + has_up.astype(jnp.int32) + has_down.astype(jnp.int32))
-
-    def begin_side(kinds):
-        def run(level):
-            for along_v, along_u in kinds:
-                each(lambda m: side(m, level, along_v, along_u).start())
-
-        return run
-
-    levels(begin_side(((1, 1), (0, 1))))
-    levels(begin_side(((1, 0), (0, 0))))
-
-    def take(level, along_v, along_u):
-        where = slot(level, along_v, along_u)
+    def line(peer, slot):
+        return pltpu.make_async_remote_copy(
+            src_ref=sums.at[peer],
+            dst_ref=rows.at[slot],
+            send_sem=line_send.at[peer],
+            recv_sem=row_recv.at[slot],
+            device_id=(peer, f),
+            device_id_type=MESH,
+        )
+
+    def onward(slot, to_side, own_block=False):
+        return pltpu.make_async_remote_copy(
+            src_ref=sums.at[d] if own_block else rows.at[slot],
+            dst_ref=rows.at[slot],
+            send_sem=on_send.at[1 if to_side else 0, slot],
+            recv_sem=row_recv.at[slot],
+            device_id=(d, f_side if to_side else f_y),
+            device_id_type=MESH,
+        )
+
+    def small_copy(peer, slot):
+        return pltpu.make_async_remote_copy(
+            src_ref=small,
+            dst_ref=small_all.at[slot],
+            send_sem=small_send.at[peer],
+            recv_sem=small_recv.at[slot],
+            device_id=grid.peer(peer),
+            device_id_type=MESH,
+        )
+
+    def square_copy(peer, slot):
+        return pltpu.make_async_remote_copy(
+            src_ref=square_mine,
+            dst_ref=square_all.at[slot],
+            send_sem=square_send.at[peer],
+            recv_sem=square_recv.at[slot],
+            device_id=grid.peer(peer),
+            device_id_type=MESH,
+        )
+
+    levels = [level_of(j) for j in range(tall)]
+    own_rows = pltpu.make_async_copy(sums.at[d], rows.at[me], row_own)
+    own_rows.start()
+    for level in levels:
+        each(lambda m: load(m, level).start())
+    meet(grid.total - 1)
+
+    @pl.loop(1, grid.dp)
+    def _(step):
+        line(lax.rem(d + step, grid.dp), me).start()
+
+    for level in levels:
+        each(lambda m: side(m, level).start())
+    onward(me, False, True).start()
+    onward(me, True, True).start()
+
+    @pl.loop(1, grid.total)
+    def _(step):
+        small_copy(lax.rem(me + step, grid.total), me).start()
+
+    small_all[me] = small[...]
+
+    def first(j):
+        level = levels[j]
 
         def run(m):
-            load(m, level, along_v, along_u).wait()
-            side(m, level, along_u, along_v).wait_recv()
-            add(m, where, from_sibling, where)
+            load(m, level).wait()
+            side(m, level).wait_recv()
+            for xx in range(2):
+                for yy in range(2):
+                    total = acc[m][level, xx, yy].astype(jnp.float32) + from_side[m][level, xx, yy].astype(jnp.float32)
+                    acc[m][level, xx, yy] = total.astype(jnp.bfloat16)
+            v_copy(m, level, 1).start()
+            v_copy(m, level, 0).start()
 
         each(run)
 
-    def first(level):
-        for along_u in (1, 0):
-            take(level, 1, along_u)
-            each(lambda m: v_copy(m, level, along_u).start())
-
-    levels(first)
-
-    def second(level):
-        for along_u in (1, 0):
-            take(level, 0, along_u)
-
-            def run(m):
-                v_copy(m, level, along_u).wait_recv()
-                add(m, slot(level, 0, along_u), from_v, level * 2 + along_u)
-                if along_u:
-                    u_copy(m, level).start()
-
-            each(run)
-
-    levels(second)
-
-    def third(level):
-        where = slot(level, 0, 0)
+    def add(m, level, xx, yy, other):
+        total = acc[m][level, xx, yy].astype(jnp.float32) + other.astype(jnp.float32)
+        acc[m][level, xx, yy] = total.astype(jnp.bfloat16)
+
+    def second(j):
+        level = levels[j]
+
+        def run(m):
+            v_copy(m, level, 1).wait_recv()
+            add(m, level, ux, uy, from_v[m][level, 1])
+            u_copy(m, level).start()
+
+        each(run)
+
+    def second_own(j):
+        level = levels[j]
+
+        def run(m):
+            v_copy(m, level, 0).wait_recv()
+            add(m, level, x, y, from_v[m][level, 0])
+
+        each(run)
+
+    def third(j):
+        level = levels[j]
 
         def run(m):
             u_copy(m, level).wait_recv()
-            add(m, where, from_u, level)
+            add(m, level, x, y, from_u[m][level])
+
+            @pl.when((level >= z) & has_down)
+            def _():
+                z_copy(m, level, True).wait_recv()
+                add(m, level, x, y, from_low[m][level])
+
+            @pl.when((level <= z) & has_up)
+            def _():
+                z_copy(m, level, False).wait_recv()
+                add(m, level, x, y, from_high[m][level])
+
+            @pl.when(level > z)
+            def _():
+                z_copy(m, level, True).start()
+
+            @pl.when(level < z)
+            def _():
+                z_copy(m, level, False).start()
 
         each(run)
 
-        @pl.when((level >= z) & has_down)
-        def _():
-            def run(m):
-                z_copy(m, level, True).wait_recv()
-                add(m, where, from_low, level)
-
-            each(run)
-
-        @pl.when((level <= z) & has_up)
-        def _():
-            def run(m):
-                z_copy(m, level, False).wait_recv()
-                add(m, where, from_high, level)
-
-            each(run)
-
-        @pl.when(level > z)
-        def _():
-            each(lambda m: z_copy(m, level, True).start())
-
-        @pl.when(level < z)
-        def _():
-            each(lambda m: z_copy(m, level, False).start())
-
-    levels(third)
-
-    def finish(m):
-        outs[m][...] = acc[m][slot(z, 0, 0)].astype(jnp.float32)
-
-    each(finish)
-
-    def drain(level):
-        for along_v in (0, 1):
-            for along_u in (0, 1):
-                each(lambda m: side(m, level, along_v, along_u).wait_send())
-        for along_u in (0, 1):
-            each(lambda m: v_copy(m, level, along_u).wait_send())
+    def pass_lines():
+        @pl.loop(1, grid.dp)
+        def _(step):
+            slot = lax.rem(d + grid.dp - step, grid.dp) * grid.fs + f
+            line(d, slot).wait_recv()
+            onward(slot, False).start()
+            onward(slot, True).start()
+
+    def pass_y():
+        @pl.loop(0, grid.dp)
+        def _(step):
+            slot = lax.rem(d + grid.dp - step, grid.dp) * grid.fs + f_y
+            line(d, slot).wait_recv()
+            onward(slot, True).start()
+
+    def rows_in():
+        own_rows.wait()
+
+        @pl.loop(0, grid.dp)
+        def _(step):
+            line(d, step * grid.fs + f_side).wait_recv()
+            line(d, step * grid.fs + f_far).wait_recv()
+
+    table_rows = table_out.shape[0]
+    whole_blocks = table_rows // ROW_BLOCK
+    square_mine[...] = jnp.zeros_like(square_mine)
+
+    def fold(values):
+        n, lanes = values.shape
+        part = jnp.sum(values.reshape(n // 8, 8, lanes), 0)
+        total = part[:, :128]
+        for at in range(128, lanes, 128):
+            total = total + part[:, at : at + 128]
+        return total
+
+    def spread(start, size):
+        per = rows.shape[1]
+        group = 8
+        total = jnp.zeros((size, D), jnp.float32)
+        for g in range(0, grid.total, group):
+            place = start + lax.broadcasted_iota(jnp.int32, (size, group * per), 0)
+            wanted = ids[:, g * per : (g + group) * per]
+            hot = jnp.where(place == wanted, 1.0, 0.0).astype(jnp.bfloat16)
+            total = total + matmul(hot, rows[g : g + group].reshape(group * per, D))
+        low = total.astype(jnp.bfloat16)
+        table_out[pl.ds(start, size), :] = low
+        wide = low.astype(jnp.float32)
+        square_mine[8:16, :] += fold(wide * wide)
+
+    def spread_blocks(first_block, last_block):
+        @pl.loop(first_block, last_block)
+        def _(block):
+            spread(pl.multiple_of(block * ROW_BLOCK, ROW_BLOCK), ROW_BLOCK)
+
+    for j in range(tall):
+        first(j)
+    pass_lines()
+    second(0)
+    second_own(0)
+    second(1)
+    second_own(1)
+    third(0)
+    pass_y()
+    second(2)
+    second_own(2)
+    third(1)
+    second(3)
+    second_own(3)
+    rows_in()
+    spread_blocks(0, whole_blocks // 2)
+    third(2)
+    spread_blocks(whole_blocks // 2, whole_blocks)
+    if table_rows % ROW_BLOCK:
+        spread(whole_blocks * ROW_BLOCK, table_rows % ROW_BLOCK)
+    third(3)
+
+    def give(m):
+        wide = acc[m][z, x, y].astype(jnp.float32)
+        outs[m][...] = wide
+        square_mine[0:8, :] += fold(wide * wide)
+
+    each(give)
+
+    @pl.loop(1, grid.total)
+    def _(step):
+        square_copy(lax.rem(me + step, grid.total), me).start()
+
+    square_all[me] = square_mine[...]
+
+    @pl.loop(1, grid.total)
+    def _(step):
+        peer = lax.rem(me + step, grid.total)
+        small_copy(peer, peer).wait_recv()
+
+    small_out[...] = jnp.sum(small_all[...], 0)
+
+    for level in levels:
+        each(lambda m: side(m, level).wait_send())
+        each(lambda m: v_copy(m, level, 0).wait_send())
+        each(lambda m: v_copy(m, level, 1).wait_send())
         each(lambda m: u_copy(m, level).wait_send())
 
         @pl.when(level != z)
         def _():
             each(lambda m: z_copy(m, level, True).wait_send())
 
-    levels(drain)
-
-
-def scatter(srcs, number):
+    @pl.loop(0, grid.dp)
+    def _(step):
+        onward(step * grid.fs + f, False).wait_send()
+        onward(step * grid.fs + f, True).wait_send()
+        onward(step * grid.fs + f_y, True).wait_send()
+
+    @pl.loop(1, grid.dp)
+    def _(step):
+        line(lax.rem(d + step, grid.dp), me).wait_send()
+
+    @pl.loop(1, grid.total)
+    def _(step):
+        peer = lax.rem(me + step, grid.total)
+        square_copy(peer, peer).wait_recv()
+        square_copy(peer, peer).wait_send()
+        small_copy(peer, peer).wait_send()
+
+    square_out[...] = jnp.sum(square_all[...], 0)
+
+
+def finish(srcs, sums, ids, small, vocab_rows, number):
     grid = Grid()
     count = len(srcs)
     tall = grid.tall
     blocks = [src.shape[1:] for src in srcs]
-    buffers = [
-        pltpu.VMEM((number_of,) + block, jnp.bfloat16)
-        for number_of in (4 * tall, 4 * tall, 2 * tall, tall, tall, tall)
-        for block in blocks
+    srcs = [src.reshape((tall, 2, 2, 2) + src.shape[1:]) for src in srcs]
+    leads = ((tall, 2, 2), (tall, 2, 2), (tall, 2), (tall,), (tall,), (tall,))
+    buffers = [pltpu.VMEM(lead + block, jnp.bfloat16) for lead in leads for block in blocks]
+    cap = sums.shape[1]
+    buffers += [
+        pltpu.VMEM((grid.total, cap, D), jnp.bfloat16),
+        pltpu.VMEM((grid.total,) + small.shape, jnp.float32),
+        pltpu.VMEM((16, 128), jnp.float32),
+        pltpu.VMEM((grid.total, 16, 128), jnp.float32),
     ]
-    semaphores = [
-        pltpu.SemaphoreType.DMA((count, number_of))
-        for number_of in (4 * tall, 4 * tall, 4 * tall, 2 * tall, 2 * tall, tall, tall, tall, tall, tall)
-    ]
-    return pl.pallas_call(
-        functools.partial(scatter_kernel, grid, count),
-        out_shape=[jax.ShapeDtypeStruct(block, jnp.float32) for block in blocks],
-        in_specs=[pl.BlockSpec(memory_space=pl.ANY)] * count,
-        out_specs=[pl.BlockSpec(memory_space=pltpu.VMEM)] * count,
+    dma = pltpu.SemaphoreType.DMA
+    by_level = dma((count, tall))
+    semaphores = [by_level, by_level, by_level, dma((count, tall, 2)), dma((count, tall, 2))] + [by_level] * 5
+    by_device = dma((grid.total,))
+    semaphores += [dma, dma((grid.dp,)), dma((2, grid.total)), by_device, by_device, by_device, by_device, by_device]
+    anywhere, inside = pl.BlockSpec(memory_space=pl.ANY), pl.BlockSpec(memory_space=pltpu.VMEM)
+    results = pl.pallas_call(
+        functools.partial(finish_kernel, grid, count),
+        out_shape=[jax.ShapeDtypeStruct(block, jnp.float32) for block in blocks]
+        + [
+            jax.ShapeDtypeStruct((vocab_rows, D), jnp.bfloat16),
+            jax.ShapeDtypeStruct(small.shape, jnp.float32),
+            jax.ShapeDtypeStruct((16, 128), jnp.float32),
+        ],
+        in_specs=[anywhere] * (count + 1) + [inside] * 2,
+        out_specs=[inside] * (count + 3),
         scratch_shapes=buffers + semaphores,
         compiler_params=pltpu.CompilerParams(
-            collective_id=number, has_side_effects=True, vmem_limit_bytes=56 * 1024 * 1024
+            collective_id=number, has_side_effects=True, vmem_limit_bytes=62 * 1024 * 1024
         ),
-    )(*srcs)
-
-
-def rows_kernel(grid, src, out, own_sem, line_send, side_send, y_send, recv_sem):
-    d, f = lax.axis_index("dp"), lax.axis_index("fsdp")
-    me = d * grid.fs + f
-    f_side = f + 1 - 2 * lax.rem(f, 2)
-    f_y = lax.rem(f + 2, grid.fs)
-    f_y_side = lax.rem(f_side + 2, grid.fs)
-    own = pltpu.make_async_copy(src.at[d], out.at[me], own_sem)
-    own.start()
-
-    @pl.loop(1, grid.dp)
-    def _(step):
-        greet((lax.rem(d + step, grid.dp), f))
-
-    greet((d, f_side))
-    greet((d, f_y))
-    meet(count=grid.dp + 1)
-
-    def line(peer, slot):
-        return pltpu.make_async_remote_copy(
-            src_ref=src.at[peer],
-            dst_ref=out.at[slot],
-            send_sem=line_send.at[peer],
-            recv_sem=recv_sem.at[slot],
-            device_id=(peer, f),
-            device_id_type=MESH,
-        )
-
-    def onward(slot, column, sem, own_block):
-        return pltpu.make_async_remote_copy(
-            src_ref=src.at[d] if own_block else out.at[slot],
-            dst_ref=out.at[slot],
-            send_sem=sem.at[slot],
-            recv_sem=recv_sem.at[slot],
-            device_id=(d, column),
-            device_id_type=MESH,
-        )
-
-    onward(me, f_y, y_send, True).start()
-    onward(me, f_side, side_send, True).start()
-
-    @pl.loop(1, grid.dp)
-    def _(step):
-        peer = lax.rem(d + step, grid.dp)
-        line(peer, me).start()
-
-    @pl.loop(1, grid.dp)
-    def _(step):
-        slot = lax.rem(d + grid.dp - step, grid.dp) * grid.fs + f
-        line(d, slot).wait_recv()
-        onward(slot, f_y, y_send, False).start()
-        onward(slot, f_side, side_send, False).start()
-
-    @pl.loop(0, grid.dp)
-    def _(step):
-        slot = lax.rem(d + grid.dp - step, grid.dp) * grid.fs + f_y
-        line(d, slot).wait_recv()
-        onward(slot, f_side, side_send, False).start()
-
-    @pl.loop(0, grid.dp)
-    def _(step):
-        line(d, step * grid.fs + f_side).wait_recv()
-        line(d, step * grid.fs + f_y_side).wait_recv()
-        onward(step * grid.fs + f, f_y, y_send, False).wait_send()
-        onward(step * grid.fs + f, f_side, side_send, False).wait_send()
-        onward(step * grid.fs + f_y, f_side, side_send, False).wait_send()
-
-    @pl.loop(1, grid.dp)
-    def _(step):
-        line(lax.rem(d + step, grid.dp), me).wait_send()
-
-    own.wait()
-
-
-def share_rows(src, number):
-    grid = Grid()
-    return pl.pallas_call(
-        functools.partial(rows_kernel, grid),
-        out_shape=jax.ShapeDtypeStruct((grid.total,) + src.shape[1:], src.dtype),
-        in_specs=[pl.BlockSpec(memory_space=pl.ANY)],
-        out_specs=pl.BlockSpec(memory_space=pl.ANY),
-        scratch_shapes=[
-            pltpu.SemaphoreType.DMA,
-            pltpu.SemaphoreType.DMA((grid.dp,)),
-            pltpu.SemaphoreType.DMA((grid.total,)),
-            pltpu.SemaphoreType.DMA((grid.total,)),
-            pltpu.SemaphoreType.DMA((grid.total,)),
-        ],
-        compiler_params=pltpu.CompilerParams(collective_id=number, has_side_effects=True),
-    )(src)
-
-
-def spread_kernel(vocab_rows, ids_ref, rows_ref, out_ref, square_ref):
-    block = out_ref.shape[0]
-    base = pl.program_id(0) * block
-    place = base + lax.broadcasted_iota(jnp.int32, (block, ids_ref.shape[1]), 0)
-    hot = jnp.where(place == ids_ref[...], 1.0, 0.0).astype(jnp.bfloat16)
-    total = matmul(hot, rows_ref[...])
-    low = total.astype(jnp.bfloat16)
-    out_ref[...] = low
-    wide = low.astype(jnp.float32)
-    part = jnp.sum((wide * wide).reshape(block // 8, 8, D), 0)
-
-    @pl.when(pl.program_id(0) == 0)
-    def _():
-        square_ref[...] = jnp.zeros_like(square_ref)
-
-    square_ref[...] += part
-
-
-def spread_rows(ids, rows, vocab_rows):
-    count = rows.shape[0]
-    block = 512
-    steps = -(-vocab_rows // block)
-    return pl.pallas_call(
-        functools.partial(spread_kernel, vocab_rows),
-        grid=(steps,),
-        out_shape=[
-            jax.ShapeDtypeStruct((vocab_rows, D), jnp.bfloat16),
-            jax.ShapeDtypeStruct((8, D), jnp.float32),
-        ],
-        in_specs=[
-            pl.BlockSpec((1, count), lambda i: (0, 0)),
-            pl.BlockSpec((count, D), lambda i: (0, 0)),
-        ],
-        out_specs=[pl.BlockSpec((block, D), lambda i: (i, 0)), pl.BlockSpec((8, D), lambda i: (0, 0))],
-        compiler_params=pltpu.CompilerParams(vmem_limit_bytes=48 * 1024 * 1024),
-    )(ids.reshape(1, count), rows)
+    )(*srcs, sums, ids.reshape(1, -1), small)
+    return (results[:count], *results[count:])
 
 
 def plain_body(
@@ -1222,30 +1248,23 @@
         grad.astype(jnp.bfloat16).reshape(total, -1, grad.shape[1])
         for grad in (*matrix_grads, grad_proj_head)
     ]
-    weight_grads = scatter(partials, 4)
-
+    small_local = jnp.concatenate([gain_one, gain_two, gain_three, grad_bias_table.reshape(-1)])
+    width = -(-small_local.shape[0] // 1024) * 8
+    small_local = jnp.pad(small_local, (0, width * 128 - small_local.shape[0]))
     grad_low = grad_rows.astype(jnp.bfloat16)
     slot_sums = matmul_tn(slot_hot, grad_low).astype(jnp.bfloat16).reshape(dp_count, CAP, D)
-    all_rows = share_rows(slot_sums, 5)
-    table_grad, table_squares = spread_rows(
-        asked.reshape(-1), all_rows.reshape(total * CAP, D), vocab_rows
-    )
-    table_squares = jnp.sum(table_squares)
+    weight_grads, table_grad, summed, squares = finish(
+        partials, slot_sums, asked.reshape(-1), small_local.reshape(width, 128), vocab_rows, 4
+    )
+    table_squares = jnp.sum(squares[8:])
     table_grad, table_squares = once(
-        any_spilled, lambda _: with_squares(dense_table_grad(ids_flat, grad_low, vocab_rows, row_base)), (table_grad, table_squares)
-    )
-    squares = table_squares / fsdp_count
-    for gradient in weight_grads:
-        squares = squares + jnp.sum(gradient * gradient)
-    small_local = jnp.concatenate(
-        [gain_one, gain_two, gain_three, grad_bias_table.reshape(-1), squares[None]]
-    )
-    width = -(-small_local.shape[0] // 1024) * 8
-    small_local = jnp.pad(small_local, (0, width * 128 - small_local.shape[0]))
-    summed = jnp.sum(exchange(small_local.reshape(width, 128), False, 6), 0).reshape(-1)
+        any_spilled,
+        lambda _: with_squares(dense_table_grad(ids_flat, grad_low, vocab_rows, row_base)),
+        (table_grad, table_squares),
+    )
     small_size = small_params.shape[0]
-    total_squares = summed[small_size - 1]
-    small_grad = jnp.concatenate([summed[: small_size - 1], grad_log_scale[None]])
+    total_squares = jnp.sum(squares[:8]) + table_squares / fsdp_count
+    small_grad = jnp.concatenate([summed.reshape(-1)[: small_size - 1], grad_log_scale[None]])
     norm_value = jnp.sqrt(total_squares + jnp.sum(small_grad * small_grad))
     factor = jnp.minimum(1.0, CLIP / (norm_value + 1e-06))
     updates = (
@@ -1265,7 +1284,7 @@
 
 def with_squares(table_grad):
     wide = table_grad.astype(jnp.float32)
-    return (table_grad, jnp.sum(wide * wide))
+    return (table_grad, lax.psum(jnp.sum(wide * wide), ("dp", "fsdp")))
 
 
 def solution(mesh):

time: 642 us -> 576 us (0.90)
  Pallas kernels: 341 us -> 285 us
  other arithmetic: 96.6 us -> 80.2 us
  matrix products: 113 us -> 122 us
    pallas_call x3 -> x1, Pallas kernels: 194 us -> 157 us  [finish(): pl.pallas_call(functools.partial(finish_kernel, grid, count), out_shape=[...]
    pallas_call x3 -> x2, Pallas kernels: 43.8 us -> 25.1 us  [exchange(): pl.pallas_call(functools.partial(exchange_kernel, grid, spread), out_shap...]
    dot_general x7, matrix products: 28.6 us -> 38.4 us  [matmul(): return jnp.dot(left_side, right_side, preferred_element_type=jnp.float32)]
    reduce_sum x7 -> x1, other arithmetic: 9.53 us -> 1.29 us  [fast_body(): table_squares = jnp.sum(squares[8:])]
where the time goes in v2:
time: 576 us; the launch traced here: 566 us
  Pallas kernels  285 us (49%)
  matrix products  122 us (21%)
  other arithmetic  80.2 us (14%)
  local copies, waits for them, and re-layouts  56.5 us (10%)
  between operations  21.7 us (4%)
    pallas_call x1, Pallas kernels, finish(): pl.pallas_call(functools.partial(finish_kernel, grid, count), out_shape=[...  157 us
    pallas_call x1, Pallas kernels, gather(): pl.pallas_call(functools.partial(gather_kernel, grid, count), out_shape=[...  103 us
    dot_general x7, matrix products, matmul(): return jnp.dot(left_side, right_side, preferred_element_type=jnp.float32)  38.4 us
    sub x6, other arithmetic, adam_update(): return (first_new, second_new, param - rate * (direction + decay * param))  34.1 us
    dot_general x7, matrix products, matmul_tn(): lax.dot_general(left_side, right_side, (((0,), (0,)), ((), ())), preferre...  33.7 us
    dot_general x6, matrix products, matmul_nt(): lax.dot_general(left_side, right_side, (((1,), (1,)), ((), ())), preferre...  29.8 us
    pallas_call x2, Pallas kernels, exchange(): pl.pallas_call(functools.partial(exchange_kernel, grid, spread), out_shap...  25.1 us
    unnamed x180, local copies, waits for them, and re-layouts  11.7 us

profile of v2, /device:TPU:0, one launch (start us, length us, event | category | flops | bytes accessed | tf_op | source)
XLA Modules:
  0.0 565.9 jit_solution(14476968154656633895)
XLA Ops:
  15.5 12.3 %shard_map.416 = s32[32,8,128]{2,1,0:T(8,128)} custom-call(s32[32,8,128]{2,1,0:T(8,128)} %pad_add_fusion.src), custom_call_target="tpu_custom_call" | custom-call | tf_op jit(solution)/shard_map/pallas_call | solution.py:284
  40.8 9.0 %gather_fusion.1 = bf16[1024,768]{1,0:T(8,128)(2,1)S(1)} fusion(f32[4016,768]{1,0:T(8,128)} %param.38, s32[1024]{0:T(1024)S(1)} %bitcast_clamp_fusion), kind=kCustom, calls=%fused_computation.1 | custom fusion | bytes 3149824 | tf_op jit(solution)/shard_map/jit(_take)/gather | solution.py:1185
  51.3 102.5 %shard_map.417 = (bf16[32,24,2304]{2,1,0:T(8,128)(2,1)}, bf16[32,24,768]{2,1,0:T(8,128)(2,1)}, bf16[32,24,3072]{2,1,0:T(8,128)(2,1)}, bf16[32,96,768]{2,1,0:T(8,...) custom-call(bf16[24,2304]{1,0:T(8,128)(2,1)} %convert_element_type.174.refs_0_, ...), custom_call_target="tpu_custom_call" | custom-call | tf_op jit(solution)/shard_map/pallas_call | solution.py:466
  157.2 5.0 fusion.19
  162.3 7.8 %convert.9 = bf16[4016,768]{1,0:T(8,128)(2,1)} convert(f32[4016,768]{1,0:T(8,128)} %param.38) | non-fusion elementwise | flops 3084288 | bytes 18505728
  173.1 7.7 %convolution_convert_fusion = bf16[1024,2304]{1,0:T(8,128)(2,1)} fusion(bf16[768,2304]{1,0:T(8,128)(2,1)} %bitcast.228, f32[1024,768]{1,0:T(8,128)S(1)} %copy-done.8, f32[768]{0:T(1024)S(1)} %copy-done.60, f32[1024]{0:T(1024)S(1)} %add_rsqrt_fusion.2), kind=kOutput, calls=%fused_computation.38 | convolution fusion | flops 3628597248 | bytes 11410432 | tf_op jit(solution)/shard_map/dot_general | solution.py:49
  180.8 6.6 %copy.112 = bf16[1024,2304]{0,1:T(8,128)(2,1)} copy(bf16[1024,2304]{1,0:T(8,128)(2,1)} %convolution_convert_fusion) | data formatting | bytes 9437184 | tf_op jit(solution)/shard_map/convert_element_type | solution.py:96
  187.5 3.6 copy.140
  197.7 3.3 fusion.94
  209.1 13.8 %fusion.83 = f32[1024,3072]{1,0:T(8,128)S(1)} fusion(bf16[768,3072]{1,0:T(8,128)(2,1)S(1)} %bitcast.220, f32[1024,768]{1,0:T(8,128)S(1)} %get-tuple-element.268, f32[768]{0:T(1024)S(1)} %copy-done.62, f32[1024]{0:T(1024)S(1)} %add_rsqrt_fusion.1), kind=kOutput, calls=%fused_computation.209 | convolution fusion | flops 4834197504 | bytes 20454400 | tf_op jit(solution)/shard_map/dot_general | solution.py:49
  223.0 7.5 %multiply_reduce_fusion.7 = (f32[1024]{0:T(1024)S(1)}, f32[1024,768]{1,0:T(8,128)S(1)}) fusion(f32[1024,768]{1,0:T(8,128)S(1)} %get-tuple-element.268, bf16[3072,768]{1,0:T(8,128)(2,1)S(1)} %bitcast.227, f32[1024,3072]{1,0:T(8,128)S(1)} %fusion.83), kind=kOutput, calls=%fused_computation.75 | convolution fusion | flops 4862508032 | bytes 23597056 | tf_op jit(solution)/shard_map/dot_general | solution.py:49
  234.2 12.8 %shard_map.418 = bf16[32,16,384]{2,1,0:T(8,128)(2,1)} custom-call(bf16[16,384]{1,0:T(8,128)(2,1)} %reshape.479.src), custom_call_target="tpu_custom_call" | custom-call | tf_op jit(solution)/shard_map/pallas_call | solution.py:284
  261.3 15.2 %fusion.12 = bf16[1024,3072]{1,0:T(8,128)(2,1)S(1)} fusion(f32[1024,3072]{1,0:T(8,128)} %copy-done.79, bf16[1024,768]{1,0:T(8,128)(2,1)S(1)} %fusion.38, bf16[3072,768]{1,0:T(8,128)(2,1)} %bitcast.224), kind=kOutput, calls=%fused_computation.25 | convolution fusion | flops 4894752768 | bytes 25165824 | tf_op jit(solution)/shard_map/dot_general | solution.py:59
  276.6 5.5 multiply_reduce_fusion.2
  290.9 6.5 %convolution_bitcast_fusion = bf16[8,128,1,12,64]{1,4,3,0,2:T(8,128)(2,1)} fusion(bf16[8,128,12,64]{1,0,3,2:T(8,128)(2,1)S(1)} %bitcast.182, f32[8,12,128,128]{2,3,1,0:T(8,128)} %copy-done, f32[8,12,128]{2,1,0:T(8,128)S(1)} %copy-done.19), kind=kOutput, calls=%fused_computation.89 | convolution fusion | flops 204472320 | bytes 9486336 | tf_op jit(solution)/shard_map/bhqk,bqhd->bkhd/dot_general | solution.py:166
  302.0 3.8 multiply_bitcast_fusion
  308.0 9.3 %copy.126 = bf16[8,128,3,12,64]{1,0,4,3,2:T(8,128)(2,1)S(1)} copy(bf16[8,128,3,12,64]{1,4,3,0,2:T(8,128)(2,1)S(1)} %maximum_convert_fusion) | data formatting | bytes 9437184 | tf_op jit(solution)/shard_map/convert_element_type | solution.py:182
  317.4 5.9 %convolution_convert_fusion.3 = bf16[768,2304]{1,0:T(8,128)(2,1)} fusion(bf16[288,8,8,128]{3,2,1,0:T(8,128)(2,1)S(1)} %bitcast.190, f32[1024,768]{1,0:T(8,128)S(1)} %copy-done.10, f32[768]{0:T(1024)S(1)} %copy-done.61, f32[1024]{0:T(1024)S(1)} %add_rsqrt_fusion.2), kind=kOutput, calls=%fused_computation.41 | convolution fusion | flops 3628007424 | bytes 11410432 | tf_op jit(solution)/shard_map/dot_general | solution.py:53
  325.9 7.2 %convolution_convert_fusion.2 = bf16[768,3072]{1,0:T(8,128)(2,1)} fusion(bf16[1024,3072]{1,0:T(8,128)(2,1)S(1)} %bitcast.234, f32[1024,768]{1,0:T(8,128)S(1)} %copy-done.17, f32[768]{0:T(1024)S(1)} %copy-done.63, f32[1024]{0:T(1024)S(1)} %copy-done.59), kind=kOutput, calls=%fused_computation.40 | convolution fusion | flops 4836556800 | bytes 14162944 | tf_op jit(solution)/shard_map/dot_general | solution.py:53
  333.1 12.2 %convolution_convert_fusion.1 = bf16[3072,768]{1,0:T(8,128)(2,1)} fusion(bf16[1024,768]{1,0:T(8,128)(2,1)S(1)} %copy-done.23, f32[1024,3072]{1,0:T(8,128)} %copy-done.79), kind=kOutput, calls=%fused_computation.39 | convolution fusion | flops 4862509056 | bytes 18874368 | tf_op jit(solution)/shard_map/dot_general | solution.py:53
  346.9 4.5 multiply_reduce_fusion.3
  352.4 3.5 fusion.39
  360.8 157.3 %shard_map.419 = (f32[24,2304]{1,0:T(8,128)}, f32[24,768]{1,0:T(8,128)}, f32[24,3072]{1,0:T(8,128)}, f32[96,768]{1,0:T(8,128)}, f32[24,768]{1,0:T(8,128)}, /*ind...) custom-call(bf16[4,2,2,2,24,2304]{5,4,3,2,1,0:T(8,128)(2,1)} %bitcast.196, ...), custom_call_target="tpu_custom_call" | custom-call | tf_op jit(solution)/shard_map/pallas_call | solution.py:851
  523.2 29.6 %multiply_subtract_fusion = (f32[4016,768]{1,0:T(8,128)}, f32[4016,768]{1,0:T(8,128)}, f32[4016,768]{1,0:T(8,128)}) fusion(f32[4016,768]{1,0:T(8,128)} %param.38, f32[]{:T(128)S(6)} %min.11, bf16[4016,768]{1,0:T(8,128)(2,1)} %get-tuple-element.154, f32[4016,768]{1,0:T(8,128)} %param.40, f32[4016,768]{1,0:T(8,128)} %param.39), kind=kLoop, calls=%fused_computation.28 | loop fusion | flops 52432896 | bytes 80191488 | tf_op jit(solution)/shard_map/sub | solution.py:207
  (274 shorter events, 91.8 us)
Async XLA Ops:
  14.2 143.0 %copy-start.66 = (s32[1024]{0:T(1024)}, s32[1024]{0:T(1024)S(1)}, u32[]{:S(2)}) copy-start(s32[1024]{0:T(1024)S(1)} %get-tuple-element.262) | copy-start | bytes 12292
  49.7 104.0 %copy-start.64 = (s32[2,4,128]{2,1,0:T(4,128)S(1)}, s32[2,4,128]{2,1,0:T(4,128)}, u32[]{:S(2)}) copy-start(s32[2,4,128]{2,1,0:T(4,128)} %param.36) | copy-start | bytes 12292
  49.8 104.6 %copy-start.56 = (f32[2689]{0:T(1024)S(1)}, f32[2689]{0:T(1024)}, u32[]{:S(2)}) copy-start(f32[2689]{0:T(1024)} %param.56) | copy-start | bytes 32272
  206.7 16.2 %slice-start.6 = ((s8[4718592]{0:T(1024)(128)(4,1)}), s8[4194304]{0:T(1024)(128)(4,1)S(1)}, s32[]{:S(2)}) async-start(s8[4718592]{0:T(1024)(128)(4,1)} %bitcast.225), calls=%async_computation.10 | async-start | bytes 8388608
  260.1 16.4 %slice-start.4 = ((s8[4718592]{0:T(1024)(128)(4,1)}), s8[4194304]{0:T(1024)(128)(4,1)S(1)}, s32[]{:S(2)}) async-start(s8[4718592]{0:T(1024)(128)(4,1)} %bitcast.221), calls=%async_computation.8 | async-start | bytes 8388608
  261.2 15.3 %copy-start.16 = (f32[1024,768]{1,0:T(8,128)S(1)}, f32[1024,768]{1,0:T(8,128)}, u32[]{:S(2)}) copy-start(f32[1024,768]{1,0:T(8,128)} %copy-done.15) | copy-start | bytes 9437188
  308.0 17.9 %slice-start.8 = ((s8[6291456]{0:T(1024)(128)(4,1)}), s8[4194304]{0:T(1024)(128)(4,1)S(1)}, s32[]{:S(2)}) async-start(s8[6291456]{0:T(1024)(128)(4,1)} %bitcast.233), calls=%async_computation.12 | async-start | bytes 8388608
  360.8 158.6 %copy-start.30 = (s32[2,4,128]{2,1,0:T(4,128)S(1)}, s32[2,4,128]{2,1,0:T(4,128)}, u32[]{:S(2)}) copy-start(s32[2,4,128]{2,1,0:T(4,128)} %param.35) | copy-start | bytes 12292
  523.0 29.8 %copy-start.26 = (f32[24,2304]{1,0:T(8,128)S(1)}, f32[24,2304]{1,0:T(8,128)}, u32[]{:S(2)}) copy-start(f32[24,2304]{1,0:T(8,128)} %param.41) | copy-start | bytes 663556
  523.0 29.8 %copy-start.39 = (f32[24,2304]{1,0:T(8,128)S(1)}, f32[24,2304]{1,0:T(8,128)}, u32[]{:S(2)}) copy-start(f32[24,2304]{1,0:T(8,128)} %param.43) | copy-start | bytes 663556
  523.0 29.8 %copy-start.40 = (f32[24,2304]{1,0:T(8,128)S(1)}, f32[24,2304]{1,0:T(8,128)}, u32[]{:S(2)}) copy-start(f32[24,2304]{1,0:T(8,128)} %param.42) | copy-start | bytes 663556
  523.0 29.8 %copy-start.41 = (f32[24,2304]{1,0:T(8,128)S(1)}, f32[24,2304]{1,0:T(8,128)}, u32[]{:S(2)}) copy-start(f32[24,2304]{1,0:T(8,128)} %get-tuple-element.155) | copy-start | bytes 663556
  523.0 30.8 %copy-start.37 = (f32[24,768]{1,0:T(8,128)S(1)}, f32[24,768]{1,0:T(8,128)}, u32[]{:S(2)}) copy-start(f32[24,768]{1,0:T(8,128)} %param.44) | copy-start | bytes 221188
  523.0 30.8 %copy-start.38 = (f32[24,768]{1,0:T(8,128)S(1)}, f32[24,768]{1,0:T(8,128)}, u32[]{:S(2)}) copy-start(f32[24,768]{1,0:T(8,128)} %param.53) | copy-start | bytes 221188
  523.1 30.8 %copy-start.48 = (f32[24,768]{1,0:T(8,128)S(1)}, f32[24,768]{1,0:T(8,128)}, u32[]{:S(2)}) copy-start(f32[24,768]{1,0:T(8,128)} %param.55) | copy-start | bytes 221188
  523.1 30.8 %copy-start.49 = (f32[24,768]{1,0:T(8,128)S(1)}, f32[24,768]{1,0:T(8,128)}, u32[]{:S(2)}) copy-start(f32[24,768]{1,0:T(8,128)} %param.54) | copy-start | bytes 221188
  523.1 30.8 %copy-start.50 = (f32[24,768]{1,0:T(8,128)S(1)}, f32[24,768]{1,0:T(8,128)}, u32[]{:S(2)}) copy-start(f32[24,768]{1,0:T(8,128)} %param.46) | copy-start | bytes 221188
  523.1 30.8 %copy-start.51 = (f32[24,768]{1,0:T(8,128)S(1)}, f32[24,768]{1,0:T(8,128)}, u32[]{:S(2)}) copy-start(f32[24,768]{1,0:T(8,128)} %param.45) | copy-start | bytes 221188
  523.1 30.8 %copy-start.52 = (f32[24,768]{1,0:T(8,128)S(1)}, f32[24,768]{1,0:T(8,128)}, u32[]{:S(2)}) copy-start(f32[24,768]{1,0:T(8,128)} %get-tuple-element.156) | copy-start | bytes 221188
  523.1 30.8 %copy-start.53 = (f32[24,768]{1,0:T(8,128)S(1)}, f32[24,768]{1,0:T(8,128)}, u32[]{:S(2)}) copy-start(f32[24,768]{1,0:T(8,128)} %get-tuple-element.159) | copy-start | bytes 221188
  523.1 31.6 %copy-start.24 = (f32[24,3072]{1,0:T(8,128)S(1)}, f32[24,3072]{1,0:T(8,128)}, u32[]{:S(2)}) copy-start(f32[24,3072]{1,0:T(8,128)} %param.47) | copy-start | bytes 884740
  523.1 31.6 %copy-start.31 = (f32[24,3072]{1,0:T(8,128)S(1)}, f32[24,3072]{1,0:T(8,128)}, u32[]{:S(2)}) copy-start(f32[24,3072]{1,0:T(8,128)} %param.49) | copy-start | bytes 884740
  523.2 31.6 %copy-start.32 = (f32[24,3072]{1,0:T(8,128)S(1)}, f32[24,3072]{1,0:T(8,128)}, u32[]{:S(2)}) copy-start(f32[24,3072]{1,0:T(8,128)} %param.48) | copy-start | bytes 884740
  523.2 31.6 %copy-start.36 = (f32[24,3072]{1,0:T(8,128)S(1)}, f32[24,3072]{1,0:T(8,128)}, u32[]{:S(2)}) copy-start(f32[24,3072]{1,0:T(8,128)} %get-tuple-element.157) | copy-start | bytes 884740
  (64 other events, 377.0 us)

commit v3 on v2

--- a/solution.py
+++ b/solution.py
@@ -864,6 +864,530 @@
         ),
     )(*srcs, sums, ids.reshape(1, -1), small)
     return (results[:count], *results[count:])
+
+
+WIDE = 3 * D
+PACKED = WIDE + D + 4 * D + D
+TILE_SEQS = 4
+
+
+def lane_is(shape, low, high):
+    lanes = lax.broadcasted_iota(jnp.int32, shape, len(shape) - 1)
+    return (lanes >= low) & (lanes < high)
+
+
+def gelu_parts(t):
+    inner = np.float32(np.sqrt(2 / np.pi)) * (t + 0.044715 * (t * t * t))
+    tan = jnp.tanh(inner)
+    return 0.5 * (1.0 + tan), tan
+
+
+def forward_kernel(
+    x0_ref,
+    mask_col_ref,
+    gains_ref,
+    bias_ref,
+    packed_hbm,
+    down_hbm,
+    mixed_ref,
+    attended_ref,
+    total_ref,
+    after_ref,
+    pre_ref,
+    final_ref,
+    pooled_ref,
+    projected_ref,
+    packed,
+    down,
+    load_sem,
+):
+    step = pl.program_id(0)
+    tile_seqs = x0_ref.shape[0] // L
+    edges = (0, WIDE, WIDE + D, WIDE + 5 * D, PACKED)
+
+    def load(k):
+        if k == 4:
+            return pltpu.make_async_copy(down_hbm, down, load_sem.at[k])
+        part = pl.ds(edges[k], edges[k + 1] - edges[k])
+        return pltpu.make_async_copy(packed_hbm.at[:, part], packed.at[:, part], load_sem.at[k])
+
+    def loaded(k):
+        @pl.when(step == 0)
+        def _():
+            load(k).wait()
+
+    @pl.when(step == 0)
+    def _():
+        for k in (0, 1, 2, 4, 3):
+            load(k).start()
+
+    x0 = x0_ref[...]
+    act_one = normalize(x0, gains_ref[0:1, :])[0].astype(jnp.bfloat16)
+    loaded(0)
+    for at in range(0, WIDE, D):
+        mixed_ref[:, at : at + D] = matmul(act_one, packed[:, at : at + D]).astype(jnp.bfloat16)
+
+    zero = jnp.zeros((), jnp.bfloat16)
+    for s in range(tile_seqs):
+        rows = slice(s * L, (s + 1) * L)
+        keep = jnp.where(mask_col_ref[rows, :] > 0, 0.0, -1000000000.0)
+        for pair in range(HEADS // 2):
+            at = pair * 128
+            query = mixed_ref[rows, at : at + 128]
+            key = mixed_ref[rows, D + at : D + at + 128]
+            value = mixed_ref[rows, 2 * D + at : 2 * D + at + 128]
+            mine = lane_is((L, 128), 0, HD)
+            keys = jnp.concatenate([jnp.where(mine, key, zero), jnp.where(mine, zero, key)], 0)
+            scores = (matmul_nt(keys, query) * SCALE).reshape(2, L, L)
+            scores = scores + bias_ref[2 * pair : 2 * pair + 2] + keep[None]
+            row_max = jnp.max(scores, 1, keepdims=True)
+            powers = jnp.exp(scores - row_max)
+            row_sum = jnp.sum(powers, 1, keepdims=True)
+            prob = (powers * (1.0 / row_sum)).astype(jnp.bfloat16)
+            total_ref[s, 2 * pair : 2 * pair + 2, :] = (row_max + jnp.log(row_sum))[:, 0, :]
+            flipped = jnp.transpose(value)
+            both = jnp.concatenate([matmul(flipped[:HD], prob[0]), matmul(flipped[HD:], prob[1])], 0)
+            both = jnp.transpose(both)
+            attended_ref[rows, at : at + 128] = both.astype(jnp.bfloat16)
+
+    loaded(1)
+    after = x0 + matmul(attended_ref[...], packed[:, WIDE : WIDE + D])
+    after_ref[...] = after
+    act_two = normalize(after, gains_ref[1:2, :])[0].astype(jnp.bfloat16)
+    loaded(2)
+    loaded(4)
+    final = after
+    for j in range(4):
+        at = WIDE + D + j * D
+        pre = matmul(act_two, packed[:, at : at + D])
+        pre_ref[:, j * D : (j + 1) * D] = pre
+        hidden = (pre * gelu_parts(pre)[0]).astype(jnp.bfloat16)
+        final = final + matmul(hidden, down[j * D : (j + 1) * D, :])
+    final_ref[...] = final
+    normed = normalize(final, gains_ref[2:3, :])[0]
+    weight = mask_col_ref[...]
+    for s in range(tile_seqs):
+        rows = slice(s * L, (s + 1) * L)
+        count = jnp.sum(weight[rows], 0, keepdims=True)
+        row = jnp.sum(normed[rows] * weight[rows], 0, keepdims=True) / count
+        pooled_ref[pl.ds(step * tile_seqs + s, 1), :] = row
+
+    @pl.when(step == pl.num_programs(0) - 1)
+    def _():
+        load(3).wait()
+        projected_ref[...] = matmul(pooled_ref[...].astype(jnp.bfloat16), packed[:, PACKED - D :])
+
+
+def run_forward(x0, mask_col, gains, bias_full, packed, down):
+    tokens = x0.shape[0]
+    seqs = tokens // L
+    tile = TILE_SEQS * L
+    steps = tokens // tile
+
+    def rows(width):
+        return pl.BlockSpec((tile, width), lambda i: (i, 0))
+
+    def whole(*shape):
+        return pl.BlockSpec(shape, lambda i: (0,) * len(shape), pipeline_mode=pl.Buffered(1))
+
+    def kept(width, dtype):
+        return jax.ShapeDtypeStruct((tokens, width), dtype)
+
+    anywhere = pl.BlockSpec(memory_space=pl.ANY)
+    return pl.pallas_call(
+        forward_kernel,
+        grid=(steps,),
+        out_shape=[
+            kept(WIDE, jnp.bfloat16),
+            kept(D, jnp.bfloat16),
+            jax.ShapeDtypeStruct((seqs, HEADS, L), jnp.float32),
+            kept(D, jnp.float32),
+            kept(4 * D, jnp.float32),
+            kept(D, jnp.float32),
+            jax.ShapeDtypeStruct((seqs, D), jnp.float32),
+            jax.ShapeDtypeStruct((seqs, D), jnp.float32),
+        ],
+        in_specs=[
+            rows(D),
+            rows(1),
+            whole(3, D),
+            whole(HEADS, L, L),
+            anywhere,
+            anywhere,
+        ],
+        out_specs=[rows(WIDE), rows(D), pl.BlockSpec((TILE_SEQS, HEADS, L), lambda i: (i, 0, 0)), rows(D), rows(4 * D), rows(D), whole(seqs, D), whole(seqs, D)],
+        scratch_shapes=[
+            pltpu.VMEM((D, PACKED), jnp.bfloat16),
+            pltpu.VMEM((4 * D, D), jnp.bfloat16),
+            pltpu.SemaphoreType.DMA((5,)),
+        ],
+        compiler_params=pltpu.CompilerParams(vmem_limit_bytes=60 * 1024 * 1024),
+    )(x0, mask_col, gains, bias_full, packed, down)
+
+
+BACK_SEQS = 2
+
+
+def backward_kernel(
+    x0_ref,
+    mask_col_ref,
+    mixed_ref,
+    attended,
+    total_ref,
+    after_ref,
+    pre_hbm,
+    final_ref,
+    gains_ref,
+    bias_ref,
+    pooled_ref,
+    grad_proj_ref,
+    packed_hbm,
+    down_hbm,
+    rows_ref,
+    grad_gains_ref,
+    grad_bias_ref,
+    grad_packed_hbm,
+    grad_down_hbm,
+    packed,
+    down,
+    hidden,
+    grad_pre,
+    act_one,
+    act_two,
+    branch_two,
+    branch_one,
+    grad_mixed,
+    grad_pooled,
+    stage,
+    pre_buffer,
+    load_sem,
+    store_sem,
+    pre_sem,
+):
+    step = pl.program_id(0)
+    tile_seqs = x0_ref.shape[0] // L
+    tile = tile_seqs * L
+    base = pl.multiple_of(step * tile, tile)
+    edges = (0, WIDE, WIDE + D, WIDE + 5 * D, PACKED)
+
+    def load(k):
+        if k == 4:
+            return pltpu.make_async_copy(down_hbm, down, load_sem.at[k])
+        part = pl.ds(edges[k], edges[k + 1] - edges[k])
+        to = stage.at[0] if k == 3 else packed.at[:, part]
+        return pltpu.make_async_copy(packed_hbm.at[:, part], to, load_sem.at[k])
+
+    def loaded(k):
+        @pl.when(step == 0)
+        def _():
+            load(k).wait()
+
+    def load_pre(number):
+        start = pl.multiple_of(number // 4 * tile, tile)
+        across = pl.multiple_of(lax.rem(number, 4) * D, D)
+        slot = lax.rem(number, 2)
+        return pltpu.make_async_copy(
+            pre_hbm.at[pl.ds(start, tile), pl.ds(across, D)], pre_buffer.at[slot], pre_sem.at[slot]
+        )
+
+    @pl.when(step == 0)
+    def _():
+        load_pre(0).start()
+        for k in (3, 4, 2, 1, 0):
+            load(k).start()
+        grad_gains_ref[...] = jnp.zeros_like(grad_gains_ref)
+        grad_bias_ref[...] = jnp.zeros_like(grad_bias_ref)
+        load(3).wait()
+        grad_pooled[...] = matmul_nt(grad_proj_ref[...], stage[0])
+
+    def gain_back(k, grad_out, inputs):
+        gain = gains_ref[k : k + 1, :]
+        factor = lax.rsqrt(jnp.mean(inputs * inputs, -1, keepdims=True) + EPS)
+        scaled = grad_out * gain
+        grad_gains_ref[k : k + 1, :] += jnp.sum(grad_out * inputs * factor, 0, keepdims=True)
+        return factor * (
+            scaled - inputs * (factor * factor * jnp.mean(scaled * inputs, -1, keepdims=True))
+        )
+
+    rows = pl.ds(base, tile)
+    weight = mask_col_ref[...]
+    pieces = []
+    for s in range(tile_seqs):
+        part = weight[s * L : (s + 1) * L]
+        count = jnp.sum(part, 0, keepdims=True)
+        pieces.append(part * (grad_pooled[pl.ds(step * tile_seqs + s, 1), :] / count))
+    grad_final = gain_back(2, jnp.concatenate(pieces, 0), final_ref[...])
+    branch = grad_final.astype(jnp.bfloat16)
+    branch_two[rows, :] = branch
+    loaded(4)
+    loaded(2)
+    grad_act = jnp.zeros((tile, D), jnp.float32)
+    for j in range(4):
+        part = slice(j * D, (j + 1) * D)
+        grad_hidden = matmul_nt(branch, down[part, :])
+        number = step * 4 + j
+        pl.when(number + 1 < pl.num_programs(0) * 4)(lambda: load_pre(number + 1).start())
+        load_pre(number).wait()
+        pre = pre_buffer[j % 2]
+        half, tan = gelu_parts(pre)
+        hidden[rows, part] = (pre * half).astype(jnp.bfloat16)
+        slope = np.float32(np.sqrt(2 / np.pi)) * (1.0 + (3 * 0.044715) * (pre * pre))
+        grad_part = (grad_hidden * (half + 0.5 * pre * (1.0 - tan * tan) * slope)).astype(jnp.bfloat16)
+        grad_pre[rows, part] = grad_part
+        at = WIDE + D + j * D
+        grad_act = grad_act + matmul_nt(grad_part, packed[:, at : at + D])
+    after = after_ref[...]
+    act_two[rows, :] = normalize(after, gains_ref[1:2, :])[0].astype(jnp.bfloat16)
+    grad_after = grad_final + gain_back(1, grad_act, after)
+    branch = grad_after.astype(jnp.bfloat16)
+    branch_one[rows, :] = branch
+    loaded(1)
+    grad_attended = matmul_nt(branch, packed[:, WIDE : WIDE + D]).astype(jnp.bfloat16)
+    zero = jnp.zeros((), jnp.bfloat16)
+    mine = lane_is((L, 128), 0, HD)
+    for s in range(tile_seqs):
+        part = slice(s * L, (s + 1) * L)
+        here = pl.ds(pl.multiple_of(base + s * L, L), L)
+        keep = jnp.where(weight[part] > 0, 0.0, -1000000000.0)
+        for pair in range(HEADS // 2):
+            at = pair * 128
+            query = mixed_ref[part, at : at + 128]
+            key = mixed_ref[part, D + at : D + at + 128]
+            value = mixed_ref[part, 2 * D + at : 2 * D + at + 128]
+            grad_out = grad_attended[part, at : at + 128]
+            keys = jnp.concatenate([jnp.where(mine, key, zero), jnp.where(mine, zero, key)], 0)
+            values = jnp.concatenate([jnp.where(mine, value, zero), jnp.where(mine, zero, value)], 0)
+            scores = (matmul_nt(keys, query) * SCALE).reshape(2, L, L)
+            scores = scores + bias_ref[2 * pair : 2 * pair + 2] + keep[None]
+            prob = jnp.exp(scores - total_ref[s, 2 * pair : 2 * pair + 2, :][:, None, :])
+            grad_prob = matmul_nt(values, grad_out).reshape(2, L, L)
+            mean = jnp.sum(prob * grad_prob, 1, keepdims=True)
+            grad_scores = (prob * (grad_prob - mean)).astype(jnp.bfloat16)
+            grad_bias_ref[2 * pair : 2 * pair + 2] += grad_scores.astype(jnp.float32)
+            prob_low = prob.astype(jnp.bfloat16)
+            flipped = jnp.transpose(key)
+            grad_query = jnp.concatenate(
+                [matmul(flipped[:HD], grad_scores[0]), matmul(flipped[HD:], grad_scores[1])], 0
+            )
+            grad_mixed[here, at : at + 128] = (jnp.transpose(grad_query) * SCALE).astype(jnp.bfloat16)
+            grad_keys = matmul(grad_scores.reshape(2 * L, L), query)
+            grad_key = jnp.where(mine, grad_keys[:L], grad_keys[L:]) * SCALE
+            grad_mixed[here, D + at : D + at + 128] = grad_key.astype(jnp.bfloat16)
+            grad_values = matmul(prob_low.reshape(2 * L, L), grad_out)
+            grad_value = jnp.where(mine, grad_values[:L], grad_values[L:])
+            grad_mixed[here, 2 * D + at : 2 * D + at + 128] = grad_value.astype(jnp.bfloat16)
+    loaded(0)
+    x0 = x0_ref[...]
+    act_one[rows, :] = normalize(x0, gains_ref[0:1, :])[0].astype(jnp.bfloat16)
+    grad_act = matmul_nt(grad_mixed[rows, :], packed[:, :WIDE])
+    rows_ref[...] = (grad_after + gain_back(0, grad_act, x0)).astype(jnp.bfloat16)
+
+    @pl.when(step == pl.num_programs(0) - 1)
+    def _():
+        jobs = []
+        for j in range(4):
+            part = slice(j * D, (j + 1) * D)
+            jobs.append((hidden, part, branch_two, slice(0, D), grad_down_hbm.at[pl.ds(j * D, D), :]))
+        for j in range(4):
+            part = slice(j * D, (j + 1) * D)
+            jobs.append((act_two, slice(0, D), grad_pre, part, grad_packed_hbm.at[:, pl.ds(WIDE + D + j * D, D)]))
+        jobs.append((attended, slice(0, D), branch_one, slice(0, D), grad_packed_hbm.at[:, pl.ds(WIDE, D)]))
+        for j in range(3):
+            part = slice(j * D, (j + 1) * D)
+            jobs.append((act_one, slice(0, D), grad_mixed, part, grad_packed_hbm.at[:, pl.ds(j * D, D)]))
+        copies = []
+        for number, (left, left_part, right, right_part, to) in enumerate(jobs):
+            slot = number % 2
+            if number >= 2:
+                copies[number - 2].wait()
+            stage[slot] = matmul_tn(left[:, left_part], right[:, right_part]).astype(jnp.bfloat16)
+            copies.append(pltpu.make_async_copy(stage.at[slot], to, store_sem.at[slot]))
+            copies[-1].start()
+        copies[-2].wait()
+        stage[0] = matmul_tn(pooled_ref[...].astype(jnp.bfloat16), grad_proj_ref[...]).astype(jnp.bfloat16)
+        last = pltpu.make_async_copy(stage.at[0], grad_packed_hbm.at[:, pl.ds(PACKED - D, D)], store_sem.at[0])
+        last.start()
+        copies[-1].wait()
+        last.wait()
+
+
+def run_backward(
+    x0, mask_col, mixed, attended, totals, after, pre, final, gains, bias_full, pooled, grad_proj, packed, down
+):
+    tokens = x0.shape[0]
+    seqs = tokens // L
+    tile = BACK_SEQS * L
+    steps = tokens // tile
+
+    def rows(width, **mode):
+        return pl.BlockSpec((tile, width), lambda i: (i, 0), **mode)
+
+    def whole(*shape):
+        return pl.BlockSpec(shape, lambda i: (0,) * len(shape), pipeline_mode=pl.Buffered(1))
+
+    def low(*shape):
+        return pltpu.VMEM(shape, jnp.bfloat16)
+
+    anywhere = pl.BlockSpec(memory_space=pl.ANY)
+    return pl.pallas_call(
+        backward_kernel,
+        grid=(steps,),
+        out_shape=[
+            jax.ShapeDtypeStruct((tokens, D), jnp.bfloat16),
+            jax.ShapeDtypeStruct((3, D), jnp.float32),
+            jax.ShapeDtypeStruct((HEADS, L, L), jnp.float32),
+            jax.ShapeDtypeStruct(packed.shape, jnp.bfloat16),
+            jax.ShapeDtypeStruct(down.shape, jnp.bfloat16),
+        ],
+        in_specs=[
+            rows(D),
+            rows(1),
+            rows(WIDE),
+            whole(tokens, D),
+            pl.BlockSpec((BACK_SEQS, HEADS, L), lambda i: (i, 0, 0)),
+            rows(D),
+            anywhere,
+            rows(D),
+            whole(3, D),
+            whole(HEADS, L, L),
+            whole(seqs, D),
+            whole(seqs, D),
+            anywhere,
+            anywhere,
+        ],
+        out_specs=[rows(D), whole(3, D), whole(HEADS, L, L), anywhere, anywhere],
+        scratch_shapes=[
+            low(D, PACKED - D),
+            low(4 * D, D),
+            low(tokens, 4 * D),
+            low(tokens, 4 * D),
+            low(tokens, D),
+            low(tokens, D),
+            low(tokens, D),
+            low(tokens, D),
+            low(tokens, WIDE),
+            pltpu.VMEM((seqs, D), jnp.float32),
+            low(2, D, D),
+            pltpu.VMEM((2, tile, D), jnp.float32),
+            pltpu.SemaphoreType.DMA((5,)),
+            pltpu.SemaphoreType.DMA((2,)),
+            pltpu.SemaphoreType.DMA((2,)),
+        ],
+        compiler_params=pltpu.CompilerParams(vmem_limit_bytes=62 * 1024 * 1024),
+    )(x0, mask_col, mixed, attended, totals, after, pre, final, gains, bias_full, pooled, grad_proj, packed, down)
+
+
+def loss_kernel(
+    grid, pairs_here, projected_ref, target_ref, scale_ref, grad_ref, loss_ref, mine, others, grads, send_sem, recv_sem
+):
+    me = lax.axis_index("dp") * grid.fs + lax.axis_index("fsdp")
+    each = 2 * pairs_here
+    half = D // 2
+
+    @pl.loop(1, grid.total)
+    def _(step):
+        greet(grid.peer(lax.rem(me + step, grid.total)))
+
+    projected = projected_ref[...]
+    factor = lax.rsqrt(jnp.sum(projected * projected, -1, keepdims=True) + EPS)
+    unit = projected * factor
+    mine[...] = jnp.concatenate([unit[:, :half], unit[:, half:]], 0).astype(jnp.bfloat16)
+    meet(grid.total - 1)
+
+    def copy(peer, slot):
+        return pltpu.make_async_remote_copy(
+            src_ref=mine,
+            dst_ref=others.at[slot],
+            send_sem=send_sem.at[peer],
+            recv_sem=recv_sem.at[slot],
+            device_id=grid.peer(peer),
+            device_id_type=MESH,
+        )
+
+    @pl.loop(1, grid.total)
+    def _(step):
+        copy(lax.rem(me + step, grid.total), me).start()
+
+    others[me] = mine[...]
+
+    @pl.loop(1, grid.total)
+    def _(step):
+        peer = lax.rem(me + step, grid.total)
+        copy(peer, peer).wait_recv()
+
+    count = grid.total * each
+    wide = others[...].astype(jnp.float32)
+    units = jnp.concatenate(
+        [wide[:, :each].reshape(count, half), wide[:, each:].reshape(count, half)], 1
+    ).astype(jnp.bfloat16)
+    similar = matmul_nt(units, units)
+    row = lax.broadcasted_iota(jnp.int32, (count, count), 0)
+    column = lax.broadcasted_iota(jnp.int32, (count, count), 1)
+    used = (lax.rem(row, each) < pairs_here) & (lax.rem(column, each) >= pairs_here)
+    own = used & (column == row + pairs_here)
+    negative = used & (column == target_ref[...])
+    sim_scale = jnp.exp(scale_ref[...])
+    own_mask = jnp.where(own, 1.0, 0.0)
+    negative_mask = jnp.where(negative, 1.0, 0.0)
+    logits = sim_scale * similar - MARGIN * own_mask
+    diagonal = jnp.sum(logits * own_mask, 1, keepdims=True)
+    hardest = jnp.sum(logits * negative_mask, 1, keepdims=True)
+    row_max = jnp.max(jnp.where(used, logits, -3e38), 1, keepdims=True)
+    powers = jnp.where(used, jnp.exp(jnp.minimum(logits - row_max, 0.0)), 0.0)
+    row_sum = jnp.sum(powers, 1, keepdims=True)
+    is_query = lax.rem(lax.broadcasted_iota(jnp.int32, (count, 1), 0), each) < pairs_here
+    gap = hardest - diagonal
+    softplus = jnp.maximum(gap, 0.0) + jnp.log(1.0 + jnp.exp(-jnp.abs(gap)))
+    row_sum = jnp.where(is_query, row_sum, 1.0)
+    losses = jnp.where(is_query, row_max + jnp.log(row_sum) - diagonal + softplus, 0.0)
+    gate = 1.0 / (1.0 + jnp.exp(-gap))
+    grad_logits = jnp.where(
+        used, powers / row_sum - own_mask + gate * (negative_mask - own_mask), 0.0
+    )
+    loss_ref[0:1, :] = jnp.broadcast_to(jnp.sum(losses, 0, keepdims=True), (1, 128))
+    grad_scale = sim_scale * jnp.sum(
+        jnp.sum(grad_logits * similar, 1, keepdims=True), 0, keepdims=True
+    )
+    loss_ref[1:2, :] = jnp.broadcast_to(grad_scale, (1, 128))
+    loss_ref[2:8, :] = jnp.zeros((6, 128), jnp.float32)
+    grad_similar = sim_scale * grad_logits
+    grads[...] = grad_similar + jnp.transpose(grad_similar)
+    first = pl.multiple_of(me * each, each)
+    grad_units = matmul(grads[pl.ds(first, each), :].astype(jnp.bfloat16), units)
+    grad_units = grad_units.astype(jnp.bfloat16).astype(jnp.float32)
+    grad_ref[...] = (
+        factor * (grad_units - unit * jnp.sum(grad_units * unit, -1, keepdims=True))
+    ).astype(jnp.bfloat16)
+
+    @pl.loop(1, grid.total)
+    def _(step):
+        peer = lax.rem(me + step, grid.total)
+        copy(peer, peer).wait_send()
+
+
+def run_loss(projected, target, log_scale, number):
+    grid = Grid()
+    each = projected.shape[0]
+    count = grid.total * each
+    inside = pl.BlockSpec(memory_space=pltpu.VMEM)
+    dma = pltpu.SemaphoreType.DMA((grid.total,))
+    return pl.pallas_call(
+        functools.partial(loss_kernel, grid, each // 2),
+        out_shape=[
+            jax.ShapeDtypeStruct((each, D), jnp.bfloat16),
+            jax.ShapeDtypeStruct((8, 128), jnp.float32),
+        ],
+        in_specs=[inside] * 3,
+        out_specs=[inside] * 2,
+        scratch_shapes=[
+            pltpu.VMEM((2 * each, D // 2), jnp.bfloat16),
+            pltpu.VMEM((grid.total, 2 * each, D // 2), jnp.bfloat16),
+            pltpu.VMEM((count, count), jnp.float32),
+            dma,
+            dma,
+        ],
+        compiler_params=pltpu.CompilerParams(collective_id=number, has_side_effects=True),
+    )(projected, target, log_scale)
 
 
 def plain_body(
@@ -1149,7 +1673,7 @@
     gain_rows = small_params[: 3 * D].reshape(3, D)
     bias_table = small_params[3 * D : 3 * D + NB * HEADS].reshape(NB, HEADS)
     log_scale = small_params[3 * D + NB * HEADS]
-    buckets = jnp.asarray(bucket_table(L, NB).reshape(-1), jnp.int32)
+    buckets = jnp.asarray(bucket_table(L, NB).T.reshape(-1), jnp.int32)
     bucket_hot = (buckets[:, None] == jnp.arange(NB, dtype=jnp.int32)[None, :]).astype(jnp.float32)
     bias_full = (
         jnp.dot(bucket_hot, bias_table, precision=HIGH).reshape(L, L, HEADS).transpose(2, 0, 1)
@@ -1184,74 +1708,31 @@
     )
     answers = jnp.take(table, jnp.maximum(mine_asked.reshape(-1), 0), axis=0).astype(jnp.bfloat16)
     shards = (
-        attn_in.astype(jnp.bfloat16),
-        attn_out.astype(jnp.bfloat16),
-        ffn_in.astype(jnp.bfloat16),
+        jnp.concatenate([attn_in, attn_out, ffn_in, proj_head], 1).astype(jnp.bfloat16),
         ffn_out.astype(jnp.bfloat16),
-        proj_head.astype(jnp.bfloat16),
     )
     gathered, found = gather(shards, answers.reshape(dp_count, CAP, D), 2)
-    gathered = [matrix.reshape(-1, matrix.shape[-1]) for matrix in gathered]
+    packed, down = [matrix.reshape(-1, matrix.shape[-1]) for matrix in gathered]
     slot_hot = (slot[:, None] == slots[None, :]).astype(jnp.bfloat16)
     embedded = matmul(slot_hot, found.reshape(dp_count * CAP, D))
     embedded = once(any_spilled, lambda _: dense_rows(ids_flat, table, row_base), embedded)
 
-    final_rows, kept = layer_forward(embedded, mask_rows, gathered[:4], gain_rows, bias_full)
-    normed_three, factor_three = normalize(final_rows, gain_rows[2])
-    mask_weight = mask_rows.astype(jnp.float32)[:, :, None]
-    counts = jnp.sum(mask_weight, 1)
-    pooled = jnp.sum(normed_three.reshape(seq_count, L, D) * mask_weight, 1) / counts
-    pooled_low = pooled.astype(jnp.bfloat16)
-    projected = matmul(pooled_low, gathered[4])
-    proj_factor = lax.rsqrt(jnp.sum(projected * projected, -1, keepdims=True) + EPS)
-    unit_rows = projected * proj_factor
-    unit_low = unit_rows.astype(jnp.bfloat16)
-    all_units = exchange(unit_low.reshape(2 * seq_count, D // 2), False, 3)
-    all_units = all_units.reshape(total, 2, pairs_here, D)
-    all_query = all_units[:, 0].reshape(pairs_total, D)
-    all_pass = all_units[:, 1].reshape(pairs_total, D)
-    similar = matmul_nt(all_query, all_pass)
-    sim_scale = jnp.exp(log_scale)
-    columns = jnp.arange(pairs_total, dtype=jnp.int32)
-    own_mask = (columns[None, :] == columns[:, None]).astype(jnp.float32)
-    negative = (columns[None, :] == negatives[:, None]).astype(jnp.float32)
-    logits = sim_scale * similar - MARGIN * own_mask
-    diagonal = jnp.sum(logits * own_mask, 1)
-    hardest = jnp.sum(logits * negative, 1)
-    row_max = jnp.max(logits, 1, keepdims=True)
-    log_total = row_max + jnp.log(jnp.sum(jnp.exp(logits - row_max), 1, keepdims=True))
-    loss_sum = jnp.sum(log_total[:, 0] - diagonal + jax.nn.softplus(hardest - diagonal))
-    hinge_gate = jax.nn.sigmoid(hardest - diagonal)
-    grad_logits = (
-        jnp.exp(logits - log_total) - own_mask + hinge_gate[:, None] * (negative - own_mask)
-    )
-    grad_log_scale = sim_scale * jnp.sum(grad_logits * similar)
-    grad_similar = (sim_scale * grad_logits).astype(jnp.bfloat16)
-    own_first = device_flat * pairs_here
-    mine_rows = lax.dynamic_slice_in_dim(grad_similar, own_first, pairs_here, 0)
-    mine_columns = lax.dynamic_slice_in_dim(grad_similar, own_first, pairs_here, 1)
-    grad_query = matmul(mine_rows, all_pass).astype(jnp.bfloat16)
-    grad_pass = matmul_tn(mine_columns, all_query).astype(jnp.bfloat16)
-    grad_units = jnp.concatenate([grad_query, grad_pass], 0).astype(jnp.float32)
-    grad_proj = (
-        proj_factor * (grad_units - unit_rows * jnp.sum(grad_units * unit_rows, -1, keepdims=True))
-    ).astype(jnp.bfloat16)
-    grad_proj_head = matmul_tn(pooled_low, grad_proj)
-    grad_pooled = matmul_nt(grad_proj, gathered[4])
-    grad_normed = ((grad_pooled / counts)[:, None, :] * mask_weight).reshape(-1, D)
-    grad_final, gain_three = normalize_back(grad_normed, final_rows, factor_three, gain_rows[2])
-    grad_rows, matrix_grads, gain_one, gain_two, grad_bias = layer_backward(
-        grad_final, kept, mask_rows, gathered[:4], gain_rows, bias_full
+    mask_col = mask_rows.astype(jnp.float32).reshape(tokens, 1)
+    *kept, pooled, projected = run_forward(embedded, mask_col, gain_rows, bias_full, packed, down)
+    target = negatives // pairs_here * seq_count + pairs_here + negatives % pairs_here
+    target = jnp.concatenate(
+        [target.reshape(total, pairs_here), jnp.full((total, pairs_here), -1, jnp.int32)], 1
+    ).reshape(-1, 1)
+    grad_proj, loss_parts = run_loss(projected, target, log_scale.reshape(1, 1), 3)
+    loss_sum, grad_log_scale = loss_parts[0, 0], loss_parts[1, 0]
+    grad_low, grad_gains, grad_bias, grad_packed, grad_down = run_backward(
+        embedded, mask_col, *kept, gain_rows, bias_full, pooled, grad_proj, packed, down
     )
     grad_bias_table = jnp.dot(grad_bias.reshape(HEADS, L * L), bucket_hot, precision=HIGH).T
-    partials = [
-        grad.astype(jnp.bfloat16).reshape(total, -1, grad.shape[1])
-        for grad in (*matrix_grads, grad_proj_head)
-    ]
-    small_local = jnp.concatenate([gain_one, gain_two, gain_three, grad_bias_table.reshape(-1)])
+    partials = [grad.reshape(total, -1, grad.shape[1]) for grad in (grad_packed, grad_down)]
+    small_local = jnp.concatenate([grad_gains.reshape(-1), grad_bias_table.reshape(-1)])
     width = -(-small_local.shape[0] // 1024) * 8
     small_local = jnp.pad(small_local, (0, width * 128 - small_local.shape[0]))
-    grad_low = grad_rows.astype(jnp.bfloat16)
     slot_sums = matmul_tn(slot_hot, grad_low).astype(jnp.bfloat16).reshape(dp_count, CAP, D)
     weight_grads, table_grad, summed, squares = finish(
         partials, slot_sums, asked.reshape(-1), small_local.reshape(width, 128), vocab_rows, 4
@@ -1267,13 +1748,16 @@
     small_grad = jnp.concatenate([summed.reshape(-1)[: small_size - 1], grad_log_scale[None]])
     norm_value = jnp.sqrt(total_squares + jnp.sum(small_grad * small_grad))
     factor = jnp.minimum(1.0, CLIP / (norm_value + 1e-06))
+    grad_in, grad_out, grad_up, grad_head = jnp.split(
+        weight_grads[0], (WIDE, WIDE + D, WIDE + 5 * D), 1
+    )
     updates = (
         (table, table_first, table_second, table_grad.astype(jnp.float32)),
-        (attn_in, attn_in_first, attn_in_second, weight_grads[0]),
-        (attn_out, attn_out_first, attn_out_second, weight_grads[1]),
-        (ffn_in, ffn_in_first, ffn_in_second, weight_grads[2]),
-        (ffn_out, ffn_out_first, ffn_out_second, weight_grads[3]),
-        (proj_head, proj_head_first, proj_head_second, weight_grads[4]),
+        (attn_in, attn_in_first, attn_in_second, grad_in),
+        (attn_out, attn_out_first, attn_out_second, grad_out),
+        (ffn_in, ffn_in_first, ffn_in_second, grad_up),
+        (ffn_out, ffn_out_first, ffn_out_second, weight_grads[1]),
+        (proj_head, proj_head_first, proj_head_second, grad_head),
         (small_params, small_first, small_second, small_grad),
     )
     results = [loss_sum, norm_value]

time: 576 us -> 527 us (0.915)
  Pallas kernels: 285 us -> 405 us
  matrix products: 122 us -> 10.5 us
  local copies, waits for them, and re-layouts: 56.5 us -> 19.2 us
  other arithmetic: 80.2 us -> 63.5 us
    pallas_call x0 -> x3, Pallas kernels: none -> 139 us  [the longest x1 94.6 us: run_backward(): pl.pallas_call(backward_kernel, grid=(steps,), out_shape=[jax.ShapeDtypeS...]
    dot_general x12 -> x0, matrix products: 47.1 us -> none  [the longest x6 29.8 us: matmul_nt(): lax.dot_general(left_side, right_side, (((1,), (1,)), ((), ())), preferre...]
    dot_general x7 -> x1, matrix products: 38.4 us -> 5.07 us  [matmul(): return jnp.dot(left_side, right_side, preferred_element_type=jnp.float32)]
    dot_general x7 -> x1, matrix products: 33.7 us -> 3.5 us  [matmul_tn(): lax.dot_general(left_side, right_side, (((0,), (0,)), ((), ())), preferre...]
    convert_element_type x4 -> x1, local copies, waits for them, and re-layouts: 19.3 us -> 1.03 us  [fast_body(): mask_col = mask_rows.astype(jnp.float32).reshape(tokens, 1)]
    pallas_call x2 -> x1, Pallas kernels: 25.1 us -> 12.3 us  [exchange(): pl.pallas_call(functools.partial(exchange_kernel, grid, spread), out_shap...]
    reduce_sum x10 -> x0, other arithmetic: 12.8 us -> none  [the longest x1 2.92 us: layer_backward(): grad_bias = jnp.sum(grad_scores, 0, dtype=jnp.float32)]
    unnamed x180 -> x49, local copies, waits for them, and re-layouts: 11.7 us -> 1.38 us
where the time goes in v3:
time: 527 us; the launch traced here: 518 us
  Pallas kernels  405 us (77%)
  other arithmetic  63.5 us (12%)
  local copies, waits for them, and re-layouts  19.2 us (4%)
  between operations  19.2 us (4%)
  matrix products  10.5 us (2%)
    pallas_call x1, Pallas kernels, finish(): pl.pallas_call(functools.partial(finish_kernel, grid, count), out_shape=[...  157 us
    pallas_call x1, Pallas kernels, gather(): pl.pallas_call(functools.partial(gather_kernel, grid, count), out_shape=[...  97.2 us
    pallas_call x1, Pallas kernels, run_backward(): pl.pallas_call(backward_kernel, grid=(steps,), out_shape=[jax.ShapeDtypeS...  94.6 us
    sub x6, other arithmetic, adam_update(): return (first_new, second_new, param - rate * (direction + decay * param))  36.5 us
    pallas_call x1, Pallas kernels, run_forward(): pl.pallas_call(forward_kernel, grid=(steps,), out_shape=[kept(WIDE, jnp.b...  30.8 us
    pallas_call x1, Pallas kernels, run_loss(): pl.pallas_call(functools.partial(loss_kernel, grid, each // 2), out_shape...  13.8 us
    pallas_call x1, Pallas kernels, exchange(): pl.pallas_call(functools.partial(exchange_kernel, grid, spread), out_shap...  12.3 us

profile of v3, /device:TPU:0, one launch (start us, length us, event | category | flops | bytes accessed | tf_op | source)
XLA Modules:
  0.0 518.1 jit_solution(7387885380581525694)
XLA Ops:
  8.6 1.3 fusion.10
  9.8 2.2 convert_reduce_fusion
  15.5 12.3 %shard_map.416 = s32[32,8,128]{2,1,0:T(8,128)} custom-call(s32[32,8,128]{2,1,0:T(8,128)} %pad_add_fusion.src), custom_call_target="tpu_custom_call" | custom-call | tf_op jit(solution)/shard_map/pallas_call | solution.py:284
  27.9 1.6 slice_reduce_fusion
  34.6 1.6 convert_element_type.60.refs_1_
  36.2 1.5 slice_bitcast_fusion.1
  37.8 9.0 %gather_fusion.1 = bf16[1024,768]{1,0:T(8,128)(2,1)S(1)} fusion(f32[4016,768]{1,0:T(8,128)} %param.38, s32[1024]{0:T(1024)S(1)} %bitcast_clamp_fusion), kind=kCustom, calls=%fused_computation.1 | custom fusion | bytes 3149824 | tf_op jit(solution)/shard_map/jit(_take)/gather | solution.py:1709
  46.8 1.5 select_convert_fusion.1.refs_2_
  48.2 97.2 %shard_map.417 = (bf16[32,24,6912]{2,1,0:T(8,128)(2,1)}, bf16[32,96,768]{2,1,0:T(8,128)(2,1)}, bf16[8,128,768]{2,1,0:T(8,128)(2,1)}) custom-call(bf16[24,6912]{1,0:T(8,128)(2,1)} %pad_maximum_fusion.refs_0_, bf16[96,768]{1,0:T(8,128)(2,1)} %convert_element_type.60.refs_1_, bf16[8,128,768]{2,1,0:T(8,128)(2,1)} %select_convert_fusion.1.refs_2_), custom_call_target="tpu_custom_call" | custom-call | tf_op jit(solution)/shard_map/pallas_call | solution.py:466
  145.5 5.1 fusion.8
  150.6 7.8 %convert.25 = bf16[4016,768]{1,0:T(8,128)(2,1)} convert(f32[4016,768]{1,0:T(8,128)} %param.38) | non-fusion elementwise | flops 3084288 | bytes 18505728
  161.6 1.1 copy.86
  162.7 30.8 %shard_map.418 = (bf16[1024,2304]{1,0:T(8,128)(2,1)}, bf16[1024,768]{1,0:T(8,128)(2,1)}, f32[8,12,128]{2,1,0:T(8,128)}, f32[1024,768]{1,0:T(8,128)}, f32[1024,30...) custom-call(f32[1024,768]{1,0:T(8,128)} %get-tuple-element.153.x0_ref, ...), custom_call_target="tpu_custom_call" | custom-call | tf_op jit(solution)/shard_map/pallas_call | solution.py:997
  195.8 13.8 %shard_map.419 = (bf16[8,768]{1,0:T(8,128)(2,1)}, f32[8,128]{1,0:T(8,128)}) custom-call(f32[8,768]{1,0:T(8,128)} %get-tuple-element.156.projected_ref, s32[256,1]{1,0:T(8,128)} %reshape.392.target_ref, f32[1,1]{1,0:T(1,128)} %bitcast.18.scale_ref), custom_call_target="tpu_custom_call" | custom-call | tf_op jit(solution)/shard_map/pallas_call | solution.py:1374
  209.6 1.3 fusion.42
  211.0 94.6 %shard_map.420 = (bf16[1024,768]{1,0:T(8,128)(2,1)S(1)}, f32[3,768]{1,0:T(4,128)}, f32[12,128,128]{2,1,0:T(8,128)}, bf16[768,6912]{1,0:T(8,128)(2,1)}, bf16[3072,768]{1,0:T(8,128)(2,1)}) custom-call(f32[1024,768]{1,0:T(8,128)} %get-tuple-element.153.x0_ref, f32[1024,1]{1,0:T(8,128)} %copy.73.mask_col_ref, bf16[1024,2304]{1,0:T(8,128)(2,1)} %get-tuple-element.158.mixed_ref, ...), custom_call_target="tpu_custom_call" | custom-call | tf_op jit(solution)/shard_map/pallas_call | solution.py:1232
  305.7 3.5 fusion.17
  309.9 1.2 fusion.16
  311.8 156.5 %shard_map.421 = (f32[24,6912]{1,0:T(8,128)}, f32[96,768]{1,0:T(8,128)}, bf16[4016,768]{1,0:T(8,128)(2,1)}, f32[24,128]{1,0:T(8,128)}, f32[16,128]{1,0:T(8,128)}) custom-call(bf16[4,2,2,2,24,6912]{5,4,3,2,1,0:T(8,128)(2,1)} %bitcast.81, bf16[4,2,2,2,96,768]{5,4,3,2,1,0:T(8,128)(2,1)} %bitcast.86, bf16[8,128,768]{2,1,0:T(8,128)(2,1)} %bitcast.89, ...), custom_call_target="tpu_custom_call" | custom-call | tf_op jit(solution)/shard_map/pallas_call | solution.py:851
  468.4 1.3 slice_reduce_fusion.1
  471.2 1.3 multiply_reduce_fusion.1
  473.4 29.6 %multiply_subtract_fusion = (f32[4016,768]{1,0:T(8,128)}, f32[4016,768]{1,0:T(8,128)}, f32[4016,768]{1,0:T(8,128)}) fusion(f32[4016,768]{1,0:T(8,128)} %param.38, f32[]{:T(128)S(6)} %min.11, bf16[4016,768]{1,0:T(8,128)(2,1)} %get-tuple-element.175, f32[4016,768]{1,0:T(8,128)} %param.40, f32[4016,768]{1,0:T(8,128)} %param.39), kind=kLoop, calls=%fused_computation.18 | loop fusion | flops 52432896 | bytes 80191488 | tf_op jit(solution)/shard_map/sub | solution.py:207
  503.9 1.8 multiply_subtract_fusion.4
  507.9 2.1 add_subtract_fusion
  (88 shorter events, 18.9 us)
Async XLA Ops:
  14.2 136.4 %copy-start.20 = (s32[1024]{0:T(1024)}, s32[1024]{0:T(1024)S(1)}, u32[]{:S(2)}) copy-start(s32[1024]{0:T(1024)S(1)} %get-tuple-element.260) | copy-start | bytes 12292
  150.6 7.8 %copy-start.7 = (s32[2,4,128]{2,1,0:T(4,128)S(1)}, s32[2,4,128]{2,1,0:T(4,128)}, u32[]{:S(2)}) copy-start(s32[2,4,128]{2,1,0:T(4,128)} %param.35) | copy-start | bytes 12292
  158.4 0.7 copy-start.24
  158.4 1.7 copy-start.19
  158.4 2.4 copy-start.18
  211.0 94.7 %copy-start.21 = (s32[1024]{0:T(1024)S(1)}, s32[1024]{0:T(1024)}, u32[]{:S(2)}) copy-start(s32[1024]{0:T(1024)} %copy-done.20) | copy-start | bytes 12292
  305.6 3.5 copy-start.5
  305.6 4.3 copy-start.17
  305.7 5.6 %copy-start.23 = (f32[3,768]{1,0:T(4,128)S(1)}, f32[3,768]{1,0:T(4,128)}, u32[]{:S(2)}) copy-start(f32[3,768]{1,0:T(4,128)} %get-tuple-element.169) | copy-start | bytes 27652
  469.7 1.5 copy-start.22
  473.2 29.7 %copy-start.4 = (f32[24,2304]{1,0:T(8,128)S(1)}, f32[24,2304]{1,0:T(8,128)}, u32[]{:S(2)}) copy-start(f32[24,2304]{1,0:T(8,128)} %param.41) | copy-start | bytes 663556
  473.2 29.7 %copy-start.6 = (f32[24,6912]{1,0:T(8,128)S(1)}, f32[24,6912]{1,0:T(8,128)}, u32[]{:S(2)}) copy-start(f32[24,6912]{1,0:T(8,128)} %get-tuple-element.176) | copy-start | bytes 1990660
  473.2 29.7 %copy-start.15 = (f32[24,2304]{1,0:T(8,128)S(1)}, f32[24,2304]{1,0:T(8,128)}, u32[]{:S(2)}) copy-start(f32[24,2304]{1,0:T(8,128)} %param.43) | copy-start | bytes 663556
  473.2 29.7 %copy-start.16 = (f32[24,2304]{1,0:T(8,128)S(1)}, f32[24,2304]{1,0:T(8,128)}, u32[]{:S(2)}) copy-start(f32[24,2304]{1,0:T(8,128)} %param.42) | copy-start | bytes 663556
  473.2 30.6 %copy-start.13 = (f32[24,768]{1,0:T(8,128)S(1)}, f32[24,768]{1,0:T(8,128)}, u32[]{:S(2)}) copy-start(f32[24,768]{1,0:T(8,128)} %param.53) | copy-start | bytes 221188
  473.3 30.6 %copy-start.14 = (f32[24,768]{1,0:T(8,128)S(1)}, f32[24,768]{1,0:T(8,128)}, u32[]{:S(2)}) copy-start(f32[24,768]{1,0:T(8,128)} %param.44) | copy-start | bytes 221188
  473.3 32.4 %copy-start.2 = (f32[24,3072]{1,0:T(8,128)S(1)}, f32[24,3072]{1,0:T(8,128)}, u32[]{:S(2)}) copy-start(f32[24,3072]{1,0:T(8,128)} %param.47) | copy-start | bytes 884740
  473.3 32.4 %copy-start.8 = (f32[24,3072]{1,0:T(8,128)S(1)}, f32[24,3072]{1,0:T(8,128)}, u32[]{:S(2)}) copy-start(f32[24,3072]{1,0:T(8,128)} %param.49) | copy-start | bytes 884740
  473.3 32.4 %copy-start.9 = (f32[24,3072]{1,0:T(8,128)S(1)}, f32[24,3072]{1,0:T(8,128)}, u32[]{:S(2)}) copy-start(f32[24,3072]{1,0:T(8,128)} %param.48) | copy-start | bytes 884740
  473.3 33.5 %copy-start.3 = (f32[96,768]{1,0:T(8,128)S(1)}, f32[96,768]{1,0:T(8,128)}, u32[]{:S(2)}) copy-start(f32[96,768]{1,0:T(8,128)} %param.50) | copy-start | bytes 884740
  473.3 33.5 %copy-start.10 = (f32[96,768]{1,0:T(8,128)S(1)}, f32[96,768]{1,0:T(8,128)}, u32[]{:S(2)}) copy-start(f32[96,768]{1,0:T(8,128)} %param.52) | copy-start | bytes 884740
  473.3 33.5 %copy-start.11 = (f32[96,768]{1,0:T(8,128)S(1)}, f32[96,768]{1,0:T(8,128)}, u32[]{:S(2)}) copy-start(f32[96,768]{1,0:T(8,128)} %param.51) | copy-start | bytes 884740
  473.3 33.5 %copy-start.12 = (f32[96,768]{1,0:T(8,128)S(1)}, f32[96,768]{1,0:T(8,128)}, u32[]{:S(2)}) copy-start(f32[96,768]{1,0:T(8,128)} %get-tuple-element.177) | copy-start | bytes 884740

commit v4 on v2

--- a/solution.py
+++ b/solution.py
@@ -27,7 +27,7 @@
 DECAYS = (0.001, 0.001, 0.001, 0.001, 0.001, 0.001, 0.0)
 HIGH = lax.Precision.HIGHEST
 MESH = pl.DeviceIdType.MESH
-CAP = 128
+CAP = 112
 
 
 def bucket_table(length, count):
@@ -244,60 +244,47 @@
     pl.semaphore_wait(pltpu.get_barrier_semaphore(), count)
 
 
-def exchange_kernel(grid, spread, src, out, send_sem, recv_sem, own_sem):
-    me = lax.axis_index("dp") * grid.fs + lax.axis_index("fsdp")
-    own = pltpu.make_async_copy(src.at[me] if spread else src, out.at[me], own_sem)
-    own.start()
-
-    @pl.loop(1, grid.total)
-    def _(step):
-        greet(grid.peer(lax.rem(me + step, grid.total)))
-
-    meet(count=grid.total - 1)
-
-    def copy(peer, slot):
-        return pltpu.make_async_remote_copy(
-            src_ref=src.at[peer] if spread else src,
-            dst_ref=out.at[slot],
-            send_sem=send_sem.at[peer],
-            recv_sem=recv_sem.at[slot],
-            device_id=grid.peer(peer),
-            device_id_type=MESH,
-        )
-
-    @pl.loop(1, grid.total)
-    def _(step):
-        copy(lax.rem(me + step, grid.total), me).start()
-
-    own.wait()
-
-    @pl.loop(1, grid.total)
-    def _(step):
-        peer = lax.rem(me + step, grid.total)
-        copy(peer, peer).wait_recv()
-        copy(peer, peer).wait_send()
-
-
-def exchange(src, spread, number):
-    grid = Grid()
-    block = src.shape[1:] if spread else src.shape
-    return pl.pallas_call(
-        functools.partial(exchange_kernel, grid, spread),
-        out_shape=jax.ShapeDtypeStruct((grid.total,) + block, src.dtype),
-        in_specs=[pl.BlockSpec(memory_space=pltpu.VMEM)],
-        out_specs=pl.BlockSpec(memory_space=pltpu.VMEM),
-        scratch_shapes=[
-            pltpu.SemaphoreType.DMA((grid.total,)),
-            pltpu.SemaphoreType.DMA((grid.total,)),
-            pltpu.SemaphoreType.DMA,
-        ],
-        compiler_params=pltpu.CompilerParams(collective_id=number, has_side_effects=True),
-    )(src)
-
-
-def gather_kernel(grid, count, *refs):
-    srcs, rows, outs, got_rows = refs[:count], refs[count], refs[count + 1 : 2 * count + 1], refs[2 * count + 1]
-    send_sem, recv_sem, own_sem, row_send, row_recv, row_own = refs[2 * count + 2 :]
+ROW_BLOCK = 512
+WIDE = 3 * D
+PACKED = WIDE + D + 4 * D + D
+TILE_SEQS = 4
+
+
+def head_kernel(
+    grid,
+    col_ref,
+    row_ref,
+    negative_ref,
+    in_ref,
+    out_ref,
+    up_ref,
+    proj_ref,
+    down_ref,
+    table_hbm,
+    packed_out,
+    down_out,
+    heard,
+    slot_ref,
+    x0_ref,
+    packed_mine,
+    down_mine,
+    table,
+    total,
+    answers,
+    found,
+    messages,
+    send_sem,
+    recv_sem,
+    own_sem,
+    row_send,
+    row_recv,
+    note_send,
+    note_recv,
+    note_on,
+    table_sem,
+):
+    srcs, outs = (packed_mine, down_mine), (packed_out, down_out)
+    count = 2
     z, x, y, core = grid.here()
     tall = grid.tall
     d, f = lax.axis_index("dp"), lax.axis_index("fsdp")
@@ -308,29 +295,26 @@
     sibling = grid.device(z, x, y, 1 - core)
     has_up, has_down = z < tall - 1, z > 0
     me = grid.flat(z, x, y, core)
-    local = [pltpu.make_async_copy(srcs[m], outs[m].at[me], own_sem.at[m]) for m in range(count)]
-    local.append(pltpu.make_async_copy(rows.at[d], got_rows.at[d], row_own))
-    for item in local:
-        item.start()
+    f_side, f_y, f_far = y * 2 + 1 - core, (1 - y) * 2 + core, (1 - y) * 2 + 1 - core
 
     @pl.loop(1, grid.dp)
     def _(step):
         greet((lax.rem(d + step, grid.dp), f))
 
-    greet(v_device)
+    greet((d, f_y))
     greet(sibling)
-    greet(u_device)
-    meet(count=grid.dp + 2)
-
-    def row_copy(peer, slot):
-        return pltpu.make_async_remote_copy(
-            src_ref=rows.at[peer],
-            dst_ref=got_rows.at[slot],
-            send_sem=row_send.at[peer],
-            recv_sem=row_recv.at[slot],
-            device_id=(peer, f),
-            device_id_type=MESH,
-        )
+    vocab_rows = table_hbm.shape[0]
+    fetch = pltpu.make_async_copy(table_hbm, table.at[pl.ds(0, vocab_rows), :], table_sem)
+    fetch.start()
+    at = 0
+    for ref in (in_ref, out_ref, up_ref, proj_ref):
+        packed_mine[:, at : at + ref.shape[1]] = ref[...].astype(jnp.bfloat16)
+        at += ref.shape[1]
+    down_mine[...] = down_ref[...].astype(jnp.bfloat16)
+    local = [pltpu.make_async_copy(srcs[m], outs[m].at[me], own_sem.at[m]) for m in range(count)]
+    for item in local:
+        item.start()
+    meet(grid.dp + 1)
 
     def copy(m, shard, device, way, own):
         return pltpu.make_async_remote_copy(
@@ -366,9 +350,84 @@
     send(me, v_device, 3, True)
     send(me, sibling, 4, True)
 
+    tokens = col_ref.shape[0]
+    chunk = 128
+    ids_row = row_ref[...]
+    place_row = lax.broadcasted_iota(jnp.int32, (chunk, tokens), 1)
+    place_col = lax.broadcasted_iota(jnp.int32, (chunk, tokens), 0)
+
+    def see(step, repeated):
+        start = pl.multiple_of(step * chunk, chunk)
+        again = (col_ref[pl.ds(start, chunk), :] == ids_row) & (place_col + start < place_row)
+        return jnp.maximum(repeated, jnp.max(jnp.where(again, 1.0, 0.0), 0, keepdims=True))
+
+    repeated = lax.fori_loop(0, tokens // chunk, see, jnp.zeros((1, tokens), jnp.float32))
+    firsts = jnp.where(repeated > 0.5, -1.0, ids_row)
+    lane = lax.broadcasted_iota(jnp.int32, (chunk, 128), 1).astype(jnp.float32)
+
+    def rank_some(step, carry):
+        listed, most = carry
+        start = pl.multiple_of(step * chunk, chunk)
+        ids = col_ref[pl.ds(start, chunk), :]
+        owner = jnp.zeros_like(ids)
+        for other in range(1, grid.dp):
+            owner = owner + jnp.where(ids >= float(other * vocab_rows), 1.0, 0.0)
+        first_id = owner * float(vocab_rows)
+        rank = jnp.sum(jnp.where((firsts >= first_id) & (firsts < ids), 1.0, 0.0), 1, keepdims=True)
+        slot = jnp.where(rank < float(CAP), owner * float(CAP) + rank, -1.0)
+        slot_ref[pl.ds(start, chunk), :] = slot
+        rows = []
+        for other in range(grid.dp):
+            hit = (slot == lane + float(other * CAP)) & (lane < float(CAP))
+            rows.append(jnp.max(jnp.where(hit, ids - first_id + 1.0, 0.0), 0, keepdims=True))
+        return (jnp.maximum(listed, jnp.concatenate(rows, 0)), jnp.maximum(most, jnp.max(rank, 0, keepdims=True)))
+
+    listed, most = lax.fori_loop(
+        0,
+        tokens // chunk,
+        rank_some,
+        (jnp.zeros((grid.dp, 128), jnp.float32), jnp.zeros((1, 1), jnp.float32)),
+    )
+    spilled = jnp.broadcast_to(jnp.where(most >= float(CAP), 1.0, 0.0), (1, 128))
+    rest = jnp.concatenate([negative_ref[...], spilled, jnp.zeros((5, 128), jnp.float32)], 0)
+    for other in range(grid.dp):
+        messages[other] = jnp.concatenate([listed[other : other + 1] - 1.0, rest], 0)
+
+    def note(peer, slot):
+        return pltpu.make_async_remote_copy(
+            src_ref=messages.at[peer],
+            dst_ref=heard.at[slot],
+            send_sem=note_send.at[peer],
+            recv_sem=note_recv.at[slot],
+            device_id=(peer, f),
+            device_id_type=MESH,
+        )
+
+    def note_onward(slot, to_side):
+        return pltpu.make_async_remote_copy(
+            src_ref=heard.at[slot],
+            dst_ref=heard.at[slot],
+            send_sem=note_on.at[1 if to_side else 0, slot],
+            recv_sem=note_recv.at[slot],
+            device_id=(d, f_side if to_side else f_y),
+            device_id_type=MESH,
+        )
+
     @pl.loop(1, grid.dp)
     def _(step):
-        row_copy(lax.rem(d + step, grid.dp), d).start()
+        note(lax.rem(d + step, grid.dp), me).start()
+
+    heard[me] = messages[d]
+
+    def row_copy(peer, slot):
+        return pltpu.make_async_remote_copy(
+            src_ref=answers.at[peer],
+            dst_ref=found.at[slot],
+            send_sem=row_send.at[peer],
+            recv_sem=row_recv.at[slot],
+            device_id=(peer, f),
+            device_id_type=MESH,
+        )
 
     def pass_z(k):
         low, high = z - k, z + k
@@ -420,20 +479,92 @@
         arrived(shard)
         send(shard, sibling, 4)
 
-    for k in range(tall + 1):
-        if 0 < k < tall:
+    both(0, pass_u)
+
+    @pl.loop(1, grid.dp)
+    def _(step):
+        note(d, lax.rem(d + step, grid.dp) * grid.fs + f).wait_recv()
+
+    @pl.loop(0, grid.dp)
+    def _(peer):
+        note_onward(peer * grid.fs + f, False).start()
+        note_onward(peer * grid.fs + f, True).start()
+
+    pass_z(1)
+    fetch.wait()
+    padding = table.shape[0] - vocab_rows
+    if padding:
+        table[vocab_rows:, :] = jnp.zeros((padding, D), jnp.float32)
+    asked = jnp.concatenate([heard[peer * grid.fs + f, 0:1, :] for peer in range(grid.dp)], 0)
+    asked = jnp.transpose(asked)
+    block = ROW_BLOCK
+    total[...] = jnp.zeros_like(total)
+    lanes = lax.broadcasted_iota(jnp.int32, (CAP, block), 1).astype(jnp.float32)
+
+    def pick(step):
+        start = pl.multiple_of(step * block, block)
+        some = table[pl.ds(start, block), :].astype(jnp.bfloat16)
+        wanted = lanes + (step * block).astype(jnp.float32)
+        hot = jnp.concatenate(
+            [
+                jnp.where(asked[:CAP, peer : peer + 1] == wanted, 1.0, 0.0)
+                for peer in range(grid.dp)
+            ],
+            0,
+        ).astype(jnp.bfloat16)
+        total[...] += matmul(hot, some)
+
+    steps = table.shape[0] // block
+    pl.loop(0, steps)(pick)
+    answers[...] = total[...].reshape(answers.shape).astype(jnp.bfloat16)
+    found[d] = answers[d]
+
+    @pl.loop(1, grid.dp)
+    def _(step):
+        row_copy(lax.rem(d + step, grid.dp), d).start()
+
+    both(0, pass_v)
+    for k in range(1, tall + 1):
+        if 1 < k < tall:
             pass_z(k)
         if k < tall:
             both(k, pass_u)
             both(k, pass_v)
-        if k:
-            both(k - 1, pass_far)
+        both(k - 1, pass_far)
+
+    @pl.loop(1, grid.dp)
+    def _(step):
+        row_copy(d, lax.rem(d + step, grid.dp)).wait_recv()
+
+    slots = grid.dp * CAP
+    some = tokens // 4
+    wide_lane = lax.broadcasted_iota(jnp.int32, (some, slots), 1).astype(jnp.float32)
+    rows = found[...].reshape(slots, D)
+
+    @pl.loop(0, 4)
+    def _(step):
+        start = pl.multiple_of(step * some, some)
+        hot = jnp.where(slot_ref[pl.ds(start, some), :] == wide_lane, 1.0, 0.0).astype(jnp.bfloat16)
+        x0_ref[pl.ds(start, some), :] = matmul(hot, rows)
+
+    @pl.loop(0, grid.dp)
+    def _(peer):
+        note(d, peer * grid.fs + f_y).wait_recv()
+        note_onward(peer * grid.fs + f_y, True).start()
+
+    @pl.loop(0, grid.dp)
+    def _(peer):
+        note(d, peer * grid.fs + f_side).wait_recv()
+        note(d, peer * grid.fs + f_far).wait_recv()
+        note_onward(peer * grid.fs + f, False).wait_send()
+        note_onward(peer * grid.fs + f, True).wait_send()
+        note_onward(peer * grid.fs + f_y, True).wait_send()
 
     @pl.loop(1, grid.dp)
     def _(step):
         peer = lax.rem(d + step, grid.dp)
-        row_copy(peer, peer).wait_recv()
-        row_copy(peer, peer).wait_send()
+        row_copy(peer, d).wait_send()
+        note(peer, me).wait_send()
 
     @pl.loop(0, tall)
     def _(level):
@@ -459,30 +590,566 @@
         item.wait()
 
 
-def gather(srcs, rows, number):
+def run_head(ids, negatives, attn_in, attn_out, ffn_in, proj_head, ffn_out, table, number):
     grid = Grid()
-    count = len(srcs)
+    tokens = ids.shape[0]
+    wide = ids.astype(jnp.float32)
+    row = jnp.zeros((1, 128), jnp.float32).at[0, : negatives.shape[0]].set(negatives.astype(jnp.float32))
+    shapes = ((attn_in.shape[0], PACKED), ffn_out.shape)
+    blocks = -(-table.shape[0] // ROW_BLOCK)
+    anywhere, inside = pl.BlockSpec(memory_space=pl.ANY), pl.BlockSpec(memory_space=pltpu.VMEM)
+    dma = pltpu.SemaphoreType.DMA
+    line, everyone = dma((grid.dp,)), dma((grid.total,))
+    return pl.pallas_call(
+        functools.partial(head_kernel, grid),
+        out_shape=[jax.ShapeDtypeStruct((grid.total,) + shape, jnp.bfloat16) for shape in shapes]
+        + [
+            jax.ShapeDtypeStruct((grid.total, 8, 128), jnp.float32),
+            jax.ShapeDtypeStruct((tokens, 1), jnp.float32),
+            jax.ShapeDtypeStruct((tokens, D), jnp.float32),
+        ],
+        in_specs=[inside] * 8 + [anywhere],
+        out_specs=[anywhere] * 2 + [inside] * 3,
+        scratch_shapes=[pltpu.VMEM(shape, jnp.bfloat16) for shape in shapes]
+        + [
+            pltpu.VMEM((blocks * ROW_BLOCK, D), jnp.float32),
+            pltpu.VMEM((grid.dp * CAP, D), jnp.float32),
+            pltpu.VMEM((grid.dp, CAP, D), jnp.bfloat16),
+            pltpu.VMEM((grid.dp, CAP, D), jnp.bfloat16),
+            pltpu.VMEM((grid.dp, 8, 128), jnp.float32),
+            dma((5, 2, grid.total)),
+            dma((2, grid.total)),
+            dma((2,)),
+            line,
+            line,
+            line,
+            everyone,
+            dma((2, grid.total)),
+            dma,
+        ],
+        compiler_params=pltpu.CompilerParams(
+            collective_id=number, has_side_effects=True, vmem_limit_bytes=48 * 1024 * 1024
+        ),
+    )(wide.reshape(tokens, 1), wide.reshape(1, tokens), row, attn_in, attn_out, ffn_in, proj_head, ffn_out, table)
+
+
+def lane_is(shape, low, high):
+    lanes = lax.broadcasted_iota(jnp.int32, shape, len(shape) - 1)
+    return (lanes >= low) & (lanes < high)
+
+
+def gelu_parts(t):
+    inner = np.float32(np.sqrt(2 / np.pi)) * (t + 0.044715 * (t * t * t))
+    tan = jnp.tanh(inner)
+    return 0.5 * (1.0 + tan), tan
+
+
+def forward_kernel(
+    x0_ref,
+    mask_col_ref,
+    gains_ref,
+    bias_ref,
+    packed_hbm,
+    down_hbm,
+    mixed_ref,
+    attended_ref,
+    total_ref,
+    after_ref,
+    pre_ref,
+    final_ref,
+    pooled_ref,
+    projected_ref,
+    packed,
+    down,
+    load_sem,
+):
+    step = pl.program_id(0)
+    tile_seqs = x0_ref.shape[0] // L
+    edges = (0, WIDE, WIDE + D, WIDE + 5 * D, PACKED)
+
+    def load(k):
+        if k == 4:
+            return pltpu.make_async_copy(down_hbm, down, load_sem.at[k])
+        part = pl.ds(edges[k], edges[k + 1] - edges[k])
+        return pltpu.make_async_copy(packed_hbm.at[:, part], packed.at[:, part], load_sem.at[k])
+
+    def loaded(k):
+        @pl.when(step == 0)
+        def _():
+            load(k).wait()
+
+    @pl.when(step == 0)
+    def _():
+        for k in (0, 1, 2, 4, 3):
+            load(k).start()
+
+    x0 = x0_ref[...]
+    act_one = normalize(x0, gains_ref[0:1, :])[0].astype(jnp.bfloat16)
+    loaded(0)
+    for at in range(0, WIDE, D):
+        mixed_ref[:, at : at + D] = matmul(act_one, packed[:, at : at + D]).astype(jnp.bfloat16)
+
+    zero = jnp.zeros((), jnp.bfloat16)
+    for s in range(tile_seqs):
+        rows = slice(s * L, (s + 1) * L)
+        keep = jnp.where(mask_col_ref[rows, :] > 0, 0.0, -1000000000.0)
+        for pair in range(HEADS // 2):
+            at = pair * 128
+            query = mixed_ref[rows, at : at + 128]
+            key = mixed_ref[rows, D + at : D + at + 128]
+            value = mixed_ref[rows, 2 * D + at : 2 * D + at + 128]
+            mine = lane_is((L, 128), 0, HD)
+            keys = jnp.concatenate([jnp.where(mine, key, zero), jnp.where(mine, zero, key)], 0)
+            scores = (matmul_nt(keys, query) * SCALE).reshape(2, L, L)
+            scores = scores + bias_ref[2 * pair : 2 * pair + 2] + keep[None]
+            row_max = jnp.max(scores, 1, keepdims=True)
+            powers = jnp.exp(scores - row_max)
+            row_sum = jnp.sum(powers, 1, keepdims=True)
+            prob = (powers * (1.0 / row_sum)).astype(jnp.bfloat16)
+            total_ref[s, 2 * pair : 2 * pair + 2, :] = (row_max + jnp.log(row_sum))[:, 0, :]
+            flipped = jnp.transpose(value)
+            both = jnp.concatenate([matmul(flipped[:HD], prob[0]), matmul(flipped[HD:], prob[1])], 0)
+            both = jnp.transpose(both)
+            attended_ref[rows, at : at + 128] = both.astype(jnp.bfloat16)
+
+    loaded(1)
+    after = x0 + matmul(attended_ref[...], packed[:, WIDE : WIDE + D])
+    after_ref[...] = after
+    act_two = normalize(after, gains_ref[1:2, :])[0].astype(jnp.bfloat16)
+    loaded(2)
+    loaded(4)
+    final = after
+    for j in range(4):
+        at = WIDE + D + j * D
+        pre = matmul(act_two, packed[:, at : at + D])
+        pre_ref[:, j * D : (j + 1) * D] = pre
+        hidden = (pre * gelu_parts(pre)[0]).astype(jnp.bfloat16)
+        final = final + matmul(hidden, down[j * D : (j + 1) * D, :])
+    final_ref[...] = final
+    normed = normalize(final, gains_ref[2:3, :])[0]
+    weight = mask_col_ref[...]
+    for s in range(tile_seqs):
+        rows = slice(s * L, (s + 1) * L)
+        count = jnp.sum(weight[rows], 0, keepdims=True)
+        row = jnp.sum(normed[rows] * weight[rows], 0, keepdims=True) / count
+        pooled_ref[pl.ds(step * tile_seqs + s, 1), :] = row
+
+    @pl.when(step == pl.num_programs(0) - 1)
+    def _():
+        load(3).wait()
+        projected_ref[...] = matmul(pooled_ref[...].astype(jnp.bfloat16), packed[:, PACKED - D :])
+
+
+def run_forward(x0, mask_col, gains, bias_full, packed, down):
+    tokens = x0.shape[0]
+    seqs = tokens // L
+    tile = TILE_SEQS * L
+    steps = tokens // tile
+
+    def rows(width):
+        return pl.BlockSpec((tile, width), lambda i: (i, 0))
+
+    def whole(*shape):
+        return pl.BlockSpec(shape, lambda i: (0,) * len(shape), pipeline_mode=pl.Buffered(1))
+
+    def kept(width, dtype):
+        return jax.ShapeDtypeStruct((tokens, width), dtype)
+
     anywhere = pl.BlockSpec(memory_space=pl.ANY)
-    results = pl.pallas_call(
-        functools.partial(gather_kernel, grid, count),
-        out_shape=[jax.ShapeDtypeStruct((grid.total,) + src.shape, src.dtype) for src in srcs]
-        + [jax.ShapeDtypeStruct(rows.shape, rows.dtype)],
-        in_specs=[anywhere] * (count + 1),
-        out_specs=[anywhere] * (count + 1),
+    return pl.pallas_call(
+        forward_kernel,
+        grid=(steps,),
+        out_shape=[
+            kept(WIDE, jnp.bfloat16),
+            kept(D, jnp.bfloat16),
+            jax.ShapeDtypeStruct((seqs, HEADS, L), jnp.float32),
+            kept(D, jnp.float32),
+            kept(4 * D, jnp.float32),
+            kept(D, jnp.float32),
+            jax.ShapeDtypeStruct((seqs, D), jnp.float32),
+            jax.ShapeDtypeStruct((seqs, D), jnp.float32),
+        ],
+        in_specs=[
+            rows(D),
+            rows(1),
+            whole(3, D),
+            whole(HEADS, L, L),
+            anywhere,
+            anywhere,
+        ],
+        out_specs=[rows(WIDE), rows(D), pl.BlockSpec((TILE_SEQS, HEADS, L), lambda i: (i, 0, 0)), rows(D), rows(4 * D), rows(D), whole(seqs, D), whole(seqs, D)],
         scratch_shapes=[
-            pltpu.SemaphoreType.DMA((5, count, grid.total)),
-            pltpu.SemaphoreType.DMA((count, grid.total)),
-            pltpu.SemaphoreType.DMA((count,)),
-            pltpu.SemaphoreType.DMA((grid.dp,)),
-            pltpu.SemaphoreType.DMA((grid.dp,)),
-            pltpu.SemaphoreType.DMA,
+            pltpu.VMEM((D, PACKED), jnp.bfloat16),
+            pltpu.VMEM((4 * D, D), jnp.bfloat16),
+            pltpu.SemaphoreType.DMA((5,)),
+        ],
+        compiler_params=pltpu.CompilerParams(vmem_limit_bytes=60 * 1024 * 1024),
+    )(x0, mask_col, gains, bias_full, packed, down)
+
+
+def loss_kernel(
+    grid, pairs_here, projected_ref, target_ref, scale_ref, grad_ref, loss_ref, mine, others, grads, send_sem, recv_sem
+):
+    me = lax.axis_index("dp") * grid.fs + lax.axis_index("fsdp")
+    each = 2 * pairs_here
+    half = D // 2
+
+    @pl.loop(1, grid.total)
+    def _(step):
+        greet(grid.peer(lax.rem(me + step, grid.total)))
+
+    projected = projected_ref[...]
+    factor = lax.rsqrt(jnp.sum(projected * projected, -1, keepdims=True) + EPS)
+    unit = projected * factor
+    mine[...] = jnp.concatenate([unit[:, :half], unit[:, half:]], 0).astype(jnp.bfloat16)
+    meet(grid.total - 1)
+
+    def copy(peer, slot):
+        return pltpu.make_async_remote_copy(
+            src_ref=mine,
+            dst_ref=others.at[slot],
+            send_sem=send_sem.at[peer],
+            recv_sem=recv_sem.at[slot],
+            device_id=grid.peer(peer),
+            device_id_type=MESH,
+        )
+
+    @pl.loop(1, grid.total)
+    def _(step):
+        copy(lax.rem(me + step, grid.total), me).start()
+
+    others[me] = mine[...]
+
+    @pl.loop(1, grid.total)
+    def _(step):
+        peer = lax.rem(me + step, grid.total)
+        copy(peer, peer).wait_recv()
+
+    count = grid.total * each
+    wide = others[...].astype(jnp.float32)
+    units = jnp.concatenate(
+        [wide[:, :each].reshape(count, half), wide[:, each:].reshape(count, half)], 1
+    ).astype(jnp.bfloat16)
+    similar = matmul_nt(units, units)
+    row = lax.broadcasted_iota(jnp.int32, (count, count), 0)
+    column = lax.broadcasted_iota(jnp.int32, (count, count), 1)
+    used = (lax.rem(row, each) < pairs_here) & (lax.rem(column, each) >= pairs_here)
+    own = used & (column == row + pairs_here)
+    negative = used & (column == target_ref[...])
+    sim_scale = jnp.exp(scale_ref[...])
+    own_mask = jnp.where(own, 1.0, 0.0)
+    negative_mask = jnp.where(negative, 1.0, 0.0)
+    logits = sim_scale * similar - MARGIN * own_mask
+    diagonal = jnp.sum(logits * own_mask, 1, keepdims=True)
+    hardest = jnp.sum(logits * negative_mask, 1, keepdims=True)
+    row_max = jnp.max(jnp.where(used, logits, -3e38), 1, keepdims=True)
+    powers = jnp.where(used, jnp.exp(jnp.minimum(logits - row_max, 0.0)), 0.0)
+    row_sum = jnp.sum(powers, 1, keepdims=True)
+    is_query = lax.rem(lax.broadcasted_iota(jnp.int32, (count, 1), 0), each) < pairs_here
+    gap = hardest - diagonal
+    softplus = jnp.maximum(gap, 0.0) + jnp.log(1.0 + jnp.exp(-jnp.abs(gap)))
+    row_sum = jnp.where(is_query, row_sum, 1.0)
+    losses = jnp.where(is_query, row_max + jnp.log(row_sum) - diagonal + softplus, 0.0)
+    gate = 1.0 / (1.0 + jnp.exp(-gap))
+    grad_logits = jnp.where(
+        used, powers / row_sum - own_mask + gate * (negative_mask - own_mask), 0.0
+    )
+    loss_ref[0:1, :] = jnp.broadcast_to(jnp.sum(losses, 0, keepdims=True), (1, 128))
+    grad_scale = sim_scale * jnp.sum(
+        jnp.sum(grad_logits * similar, 1, keepdims=True), 0, keepdims=True
+    )
+    loss_ref[1:2, :] = jnp.broadcast_to(grad_scale, (1, 128))
+    loss_ref[2:8, :] = jnp.zeros((6, 128), jnp.float32)
+    grad_similar = sim_scale * grad_logits
+    grads[...] = grad_similar + jnp.transpose(grad_similar)
+    first = pl.multiple_of(me * each, each)
+    grad_units = matmul(grads[pl.ds(first, each), :].astype(jnp.bfloat16), units)
+    grad_units = grad_units.astype(jnp.bfloat16).astype(jnp.float32)
+    grad_ref[...] = (
+        factor * (grad_units - unit * jnp.sum(grad_units * unit, -1, keepdims=True))
+    ).astype(jnp.bfloat16)
+
+    @pl.loop(1, grid.total)
+    def _(step):
+        peer = lax.rem(me + step, grid.total)
+        copy(peer, peer).wait_send()
+
+
+def run_loss(projected, target, log_scale, number):
+    grid = Grid()
+    each = projected.shape[0]
+    count = grid.total * each
+    inside = pl.BlockSpec(memory_space=pltpu.VMEM)
+    dma = pltpu.SemaphoreType.DMA((grid.total,))
+    return pl.pallas_call(
+        functools.partial(loss_kernel, grid, each // 2),
+        out_shape=[
+            jax.ShapeDtypeStruct((each, D), jnp.bfloat16),
+            jax.ShapeDtypeStruct((8, 128), jnp.float32),
+        ],
+        in_specs=[inside] * 3,
+        out_specs=[inside] * 2,
+        scratch_shapes=[
+            pltpu.VMEM((2 * each, D // 2), jnp.bfloat16),
+            pltpu.VMEM((grid.total, 2 * each, D // 2), jnp.bfloat16),
+            pltpu.VMEM((count, count), jnp.float32),
+            dma,
+            dma,
         ],
         compiler_params=pltpu.CompilerParams(collective_id=number, has_side_effects=True),
-    )(*srcs, rows)
-    return (results[:count], results[count])
-
-
-ROW_BLOCK = 512
+    )(projected, target, log_scale)
+
+
+BACK_SEQS = 2
+
+
+def backward_kernel(
+    x0_ref,
+    mask_col_ref,
+    mixed_ref,
+    attended,
+    total_ref,
+    after_ref,
+    pre_hbm,
+    final_ref,
+    gains_ref,
+    bias_ref,
+    pooled_ref,
+    grad_proj_ref,
+    packed_hbm,
+    down_hbm,
+    rows_ref,
+    grad_gains_ref,
+    grad_bias_ref,
+    grad_packed_hbm,
+    grad_down_hbm,
+    packed,
+    down,
+    hidden,
+    grad_pre,
+    act_one,
+    act_two,
+    branch_two,
+    branch_one,
+    grad_mixed,
+    grad_pooled,
+    stage,
+    pre_buffer,
+    load_sem,
+    store_sem,
+    pre_sem,
+):
+    step = pl.program_id(0)
+    tile_seqs = x0_ref.shape[0] // L
+    tile = tile_seqs * L
+    base = pl.multiple_of(step * tile, tile)
+    edges = (0, WIDE, WIDE + D, WIDE + 5 * D, PACKED)
+
+    def load(k):
+        if k == 4:
+            return pltpu.make_async_copy(down_hbm, down, load_sem.at[k])
+        part = pl.ds(edges[k], edges[k + 1] - edges[k])
+        to = stage.at[0] if k == 3 else packed.at[:, part]
+        return pltpu.make_async_copy(packed_hbm.at[:, part], to, load_sem.at[k])
+
+    def loaded(k):
+        @pl.when(step == 0)
+        def _():
+            load(k).wait()
+
+    def load_pre(number):
+        start = pl.multiple_of(number // 4 * tile, tile)
+        across = pl.multiple_of(lax.rem(number, 4) * D, D)
+        slot = lax.rem(number, 2)
+        return pltpu.make_async_copy(
+            pre_hbm.at[pl.ds(start, tile), pl.ds(across, D)], pre_buffer.at[slot], pre_sem.at[slot]
+        )
+
+    @pl.when(step == 0)
+    def _():
+        load_pre(0).start()
+        for k in (3, 4, 2, 1, 0):
+            load(k).start()
+        grad_gains_ref[...] = jnp.zeros_like(grad_gains_ref)
+        grad_bias_ref[...] = jnp.zeros_like(grad_bias_ref)
+        load(3).wait()
+        grad_pooled[...] = matmul_nt(grad_proj_ref[...], stage[0])
+
+    def gain_back(k, grad_out, inputs):
+        gain = gains_ref[k : k + 1, :]
+        factor = lax.rsqrt(jnp.mean(inputs * inputs, -1, keepdims=True) + EPS)
+        scaled = grad_out * gain
+        grad_gains_ref[k : k + 1, :] += jnp.sum(grad_out * inputs * factor, 0, keepdims=True)
+        return factor * (
+            scaled - inputs * (factor * factor * jnp.mean(scaled * inputs, -1, keepdims=True))
+        )
+
+    rows = pl.ds(base, tile)
+    weight = mask_col_ref[...]
+    pieces = []
+    for s in range(tile_seqs):
+        part = weight[s * L : (s + 1) * L]
+        count = jnp.sum(part, 0, keepdims=True)
+        pieces.append(part * (grad_pooled[pl.ds(step * tile_seqs + s, 1), :] / count))
+    grad_final = gain_back(2, jnp.concatenate(pieces, 0), final_ref[...])
+    branch = grad_final.astype(jnp.bfloat16)
+    branch_two[rows, :] = branch
+    loaded(4)
+    loaded(2)
+    grad_act = jnp.zeros((tile, D), jnp.float32)
+    for j in range(4):
+        part = slice(j * D, (j + 1) * D)
+        grad_hidden = matmul_nt(branch, down[part, :])
+        number = step * 4 + j
+        pl.when(number + 1 < pl.num_programs(0) * 4)(lambda: load_pre(number + 1).start())
+        load_pre(number).wait()
+        pre = pre_buffer[j % 2]
+        half, tan = gelu_parts(pre)
+        hidden[rows, part] = (pre * half).astype(jnp.bfloat16)
+        slope = np.float32(np.sqrt(2 / np.pi)) * (1.0 + (3 * 0.044715) * (pre * pre))
+        grad_part = (grad_hidden * (half + 0.5 * pre * (1.0 - tan * tan) * slope)).astype(jnp.bfloat16)
+        grad_pre[rows, part] = grad_part
+        at = WIDE + D + j * D
+        grad_act = grad_act + matmul_nt(grad_part, packed[:, at : at + D])
+    after = after_ref[...]
+    act_two[rows, :] = normalize(after, gains_ref[1:2, :])[0].astype(jnp.bfloat16)
+    grad_after = grad_final + gain_back(1, grad_act, after)
+    branch = grad_after.astype(jnp.bfloat16)
+    branch_one[rows, :] = branch
+    loaded(1)
+    grad_attended = matmul_nt(branch, packed[:, WIDE : WIDE + D]).astype(jnp.bfloat16)
+    zero = jnp.zeros((), jnp.bfloat16)
+    mine = lane_is((L, 128), 0, HD)
+    for s in range(tile_seqs):
+        part = slice(s * L, (s + 1) * L)
+        here = pl.ds(pl.multiple_of(base + s * L, L), L)
+        keep = jnp.where(weight[part] > 0, 0.0, -1000000000.0)
+        for pair in range(HEADS // 2):
+            at = pair * 128
+            query = mixed_ref[part, at : at + 128]
+            key = mixed_ref[part, D + at : D + at + 128]
+            value = mixed_ref[part, 2 * D + at : 2 * D + at + 128]
+            grad_out = grad_attended[part, at : at + 128]
+            keys = jnp.concatenate([jnp.where(mine, key, zero), jnp.where(mine, zero, key)], 0)
+            values = jnp.concatenate([jnp.where(mine, value, zero), jnp.where(mine, zero, value)], 0)
+            scores = (matmul_nt(keys, query) * SCALE).reshape(2, L, L)
+            scores = scores + bias_ref[2 * pair : 2 * pair + 2] + keep[None]
+            prob = jnp.exp(scores - total_ref[s, 2 * pair : 2 * pair + 2, :][:, None, :])
+            grad_prob = matmul_nt(values, grad_out).reshape(2, L, L)
+            mean = jnp.sum(prob * grad_prob, 1, keepdims=True)
+            grad_scores = (prob * (grad_prob - mean)).astype(jnp.bfloat16)
+            grad_bias_ref[2 * pair : 2 * pair + 2] += grad_scores.astype(jnp.float32)
+            prob_low = prob.astype(jnp.bfloat16)
+            flipped = jnp.transpose(key)
+            grad_query = jnp.concatenate(
+                [matmul(flipped[:HD], grad_scores[0]), matmul(flipped[HD:], grad_scores[1])], 0
+            )
+            grad_mixed[here, at : at + 128] = (jnp.transpose(grad_query) * SCALE).astype(jnp.bfloat16)
+            grad_keys = matmul(grad_scores.reshape(2 * L, L), query)
+            grad_key = jnp.where(mine, grad_keys[:L], grad_keys[L:]) * SCALE
+            grad_mixed[here, D + at : D + at + 128] = grad_key.astype(jnp.bfloat16)
+            grad_values = matmul(prob_low.reshape(2 * L, L), grad_out)
+            grad_value = jnp.where(mine, grad_values[:L], grad_values[L:])
+            grad_mixed[here, 2 * D + at : 2 * D + at + 128] = grad_value.astype(jnp.bfloat16)
+    loaded(0)
+    x0 = x0_ref[...]
+    act_one[rows, :] = normalize(x0, gains_ref[0:1, :])[0].astype(jnp.bfloat16)
+    grad_act = matmul_nt(grad_mixed[rows, :], packed[:, :WIDE])
+    rows_ref[...] = (grad_after + gain_back(0, grad_act, x0)).astype(jnp.bfloat16)
+
+    @pl.when(step == pl.num_programs(0) - 1)
+    def _():
+        jobs = []
+        for j in range(4):
+            part = slice(j * D, (j + 1) * D)
+            jobs.append((hidden, part, branch_two, slice(0, D), grad_down_hbm.at[pl.ds(j * D, D), :]))
+        for j in range(4):
+            part = slice(j * D, (j + 1) * D)
+            jobs.append((act_two, slice(0, D), grad_pre, part, grad_packed_hbm.at[:, pl.ds(WIDE + D + j * D, D)]))
+        jobs.append((attended, slice(0, D), branch_one, slice(0, D), grad_packed_hbm.at[:, pl.ds(WIDE, D)]))
+        for j in range(3):
+            part = slice(j * D, (j + 1) * D)
+            jobs.append((act_one, slice(0, D), grad_mixed, part, grad_packed_hbm.at[:, pl.ds(j * D, D)]))
+        copies = []
+        for number, (left, left_part, right, right_part, to) in enumerate(jobs):
+            slot = number % 2
+            if number >= 2:
+                copies[number - 2].wait()
+            stage[slot] = matmul_tn(left[:, left_part], right[:, right_part]).astype(jnp.bfloat16)
+            copies.append(pltpu.make_async_copy(stage.at[slot], to, store_sem.at[slot]))
+            copies[-1].start()
+        copies[-2].wait()
+        stage[0] = matmul_tn(pooled_ref[...].astype(jnp.bfloat16), grad_proj_ref[...]).astype(jnp.bfloat16)
+        last = pltpu.make_async_copy(stage.at[0], grad_packed_hbm.at[:, pl.ds(PACKED - D, D)], store_sem.at[0])
+        last.start()
+        copies[-1].wait()
+        last.wait()
+
+
+def run_backward(
+    x0, mask_col, mixed, attended, totals, after, pre, final, gains, bias_full, pooled, grad_proj, packed, down
+):
+    tokens = x0.shape[0]
+    seqs = tokens // L
+    tile = BACK_SEQS * L
+    steps = tokens // tile
+
+    def rows(width, **mode):
+        return pl.BlockSpec((tile, width), lambda i: (i, 0), **mode)
+
+    def whole(*shape):
+        return pl.BlockSpec(shape, lambda i: (0,) * len(shape), pipeline_mode=pl.Buffered(1))
+
+    def low(*shape):
+        return pltpu.VMEM(shape, jnp.bfloat16)
+
+    anywhere = pl.BlockSpec(memory_space=pl.ANY)
+    return pl.pallas_call(
+        backward_kernel,
+        grid=(steps,),
+        out_shape=[
+            jax.ShapeDtypeStruct((tokens, D), jnp.bfloat16),
+            jax.ShapeDtypeStruct((3, D), jnp.float32),
+            jax.ShapeDtypeStruct((HEADS, L, L), jnp.float32),
+            jax.ShapeDtypeStruct(packed.shape, jnp.bfloat16),
+            jax.ShapeDtypeStruct(down.shape, jnp.bfloat16),
+        ],
+        in_specs=[
+            rows(D),
+            rows(1),
+            rows(WIDE),
+            whole(tokens, D),
+            pl.BlockSpec((BACK_SEQS, HEADS, L), lambda i: (i, 0, 0)),
+            rows(D),
+            anywhere,
+            rows(D),
+            whole(3, D),
+            whole(HEADS, L, L),
+            whole(seqs, D),
+            whole(seqs, D),
+            anywhere,
+            anywhere,
+        ],
+        out_specs=[rows(D), whole(3, D), whole(HEADS, L, L), anywhere, anywhere],
+        scratch_shapes=[
+            low(D, PACKED - D),
+            low(4 * D, D),
+            low(tokens, 4 * D),
+            low(tokens, 4 * D),
+            low(tokens, D),
+            low(tokens, D),
+            low(tokens, D),
+            low(tokens, D),
+            low(tokens, WIDE),
+            pltpu.VMEM((seqs, D), jnp.float32),
+            low(2, D, D),
+            pltpu.VMEM((2, tile, D), jnp.float32),
+            pltpu.SemaphoreType.DMA((5,)),
+            pltpu.SemaphoreType.DMA((2,)),
+            pltpu.SemaphoreType.DMA((2,)),
+        ],
+        compiler_params=pltpu.CompilerParams(vmem_limit_bytes=62 * 1024 * 1024),
+    )(x0, mask_col, mixed, attended, totals, after, pre, final, gains, bias_full, pooled, grad_proj, packed, down)
 
 
 def finish_kernel(grid, count, *refs):
@@ -494,7 +1161,8 @@
         refs[k * count : (k + 1) * count] for k in range(6)
     ]
     refs = refs[6 * count :]
-    rows, small_all, square_mine, square_all = refs[:4]
+    rows, small_stage, small_in, square_stage, square_in = refs[:5]
+    refs = refs[1:]
     load_sem, side_send, side_recv, v_send, v_recv, u_send, u_recv, z_send, low_recv, high_recv = refs[4:14]
     row_own, line_send, on_send, row_recv, small_send, small_recv, square_send, square_recv = refs[14:]
     z, x, y, core = grid.here()
@@ -511,9 +1179,17 @@
     f_y = (1 - y) * 2 + core
     f_far = (1 - y) * 2 + 1 - core
 
-    @pl.loop(1, grid.total)
+    for level in range(tall):
+        small_in[3 + level] = jnp.zeros(small.shape, jnp.float32)
+        square_in[3 + level] = jnp.zeros((16, 128), jnp.float32)
+    x_device, y_device = grid.device(z, 1 - x, y, core), grid.device(z, x, 1 - y, core)
+
+    @pl.loop(1, grid.dp)
     def _(step):
-        greet(grid.peer(lax.rem(me + step, grid.total)))
+        greet((lax.rem(d + step, grid.dp), f))
+
+    greet(y_device)
+    greet(sibling)
 
     def each(action):
         for m in range(count):
@@ -594,32 +1270,69 @@
             device_id_type=MESH,
         )
 
-    def small_copy(peer, slot):
-        return pltpu.make_async_remote_copy(
-            src_ref=small,
-            dst_ref=small_all.at[slot],
-            send_sem=small_send.at[peer],
-            recv_sem=small_recv.at[slot],
-            device_id=grid.peer(peer),
-            device_id_type=MESH,
-        )
-
-    def square_copy(peer, slot):
-        return pltpu.make_async_remote_copy(
-            src_ref=square_mine,
-            dst_ref=square_all.at[slot],
-            send_sem=square_send.at[peer],
-            recv_sem=square_recv.at[slot],
-            device_id=grid.peer(peer),
-            device_id_type=MESH,
-        )
-
+    def total_of(stage, inbox, send_sem, recv_sem):
+        partners = (sibling, x_device, y_device)
+
+        def copy(r):
+            return pltpu.make_async_remote_copy(
+                src_ref=stage.at[r],
+                dst_ref=inbox.at[r],
+                send_sem=send_sem.at[r],
+                recv_sem=recv_sem.at[r],
+                device_id=partners[r],
+                device_id_type=MESH,
+            )
+
+        def z_send(level, slot):
+            return pltpu.make_async_remote_copy(
+                src_ref=stage.at[3],
+                dst_ref=inbox.at[3 + slot],
+                send_sem=send_sem.at[3 + level],
+                recv_sem=recv_sem.at[3 + slot],
+                device_id=grid.device(level, x, y, core),
+                device_id_type=MESH,
+            )
+
+        def others(action):
+            @pl.loop(1, tall)
+            def _(step):
+                action(lax.rem(z + step, tall))
+
+        def send(r):
+            if r < 3:
+                copy(r).start()
+            else:
+                others(lambda level: z_send(level, z).start())
+
+        def take(r):
+            if r < 3:
+                copy(r).wait_recv()
+                stage[r + 1] = stage[r] + inbox[r]
+                send(r + 1)
+            else:
+                others(lambda level: z_send(level, level).wait_recv())
+
+        def result():
+            total = stage[3]
+            for level in range(tall):
+                total = total + jnp.where(z == level, 0.0, inbox[3 + level])
+            for r in range(3):
+                copy(r).wait_send()
+            others(lambda level: z_send(level, level).wait_send())
+            return total
+
+        return send, take, result
+
+    small_stage[0] = small[...]
+    small_sends, small_take, small_result = total_of(small_stage, small_in, small_send, small_recv)
+    square_sends, square_take, square_result = total_of(square_stage, square_in, square_send, square_recv)
     levels = [level_of(j) for j in range(tall)]
     own_rows = pltpu.make_async_copy(sums.at[d], rows.at[me], row_own)
     own_rows.start()
     for level in levels:
         each(lambda m: load(m, level).start())
-    meet(grid.total - 1)
+    meet(grid.dp + 1)
+    small_sends(0)
 
     @pl.loop(1, grid.dp)
     def _(step):
@@ -629,12 +1342,6 @@
         each(lambda m: side(m, level).start())
     onward(me, False, True).start()
     onward(me, True, True).start()
-
-    @pl.loop(1, grid.total)
-    def _(step):
-        small_copy(lax.rem(me + step, grid.total), me).start()
-
-    small_all[me] = small[...]
 
     def first(j):
         level = levels[j]
@@ -726,7 +1433,7 @@
 
     table_rows = table_out.shape[0]
     whole_blocks = table_rows // ROW_BLOCK
-    square_mine[...] = jnp.zeros_like(square_mine)
+    square_stage[0] = jnp.zeros((16, 128), jnp.float32)
 
     def fold(values):
         n, lanes = values.shape
@@ -741,14 +1448,14 @@
         group = 8
         total = jnp.zeros((size, D), jnp.float32)
         for g in range(0, grid.total, group):
-            place = start + lax.broadcasted_iota(jnp.int32, (size, group * per), 0)
+            place = (start + lax.broadcasted_iota(jnp.int32, (size, group * per), 0)).astype(jnp.float32)
             wanted = ids[:, g * per : (g + group) * per]
             hot = jnp.where(place == wanted, 1.0, 0.0).astype(jnp.bfloat16)
             total = total + matmul(hot, rows[g : g + group].reshape(group * per, D))
         low = total.astype(jnp.bfloat16)
         table_out[pl.ds(start, size), :] = low
         wide = low.astype(jnp.float32)
-        square_mine[8:16, :] += fold(wide * wide)
+        square_stage[0, 8:16, :] += fold(wide * wide)
 
     def spread_blocks(first_block, last_block):
         @pl.loop(first_block, last_block)
@@ -757,6 +1464,8 @@
 
     for j in range(tall):
         first(j)
+        if j < 3:
+            small_take(j)
     pass_lines()
     second(0)
     second_own(0)
@@ -780,22 +1489,15 @@
     def give(m):
         wide = acc[m][z, x, y].astype(jnp.float32)
         outs[m][...] = wide
-        square_mine[0:8, :] += fold(wide * wide)
+        square_stage[0, 0:8, :] += fold(wide * wide)
 
     each(give)
 
-    @pl.loop(1, grid.total)
-    def _(step):
-        square_copy(lax.rem(me + step, grid.total), me).start()
-
-    square_all[me] = square_mine[...]
-
-    @pl.loop(1, grid.total)
-    def _(step):
-        peer = lax.rem(me + step, grid.total)
-        small_copy(peer, peer).wait_recv()
-
-    small_out[...] = jnp.sum(small_all[...], 0)
+    square_sends(0)
+    small_take(3)
+    small_out[...] = small_result()
+    for r in range(3):
+        square_take(r)
 
     for level in levels:
         each(lambda m: side(m, level).wait_send())
@@ -817,14 +1519,8 @@
     def _(step):
         line(lax.rem(d + step, grid.dp), me).wait_send()
 
-    @pl.loop(1, grid.total)
-    def _(step):
-        peer = lax.rem(me + step, grid.total)
-        square_copy(peer, peer).wait_recv()
-        square_copy(peer, peer).wait_send()
-        small_copy(peer, peer).wait_send()
-
-    square_out[...] = jnp.sum(square_all[...], 0)
+    square_take(3)
+    square_out[...] = square_result()
 
 
 def finish(srcs, sums, ids, small, vocab_rows, number):
@@ -838,15 +1534,16 @@
     cap = sums.shape[1]
     buffers += [
         pltpu.VMEM((grid.total, cap, D), jnp.bfloat16),
-        pltpu.VMEM((grid.total,) + small.shape, jnp.float32),
-        pltpu.VMEM((16, 128), jnp.float32),
-        pltpu.VMEM((grid.total, 16, 128), jnp.float32),
+        pltpu.VMEM((4,) + small.shape, jnp.float32),
+        pltpu.VMEM((3 + tall,) + small.shape, jnp.float32),
+        pltpu.VMEM((4, 16, 128), jnp.float32),
+        pltpu.VMEM((3 + tall, 16, 128), jnp.float32),
     ]
     dma = pltpu.SemaphoreType.DMA
     by_level = dma((count, tall))
     semaphores = [by_level, by_level, by_level, dma((count, tall, 2)), dma((count, tall, 2))] + [by_level] * 5
-    by_device = dma((grid.total,))
-    semaphores += [dma, dma((grid.dp,)), dma((2, grid.total)), by_device, by_device, by_device, by_device, by_device]
+    by_device, by_step = dma((grid.total,)), dma((3 + tall,))
+    semaphores += [dma, dma((grid.dp,)), dma((2, grid.total)), by_device] + [by_step] * 4
     anywhere, inside = pl.BlockSpec(memory_space=pl.ANY), pl.BlockSpec(memory_space=pltpu.VMEM)
     results = pl.pallas_call(
         functools.partial(finish_kernel, grid, count),
@@ -1139,8 +1836,6 @@
     dp_count = lax.axis_size("dp")
     fsdp_count = lax.axis_size("fsdp")
     total = dp_count * fsdp_count
-    column = lax.axis_index("fsdp")
-    device_flat = lax.axis_index("dp") * fsdp_count + column
     pairs_here = token_ids.shape[1]
     pairs_total = pairs_here * total
     seq_count = 2 * pairs_here
@@ -1149,7 +1844,7 @@
     gain_rows = small_params[: 3 * D].reshape(3, D)
     bias_table = small_params[3 * D : 3 * D + NB * HEADS].reshape(NB, HEADS)
     log_scale = small_params[3 * D + NB * HEADS]
-    buckets = jnp.asarray(bucket_table(L, NB).reshape(-1), jnp.int32)
+    buckets = jnp.asarray(bucket_table(L, NB).T.reshape(-1), jnp.int32)
     bucket_hot = (buckets[:, None] == jnp.arange(NB, dtype=jnp.int32)[None, :]).astype(jnp.float32)
     bias_full = (
         jnp.dot(bucket_hot, bias_table, precision=HIGH).reshape(L, L, HEADS).transpose(2, 0, 1)
@@ -1158,100 +1853,34 @@
     ids_flat = token_ids.reshape(-1)
     tokens = ids_flat.shape[0]
 
-    order = jnp.arange(tokens, dtype=jnp.int32)
-    owner = ids_flat // vocab_rows
-    earlier = (ids_flat[None, :] == ids_flat[:, None]) & (order[None, :] < order[:, None])
-    first = ~jnp.any(earlier, 1)
-    below = (owner[None, :] == owner[:, None]) & (ids_flat[None, :] < ids_flat[:, None]) & first[None, :]
-    rank = jnp.sum(below.astype(jnp.int32), 1)
-    spilled = jnp.any(rank >= CAP)
-    slot = jnp.where(rank < CAP, owner * CAP + rank, -1)
-    slots = jnp.arange(dp_count * CAP, dtype=jnp.int32)
-    lists = jnp.max(
-        jnp.where(slot[None, :] == slots[:, None], (ids_flat - owner * vocab_rows)[None, :], -1), 1
-    ).reshape(dp_count, 1, 1, CAP)
-    lists = jnp.broadcast_to(lists, (dp_count, fsdp_count, 1, CAP)).reshape(total, 1, CAP)
-    extra = jnp.zeros((7, 128), jnp.int32)
-    extra = extra.at[0, :pairs_here].set(hard_negative).at[1, 0].set(spilled.astype(jnp.int32))
-    message = jnp.concatenate([lists, jnp.broadcast_to(extra[None], (total, 7, 128))], 1)
-    heard = exchange(message, True, 1)
-    asked = heard[:, 0, :]
-    negatives = heard[:, 1, :pairs_here].reshape(-1)
-    any_spilled = jnp.max(heard[:, 2, 0]) > 0
-
-    mine_asked = lax.dynamic_index_in_dim(
-        asked.reshape(dp_count, fsdp_count, CAP), column, 1, keepdims=False
-    )
-    answers = jnp.take(table, jnp.maximum(mine_asked.reshape(-1), 0), axis=0).astype(jnp.bfloat16)
-    shards = (
-        attn_in.astype(jnp.bfloat16),
-        attn_out.astype(jnp.bfloat16),
-        ffn_in.astype(jnp.bfloat16),
-        ffn_out.astype(jnp.bfloat16),
-        proj_head.astype(jnp.bfloat16),
-    )
-    gathered, found = gather(shards, answers.reshape(dp_count, CAP, D), 2)
-    gathered = [matrix.reshape(-1, matrix.shape[-1]) for matrix in gathered]
-    slot_hot = (slot[:, None] == slots[None, :]).astype(jnp.bfloat16)
-    embedded = matmul(slot_hot, found.reshape(dp_count * CAP, D))
+    gathered_packed, gathered_down, heard, slot, embedded = run_head(
+        ids_flat, hard_negative, attn_in, attn_out, ffn_in, proj_head, ffn_out, table, 1
+    )
+    packed = gathered_packed.reshape(-1, PACKED)
+    down = gathered_down.reshape(-1, D)
+    asked = heard[:, 0, :CAP]
+    negatives = heard[:, 1, :pairs_here].reshape(-1).astype(jnp.int32)
+    any_spilled = jnp.max(heard[:, 2, 0]) > 0.5
     embedded = once(any_spilled, lambda _: dense_rows(ids_flat, table, row_base), embedded)
 
-    final_rows, kept = layer_forward(embedded, mask_rows, gathered[:4], gain_rows, bias_full)
-    normed_three, factor_three = normalize(final_rows, gain_rows[2])
-    mask_weight = mask_rows.astype(jnp.float32)[:, :, None]
-    counts = jnp.sum(mask_weight, 1)
-    pooled = jnp.sum(normed_three.reshape(seq_count, L, D) * mask_weight, 1) / counts
-    pooled_low = pooled.astype(jnp.bfloat16)
-    projected = matmul(pooled_low, gathered[4])
-    proj_factor = lax.rsqrt(jnp.sum(projected * projected, -1, keepdims=True) + EPS)
-    unit_rows = projected * proj_factor
-    unit_low = unit_rows.astype(jnp.bfloat16)
-    all_units = exchange(unit_low.reshape(2 * seq_count, D // 2), False, 3)
-    all_units = all_units.reshape(total, 2, pairs_here, D)
-    all_query = all_units[:, 0].reshape(pairs_total, D)
-    all_pass = all_units[:, 1].reshape(pairs_total, D)
-    similar = matmul_nt(all_query, all_pass)
-    sim_scale = jnp.exp(log_scale)
-    columns = jnp.arange(pairs_total, dtype=jnp.int32)
-    own_mask = (columns[None, :] == columns[:, None]).astype(jnp.float32)
-    negative = (columns[None, :] == negatives[:, None]).astype(jnp.float32)
-    logits = sim_scale * similar - MARGIN * own_mask
-    diagonal = jnp.sum(logits * own_mask, 1)
-    hardest = jnp.sum(logits * negative, 1)
-    row_max = jnp.max(logits, 1, keepdims=True)
-    log_total = row_max + jnp.log(jnp.sum(jnp.exp(logits - row_max), 1, keepdims=True))
-    loss_sum = jnp.sum(log_total[:, 0] - diagonal + jax.nn.softplus(hardest - diagonal))
-    hinge_gate = jax.nn.sigmoid(hardest - diagonal)
-    grad_logits = (
-        jnp.exp(logits - log_total) - own_mask + hinge_gate[:, None] * (negative - own_mask)
-    )
-    grad_log_scale = sim_scale * jnp.sum(grad_logits * similar)
-    grad_similar = (sim_scale * grad_logits).astype(jnp.bfloat16)
-    own_first = device_flat * pairs_here
-    mine_rows = lax.dynamic_slice_in_dim(grad_similar, own_first, pairs_here, 0)
-    mine_columns = lax.dynamic_slice_in_dim(grad_similar, own_first, pairs_here, 1)
-    grad_query = matmul(mine_rows, all_pass).astype(jnp.bfloat16)
-    grad_pass = matmul_tn(mine_columns, all_query).astype(jnp.bfloat16)
-    grad_units = jnp.concatenate([grad_query, grad_pass], 0).astype(jnp.float32)
-    grad_proj = (
-        proj_factor * (grad_units - unit_rows * jnp.sum(grad_units * unit_rows, -1, keepdims=True))
-    ).astype(jnp.bfloat16)
-    grad_proj_head = matmul_tn(pooled_low, grad_proj)
-    grad_pooled = matmul_nt(grad_proj, gathered[4])
-    grad_normed = ((grad_pooled / counts)[:, None, :] * mask_weight).reshape(-1, D)
-    grad_final, gain_three = normalize_back(grad_normed, final_rows, factor_three, gain_rows[2])
-    grad_rows, matrix_grads, gain_one, gain_two, grad_bias = layer_backward(
-        grad_final, kept, mask_rows, gathered[:4], gain_rows, bias_full
+    mask_col = mask_rows.astype(jnp.float32).reshape(tokens, 1)
+    *kept, pooled, projected = run_forward(embedded, mask_col, gain_rows, bias_full, packed, down)
+    target = negatives // pairs_here * seq_count + pairs_here + negatives % pairs_here
+    target = jnp.concatenate(
+        [target.reshape(total, pairs_here), jnp.full((total, pairs_here), -1, jnp.int32)], 1
+    ).reshape(-1, 1)
+    grad_proj, loss_parts = run_loss(projected, target, log_scale.reshape(1, 1), 3)
+    loss_sum, grad_log_scale = loss_parts[0, 0], loss_parts[1, 0]
+    grad_low, grad_gains, grad_bias, grad_packed, grad_down = run_backward(
+        embedded, mask_col, *kept, gain_rows, bias_full, pooled, grad_proj, packed, down
     )
     grad_bias_table = jnp.dot(grad_bias.reshape(HEADS, L * L), bucket_hot, precision=HIGH).T
-    partials = [
-        grad.astype(jnp.bfloat16).reshape(total, -1, grad.shape[1])
-        for grad in (*matrix_grads, grad_proj_head)
-    ]
-    small_local = jnp.concatenate([gain_one, gain_two, gain_three, grad_bias_table.reshape(-1)])
+    partials = [grad.reshape(total, -1, grad.shape[1]) for grad in (grad_packed, grad_down)]
+    small_local = jnp.concatenate([grad_gains.reshape(-1), grad_bias_table.reshape(-1)])
     width = -(-small_local.shape[0] // 1024) * 8
     small_local = jnp.pad(small_local, (0, width * 128 - small_local.shape[0]))
-    grad_low = grad_rows.astype(jnp.bfloat16)
+    slots = jnp.arange(dp_count * CAP, dtype=jnp.int32).astype(jnp.float32)
+    slot_hot = (slot == slots[None, :]).astype(jnp.bfloat16)
     slot_sums = matmul_tn(slot_hot, grad_low).astype(jnp.bfloat16).reshape(dp_count, CAP, D)
     weight_grads, table_grad, summed, squares = finish(
         partials, slot_sums, asked.reshape(-1), small_local.reshape(width, 128), vocab_rows, 4
@@ -1267,13 +1896,16 @@
     small_grad = jnp.concatenate([summed.reshape(-1)[: small_size - 1], grad_log_scale[None]])
     norm_value = jnp.sqrt(total_squares + jnp.sum(small_grad * small_grad))
     factor = jnp.minimum(1.0, CLIP / (norm_value + 1e-06))
+    grad_in, grad_out, grad_up, grad_head = jnp.split(
+        weight_grads[0], (WIDE, WIDE + D, WIDE + 5 * D), 1
+    )
     updates = (
         (table, table_first, table_second, table_grad.astype(jnp.float32)),
-        (attn_in, attn_in_first, attn_in_second, weight_grads[0]),
-        (attn_out, attn_out_first, attn_out_second, weight_grads[1]),
-        (ffn_in, ffn_in_first, ffn_in_second, weight_grads[2]),
-        (ffn_out, ffn_out_first, ffn_out_second, weight_grads[3]),
-        (proj_head, proj_head_first, proj_head_second, weight_grads[4]),
+        (attn_in, attn_in_first, attn_in_second, grad_in),
+        (attn_out, attn_out_first, attn_out_second, grad_out),
+        (ffn_in, ffn_in_first, ffn_in_second, grad_up),
+        (ffn_out, ffn_out_first, ffn_out_second, weight_grads[1]),
+        (proj_head, proj_head_first, proj_head_second, grad_head),
         (small_params, small_first, small_second, small_grad),
     )
     results = [loss_sum, norm_value]

time: 576 us -> 477 us (0.83); the launches traced: 566 us -> 477 us
  matrix products: 122 us -> 5.97 us
  Pallas kernels: 285 us -> 384 us
  local copies, waits for them, and re-layouts: 56.5 us -> 12.9 us
  other arithmetic: 80.2 us -> 55.4 us
    pallas_call x3 -> x4, Pallas kernels: 128 us -> 240 us  [the longest x1 94.9 us: run_head(): pl.pallas_call(functools.partial(head_kernel, grid), out_shape=[jax.Shape...]
    dot_general x19 -> x0, matrix products: 85.5 us -> none  [the longest x7 38.4 us: matmul(): return jnp.dot(left_side, right_side, preferred_element_type=jnp.float32)]
    dot_general x7 -> x1, matrix products: 33.7 us -> 3.18 us  [matmul_tn(): lax.dot_general(left_side, right_side, (((0,), (0,)), ((), ())), preferre...]
    convert_element_type x4 -> x3, local copies, waits for them, and re-layouts: 19.3 us -> 1.31 us  [the longest x1 1.02 us: fast_body(): mask_col = mask_rows.astype(jnp.float32).reshape(tokens, 1)]
    reduce_sum x11 -> x0, other arithmetic: 15 us -> none  [the longest x1 2.92 us: layer_backward(): grad_bias = jnp.sum(grad_scores, 0, dtype=jnp.float32)]
    pallas_call x1, Pallas kernels: 157 us -> 144 us  [finish(): pl.pallas_call(functools.partial(finish_kernel, grid, count), out_shape=[...]
    convert_element_type x11 -> x4, other arithmetic: 12.6 us -> 2.9 us  [the longest x1 0.93 us: fast_body(): negatives = heard[:, 1, :pairs_here].reshape(-1).astype(jnp.int32)]
    unnamed x180 -> x41, local copies, waits for them, and re-layouts: 11.7 us -> 2.67 us
where the time goes in v4:
time: 477 us
  Pallas kernels  384 us (81%)
  other arithmetic  55.4 us (12%)
  between operations  18.6 us (4%)
  local copies, waits for them, and re-layouts  12.9 us (3%)
  matrix products  5.97 us (1%)
    pallas_call x1, Pallas kernels, finish(): pl.pallas_call(functools.partial(finish_kernel, grid, count), out_shape=[...  144 us
    pallas_call x1, Pallas kernels, run_head(): pl.pallas_call(functools.partial(head_kernel, grid), out_shape=[jax.Shape...  94.9 us
    pallas_call x1, Pallas kernels, run_backward(): pl.pallas_call(backward_kernel, grid=(steps,), out_shape=[jax.ShapeDtypeS...  94.7 us
    sub x6, other arithmetic, adam_update(): return (first_new, second_new, param - rate * (direction + decay * param))  38.8 us
    pallas_call x1, Pallas kernels, run_forward(): pl.pallas_call(forward_kernel, grid=(steps,), out_shape=[kept(WIDE, jnp.b...  30.8 us
    pallas_call x1, Pallas kernels, run_loss(): pl.pallas_call(functools.partial(loss_kernel, grid, each // 2), out_shape...  19.5 us

profile of v4, /device:TPU:0, one launch (start us, length us, event | category | flops | bytes accessed | tf_op | source)
XLA Modules:
  0.0 477.2 jit_solution(2075190499443554846)
XLA Ops:
  7.9 1.2 slice.59
  9.1 1.3 fusion.34
  13.1 1.3 reshape.220.gains_ref
  14.5 1.0 copy.81.mask_col_ref
  15.7 1.6 fusion.10
  17.3 1.1 copy.93
  18.4 7.8 %convert.7 = bf16[4016,768]{1,0:T(8,128)(2,1)} convert(f32[4016,768]{1,0:T(8,128)} %table_hbm.1) | non-fusion elementwise | flops 3084288 | bytes 18505728
  26.3 94.9 %shard_map.416 = (bf16[32,24,6912]{2,1,0:T(8,128)(2,1)}, bf16[32,96,768]{2,1,0:T(8,128)(2,1)}, f32[32,8,128]{2,1,0:T(8,128)S(1)}, f32[1024,1]{1,0:T(8,128)S(1)}, f32[1024,768]{1,0:T(8,128)}) custom-call(f32[1024,1]{1,0:T(8,128)S(1)} %copy.78.col_ref, f32[1,1024]{1,0:T(1,128)S(1)} %bitcast.66, f32[1,128]{1,0:T(1,128)S(1)} %scatter.4.negative_ref, ...), custom_call_target="tpu_custom_call" | custom-call | tf_op jit(solution)/shard_map/pallas_call | solution.py:603
  127.1 30.8 %shard_map.417 = (bf16[1024,2304]{1,0:T(8,128)(2,1)}, bf16[1024,768]{1,0:T(8,128)(2,1)}, f32[8,12,128]{2,1,0:T(8,128)}, f32[1024,768]{1,0:T(8,128)}, f32[1024,30...) custom-call(f32[1024,768]{1,0:T(8,128)} %get-tuple-element.144.x0_ref, ...), custom_call_target="tpu_custom_call" | custom-call | tf_op jit(solution)/shard_map/pallas_call | solution.py:759
  157.9 19.5 %shard_map.418 = (bf16[8,768]{1,0:T(8,128)(2,1)}, f32[8,128]{1,0:T(8,128)}) custom-call(f32[8,768]{1,0:T(8,128)} %get-tuple-element.147.projected_ref, s32[256,1]{1,0:T(8,128)} %reshape.253.target_ref, f32[1,1]{1,0:T(1,128)} %bitcast.12.scale_ref), custom_call_target="tpu_custom_call" | custom-call | tf_op jit(solution)/shard_map/pallas_call | solution.py:884
  177.4 94.7 %shard_map.419 = (bf16[1024,768]{1,0:T(8,128)(2,1)S(1)}, f32[3,768]{1,0:T(4,128)}, f32[12,128,128]{2,1,0:T(8,128)}, bf16[768,6912]{1,0:T(8,128)(2,1)}, bf16[3072,768]{1,0:T(8,128)(2,1)}) custom-call(f32[1024,768]{1,0:T(8,128)} %get-tuple-element.144.x0_ref, f32[1024,1]{1,0:T(8,128)} %copy.81.mask_col_ref, bf16[1024,2304]{1,0:T(8,128)(2,1)} %get-tuple-element.149.mixed_ref, ...), custom_call_target="tpu_custom_call" | custom-call | tf_op jit(solution)/shard_map/pallas_call | solution.py:1107
  272.2 1.3 fusion.42
  274.1 1.2 pad.18
  276.0 1.2 fusion.12
  277.9 3.2 fusion.15
  281.1 144.0 %shard_map.420 = (f32[24,6912]{1,0:T(8,128)}, f32[96,768]{1,0:T(8,128)}, bf16[4016,768]{1,0:T(8,128)(2,1)}, f32[24,128]{1,0:T(8,128)}, f32[16,128]{1,0:T(8,128)}) custom-call(bf16[4,2,2,2,24,6912]{5,4,3,2,1,0:T(8,128)(2,1)} %bitcast.72, bf16[4,2,2,2,96,768]{5,4,3,2,1,0:T(8,128)(2,1)} %bitcast.76, bf16[8,112,768]{2,1,0:T(8,128)(2,1)} %bitcast.79, ...), custom_call_target="tpu_custom_call" | custom-call | tf_op jit(solution)/shard_map/pallas_call | solution.py:1548
  425.1 1.3 slice_reduce_fusion.2
  428.2 1.3 multiply_reduce_fusion.1
  430.2 1.3 add_subtract_fusion
  431.5 1.9 multiply_subtract_fusion.4
  433.4 2.0 multiply_subtract_fusion.1
  435.4 2.1 multiply_subtract_fusion.3
  437.5 2.1 multiply_subtract_fusion.2
  439.6 29.4 %multiply_subtract_fusion = (f32[4016,768]{1,0:T(8,128)}, f32[4016,768]{1,0:T(8,128)}, f32[4016,768]{1,0:T(8,128)}) fusion(f32[4016,768]{1,0:T(8,128)} %table_hbm.1, f32[]{:T(128)S(6)} %min.11, bf16[4016,768]{1,0:T(8,128)(2,1)} %get-tuple-element.167, f32[4016,768]{1,0:T(8,128)} %param.38, f32[4016,768]{1,0:T(8,128)} %param.37), kind=kLoop, calls=%fused_computation.17 | loop fusion | flops 52432896 | bytes 80191488 | tf_op jit(solution)/shard_map/sub | solution.py:207
  (63 shorter events, 11.3 us)
Async XLA Ops:
  7.2 19.0 %copy-start.7 = (f32[24,768]{1,0:T(8,128)S(1)}, f32[24,768]{1,0:T(8,128)}, u32[]{:S(2)}) copy-start(f32[24,768]{1,0:T(8,128)} %proj_ref.1) | copy-start | bytes 221188
  7.2 19.0 %copy-start = (f32[96,768]{1,0:T(8,128)S(1)}, f32[96,768]{1,0:T(8,128)}, u32[]{:S(2)}) copy-start(f32[96,768]{1,0:T(8,128)} %down_ref.1) | copy-start | bytes 884740
  7.2 19.0 %copy-start.2 = (f32[24,3072]{1,0:T(8,128)S(1)}, f32[24,3072]{1,0:T(8,128)}, u32[]{:S(2)}) copy-start(f32[24,3072]{1,0:T(8,128)} %up_ref.1) | copy-start | bytes 884740
  7.2 19.0 %copy-start.6 = (f32[24,768]{1,0:T(8,128)S(1)}, f32[24,768]{1,0:T(8,128)}, u32[]{:S(2)}) copy-start(f32[24,768]{1,0:T(8,128)} %out_ref.1) | copy-start | bytes 221188
  7.2 19.0 %copy-start.4 = (f32[24,2304]{1,0:T(8,128)S(1)}, f32[24,2304]{1,0:T(8,128)}, u32[]{:S(2)}) copy-start(f32[24,2304]{1,0:T(8,128)} %in_ref.1) | copy-start | bytes 663556
  18.4 104.7 %copy-start.11 = (s32[2,4,128]{2,1,0:T(4,128)S(1)}, s32[2,4,128]{2,1,0:T(4,128)}, u32[]{:S(2)}) copy-start(s32[2,4,128]{2,1,0:T(4,128)} %param.33) | copy-start | bytes 12292
  121.2 0.7 copy-start.8
  177.4 98.6 %copy-start.15 = (s32[16384]{0:T(1024)S(1)}, s32[16384]{0:T(1024)}, u32[]{:S(2)}) copy-start(s32[16384]{0:T(1024)} %constant.209.clone) | copy-start | bytes 196612
  177.4 100.5 %copy-start.20 = (f32[896]{0:T(1024)S(1)}, f32[896]{0:T(1024)}, u32[]{:S(2)}) copy-start(f32[896]{0:T(1024)} %iota_convert_fusion) | copy-start | bytes 10756
  426.4 1.8 copy-start.17
  426.4 3.8 copy-start.16
  426.4 3.8 copy-start.18
  426.4 3.8 copy-start.19
  426.4 7.0 %copy-start.1 = (f32[96,768]{1,0:T(8,128)S(1)}, f32[96,768]{1,0:T(8,128)}, u32[]{:S(2)}) copy-start(f32[96,768]{1,0:T(8,128)} %down_ref.1) | copy-start | bytes 884740
  426.4 7.0 %copy-start.12 = (f32[96,768]{1,0:T(8,128)S(1)}, f32[96,768]{1,0:T(8,128)}, u32[]{:S(2)}) copy-start(f32[96,768]{1,0:T(8,128)} %param.50) | copy-start | bytes 884740
  426.4 7.0 %copy-start.13 = (f32[96,768]{1,0:T(8,128)S(1)}, f32[96,768]{1,0:T(8,128)}, u32[]{:S(2)}) copy-start(f32[96,768]{1,0:T(8,128)} %param.49) | copy-start | bytes 884740
  426.4 9.0 %copy-start.5 = (f32[24,2304]{1,0:T(8,128)S(1)}, f32[24,2304]{1,0:T(8,128)}, u32[]{:S(2)}) copy-start(f32[24,2304]{1,0:T(8,128)} %in_ref.1) | copy-start | bytes 663556
  426.4 11.1 %copy-start.3 = (f32[24,3072]{1,0:T(8,128)S(1)}, f32[24,3072]{1,0:T(8,128)}, u32[]{:S(2)}) copy-start(f32[24,3072]{1,0:T(8,128)} %up_ref.1) | copy-start | bytes 884740
  426.4 11.1 %copy-start.14 = (f32[24,3072]{1,0:T(8,128)S(1)}, f32[24,3072]{1,0:T(8,128)}, u32[]{:S(2)}) copy-start(f32[24,3072]{1,0:T(8,128)} %param.47) | copy-start | bytes 884740

commit v5 on v4

--- a/solution.py
+++ b/solution.py
@@ -900,124 +900,437 @@
     )(projected, target, log_scale)
 
 
+class Tree:
+
+    @staticmethod
+    def scratch(grid, blocks):
+        count, tall = len(blocks), grid.tall
+        leads = ((tall, 2, 2), (tall, 2, 2), (tall, 2), (tall,), (tall,), (tall,))
+        dma = pltpu.SemaphoreType.DMA
+        level, pair = dma((count, tall)), dma((count, tall, 2))
+        buffers = [pltpu.VMEM(lead + block, jnp.bfloat16) for lead in leads for block in blocks]
+        return buffers + [level, level, level, pair, pair] + [level] * 5
+
+    @staticmethod
+    def size(count):
+        return 6 * count + 10
+
+    def __init__(self, grid, srcs, scratch):
+        count = len(srcs)
+        self.grid, self.count, self.srcs = grid, count, srcs
+        self.acc, self.from_side, self.from_v, self.from_u, self.from_low, self.from_high = [
+            scratch[k * count : (k + 1) * count] for k in range(6)
+        ]
+        (
+            self.load_sem,
+            self.side_send,
+            self.side_recv,
+            self.v_send,
+            self.v_recv,
+            self.u_send,
+            self.u_recv,
+            self.z_send,
+            self.low_recv,
+            self.high_recv,
+        ) = scratch[6 * count :]
+        z, x, y, core = self.place = grid.here()
+        tall = grid.tall
+        self.up, self.down = grid.device(z + 1, x, y, core), grid.device(z - 1, x, y, core)
+        self.has_up, self.has_down = z < tall - 1, z > 0
+        self.u = lax.rem(x + 1 - core, 2), lax.rem(y + core, 2)
+        self.v = lax.rem(x + core, 2), lax.rem(y + 1 - core, 2)
+        self.u_device = grid.device(z, *self.u, core)
+        self.v_device = grid.device(z, *self.v, core)
+        self.sibling = grid.device(z, x, y, 1 - core)
+        self.levels = [self.level_of(j) for j in range(tall)]
+
+    def greet_all(self):
+        greet(self.u_device)
+        greet(self.v_device)
+        greet(self.sibling)
+        greet(self.up, self.has_up)
+        greet(self.down, self.has_down)
+        return 3 + self.has_up.astype(jnp.int32) + self.has_down.astype(jnp.int32)
+
+    def each(self, action):
+        for m in range(self.count):
+            action(m)
+
+    def level_of(self, j):
+        tall = self.grid.tall
+        tables = [
+            sorted(range(tall), key=lambda level: (-abs(level - own), -level))[j] for own in range(tall)
+        ]
+        value = tables[0]
+        for own in range(1, tall):
+            value = jnp.where(self.place[0] == own, tables[own], value)
+        return value
+
+    def load(self, m, level):
+        core = self.place[3]
+        return pltpu.make_async_copy(
+            self.srcs[m].at[level, :, :, core], self.acc[m].at[level], self.load_sem.at[m, level]
+        )
+
+    def remote(self, src, dst, send_sem, recv_sem, device):
+        return pltpu.make_async_remote_copy(
+            src_ref=src,
+            dst_ref=dst,
+            send_sem=send_sem,
+            recv_sem=recv_sem,
+            device_id=device,
+            device_id_type=MESH,
+        )
+
+    def side(self, m, level):
+        return self.remote(
+            self.srcs[m].at[level, :, :, 1 - self.place[3]],
+            self.from_side[m].at[level],
+            self.side_send.at[m, level],
+            self.side_recv.at[m, level],
+            self.sibling,
+        )
+
+    def v_copy(self, m, level, along_u):
+        z, x, y, core = self.place
+        xx, yy = (1 - x, 1 - y) if along_u else self.v
+        return self.remote(
+            self.acc[m].at[level, xx, yy],
+            self.from_v[m].at[level, along_u],
+            self.v_send.at[m, level, along_u],
+            self.v_recv.at[m, level, along_u],
+            self.v_device,
+        )
+
+    def u_copy(self, m, level):
+        return self.remote(
+            self.acc[m].at[level, self.u[0], self.u[1]],
+            self.from_u[m].at[level],
+            self.u_send.at[m, level],
+            self.u_recv.at[m, level],
+            self.u_device,
+        )
+
+    def z_copy(self, m, level, upward):
+        z, x, y, core = self.place
+        return self.remote(
+            self.acc[m].at[level, x, y],
+            (self.from_low if upward else self.from_high)[m].at[level],
+            self.z_send.at[m, level],
+            (self.low_recv if upward else self.high_recv).at[m, level],
+            self.up if upward else self.down,
+        )
+
+    def add(self, m, level, xx, yy, other):
+        total = self.acc[m][level, xx, yy].astype(jnp.float32) + other.astype(jnp.float32)
+        self.acc[m][level, xx, yy] = total.astype(jnp.bfloat16)
+
+    def loads(self):
+        for level in self.levels:
+            self.each(lambda m: self.load(m, level).start())
+
+    def sides(self):
+        for level in self.levels:
+            self.each(lambda m: self.side(m, level).start())
+
+    def first(self, j):
+        level = self.levels[j]
+
+        def run(m):
+            self.load(m, level).wait()
+            self.side(m, level).wait_recv()
+            for xx in range(2):
+                for yy in range(2):
+                    self.add(m, level, xx, yy, self.from_side[m][level, xx, yy])
+            self.v_copy(m, level, 1).start()
+            self.v_copy(m, level, 0).start()
+
+        self.each(run)
+
+    def second(self, j):
+        z, x, y, core = self.place
+        level = self.levels[j]
+
+        def run(m):
+            self.v_copy(m, level, 1).wait_recv()
+            self.add(m, level, self.u[0], self.u[1], self.from_v[m][level, 1])
+            self.u_copy(m, level).start()
+
+        def run_own(m):
+            self.v_copy(m, level, 0).wait_recv()
+            self.add(m, level, x, y, self.from_v[m][level, 0])
+
+        self.each(run)
+        self.each(run_own)
+
+    def third(self, j):
+        z, x, y, core = self.place
+        level = self.levels[j]
+
+        def run(m):
+            self.u_copy(m, level).wait_recv()
+            self.add(m, level, x, y, self.from_u[m][level])
+
+            @pl.when((level >= z) & self.has_down)
+            def _():
+                self.z_copy(m, level, True).wait_recv()
+                self.add(m, level, x, y, self.from_low[m][level])
+
+            @pl.when((level <= z) & self.has_up)
+            def _():
+                self.z_copy(m, level, False).wait_recv()
+                self.add(m, level, x, y, self.from_high[m][level])
+
+            @pl.when(level > z)
+            def _():
+                self.z_copy(m, level, True).start()
+
+            @pl.when(level < z)
+            def _():
+                self.z_copy(m, level, False).start()
+
+        self.each(run)
+
+    def own(self, m):
+        z, x, y, core = self.place
+        return self.acc[m][z, x, y].astype(jnp.float32)
+
+    def drain(self):
+        for level in self.levels:
+            self.each(lambda m: self.side(m, level).wait_send())
+            self.each(lambda m: self.v_copy(m, level, 0).wait_send())
+            self.each(lambda m: self.v_copy(m, level, 1).wait_send())
+            self.each(lambda m: self.u_copy(m, level).wait_send())
+
+            @pl.when(level != self.place[0])
+            def _():
+                self.each(lambda m: self.z_copy(m, level, True).wait_send())
+
+
+def fold(values):
+    n, lanes = values.shape
+    part = jnp.sum(values.reshape(n // 8, 8, lanes), 0)
+    total = part[:, :128]
+    for at in range(128, lanes, 128):
+        total = total + part[:, at : at + 128]
+    return total
+
+
+def gain_back(gains_ref, grads_ref, k, grad_out, inputs):
+    factor = lax.rsqrt(jnp.mean(inputs * inputs, -1, keepdims=True) + EPS)
+    scaled = grad_out * gains_ref[k : k + 1, :]
+    grads_ref[k : k + 1, :] += jnp.sum(grad_out * inputs * factor, 0, keepdims=True)
+    return factor * (
+        scaled - inputs * (factor * factor * jnp.mean(scaled * inputs, -1, keepdims=True))
+    )
+
+
 BACK_SEQS = 2
 
 
-def backward_kernel(
-    x0_ref,
+def ffn_back_kernel(
+    final_ref,
+    after_ref,
     mask_col_ref,
-    mixed_ref,
-    attended,
-    total_ref,
-    after_ref,
-    pre_hbm,
-    final_ref,
     gains_ref,
-    bias_ref,
     pooled_ref,
     grad_proj_ref,
+    pre_hbm,
     packed_hbm,
     down_hbm,
-    rows_ref,
+    grad_after_ref,
     grad_gains_ref,
-    grad_bias_ref,
-    grad_packed_hbm,
+    grad_up_hbm,
     grad_down_hbm,
-    packed,
+    up,
+    head,
     down,
+    branch,
+    act_two,
+    wide,
     hidden,
     grad_pre,
-    act_one,
-    act_two,
-    branch_two,
-    branch_one,
-    grad_mixed,
+    grad_act,
+    pre,
     grad_pooled,
     stage,
-    pre_buffer,
     load_sem,
+    pre_sem,
     store_sem,
-    pre_sem,
 ):
+    tokens = final_ref.shape[0]
+    tile = BACK_SEQS * L
+
+    def load(k):
+        if k == 0:
+            return pltpu.make_async_copy(packed_hbm.at[:, pl.ds(PACKED - D, D)], head, load_sem.at[0])
+        if k == 1:
+            return pltpu.make_async_copy(down_hbm, down, load_sem.at[1])
+        return pltpu.make_async_copy(packed_hbm.at[:, pl.ds(WIDE + D, 4 * D)], up, load_sem.at[2])
+
+    def load_pre(j):
+        return pltpu.make_async_copy(pre_hbm.at[:, pl.ds(j * D, D)], pre.at[j % 2], pre_sem.at[j % 2])
+
+    load(0).start()
+    load_pre(0).start()
+    load(1).start()
+    load(2).start()
+    grad_gains_ref[...] = jnp.zeros_like(grad_gains_ref)
+    load(0).wait()
+    grad_pooled[...] = matmul_nt(grad_proj_ref[...], head[...])
+
+    @pl.loop(0, tokens // tile)
+    def _(step):
+        rows = pl.ds(pl.multiple_of(step * tile, tile), tile)
+        weight = mask_col_ref[rows, :]
+        pieces = []
+        for s in range(BACK_SEQS):
+            part = weight[s * L : (s + 1) * L]
+            count = jnp.sum(part, 0, keepdims=True)
+            pieces.append(part * (grad_pooled[pl.ds(step * BACK_SEQS + s, 1), :] / count))
+        grad = gain_back(gains_ref, grad_gains_ref, 2, jnp.concatenate(pieces, 0), final_ref[rows, :])
+        grad_after_ref[rows, :] = grad
+        branch[rows, :] = grad.astype(jnp.bfloat16)
+        act_two[rows, :] = normalize(after_ref[rows, :], gains_ref[1:2, :])[0].astype(jnp.bfloat16)
+
+    stores = []
+
+    def store(value, to):
+        slot = len(stores) % 2
+        if len(stores) >= 2:
+            stores[-2].wait()
+        stage[slot] = value.astype(jnp.bfloat16)
+        stores.append(pltpu.make_async_copy(stage.at[slot], to, store_sem.at[slot]))
+        stores[-1].start()
+
+    load(1).wait()
+    for j in range(4):
+        part = slice(j * D, (j + 1) * D)
+        if j < 3:
+            load_pre(j + 1).start()
+        wide[...] = matmul_nt(branch[...], down[part, :])
+        load_pre(j).wait()
+
+        @pl.loop(0, tokens // tile)
+        def _(step):
+            rows = pl.ds(pl.multiple_of(step * tile, tile), tile)
+            some = pre[j % 2, rows, :]
+            half, tan = gelu_parts(some)
+            hidden[rows, :] = (some * half).astype(jnp.bfloat16)
+            slope = np.float32(np.sqrt(2 / np.pi)) * (1.0 + (3 * 0.044715) * (some * some))
+            slope = half + 0.5 * some * (1.0 - tan * tan) * slope
+            grad_pre[rows, :] = (wide[rows, :] * slope).astype(jnp.bfloat16)
+
+        if j == 0:
+            load(2).wait()
+            grad_act[...] = matmul_nt(grad_pre[...], up[:, part])
+        else:
+            grad_act[...] += matmul_nt(grad_pre[...], up[:, part])
+        store(matmul_tn(hidden[...], branch[...]), grad_down_hbm.at[pl.ds(j * D, D), :])
+        store(matmul_tn(act_two[...], grad_pre[...]), grad_up_hbm.at[:, pl.ds(j * D, D)])
+    store(
+        matmul_tn(pooled_ref[...].astype(jnp.bfloat16), grad_proj_ref[...]),
+        grad_up_hbm.at[:, pl.ds(4 * D, D)],
+    )
+
+    @pl.loop(0, tokens // tile)
+    def _(step):
+        rows = pl.ds(pl.multiple_of(step * tile, tile), tile)
+        grad = gain_back(gains_ref, grad_gains_ref, 1, grad_act[rows, :], after_ref[rows, :])
+        grad_after_ref[rows, :] += grad
+
+    stores[-2].wait()
+    stores[-1].wait()
+
+
+def run_ffn_back(final, after, mask_col, gains, pooled, grad_proj, pre, packed, down):
+    tokens, seqs = final.shape[0], pooled.shape[0]
+    anywhere, inside = pl.BlockSpec(memory_space=pl.ANY), pl.BlockSpec(memory_space=pltpu.VMEM)
+
+    def low(*shape):
+        return pltpu.VMEM(shape, jnp.bfloat16)
+
+    def full(*shape):
+        return pltpu.VMEM(shape, jnp.float32)
+
+    return pl.pallas_call(
+        ffn_back_kernel,
+        out_shape=[
+            jax.ShapeDtypeStruct((tokens, D), jnp.float32),
+            jax.ShapeDtypeStruct((3, D), jnp.float32),
+            jax.ShapeDtypeStruct((D, 5 * D), jnp.bfloat16),
+            jax.ShapeDtypeStruct((4 * D, D), jnp.bfloat16),
+        ],
+        in_specs=[inside] * 6 + [anywhere] * 3,
+        out_specs=[inside] * 2 + [anywhere] * 2,
+        scratch_shapes=[
+            low(D, 4 * D),
+            low(D, D),
+            low(4 * D, D),
+            low(tokens, D),
+            low(tokens, D),
+            full(tokens, D),
+            low(tokens, D),
+            low(tokens, D),
+            full(tokens, D),
+            full(2, tokens, D),
+            full(seqs, D),
+            low(2, D, D),
+            pltpu.SemaphoreType.DMA((3,)),
+            pltpu.SemaphoreType.DMA((2,)),
+            pltpu.SemaphoreType.DMA((2,)),
+        ],
+        compiler_params=pltpu.CompilerParams(vmem_limit_bytes=62 * 1024 * 1024),
+    )(final, after, mask_col, gains, pooled, grad_proj, pre, packed, down)
+
+
+def attn_back_kernel(grid, *refs):
+    x0_ref, mask_col_ref, mixed_ref, attended, total_ref, grad_after_ref, gains_ref, bias_ref, packed_hbm = refs[:9]
+    srcs = refs[9:11]
+    rows_ref, grad_gains_ref, grad_bias_ref, grad_attn_hbm = refs[11:15]
+    outs, square_ref = refs[15:17], refs[17]
+    packed, act_one, branch_one, grad_mixed, stage, load_sem, store_sem = refs[18:25]
+    tree = Tree(grid, srcs, refs[25:])
     step = pl.program_id(0)
+    last_step = pl.num_programs(0) - 1
     tile_seqs = x0_ref.shape[0] // L
     tile = tile_seqs * L
     base = pl.multiple_of(step * tile, tile)
-    edges = (0, WIDE, WIDE + D, WIDE + 5 * D, PACKED)
 
     def load(k):
-        if k == 4:
-            return pltpu.make_async_copy(down_hbm, down, load_sem.at[k])
-        part = pl.ds(edges[k], edges[k + 1] - edges[k])
-        to = stage.at[0] if k == 3 else packed.at[:, part]
-        return pltpu.make_async_copy(packed_hbm.at[:, part], to, load_sem.at[k])
-
-    def loaded(k):
-        @pl.when(step == 0)
-        def _():
-            load(k).wait()
-
-    def load_pre(number):
-        start = pl.multiple_of(number // 4 * tile, tile)
-        across = pl.multiple_of(lax.rem(number, 4) * D, D)
-        slot = lax.rem(number, 2)
-        return pltpu.make_async_copy(
-            pre_hbm.at[pl.ds(start, tile), pl.ds(across, D)], pre_buffer.at[slot], pre_sem.at[slot]
-        )
+        part = pl.ds(WIDE, D) if k else pl.ds(0, WIDE)
+        return pltpu.make_async_copy(packed_hbm.at[:, part], packed.at[:, part], load_sem.at[k])
 
     @pl.when(step == 0)
     def _():
-        load_pre(0).start()
-        for k in (3, 4, 2, 1, 0):
-            load(k).start()
+        friends = tree.greet_all()
+        load(1).start()
+        load(0).start()
+        tree.loads()
         grad_gains_ref[...] = jnp.zeros_like(grad_gains_ref)
         grad_bias_ref[...] = jnp.zeros_like(grad_bias_ref)
-        load(3).wait()
-        grad_pooled[...] = matmul_nt(grad_proj_ref[...], stage[0])
-
-    def gain_back(k, grad_out, inputs):
-        gain = gains_ref[k : k + 1, :]
-        factor = lax.rsqrt(jnp.mean(inputs * inputs, -1, keepdims=True) + EPS)
-        scaled = grad_out * gain
-        grad_gains_ref[k : k + 1, :] += jnp.sum(grad_out * inputs * factor, 0, keepdims=True)
-        return factor * (
-            scaled - inputs * (factor * factor * jnp.mean(scaled * inputs, -1, keepdims=True))
-        )
+        meet(friends)
+        tree.sides()
+        load(1).wait()
 
     rows = pl.ds(base, tile)
+    grad_after = grad_after_ref[...]
     weight = mask_col_ref[...]
-    pieces = []
-    for s in range(tile_seqs):
-        part = weight[s * L : (s + 1) * L]
-        count = jnp.sum(part, 0, keepdims=True)
-        pieces.append(part * (grad_pooled[pl.ds(step * tile_seqs + s, 1), :] / count))
-    grad_final = gain_back(2, jnp.concatenate(pieces, 0), final_ref[...])
-    branch = grad_final.astype(jnp.bfloat16)
-    branch_two[rows, :] = branch
-    loaded(4)
-    loaded(2)
-    grad_act = jnp.zeros((tile, D), jnp.float32)
-    for j in range(4):
-        part = slice(j * D, (j + 1) * D)
-        grad_hidden = matmul_nt(branch, down[part, :])
-        number = step * 4 + j
-        pl.when(number + 1 < pl.num_programs(0) * 4)(lambda: load_pre(number + 1).start())
-        load_pre(number).wait()
-        pre = pre_buffer[j % 2]
-        half, tan = gelu_parts(pre)
-        hidden[rows, part] = (pre * half).astype(jnp.bfloat16)
-        slope = np.float32(np.sqrt(2 / np.pi)) * (1.0 + (3 * 0.044715) * (pre * pre))
-        grad_part = (grad_hidden * (half + 0.5 * pre * (1.0 - tan * tan) * slope)).astype(jnp.bfloat16)
-        grad_pre[rows, part] = grad_part
-        at = WIDE + D + j * D
-        grad_act = grad_act + matmul_nt(grad_part, packed[:, at : at + D])
-    after = after_ref[...]
-    act_two[rows, :] = normalize(after, gains_ref[1:2, :])[0].astype(jnp.bfloat16)
-    grad_after = grad_final + gain_back(1, grad_act, after)
     branch = grad_after.astype(jnp.bfloat16)
     branch_one[rows, :] = branch
-    loaded(1)
-    grad_attended = matmul_nt(branch, packed[:, WIDE : WIDE + D]).astype(jnp.bfloat16)
+    grad_attended = matmul_nt(branch, packed[:, WIDE:]).astype(jnp.bfloat16)
+    act_one[rows, :] = normalize(x0_ref[...], gains_ref[0:1, :])[0].astype(jnp.bfloat16)
+
+    def at_step(number, action, *levels):
+        @pl.when(step == number)
+        def _():
+            for j in levels:
+                action(j)
+
+    at_step(0, tree.first, 0, 1)
+    at_step(1, tree.second, 0)
+    at_step(2, tree.third, 0)
+    at_step(3, tree.third, 1)
     zero = jnp.zeros((), jnp.bfloat16)
     mine = lane_is((L, 128), 0, HD)
     for s in range(tile_seqs):
@@ -1051,51 +1364,62 @@
             grad_values = matmul(prob_low.reshape(2 * L, L), grad_out)
             grad_value = jnp.where(mine, grad_values[:L], grad_values[L:])
             grad_mixed[here, 2 * D + at : 2 * D + at + 128] = grad_value.astype(jnp.bfloat16)
-    loaded(0)
-    x0 = x0_ref[...]
-    act_one[rows, :] = normalize(x0, gains_ref[0:1, :])[0].astype(jnp.bfloat16)
+
+    @pl.when(step == 0)
+    def _():
+        tree.first(2)
+        tree.first(3)
+        load(0).wait()
+
+    at_step(1, tree.second, 1)
+    at_step(2, tree.second, 2)
+    at_step(3, tree.second, 3)
     grad_act = matmul_nt(grad_mixed[rows, :], packed[:, :WIDE])
-    rows_ref[...] = (grad_after + gain_back(0, grad_act, x0)).astype(jnp.bfloat16)
-
-    @pl.when(step == pl.num_programs(0) - 1)
+    grad_low = gain_back(gains_ref, grad_gains_ref, 0, grad_act, x0_ref[...])
+    rows_ref[...] = (grad_after + grad_low).astype(jnp.bfloat16)
+
+    @pl.when(step == last_step)
     def _():
-        jobs = []
-        for j in range(4):
-            part = slice(j * D, (j + 1) * D)
-            jobs.append((hidden, part, branch_two, slice(0, D), grad_down_hbm.at[pl.ds(j * D, D), :]))
-        for j in range(4):
-            part = slice(j * D, (j + 1) * D)
-            jobs.append((act_two, slice(0, D), grad_pre, part, grad_packed_hbm.at[:, pl.ds(WIDE + D + j * D, D)]))
-        jobs.append((attended, slice(0, D), branch_one, slice(0, D), grad_packed_hbm.at[:, pl.ds(WIDE, D)]))
+        tree.third(2)
+        jobs = [(attended, branch_one, slice(0, D), 3)]
         for j in range(3):
-            part = slice(j * D, (j + 1) * D)
-            jobs.append((act_one, slice(0, D), grad_mixed, part, grad_packed_hbm.at[:, pl.ds(j * D, D)]))
+            jobs.append((act_one, grad_mixed, slice(j * D, (j + 1) * D), j))
         copies = []
-        for number, (left, left_part, right, right_part, to) in enumerate(jobs):
+        for number, (left, right, part, at) in enumerate(jobs):
             slot = number % 2
             if number >= 2:
                 copies[number - 2].wait()
-            stage[slot] = matmul_tn(left[:, left_part], right[:, right_part]).astype(jnp.bfloat16)
+            stage[slot] = matmul_tn(left[...], right[:, part]).astype(jnp.bfloat16)
+            to = grad_attn_hbm.at[:, pl.ds(at * D, D)]
             copies.append(pltpu.make_async_copy(stage.at[slot], to, store_sem.at[slot]))
             copies[-1].start()
+        tree.third(3)
+        square_ref[...] = jnp.zeros_like(square_ref)
+
+        def give(m):
+            wide = tree.own(m)
+            outs[m][...] = wide
+            square_ref[0:8, :] += fold(wide * wide)
+
+        tree.each(give)
         copies[-2].wait()
-        stage[0] = matmul_tn(pooled_ref[...].astype(jnp.bfloat16), grad_proj_ref[...]).astype(jnp.bfloat16)
-        last = pltpu.make_async_copy(stage.at[0], grad_packed_hbm.at[:, pl.ds(PACKED - D, D)], store_sem.at[0])
-        last.start()
         copies[-1].wait()
-        last.wait()
-
-
-def run_backward(
-    x0, mask_col, mixed, attended, totals, after, pre, final, gains, bias_full, pooled, grad_proj, packed, down
+        tree.drain()
+
+
+def run_attn_back(
+    x0, mask_col, mixed, attended, totals, grad_after, gains, bias_full, packed, grad_up, grad_down, number
 ):
+    grid = Grid()
     tokens = x0.shape[0]
-    seqs = tokens // L
     tile = BACK_SEQS * L
     steps = tokens // tile
-
-    def rows(width, **mode):
-        return pl.BlockSpec((tile, width), lambda i: (i, 0), **mode)
+    srcs = [grad.reshape(grid.total, -1, grad.shape[1]) for grad in (grad_up, grad_down)]
+    blocks = [src.shape[1:] for src in srcs]
+    srcs = [src.reshape((grid.tall, 2, 2, 2) + src.shape[1:]) for src in srcs]
+
+    def rows(width):
+        return pl.BlockSpec((tile, width), lambda i: (i, 0))
 
     def whole(*shape):
         return pl.BlockSpec(shape, lambda i: (0,) * len(shape), pipeline_mode=pl.Buffered(1))
@@ -1105,15 +1429,16 @@
 
     anywhere = pl.BlockSpec(memory_space=pl.ANY)
     return pl.pallas_call(
-        backward_kernel,
+        functools.partial(attn_back_kernel, grid),
         grid=(steps,),
         out_shape=[
             jax.ShapeDtypeStruct((tokens, D), jnp.bfloat16),
-            jax.ShapeDtypeStruct((3, D), jnp.float32),
+            jax.ShapeDtypeStruct((1, D), jnp.float32),
             jax.ShapeDtypeStruct((HEADS, L, L), jnp.float32),
-            jax.ShapeDtypeStruct(packed.shape, jnp.bfloat16),
-            jax.ShapeDtypeStruct(down.shape, jnp.bfloat16),
-        ],
+            jax.ShapeDtypeStruct((D, WIDE + D), jnp.bfloat16),
+        ]
+        + [jax.ShapeDtypeStruct(block, jnp.float32) for block in blocks]
+        + [jax.ShapeDtypeStruct((16, 128), jnp.float32)],
         in_specs=[
             rows(D),
             rows(1),
@@ -1121,64 +1446,48 @@
             whole(tokens, D),
             pl.BlockSpec((BACK_SEQS, HEADS, L), lambda i: (i, 0, 0)),
             rows(D),
-            anywhere,
-            rows(D),
             whole(3, D),
             whole(HEADS, L, L),
-            whole(seqs, D),
-            whole(seqs, D),
+            anywhere,
             anywhere,
             anywhere,
         ],
-        out_specs=[rows(D), whole(3, D), whole(HEADS, L, L), anywhere, anywhere],
+        out_specs=[rows(D), whole(1, D), whole(HEADS, L, L), anywhere]
+        + [whole(*block) for block in blocks]
+        + [whole(16, 128)],
         scratch_shapes=[
-            low(D, PACKED - D),
-            low(4 * D, D),
-            low(tokens, 4 * D),
-            low(tokens, 4 * D),
-            low(tokens, D),
-            low(tokens, D),
+            low(D, WIDE + D),
             low(tokens, D),
             low(tokens, D),
             low(tokens, WIDE),
-            pltpu.VMEM((seqs, D), jnp.float32),
             low(2, D, D),
-            pltpu.VMEM((2, tile, D), jnp.float32),
-            pltpu.SemaphoreType.DMA((5,)),
             pltpu.SemaphoreType.DMA((2,)),
             pltpu.SemaphoreType.DMA((2,)),
-        ],
-        compiler_params=pltpu.CompilerParams(vmem_limit_bytes=62 * 1024 * 1024),
-    )(x0, mask_col, mixed, attended, totals, after, pre, final, gains, bias_full, pooled, grad_proj, packed, down)
+        ]
+        + Tree.scratch(grid, blocks),
+        compiler_params=pltpu.CompilerParams(
+            collective_id=number, has_side_effects=True, vmem_limit_bytes=62 * 1024 * 1024
+        ),
+    )(x0, mask_col, mixed, attended, totals, grad_after, gains, bias_full, packed, *srcs)
 
 
 def finish_kernel(grid, count, *refs):
-    srcs, (sums, ids, small) = refs[:count], refs[count : count + 3]
-    refs = refs[count + 3 :]
+    srcs, (sums, ids, small, square_ref) = refs[:count], refs[count : count + 4]
+    refs = refs[count + 4 :]
     outs, (table_out, small_out, square_out) = refs[:count], refs[count : count + 3]
     refs = refs[count + 3 :]
-    acc, from_side, from_v, from_u, from_low, from_high = [
-        refs[k * count : (k + 1) * count] for k in range(6)
-    ]
-    refs = refs[6 * count :]
+    tree = Tree(grid, srcs, refs[: Tree.size(count)])
+    refs = refs[Tree.size(count) :]
     rows, small_stage, small_in, square_stage, square_in = refs[:5]
-    refs = refs[1:]
-    load_sem, side_send, side_recv, v_send, v_recv, u_send, u_recv, z_send, low_recv, high_recv = refs[4:14]
-    row_own, line_send, on_send, row_recv, small_send, small_recv, square_send, square_recv = refs[14:]
+    row_own, line_send, on_send, row_recv, small_send, small_recv, square_send, square_recv = refs[5:]
     z, x, y, core = grid.here()
     tall = grid.tall
     d, f = lax.axis_index("dp"), lax.axis_index("fsdp")
     me = d * grid.fs + f
-    up, down = grid.device(z + 1, x, y, core), grid.device(z - 1, x, y, core)
-    has_up, has_down = z < tall - 1, z > 0
-    ux, uy = lax.rem(x + 1 - core, 2), lax.rem(y + core, 2)
-    vx, vy = lax.rem(x + core, 2), lax.rem(y + 1 - core, 2)
-    u_device, v_device = grid.device(z, ux, uy, core), grid.device(z, vx, vy, core)
-    sibling = grid.device(z, x, y, 1 - core)
+    sibling = tree.sibling
     f_side = y * 2 + 1 - core
     f_y = (1 - y) * 2 + core
     f_far = (1 - y) * 2 + 1 - core
-
     for level in range(tall):
         small_in[3 + level] = jnp.zeros(small.shape, jnp.float32)
         square_in[3 + level] = jnp.zeros((16, 128), jnp.float32)
@@ -1190,65 +1499,6 @@
 
     greet(y_device)
     greet(sibling)
-
-    def each(action):
-        for m in range(count):
-            action(m)
-
-    def level_of(j):
-        tables = []
-        for own in range(tall):
-            tables.append(sorted(range(tall), key=lambda level: (-abs(level - own), -level))[j])
-        value = tables[0]
-        for own in range(1, tall):
-            value = jnp.where(z == own, tables[own], value)
-        return value
-
-    def load(m, level):
-        return pltpu.make_async_copy(
-            srcs[m].at[level, :, :, core], acc[m].at[level], load_sem.at[m, level]
-        )
-
-    def side(m, level):
-        return pltpu.make_async_remote_copy(
-            src_ref=srcs[m].at[level, :, :, 1 - core],
-            dst_ref=from_side[m].at[level],
-            send_sem=side_send.at[m, level],
-            recv_sem=side_recv.at[m, level],
-            device_id=sibling,
-            device_id_type=MESH,
-        )
-
-    def v_copy(m, level, along_u):
-        xx, yy = (1 - x, 1 - y) if along_u else (vx, vy)
-        return pltpu.make_async_remote_copy(
-            src_ref=acc[m].at[level, xx, yy],
-            dst_ref=from_v[m].at[level, along_u],
-            send_sem=v_send.at[m, level, along_u],
-            recv_sem=v_recv.at[m, level, along_u],
-            device_id=v_device,
-            device_id_type=MESH,
-        )
-
-    def u_copy(m, level):
-        return pltpu.make_async_remote_copy(
-            src_ref=acc[m].at[level, ux, uy],
-            dst_ref=from_u[m].at[level],
-            send_sem=u_send.at[m, level],
-            recv_sem=u_recv.at[m, level],
-            device_id=u_device,
-            device_id_type=MESH,
-        )
-
-    def z_copy(m, level, upward):
-        return pltpu.make_async_remote_copy(
-            src_ref=acc[m].at[level, x, y],
-            dst_ref=(from_low if upward else from_high)[m].at[level],
-            send_sem=z_send.at[m, level],
-            recv_sem=(low_recv if upward else high_recv).at[m, level],
-            device_id=up if upward else down,
-            device_id_type=MESH,
-        )
 
     def line(peer, slot):
         return pltpu.make_async_remote_copy(
@@ -1326,11 +1576,9 @@
     small_stage[0] = small[...]
     small_sends, small_take, small_result = total_of(small_stage, small_in, small_send, small_recv)
     square_sends, square_take, square_result = total_of(square_stage, square_in, square_send, square_recv)
-    levels = [level_of(j) for j in range(tall)]
     own_rows = pltpu.make_async_copy(sums.at[d], rows.at[me], row_own)
     own_rows.start()
-    for level in levels:
-        each(lambda m: load(m, level).start())
+    tree.loads()
     meet(grid.dp + 1)
     small_sends(0)
 
@@ -1338,75 +1586,9 @@
     def _(step):
         line(lax.rem(d + step, grid.dp), me).start()
 
-    for level in levels:
-        each(lambda m: side(m, level).start())
+    tree.sides()
     onward(me, False, True).start()
     onward(me, True, True).start()
-
-    def first(j):
-        level = levels[j]
-
-        def run(m):
-            load(m, level).wait()
-            side(m, level).wait_recv()
-            for xx in range(2):
-                for yy in range(2):
-                    total = acc[m][level, xx, yy].astype(jnp.float32) + from_side[m][level, xx, yy].astype(jnp.float32)
-                    acc[m][level, xx, yy] = total.astype(jnp.bfloat16)
-            v_copy(m, level, 1).start()
-            v_copy(m, level, 0).start()
-
-        each(run)
-
-    def add(m, level, xx, yy, other):
-        total = acc[m][level, xx, yy].astype(jnp.float32) + other.astype(jnp.float32)
-        acc[m][level, xx, yy] = total.astype(jnp.bfloat16)
-
-    def second(j):
-        level = levels[j]
-
-        def run(m):
-            v_copy(m, level, 1).wait_recv()
-            add(m, level, ux, uy, from_v[m][level, 1])
-            u_copy(m, level).start()
-
-        each(run)
-
-    def second_own(j):
-        level = levels[j]
-
-        def run(m):
-            v_copy(m, level, 0).wait_recv()
-            add(m, level, x, y, from_v[m][level, 0])
-
-        each(run)
-
-    def third(j):
-        level = levels[j]
-
-        def run(m):
-            u_copy(m, level).wait_recv()
-            add(m, level, x, y, from_u[m][level])
-
-            @pl.when((level >= z) & has_down)
-            def _():
-                z_copy(m, level, True).wait_recv()
-                add(m, level, x, y, from_low[m][level])
-
-            @pl.when((level <= z) & has_up)
-            def _():
-                z_copy(m, level, False).wait_recv()
-                add(m, level, x, y, from_high[m][level])
-
-            @pl.when(level > z)
-            def _():
-                z_copy(m, level, True).start()
-
-            @pl.when(level < z)
-            def _():
-                z_copy(m, level, False).start()
-
-        each(run)
 
     def pass_lines():
         @pl.loop(1, grid.dp)
@@ -1433,15 +1615,7 @@
 
     table_rows = table_out.shape[0]
     whole_blocks = table_rows // ROW_BLOCK
-    square_stage[0] = jnp.zeros((16, 128), jnp.float32)
-
-    def fold(values):
-        n, lanes = values.shape
-        part = jnp.sum(values.reshape(n // 8, 8, lanes), 0)
-        total = part[:, :128]
-        for at in range(128, lanes, 128):
-            total = total + part[:, at : at + 128]
-        return total
+    square_stage[0] = square_ref[...]
 
     def spread(start, size):
         per = rows.shape[1]
@@ -1463,35 +1637,31 @@
             spread(pl.multiple_of(block * ROW_BLOCK, ROW_BLOCK), ROW_BLOCK)
 
     for j in range(tall):
-        first(j)
+        tree.first(j)
         if j < 3:
             small_take(j)
     pass_lines()
-    second(0)
-    second_own(0)
-    second(1)
-    second_own(1)
-    third(0)
+    tree.second(0)
+    tree.second(1)
+    tree.third(0)
     pass_y()
-    second(2)
-    second_own(2)
-    third(1)
-    second(3)
-    second_own(3)
+    tree.second(2)
+    tree.third(1)
+    tree.second(3)
     rows_in()
     spread_blocks(0, whole_blocks // 2)
-    third(2)
+    tree.third(2)
     spread_blocks(whole_blocks // 2, whole_blocks)
     if table_rows % ROW_BLOCK:
         spread(whole_blocks * ROW_BLOCK, table_rows % ROW_BLOCK)
-    third(3)
+    tree.third(3)
 
     def give(m):
-        wide = acc[m][z, x, y].astype(jnp.float32)
+        wide = tree.own(m)
         outs[m][...] = wide
         square_stage[0, 0:8, :] += fold(wide * wide)
 
-    each(give)
+    tree.each(give)
 
     square_sends(0)
     small_take(3)
@@ -1499,15 +1669,7 @@
     for r in range(3):
         square_take(r)
 
-    for level in levels:
-        each(lambda m: side(m, level).wait_send())
-        each(lambda m: v_copy(m, level, 0).wait_send())
-        each(lambda m: v_copy(m, level, 1).wait_send())
-        each(lambda m: u_copy(m, level).wait_send())
-
-        @pl.when(level != z)
-        def _():
-            each(lambda m: z_copy(m, level, True).wait_send())
+    tree.drain()
 
     @pl.loop(0, grid.dp)
     def _(step):
@@ -1523,27 +1685,26 @@
     square_out[...] = square_result()
 
 
-def finish(srcs, sums, ids, small, vocab_rows, number):
+def finish(srcs, sums, ids, small, squares, vocab_rows, number):
     grid = Grid()
     count = len(srcs)
     tall = grid.tall
     blocks = [src.shape[1:] for src in srcs]
     srcs = [src.reshape((tall, 2, 2, 2) + src.shape[1:]) for src in srcs]
-    leads = ((tall, 2, 2), (tall, 2, 2), (tall, 2), (tall,), (tall,), (tall,))
-    buffers = [pltpu.VMEM(lead + block, jnp.bfloat16) for lead in leads for block in blocks]
     cap = sums.shape[1]
-    buffers += [
+    dma = pltpu.SemaphoreType.DMA
+    by_device, by_step = dma((grid.total,)), dma((3 + tall,))
+    scratch = Tree.scratch(grid, blocks) + [
         pltpu.VMEM((grid.total, cap, D), jnp.bfloat16),
         pltpu.VMEM((4,) + small.shape, jnp.float32),
         pltpu.VMEM((3 + tall,) + small.shape, jnp.float32),
         pltpu.VMEM((4, 16, 128), jnp.float32),
         pltpu.VMEM((3 + tall, 16, 128), jnp.float32),
+        dma,
+        dma((grid.dp,)),
+        dma((2, grid.total)),
+        by_device,
     ]
-    dma = pltpu.SemaphoreType.DMA
-    by_level = dma((count, tall))
-    semaphores = [by_level, by_level, by_level, dma((count, tall, 2)), dma((count, tall, 2))] + [by_level] * 5
-    by_device, by_step = dma((grid.total,)), dma((3 + tall,))
-    semaphores += [dma, dma((grid.dp,)), dma((2, grid.total)), by_device] + [by_step] * 4
     anywhere, inside = pl.BlockSpec(memory_space=pl.ANY), pl.BlockSpec(memory_space=pltpu.VMEM)
     results = pl.pallas_call(
         functools.partial(finish_kernel, grid, count),
@@ -1553,13 +1714,13 @@
             jax.ShapeDtypeStruct(small.shape, jnp.float32),
             jax.ShapeDtypeStruct((16, 128), jnp.float32),
         ],
-        in_specs=[anywhere] * (count + 1) + [inside] * 2,
+        in_specs=[anywhere] * (count + 1) + [inside] * 3,
         out_specs=[inside] * (count + 3),
-        scratch_shapes=buffers + semaphores,
+        scratch_shapes=scratch + [by_step] * 4,
         compiler_params=pltpu.CompilerParams(
             collective_id=number, has_side_effects=True, vmem_limit_bytes=62 * 1024 * 1024
         ),
-    )(*srcs, sums, ids.reshape(1, -1), small)
+    )(*srcs, sums, ids.reshape(1, -1), small, squares)
     return (results[:count], *results[count:])
 
 
@@ -1770,9 +1931,9 @@
     ids_all = lax.all_gather(ids_flat, "dp", axis=0, tiled=True)
     picked = ids_all - row_base
     inside = (picked >= 0) & (picked < vocab_rows)
-    chosen = jnp.take(table.astype(jnp.bfloat16), jnp.clip(picked, 0, vocab_rows - 1), axis=0)
+    chosen = jnp.take(table, jnp.clip(picked, 0, vocab_rows - 1), axis=0)
     return lax.psum_scatter(
-        jnp.where(inside[:, None], chosen.astype(jnp.float32), 0.0).astype(jnp.bfloat16),
+        jnp.where(inside[:, None], chosen, 0.0).astype(jnp.bfloat16),
         "dp",
         scatter_dimension=0,
         tiled=True,
@@ -1864,26 +2025,37 @@
     embedded = once(any_spilled, lambda _: dense_rows(ids_flat, table, row_base), embedded)
 
     mask_col = mask_rows.astype(jnp.float32).reshape(tokens, 1)
-    *kept, pooled, projected = run_forward(embedded, mask_col, gain_rows, bias_full, packed, down)
+    mixed, attended, totals, after, pre, final, pooled, projected = run_forward(
+        embedded, mask_col, gain_rows, bias_full, packed, down
+    )
     target = negatives // pairs_here * seq_count + pairs_here + negatives % pairs_here
     target = jnp.concatenate(
         [target.reshape(total, pairs_here), jnp.full((total, pairs_here), -1, jnp.int32)], 1
     ).reshape(-1, 1)
     grad_proj, loss_parts = run_loss(projected, target, log_scale.reshape(1, 1), 3)
     loss_sum, grad_log_scale = loss_parts[0, 0], loss_parts[1, 0]
-    grad_low, grad_gains, grad_bias, grad_packed, grad_down = run_backward(
-        embedded, mask_col, *kept, gain_rows, bias_full, pooled, grad_proj, packed, down
-    )
+    grad_after, grad_gains, grad_up, grad_down = run_ffn_back(
+        final, after, mask_col, gain_rows, pooled, grad_proj, pre, packed, down
+    )
+    grad_low, grad_gain, grad_bias, grad_attn, up_shard, down_shard, squares = run_attn_back(
+        embedded, mask_col, mixed, attended, totals, grad_after, gain_rows, bias_full, packed, grad_up, grad_down, 4
+    )
+    grad_gains = jnp.concatenate([grad_gain, grad_gains[1:]], 0)
     grad_bias_table = jnp.dot(grad_bias.reshape(HEADS, L * L), bucket_hot, precision=HIGH).T
-    partials = [grad.reshape(total, -1, grad.shape[1]) for grad in (grad_packed, grad_down)]
     small_local = jnp.concatenate([grad_gains.reshape(-1), grad_bias_table.reshape(-1)])
     width = -(-small_local.shape[0] // 1024) * 8
     small_local = jnp.pad(small_local, (0, width * 128 - small_local.shape[0]))
     slots = jnp.arange(dp_count * CAP, dtype=jnp.int32).astype(jnp.float32)
     slot_hot = (slot == slots[None, :]).astype(jnp.bfloat16)
     slot_sums = matmul_tn(slot_hot, grad_low).astype(jnp.bfloat16).reshape(dp_count, CAP, D)
-    weight_grads, table_grad, summed, squares = finish(
-        partials, slot_sums, asked.reshape(-1), small_local.reshape(width, 128), vocab_rows, 4
+    (attn_shard,), table_grad, summed, squares = finish(
+        [grad_attn.reshape(total, -1, WIDE + D)],
+        slot_sums,
+        asked.reshape(-1),
+        small_local.reshape(width, 128),
+        squares,
+        vocab_rows,
+        5,
     )
     table_squares = jnp.sum(squares[8:])
     table_grad, table_squares = once(
@@ -1896,16 +2068,13 @@
     small_grad = jnp.concatenate([summed.reshape(-1)[: small_size - 1], grad_log_scale[None]])
     norm_value = jnp.sqrt(total_squares + jnp.sum(small_grad * small_grad))
     factor = jnp.minimum(1.0, CLIP / (norm_value + 1e-06))
-    grad_in, grad_out, grad_up, grad_head = jnp.split(
-        weight_grads[0], (WIDE, WIDE + D, WIDE + 5 * D), 1
-    )
     updates = (
         (table, table_first, table_second, table_grad.astype(jnp.float32)),
-        (attn_in, attn_in_first, attn_in_second, grad_in),
-        (attn_out, attn_out_first, attn_out_second, grad_out),
-        (ffn_in, ffn_in_first, ffn_in_second, grad_up),
-        (ffn_out, ffn_out_first, ffn_out_second, weight_grads[1]),
-        (proj_head, proj_head_first, proj_head_second, grad_head),
+        (attn_in, attn_in_first, attn_in_second, attn_shard[:, :WIDE]),
+        (attn_out, attn_out_first, attn_out_second, attn_shard[:, WIDE:]),
+        (ffn_in, ffn_in_first, ffn_in_second, up_shard[:, : 4 * D]),
+        (ffn_out, ffn_out_first, ffn_out_second, down_shard),
+        (proj_head, proj_head_first, proj_head_second, up_shard[:, 4 * D :]),
         (small_params, small_first, small_second, small_grad),
     )
     results = [loss_sum, norm_value]

time: 477 us -> 457 us (0.958); the launches traced: 477 us -> 449 us
  Pallas kernels: 384 us -> 355 us
    pallas_call x1, Pallas kernels: 144 us -> 98.9 us  [finish(): pl.pallas_call(functools.partial(finish_kernel, grid, count), out_shape=[...]
    pallas_call x1 -> x2, Pallas kernels: 94.7 us -> 111 us  [the longest x1 66.6 us: run_attn_back(): pl.pallas_call(functools.partial(attn_back_kernel, grid), grid=(steps,),...]
where the time goes in v5:
time: 457 us; the launch traced here: 449 us
  Pallas kernels  355 us (78%)
  other arithmetic  56 us (12%)
  between operations  18.9 us (4%)
  local copies, waits for them, and re-layouts  12.2 us (3%)
  matrix products  5.97 us (1%)
    pallas_call x1, Pallas kernels, finish(): pl.pallas_call(functools.partial(finish_kernel, grid, count), out_shape=[...  98.9 us
    pallas_call x1, Pallas kernels, run_head(): pl.pallas_call(functools.partial(head_kernel, grid), out_shape=[jax.Shape...  94.8 us
    pallas_call x1, Pallas kernels, run_attn_back(): pl.pallas_call(functools.partial(attn_back_kernel, grid), grid=(steps,),...  66.6 us
    pallas_call x1, Pallas kernels, run_ffn_back(): pl.pallas_call(ffn_back_kernel, out_shape=[jax.ShapeDtypeStruct((tokens,...  44.4 us
    sub x6, other arithmetic, adam_update(): return (first_new, second_new, param - rate * (direction + decay * param))  38.7 us
    pallas_call x1, Pallas kernels, run_forward(): pl.pallas_call(forward_kernel, grid=(steps,), out_shape=[kept(WIDE, jnp.b...  30.8 us
    pallas_call x1, Pallas kernels, run_loss(): pl.pallas_call(functools.partial(loss_kernel, grid, each // 2), out_shape...  19.5 us

profile of v5, /device:TPU:0, one launch (start us, length us, event | category | flops | bytes accessed | tf_op | source)
XLA Modules:
  0.0 448.9 jit_solution(16103611607623825235)
XLA Ops:
  7.9 1.2 slice.74
  9.1 1.3 fusion.34
  13.1 1.3 reshape.220.gains_ref.refs_6_
  15.7 1.6 fusion.10
  17.4 1.1 copy.97
  18.5 7.8 %convert.7 = bf16[4016,768]{1,0:T(8,128)(2,1)} convert(f32[4016,768]{1,0:T(8,128)} %table_hbm.1) | non-fusion elementwise | flops 3084288 | bytes 18505728
  26.3 94.8 %shard_map.416 = (bf16[32,24,6912]{2,1,0:T(8,128)(2,1)}, bf16[32,96,768]{2,1,0:T(8,128)(2,1)}, f32[32,8,128]{2,1,0:T(8,128)S(1)}, f32[1024,1]{1,0:T(8,128)S(1)}, f32[1024,768]{1,0:T(8,128)}) custom-call(f32[1024,1]{1,0:T(8,128)S(1)} %copy.81.col_ref, f32[1,1024]{1,0:T(1,128)S(1)} %bitcast.67, f32[1,128]{1,0:T(1,128)S(1)} %scatter.4.negative_ref, ...), custom_call_target="tpu_custom_call" | custom-call | tf_op jit(solution)/shard_map/pallas_call | solution.py:603
  127.3 30.8 %shard_map.417 = (bf16[1024,2304]{1,0:T(8,128)(2,1)}, bf16[1024,768]{1,0:T(8,128)(2,1)}, f32[8,12,128]{2,1,0:T(8,128)}, f32[1024,768]{1,0:T(8,128)}, f32[1024,30...) custom-call(f32[1024,768]{1,0:T(8,128)} %get-tuple-element.149.x0_ref.refs_0_, ...), custom_call_target="tpu_custom_call" | custom-call | tf_op jit(solution)/shard_map/pallas_call | solution.py:759
  158.1 19.5 %shard_map.418 = (bf16[8,768]{1,0:T(8,128)(2,1)}, f32[8,128]{1,0:T(8,128)}) custom-call(f32[8,768]{1,0:T(8,128)} %get-tuple-element.152.projected_ref, s32[256,1]{1,0:T(8,128)} %reshape.253.target_ref, f32[1,1]{1,0:T(1,128)} %bitcast.12.scale_ref), custom_call_target="tpu_custom_call" | custom-call | tf_op jit(solution)/shard_map/pallas_call | solution.py:884
  177.6 44.4 %shard_map.419 = (f32[1024,768]{1,0:T(8,128)}, f32[3,768]{1,0:T(4,128)}, bf16[768,3840]{1,0:T(8,128)(2,1)}, bf16[3072,768]{1,0:T(8,128)(2,1)}) custom-call(f32[1024,768]{1,0:T(8,128)} %get-tuple-element.157.final_ref, f32[1024,768]{1,0:T(8,128)} %get-tuple-element.158.after_ref, f32[1024,1]{1,0:T(8,128)} %copy.84.mask_col_ref.refs_1_, ...), custom_call_target="tpu_custom_call" | custom-call | tf_op jit(solution)/shard_map/pallas_call | solution.py:1256
  222.0 1.3 fusion.42
  223.3 66.6 %shard_map.420 = (bf16[1024,768]{1,0:T(8,128)(2,1)S(1)}, f32[1,768]{1,0:T(1,128)}, f32[12,128,128]{2,1,0:T(8,128)}, bf16[768,3072]{1,0:T(8,128)(2,1)}, f32[24,38...) custom-call(f32[1024,768]{1,0:T(8,128)} %get-tuple-element.149.x0_ref.refs_0_, ...), custom_call_target="tpu_custom_call" | custom-call | tf_op jit(solution)/shard_map/pallas_call | solution.py:1431
  290.6 1.2 pad.20
  292.5 1.2 fusion.12
  294.4 3.2 fusion.15
  297.6 98.9 %shard_map.421 = (f32[24,3072]{1,0:T(8,128)}, bf16[4016,768]{1,0:T(8,128)(2,1)}, f32[24,128]{1,0:T(8,128)}, f32[16,128]{1,0:T(8,128)}) custom-call(bf16[4,2,2,2,24,3072]{5,4,3,2,1,0:T(8,128)(2,1)} %bitcast.79, bf16[8,112,768]{2,1,0:T(8,128)(2,1)} %bitcast.82, f32[1,3584]{1,0:T(1,128)} %reshape_reshape_squeeze.3.refs_2_, f32[24,128]{1,0:T(8,128)} %fusion.27.refs_3_, ...), custom_call_target="tpu_custom_call" | custom-call | tf_op jit(solution)/shard_map/pallas_call | solution.py:1709
  396.5 1.3 slice_reduce_fusion.2
  399.7 1.3 multiply_reduce_fusion.1
  401.7 1.3 add_subtract_fusion
  403.0 1.9 multiply_subtract_fusion.4
  404.9 2.0 multiply_subtract_fusion.3
  406.9 2.0 multiply_subtract_fusion.2
  408.9 2.2 multiply_subtract_fusion.1
  411.1 29.4 %multiply_subtract_fusion = (f32[4016,768]{1,0:T(8,128)}, f32[4016,768]{1,0:T(8,128)}, f32[4016,768]{1,0:T(8,128)}) fusion(f32[4016,768]{1,0:T(8,128)} %table_hbm.1, f32[]{:T(128)S(6)} %min.11, bf16[4016,768]{1,0:T(8,128)(2,1)} %get-tuple-element.176, f32[4016,768]{1,0:T(8,128)} %param.38, f32[4016,768]{1,0:T(8,128)} %param.37), kind=kLoop, calls=%fused_computation.17 | loop fusion | flops 52432896 | bytes 80191488 | tf_op jit(solution)/shard_map/sub | solution.py:207
  (68 shorter events, 12.5 us)
Async XLA Ops:
  7.2 19.1 %copy-start.7 = (f32[24,768]{1,0:T(8,128)S(1)}, f32[24,768]{1,0:T(8,128)}, u32[]{:S(2)}) copy-start(f32[24,768]{1,0:T(8,128)} %proj_ref.1) | copy-start | bytes 221188
  7.2 19.1 %copy-start.2 = (f32[96,768]{1,0:T(8,128)S(1)}, f32[96,768]{1,0:T(8,128)}, u32[]{:S(2)}) copy-start(f32[96,768]{1,0:T(8,128)} %down_ref.1) | copy-start | bytes 884740
  7.2 19.1 %copy-start = (f32[24,3072]{1,0:T(8,128)S(1)}, f32[24,3072]{1,0:T(8,128)}, u32[]{:S(2)}) copy-start(f32[24,3072]{1,0:T(8,128)} %up_ref.1) | copy-start | bytes 884740
  7.2 19.0 %copy-start.6 = (f32[24,768]{1,0:T(8,128)S(1)}, f32[24,768]{1,0:T(8,128)}, u32[]{:S(2)}) copy-start(f32[24,768]{1,0:T(8,128)} %out_ref.1) | copy-start | bytes 221188
  7.2 19.0 %copy-start.4 = (f32[24,2304]{1,0:T(8,128)S(1)}, f32[24,2304]{1,0:T(8,128)}, u32[]{:S(2)}) copy-start(f32[24,2304]{1,0:T(8,128)} %in_ref.1) | copy-start | bytes 663556
  18.5 104.6 %copy-start.11 = (s32[2,4,128]{2,1,0:T(4,128)S(1)}, s32[2,4,128]{2,1,0:T(4,128)}, u32[]{:S(2)}) copy-start(s32[2,4,128]{2,1,0:T(4,128)} %param.33) | copy-start | bytes 12292
  121.1 0.7 copy-start.8
  223.3 66.6 %copy-start.21 = (f32[3,768]{1,0:T(4,128)S(1)}, f32[3,768]{1,0:T(4,128)}, u32[]{:S(2)}) copy-start(f32[3,768]{1,0:T(4,128)} %get-tuple-element.169) | copy-start | bytes 27652
  223.3 69.2 %copy-start.15 = (s32[16384]{0:T(1024)S(1)}, s32[16384]{0:T(1024)}, u32[]{:S(2)}) copy-start(s32[16384]{0:T(1024)} %constant.209.clone) | copy-start | bytes 196612
  223.3 71.1 %copy-start.20 = (f32[896]{0:T(1024)S(1)}, f32[896]{0:T(1024)}, u32[]{:S(2)}) copy-start(f32[896]{0:T(1024)} %iota_convert_fusion) | copy-start | bytes 10756
  397.8 1.9 copy-start.17
  397.8 3.9 copy-start.16
  397.8 3.9 copy-start.18
  397.8 3.9 copy-start.19
  397.8 5.2 %copy-start.12 = (f32[24,3840]{1,0:T(8,128)S(1)}, f32[24,3840]{1,0:T(8,128)}, u32[]{:S(2)}) copy-start(f32[24,3840]{1,0:T(8,128)} %get-tuple-element.178) | copy-start | bytes 1105924
  397.8 7.1 %copy-start.5 = (f32[24,2304]{1,0:T(8,128)S(1)}, f32[24,2304]{1,0:T(8,128)}, u32[]{:S(2)}) copy-start(f32[24,2304]{1,0:T(8,128)} %in_ref.1) | copy-start | bytes 663556
  397.8 7.0 %copy-start.14 = (f32[24,2304]{1,0:T(8,128)S(1)}, f32[24,2304]{1,0:T(8,128)}, u32[]{:S(2)}) copy-start(f32[24,2304]{1,0:T(8,128)} %param.41) | copy-start | bytes 663556
  397.8 9.0 %copy-start.1 = (f32[24,3072]{1,0:T(8,128)S(1)}, f32[24,3072]{1,0:T(8,128)}, u32[]{:S(2)}) copy-start(f32[24,3072]{1,0:T(8,128)} %up_ref.1) | copy-start | bytes 884740
  397.8 9.0 %copy-start.13 = (f32[24,3072]{1,0:T(8,128)S(1)}, f32[24,3072]{1,0:T(8,128)}, u32[]{:S(2)}) copy-start(f32[24,3072]{1,0:T(8,128)} %param.47) | copy-start | bytes 884740
  397.9 11.0 %copy-start.3 = (f32[96,768]{1,0:T(8,128)S(1)}, f32[96,768]{1,0:T(8,128)}, u32[]{:S(2)}) copy-start(f32[96,768]{1,0:T(8,128)} %down_ref.1) | copy-start | bytes 884740

commit v6 on v5

--- a/solution.py
+++ b/solution.py
@@ -788,45 +788,69 @@
 
 
 def loss_kernel(
-    grid, pairs_here, projected_ref, target_ref, scale_ref, grad_ref, loss_ref, mine, others, grads, send_sem, recv_sem
+    grid, pairs_here, projected_ref, target_ref, scale_ref, grad_ref, loss_ref, others, grads, send_sem, recv_sem
 ):
-    me = lax.axis_index("dp") * grid.fs + lax.axis_index("fsdp")
+    z, x, y, core = grid.here()
+    tall = grid.tall
     each = 2 * pairs_here
     half = D // 2
-
-    @pl.loop(1, grid.total)
-    def _(step):
-        greet(grid.peer(lax.rem(me + step, grid.total)))
-
+    x_device, y_device = grid.device(z, 1 - x, y, core), grid.device(z, x, 1 - y, core)
+    sibling = grid.device(z, x, y, 1 - core)
+
+    def other_levels(action):
+        @pl.loop(1, tall)
+        def _(step):
+            action(lax.rem(z + step, tall))
+
+    greet(x_device)
+    greet(y_device)
+    greet(sibling)
+    other_levels(lambda level: greet(grid.device(level, x, y, core)))
     projected = projected_ref[...]
     factor = lax.rsqrt(jnp.sum(projected * projected, -1, keepdims=True) + EPS)
     unit = projected * factor
-    mine[...] = jnp.concatenate([unit[:, :half], unit[:, half:]], 0).astype(jnp.bfloat16)
-    meet(grid.total - 1)
-
-    def copy(peer, slot):
+    others[core, z, x, y] = jnp.concatenate([unit[:, :half], unit[:, half:]], 0).astype(jnp.bfloat16)
+    meet(tall + 2)
+
+    def remote(blocks, device, sent, received):
         return pltpu.make_async_remote_copy(
-            src_ref=mine,
-            dst_ref=others.at[slot],
-            send_sem=send_sem.at[peer],
-            recv_sem=recv_sem.at[slot],
-            device_id=grid.peer(peer),
+            src_ref=blocks,
+            dst_ref=blocks,
+            send_sem=send_sem.at[sent],
+            recv_sem=recv_sem.at[received],
+            device_id=device,
             device_id_type=MESH,
         )
 
-    @pl.loop(1, grid.total)
-    def _(step):
-        copy(lax.rem(me + step, grid.total), me).start()
-
-    others[me] = mine[...]
-
-    @pl.loop(1, grid.total)
-    def _(step):
-        peer = lax.rem(me + step, grid.total)
-        copy(peer, peer).wait_recv()
+    along_x = remote(others.at[core, z, x, y], x_device, 0, 0)
+    along_x.start()
+    along_x.wait_recv()
+    along_y = [remote(others.at[core, z, xx, y], y_device, 1 + xx, 1 + xx) for xx in range(2)]
+    for copy in along_y:
+        copy.start()
+    for copy in along_y:
+        copy.wait_recv()
+
+    def along_z(level, origin):
+        return remote(others.at[core, origin], grid.device(level, x, y, core), 3 + level, 3 + origin)
+
+    def to_side(level):
+        return remote(others.at[core, level], sibling, 3 + tall + level, 3 + tall + level)
+
+    other_levels(lambda level: along_z(level, z).start())
+    to_side(z).start()
+
+    def pass_side(level):
+        along_z(level, level).wait_recv()
+        to_side(level).start()
+
+    other_levels(pass_side)
+    for level in range(tall):
+        to_side(level).wait_recv()
+    me = ((core * tall + z) * 2 + x) * 2 + y
 
     count = grid.total * each
-    wide = others[...].astype(jnp.float32)
+    wide = others[...].reshape(grid.total, 2 * each, half).astype(jnp.float32)
     units = jnp.concatenate(
         [wide[:, :each].reshape(count, half), wide[:, each:].reshape(count, half)], 1
     ).astype(jnp.bfloat16)
@@ -869,10 +893,12 @@
         factor * (grad_units - unit * jnp.sum(grad_units * unit, -1, keepdims=True))
     ).astype(jnp.bfloat16)
 
-    @pl.loop(1, grid.total)
-    def _(step):
-        peer = lax.rem(me + step, grid.total)
-        copy(peer, peer).wait_send()
+    along_x.wait_send()
+    for copy in along_y:
+        copy.wait_send()
+    other_levels(lambda level: along_z(level, level).wait_send())
+    for level in range(tall):
+        to_side(level).wait_send()
 
 
 def run_loss(projected, target, log_scale, number):
@@ -880,7 +906,7 @@
     each = projected.shape[0]
     count = grid.total * each
     inside = pl.BlockSpec(memory_space=pltpu.VMEM)
-    dma = pltpu.SemaphoreType.DMA((grid.total,))
+    dma = pltpu.SemaphoreType.DMA((3 + 2 * grid.tall,))
     return pl.pallas_call(
         functools.partial(loss_kernel, grid, each // 2),
         out_shape=[
@@ -890,8 +916,7 @@
         in_specs=[inside] * 3,
         out_specs=[inside] * 2,
         scratch_shapes=[
-            pltpu.VMEM((2 * each, D // 2), jnp.bfloat16),
-            pltpu.VMEM((grid.total, 2 * each, D // 2), jnp.bfloat16),
+            pltpu.VMEM((2, grid.tall, 2, 2, 2 * each, D // 2), jnp.bfloat16),
             pltpu.VMEM((count, count), jnp.float32),
             dma,
             dma,
@@ -1126,6 +1151,7 @@
 
 
 BACK_SEQS = 2
+HALF = 256
 
 
 def ffn_back_kernel(
@@ -1147,7 +1173,6 @@
     down,
     branch,
     act_two,
-    wide,
     hidden,
     grad_pre,
     grad_act,
@@ -1208,24 +1233,23 @@
         part = slice(j * D, (j + 1) * D)
         if j < 3:
             load_pre(j + 1).start()
-        wide[...] = matmul_nt(branch[...], down[part, :])
-        load_pre(j).wait()
-
-        @pl.loop(0, tokens // tile)
-        def _(step):
-            rows = pl.ds(pl.multiple_of(step * tile, tile), tile)
+        for at in range(0, tokens, HALF):
+            rows = slice(at, at + HALF)
+            wide = matmul_nt(branch[rows, :], down[part, :])
+            if at == 0:
+                load_pre(j).wait()
             some = pre[j % 2, rows, :]
             half, tan = gelu_parts(some)
             hidden[rows, :] = (some * half).astype(jnp.bfloat16)
             slope = np.float32(np.sqrt(2 / np.pi)) * (1.0 + (3 * 0.044715) * (some * some))
             slope = half + 0.5 * some * (1.0 - tan * tan) * slope
-            grad_pre[rows, :] = (wide[rows, :] * slope).astype(jnp.bfloat16)
-
-        if j == 0:
-            load(2).wait()
-            grad_act[...] = matmul_nt(grad_pre[...], up[:, part])
-        else:
-            grad_act[...] += matmul_nt(grad_pre[...], up[:, part])
+            grad_pre[rows, :] = (wide * slope).astype(jnp.bfloat16)
+            if j == 0:
+                if at == 0:
+                    load(2).wait()
+                grad_act[rows, :] = matmul_nt(grad_pre[rows, :], up[:, part])
+            else:
+                grad_act[rows, :] += matmul_nt(grad_pre[rows, :], up[:, part])
         store(matmul_tn(hidden[...], branch[...]), grad_down_hbm.at[pl.ds(j * D, D), :])
         store(matmul_tn(act_two[...], grad_pre[...]), grad_up_hbm.at[:, pl.ds(j * D, D)])
     store(
@@ -1269,7 +1293,6 @@
             low(4 * D, D),
             low(tokens, D),
             low(tokens, D),
-            full(tokens, D),
             low(tokens, D),
             low(tokens, D),
             full(tokens, D),
@@ -1478,12 +1501,12 @@
     refs = refs[count + 3 :]
     tree = Tree(grid, srcs, refs[: Tree.size(count)])
     refs = refs[Tree.size(count) :]
-    rows, small_stage, small_in, square_stage, square_in = refs[:5]
-    row_own, line_send, on_send, row_recv, small_send, small_recv, square_send, square_recv = refs[5:]
+    rows, part_sums, small_stage, small_in, square_stage, square_in = refs[:6]
+    row_own, line_send, on_send, row_recv, small_send, small_recv, square_send, square_recv = refs[6:]
     z, x, y, core = grid.here()
     tall = grid.tall
     d, f = lax.axis_index("dp"), lax.axis_index("fsdp")
-    me = d * grid.fs + f
+    me = f * grid.dp + d
     sibling = tree.sibling
     f_side = y * 2 + 1 - core
     f_y = (1 - y) * 2 + core
@@ -1593,7 +1616,7 @@
     def pass_lines():
         @pl.loop(1, grid.dp)
         def _(step):
-            slot = lax.rem(d + grid.dp - step, grid.dp) * grid.fs + f
+            slot = f * grid.dp + lax.rem(d + grid.dp - step, grid.dp)
             line(d, slot).wait_recv()
             onward(slot, False).start()
             onward(slot, True).start()
@@ -1601,40 +1624,49 @@
     def pass_y():
         @pl.loop(0, grid.dp)
         def _(step):
-            slot = lax.rem(d + grid.dp - step, grid.dp) * grid.fs + f_y
+            slot = f_y * grid.dp + lax.rem(d + grid.dp - step, grid.dp)
             line(d, slot).wait_recv()
             onward(slot, True).start()
 
-    def rows_in():
-        own_rows.wait()
-
+    def rows_in(column):
         @pl.loop(0, grid.dp)
         def _(step):
-            line(d, step * grid.fs + f_side).wait_recv()
-            line(d, step * grid.fs + f_far).wait_recv()
+            line(d, column * grid.dp + step).wait_recv()
 
     table_rows = table_out.shape[0]
     whole_blocks = table_rows // ROW_BLOCK
     square_stage[0] = square_ref[...]
 
+    per = grid.dp * rows.shape[1]
+
+    def product(column, start, size):
+        place = start + lax.broadcasted_iota(jnp.int32, (size, per), 0)
+        hot = jnp.where(place.astype(jnp.float32) == ids[pl.ds(column, 1), :], 1.0, 0.0)
+        some = rows[pl.ds(column * grid.dp, grid.dp)].reshape(per, D)
+        return matmul(hot.astype(jnp.bfloat16), some)
+
+    def spread_near():
+        @pl.loop(0, part_sums.shape[0] // ROW_BLOCK)
+        def _(block):
+            start = pl.multiple_of(block * ROW_BLOCK, ROW_BLOCK)
+            part_sums[pl.ds(start, ROW_BLOCK), :] = product(f, start, ROW_BLOCK) + product(
+                f_side, start, ROW_BLOCK
+            )
+
     def spread(start, size):
-        per = rows.shape[1]
-        group = 8
-        total = jnp.zeros((size, D), jnp.float32)
-        for g in range(0, grid.total, group):
-            place = (start + lax.broadcasted_iota(jnp.int32, (size, group * per), 0)).astype(jnp.float32)
-            wanted = ids[:, g * per : (g + group) * per]
-            hot = jnp.where(place == wanted, 1.0, 0.0).astype(jnp.bfloat16)
-            total = total + matmul(hot, rows[g : g + group].reshape(group * per, D))
+        total = part_sums[pl.ds(start, size), :] + product(f_y, start, size) + product(f_far, start, size)
         low = total.astype(jnp.bfloat16)
         table_out[pl.ds(start, size), :] = low
         wide = low.astype(jnp.float32)
         square_stage[0, 8:16, :] += fold(wide * wide)
 
-    def spread_blocks(first_block, last_block):
-        @pl.loop(first_block, last_block)
+    def spread_all():
+        @pl.loop(0, whole_blocks)
         def _(block):
             spread(pl.multiple_of(block * ROW_BLOCK, ROW_BLOCK), ROW_BLOCK)
+
+        if table_rows % ROW_BLOCK:
+            spread(whole_blocks * ROW_BLOCK, table_rows % ROW_BLOCK)
 
     for j in range(tall):
         tree.first(j)
@@ -1643,17 +1675,17 @@
     pass_lines()
     tree.second(0)
     tree.second(1)
+    own_rows.wait()
+    rows_in(f_side)
+    spread_near()
     tree.third(0)
+    tree.second(2)
     pass_y()
-    tree.second(2)
     tree.third(1)
     tree.second(3)
-    rows_in()
-    spread_blocks(0, whole_blocks // 2)
     tree.third(2)
-    spread_blocks(whole_blocks // 2, whole_blocks)
-    if table_rows % ROW_BLOCK:
-        spread(whole_blocks * ROW_BLOCK, table_rows % ROW_BLOCK)
+    rows_in(f_far)
+    spread_all()
     tree.third(3)
 
     def give(m):
@@ -1673,9 +1705,9 @@
 
     @pl.loop(0, grid.dp)
     def _(step):
-        onward(step * grid.fs + f, False).wait_send()
-        onward(step * grid.fs + f, True).wait_send()
-        onward(step * grid.fs + f_y, True).wait_send()
+        onward(f * grid.dp + step, False).wait_send()
+        onward(f * grid.dp + step, True).wait_send()
+        onward(f_y * grid.dp + step, True).wait_send()
 
     @pl.loop(1, grid.dp)
     def _(step):
@@ -1696,6 +1728,7 @@
     by_device, by_step = dma((grid.total,)), dma((3 + tall,))
     scratch = Tree.scratch(grid, blocks) + [
         pltpu.VMEM((grid.total, cap, D), jnp.bfloat16),
+        pltpu.VMEM((-(-vocab_rows // ROW_BLOCK) * ROW_BLOCK, D), jnp.float32),
         pltpu.VMEM((4,) + small.shape, jnp.float32),
         pltpu.VMEM((3 + tall,) + small.shape, jnp.float32),
         pltpu.VMEM((4, 16, 128), jnp.float32),
@@ -1720,8 +1753,77 @@
         compiler_params=pltpu.CompilerParams(
             collective_id=number, has_side_effects=True, vmem_limit_bytes=62 * 1024 * 1024
         ),
-    )(*srcs, sums, ids.reshape(1, -1), small, squares)
+    )(*srcs, sums, ids, small, squares)
     return (results[:count], *results[count:])
+
+
+def update_kernel(fs, *refs):
+    squares, summed, scale_grad, table, table_first, table_second, table_grad = refs[:7]
+    rest, shards = refs[7:22], refs[22:25]
+    norm_ref, out_first, out_second, out = refs[25:29]
+    rest_outs, factor_ref = refs[29:44], refs[44]
+
+    def row_sum(values):
+        return jnp.sum(jnp.sum(values, 1, keepdims=True), 0, keepdims=True)
+
+    @pl.when(pl.program_id(0) == 0)
+    def _():
+        total = row_sum(squares[0:8, :]) + row_sum(squares[8:16, :]) / float(fs)
+        total = total + (row_sum(summed[...] * summed[...]) + scale_grad[...] * scale_grad[...])
+        norm = jnp.sqrt(total)
+        norm_ref[...] = jnp.broadcast_to(norm, norm_ref.shape)
+        factor_ref[...] = jnp.minimum(1.0, CLIP / (norm + 1e-06))
+        attn, up, down = shards
+        grads = (attn[:, :WIDE], attn[:, WIDE:], up[:, : 4 * D], down[...], up[:, 4 * D :])
+        for k in range(5):
+            first_new, second_new, new = adam_update(
+                *[ref[...] for ref in rest[3 * k : 3 * k + 3]],
+                grads[k],
+                factor_ref[...],
+                RATES[k + 1],
+                DECAYS[k + 1],
+            )
+            rest_outs[3 * k][...] = first_new
+            rest_outs[3 * k + 1][...] = second_new
+            rest_outs[3 * k + 2][...] = new
+
+    first_new, second_new, new = adam_update(
+        table[...],
+        table_first[...],
+        table_second[...],
+        table_grad[...].astype(jnp.float32),
+        factor_ref[...],
+        RATES[0],
+        DECAYS[0],
+    )
+    out_first[...] = first_new
+    out_second[...] = second_new
+    out[...] = new
+
+
+def run_update(fs, squares, summed, scale_grad, table_arrays, table_grad, rest, shards):
+    vocab_rows = table_grad.shape[0]
+    blocks = pl.BlockSpec((ROW_BLOCK, D), lambda i: (i, 0))
+
+    def whole(array):
+        return pl.BlockSpec(
+            array.shape, lambda i: (0,) * array.ndim, pipeline_mode=pl.Buffered(1)
+        )
+
+    norm = jax.ShapeDtypeStruct((8, 128), jnp.float32)
+    return pl.pallas_call(
+        functools.partial(update_kernel, fs),
+        grid=(-(-vocab_rows // ROW_BLOCK),),
+        out_shape=[norm]
+        + [jax.ShapeDtypeStruct(table_grad.shape, jnp.float32)] * 3
+        + [jax.ShapeDtypeStruct(array.shape, jnp.float32) for array in rest],
+        in_specs=[whole(squares), whole(summed), whole(scale_grad)]
+        + [blocks] * 4
+        + [whole(array) for array in (*rest, *shards)],
+        out_specs=[whole(norm)] + [blocks] * 3 + [whole(array) for array in rest],
+        scratch_shapes=[pltpu.VMEM((1, 1), jnp.float32)],
+        compiler_params=pltpu.CompilerParams(vmem_limit_bytes=60 * 1024 * 1024),
+    )(squares, summed, scale_grad, *table_arrays, table_grad, *rest, *shards)
 
 
 def plain_body(
@@ -1931,7 +2033,9 @@
     ids_all = lax.all_gather(ids_flat, "dp", axis=0, tiled=True)
     picked = ids_all - row_base
     inside = (picked >= 0) & (picked < vocab_rows)
-    chosen = jnp.take(table, jnp.clip(picked, 0, vocab_rows - 1), axis=0)
+    chosen = lax.optimization_barrier(
+        jnp.take(table, jnp.clip(picked, 0, vocab_rows - 1), axis=0)
+    )
     return lax.psum_scatter(
         jnp.where(inside[:, None], chosen, 0.0).astype(jnp.bfloat16),
         "dp",
@@ -2028,10 +2132,16 @@
     mixed, attended, totals, after, pre, final, pooled, projected = run_forward(
         embedded, mask_col, gain_rows, bias_full, packed, down
     )
-    target = negatives // pairs_here * seq_count + pairs_here + negatives % pairs_here
+    tall, wide = dp_count // (fsdp_count // 2), fsdp_count // 2
+    owner = negatives // pairs_here
+    owner = (owner % 2 * tall + owner // (2 * wide * wide)) * wide * wide + owner // 2 % (wide * wide) % wide + (
+        owner // (2 * wide) % wide * wide
+    )
+    target = owner * seq_count + pairs_here + negatives % pairs_here
     target = jnp.concatenate(
         [target.reshape(total, pairs_here), jnp.full((total, pairs_here), -1, jnp.int32)], 1
-    ).reshape(-1, 1)
+    )
+    target = target.reshape(tall * wide * wide, 2, seq_count).transpose(1, 0, 2).reshape(-1, 1)
     grad_proj, loss_parts = run_loss(projected, target, log_scale.reshape(1, 1), 3)
     loss_sum, grad_log_scale = loss_parts[0, 0], loss_parts[1, 0]
     grad_after, grad_gains, grad_up, grad_down = run_ffn_back(
@@ -2051,41 +2161,47 @@
     (attn_shard,), table_grad, summed, squares = finish(
         [grad_attn.reshape(total, -1, WIDE + D)],
         slot_sums,
-        asked.reshape(-1),
+        asked.reshape(dp_count, fsdp_count, CAP).transpose(1, 0, 2).reshape(fsdp_count, -1),
         small_local.reshape(width, 128),
         squares,
         vocab_rows,
         5,
     )
-    table_squares = jnp.sum(squares[8:])
-    table_grad, table_squares = once(
+    table_grad, squares = once(
         any_spilled,
-        lambda _: with_squares(dense_table_grad(ids_flat, grad_low, vocab_rows, row_base)),
-        (table_grad, table_squares),
-    )
+        lambda state: with_squares(dense_table_grad(ids_flat, grad_low, vocab_rows, row_base), state[1]),
+        (table_grad, squares),
+    )
+    norm, *updated = run_update(
+        fsdp_count,
+        squares,
+        summed,
+        grad_log_scale.reshape(1, 1),
+        (table, table_first, table_second),
+        table_grad,
+        (
+            *(attn_in, attn_in_first, attn_in_second),
+            *(attn_out, attn_out_first, attn_out_second),
+            *(ffn_in, ffn_in_first, ffn_in_second),
+            *(ffn_out, ffn_out_first, ffn_out_second),
+            *(proj_head, proj_head_first, proj_head_second),
+        ),
+        (attn_shard, up_shard, down_shard),
+    )
+    norm_value = norm[0, 0]
+    factor = jnp.minimum(1.0, CLIP / (norm_value + 1e-06))
     small_size = small_params.shape[0]
-    total_squares = jnp.sum(squares[:8]) + table_squares / fsdp_count
     small_grad = jnp.concatenate([summed.reshape(-1)[: small_size - 1], grad_log_scale[None]])
-    norm_value = jnp.sqrt(total_squares + jnp.sum(small_grad * small_grad))
-    factor = jnp.minimum(1.0, CLIP / (norm_value + 1e-06))
-    updates = (
-        (table, table_first, table_second, table_grad.astype(jnp.float32)),
-        (attn_in, attn_in_first, attn_in_second, attn_shard[:, :WIDE]),
-        (attn_out, attn_out_first, attn_out_second, attn_shard[:, WIDE:]),
-        (ffn_in, ffn_in_first, ffn_in_second, up_shard[:, : 4 * D]),
-        (ffn_out, ffn_out_first, ffn_out_second, down_shard),
-        (proj_head, proj_head_first, proj_head_second, up_shard[:, 4 * D :]),
-        (small_params, small_first, small_second, small_grad),
-    )
-    results = [loss_sum, norm_value]
-    for kind_index, arrays in enumerate(updates):
-        results.extend(adam_update(*arrays, factor, RATES[kind_index], DECAYS[kind_index]))
-    return tuple(results)
-
-
-def with_squares(table_grad):
+    small_new = adam_update(
+        small_params, small_first, small_second, small_grad, factor, RATES[6], DECAYS[6]
+    )
+    return (loss_sum, norm_value, *updated, *small_new)
+
+
+def with_squares(table_grad, squares):
     wide = table_grad.astype(jnp.float32)
-    return (table_grad, lax.psum(jnp.sum(wide * wide), ("dp", "fsdp")))
+    total = lax.psum(jnp.sum(wide * wide), ("dp", "fsdp"))
+    return (table_grad, squares.at[8:].set(0.0).at[8, 0].set(total))
 
 
 def solution(mesh):

time: 457 us -> 437 us (0.956)
  other arithmetic: 56 us -> 16.1 us
  Pallas kernels: 355 us -> 377 us
    pallas_call x0 -> x1, Pallas kernels: none -> 38.5 us  [run_update(): pl.pallas_call(functools.partial(update_kernel, fs), grid=(-(-vocab_rows...]
    sub x6 -> x1, other arithmetic: 38.7 us -> 1.26 us  [adam_update(): return (first_new, second_new, param - rate * (direction + decay * param))]
    pallas_call x1, Pallas kernels: 98.9 us -> 88.6 us  [finish(): pl.pallas_call(functools.partial(finish_kernel, grid, count), out_shape=[...]
where the time goes in v6:
time: 437 us; the launch traced here: 429 us
  Pallas kernels  377 us (86%)
  other arithmetic  16.1 us (4%)
  between operations  15.9 us (4%)
  local copies, waits for them, and re-layouts  13.9 us (3%)
  matrix products  5.97 us (1%)
    pallas_call x1, Pallas kernels, run_head(): pl.pallas_call(functools.partial(head_kernel, grid), out_shape=[jax.Shape...  94.8 us
    pallas_call x1, Pallas kernels, finish(): pl.pallas_call(functools.partial(finish_kernel, grid, count), out_shape=[...  88.6 us
    pallas_call x1, Pallas kernels, run_attn_back(): pl.pallas_call(functools.partial(attn_back_kernel, grid), grid=(steps,),...  64.2 us
    pallas_call x1, Pallas kernels, run_ffn_back(): pl.pallas_call(ffn_back_kernel, out_shape=[jax.ShapeDtypeStruct((tokens,...  40 us
    pallas_call x1, Pallas kernels, run_update(): pl.pallas_call(functools.partial(update_kernel, fs), grid=(-(-vocab_rows...  38.5 us
    pallas_call x1, Pallas kernels, run_forward(): pl.pallas_call(forward_kernel, grid=(steps,), out_shape=[kept(WIDE, jnp.b...  30.8 us
    pallas_call x1, Pallas kernels, run_loss(): pl.pallas_call(functools.partial(loss_kernel, grid, each // 2), out_shape...  19.9 us

profile of v6, /device:TPU:0, one launch (start us, length us, event | category | flops | bytes accessed | tf_op | source)
XLA Modules:
  0.0 429.4 jit_solution(5014379489295579162)
XLA Ops:
  7.9 1.2 slice.95
  9.1 1.3 fusion.39
  13.1 1.3 reshape.282.gains_ref.refs_6_
  14.5 1.1 copy.91.mask_col_ref.refs_1_
  15.8 1.6 fusion.9
  17.4 1.1 copy.107
  18.5 7.8 %convert.7 = bf16[4016,768]{1,0:T(8,128)(2,1)} convert(f32[4016,768]{1,0:T(8,128)} %refs_3_.1) | non-fusion elementwise | flops 3084288 | bytes 18505728
  26.3 94.8 %shard_map.416 = (bf16[32,24,6912]{2,1,0:T(8,128)(2,1)}, bf16[32,96,768]{2,1,0:T(8,128)(2,1)}, f32[32,8,128]{2,1,0:T(8,128)S(1)}, f32[1024,1]{1,0:T(8,128)S(1)}, f32[1024,768]{1,0:T(8,128)}) custom-call(f32[1024,1]{1,0:T(8,128)S(1)} %copy.88.col_ref, f32[1,1024]{1,0:T(1,128)S(1)} %bitcast.78, f32[1,128]{1,0:T(1,128)S(1)} %scatter.10.negative_ref, ...), custom_call_target="tpu_custom_call" | custom-call | tf_op jit(solution)/shard_map/pallas_call | solution.py:603
  123.8 0.9 slice.97
  124.7 0.9 slice_convert_fusion
  126.6 0.8 reshape.317.target_ref
  127.3 30.8 %shard_map.417 = (bf16[1024,2304]{1,0:T(8,128)(2,1)}, bf16[1024,768]{1,0:T(8,128)(2,1)}, f32[8,12,128]{2,1,0:T(8,128)}, f32[1024,768]{1,0:T(8,128)}, f32[1024,30...) custom-call(f32[1024,768]{1,0:T(8,128)} %get-tuple-element.193.x0_ref.refs_0_, ...), custom_call_target="tpu_custom_call" | custom-call | tf_op jit(solution)/shard_map/pallas_call | solution.py:759
  158.1 19.9 %shard_map.418 = (bf16[8,768]{1,0:T(8,128)(2,1)}, f32[8,128]{1,0:T(8,128)}) custom-call(f32[8,768]{1,0:T(8,128)} %get-tuple-element.196.projected_ref, s32[256,1]{1,0:T(8,128)} %reshape.317.target_ref, f32[1,1]{1,0:T(1,128)} %bitcast.15.scale_ref), custom_call_target="tpu_custom_call" | custom-call | tf_op jit(solution)/shard_map/pallas_call | solution.py:910
  178.0 40.0 %shard_map.419 = (f32[1024,768]{1,0:T(8,128)}, f32[3,768]{1,0:T(4,128)}, bf16[768,3840]{1,0:T(8,128)(2,1)}, bf16[3072,768]{1,0:T(8,128)(2,1)}) custom-call(f32[1024,768]{1,0:T(8,128)} %get-tuple-element.201.final_ref, f32[1024,768]{1,0:T(8,128)} %get-tuple-element.202.after_ref, f32[1024,1]{1,0:T(8,128)} %copy.91.mask_col_ref.refs_1_, ...), custom_call_target="tpu_custom_call" | custom-call | tf_op jit(solution)/shard_map/pallas_call | solution.py:1280
  218.1 1.3 fusion.41
  219.4 64.2 %shard_map.420 = (bf16[1024,768]{1,0:T(8,128)(2,1)S(1)}, f32[1,768]{1,0:T(1,128)}, f32[12,128,128]{2,1,0:T(8,128)}, bf16[768,3072]{1,0:T(8,128)(2,1)}, f32[24,38...) custom-call(f32[1024,768]{1,0:T(8,128)} %get-tuple-element.193.x0_ref.refs_0_, ...), custom_call_target="tpu_custom_call" | custom-call | tf_op jit(solution)/shard_map/pallas_call | solution.py:1454
  283.6 0.7 pad_maximum_fusion
  284.3 1.2 pad.26
  286.2 1.2 fusion.11
  288.1 3.2 fusion.14
  291.3 88.6 %shard_map.421 = (f32[24,3072]{1,0:T(8,128)}, bf16[4016,768]{1,0:T(8,128)(2,1)}, f32[24,128]{1,0:T(8,128)}, f32[16,128]{1,0:T(8,128)S(1)}) custom-call(bf16[4,2,2,2,24,3072]{5,4,3,2,1,0:T(8,128)(2,1)} %bitcast.90, bf16[8,112,768]{2,1,0:T(8,128)(2,1)} %bitcast.93, f32[4,896]{1,0:T(4,128)} %reshape.289.refs_2_, f32[24,128]{1,0:T(8,128)} %fusion.21.refs_3_, ...), custom_call_target="tpu_custom_call" | custom-call | tf_op jit(solution)/shard_map/pallas_call | solution.py:1742
  380.6 38.5 %shard_map.422 = (f32[8,128]{1,0:T(8,128)}, f32[4016,768]{1,0:T(8,128)}, f32[4016,768]{1,0:T(8,128)}, f32[4016,768]{1,0:T(8,128)}, f32[24,2304]{1,0:T(8,128)}, /...) custom-call(f32[16,128]{1,0:T(8,128)S(1)} %get-tuple-element.218.ref, ...), custom_call_target="tpu_custom_call" | custom-call | tf_op jit(solution)/shard_map/pallas_call | solution.py:1814
  419.2 1.2 slice.100
  421.1 1.3 add_subtract_fusion
  (53 shorter events, 8.6 us)
Async XLA Ops:
  7.2 19.1 %copy-start.4 = (f32[24,768]{1,0:T(8,128)S(1)}, f32[24,768]{1,0:T(8,128)}, u32[]{:S(2)}) copy-start(f32[24,768]{1,0:T(8,128)} %refs_19_.1) | copy-start | bytes 221188
  7.2 19.1 %copy-start.1 = (f32[96,768]{1,0:T(8,128)S(1)}, f32[96,768]{1,0:T(8,128)}, u32[]{:S(2)}) copy-start(f32[96,768]{1,0:T(8,128)} %refs_16_.1) | copy-start | bytes 884740
  7.2 19.1 %copy-start = (f32[24,3072]{1,0:T(8,128)S(1)}, f32[24,3072]{1,0:T(8,128)}, u32[]{:S(2)}) copy-start(f32[24,3072]{1,0:T(8,128)} %refs_13_.1) | copy-start | bytes 884740
  7.2 19.1 %copy-start.3 = (f32[24,768]{1,0:T(8,128)S(1)}, f32[24,768]{1,0:T(8,128)}, u32[]{:S(2)}) copy-start(f32[24,768]{1,0:T(8,128)} %refs_10_.1) | copy-start | bytes 221188
  7.2 19.1 %copy-start.2 = (f32[24,2304]{1,0:T(8,128)S(1)}, f32[24,2304]{1,0:T(8,128)}, u32[]{:S(2)}) copy-start(f32[24,2304]{1,0:T(8,128)} %refs_7_.1) | copy-start | bytes 663556
  18.5 104.6 %copy-start.8 = (s32[2,4,128]{2,1,0:T(4,128)S(1)}, s32[2,4,128]{2,1,0:T(4,128)}, u32[]{:S(2)}) copy-start(s32[2,4,128]{2,1,0:T(4,128)} %param.37) | copy-start | bytes 12292
  121.2 0.7 copy-start.5
  219.3 64.3 %copy-start.15 = (f32[3,768]{1,0:T(4,128)S(1)}, f32[3,768]{1,0:T(4,128)}, u32[]{:S(2)}) copy-start(f32[3,768]{1,0:T(4,128)} %get-tuple-element.213) | copy-start | bytes 27652
  219.3 66.8 %copy-start.9 = (s32[16384]{0:T(1024)S(1)}, s32[16384]{0:T(1024)}, u32[]{:S(2)}) copy-start(s32[16384]{0:T(1024)} %constant.254.clone) | copy-start | bytes 196612
  219.3 68.8 %copy-start.14 = (f32[896]{0:T(1024)S(1)}, f32[896]{0:T(1024)}, u32[]{:S(2)}) copy-start(f32[896]{0:T(1024)} %iota_convert_fusion) | copy-start | bytes 10756
  379.9 0.7 copy-start.11
  380.6 40.5 %copy-start.10 = (f32[2689]{0:T(1024)S(1)}, f32[2689]{0:T(1024)}, u32[]{:S(2)}) copy-start(f32[2689]{0:T(1024)} %param.58) | copy-start | bytes 32272
  380.6 40.5 %copy-start.12 = (f32[2689]{0:T(1024)S(1)}, f32[2689]{0:T(1024)}, u32[]{:S(2)}) copy-start(f32[2689]{0:T(1024)} %param.60) | copy-start | bytes 32272
  380.6 40.5 %copy-start.13 = (f32[2689]{0:T(1024)S(1)}, f32[2689]{0:T(1024)}, u32[]{:S(2)}) copy-start(f32[2689]{0:T(1024)} %param.59) | copy-start | bytes 32272

commit v7 on v6

--- a/solution.py
+++ b/solution.py
@@ -288,10 +288,11 @@
     z, x, y, core = grid.here()
     tall = grid.tall
     d, f = lax.axis_index("dp"), lax.axis_index("fsdp")
-    ux, uy = lax.rem(x + 1 - core, 2), lax.rem(y + core, 2)
-    vx, vy = lax.rem(x + core, 2), lax.rem(y + 1 - core, 2)
+    u_places = ((lax.rem(x + 1 - core, 2), lax.rem(y + core, 2)), (1 - x, y))
+    v_places = ((lax.rem(x + core, 2), lax.rem(y + 1 - core, 2)), (x, 1 - y))
     up, down = grid.device(z + 1, x, y, core), grid.device(z - 1, x, y, core)
-    u_device, v_device = grid.device(z, ux, uy, core), grid.device(z, vx, vy, core)
+    u_devices = [grid.device(z, *place, core) for place in u_places]
+    v_devices = [grid.device(z, *place, core) for place in v_places]
     sibling = grid.device(z, x, y, 1 - core)
     has_up, has_down = z < tall - 1, z > 0
     me = grid.flat(z, x, y, core)
@@ -328,7 +329,7 @@
 
     def send(shard, device, way, own=False):
         for m in range(count):
-            copy(m, shard, device, way, own).start()
+            copy(m, shard, device[m] if isinstance(device, list) else device, way, own).start()
 
     def arrived(shard):
         for m in range(count):
@@ -336,7 +337,7 @@
 
     def sent(shard, device, way):
         for m in range(count):
-            copy(m, shard, device, way, False).wait_send()
+            copy(m, shard, device[m] if isinstance(device, list) else device, way, False).wait_send()
 
     @pl.when(has_up)
     def _():
@@ -346,8 +347,8 @@
     def _():
         send(me, down, 1, True)
 
-    send(me, u_device, 2, True)
-    send(me, v_device, 3, True)
+    send(me, u_devices, 2, True)
+    send(me, v_devices, 3, True)
     send(me, sibling, 4, True)
 
     tokens = col_ref.shape[0]
@@ -441,8 +442,8 @@
             def _():
                 send(shard, up, 0)
 
-            send(shard, u_device, 2)
-            send(shard, v_device, 3)
+            send(shard, u_devices, 2)
+            send(shard, v_devices, 3)
             send(shard, sibling, 4)
 
         @pl.when(high < tall)
@@ -454,8 +455,8 @@
             def _():
                 send(shard, down, 1)
 
-            send(shard, u_device, 2)
-            send(shard, v_device, 3)
+            send(shard, u_devices, 2)
+            send(shard, v_devices, 3)
             send(shard, sibling, 4)
 
     def both(k, action):
@@ -464,15 +465,17 @@
             pl.when(z + k < tall)(lambda: action(z + k))
 
     def pass_u(level):
-        shard = grid.flat(level, ux, uy, core)
-        arrived(shard)
-        send(shard, v_device, 3)
-        send(shard, sibling, 4)
+        for m in range(count):
+            shard = grid.flat(level, *u_places[m], core)
+            copy(m, shard, sibling, 4, False).wait_recv()
+            copy(m, shard, v_devices[m], 3, False).start()
+            copy(m, shard, sibling, 4, False).start()
 
     def pass_v(level):
-        shard = grid.flat(level, vx, vy, core)
-        arrived(shard)
-        send(shard, sibling, 4)
+        for m in range(count):
+            shard = grid.flat(level, *v_places[m], core)
+            copy(m, shard, sibling, 4, False).wait_recv()
+            copy(m, shard, sibling, 4, False).start()
 
     def pass_far(level):
         shard = grid.flat(level, 1 - x, 1 - y, core)
@@ -523,14 +526,19 @@
     def _(step):
         row_copy(lax.rem(d + step, grid.dp), d).start()
 
+    both(1, pass_u)
+    pass_z(2)
     both(0, pass_v)
-    for k in range(1, tall + 1):
-        if 1 < k < tall:
-            pass_z(k)
-        if k < tall:
-            both(k, pass_u)
-            both(k, pass_v)
-        both(k - 1, pass_far)
+    both(2, pass_u)
+    pass_z(3)
+    both(1, pass_v)
+    both(3, pass_u)
+    both(0, pass_far)
+    both(2, pass_v)
+    both(1, pass_far)
+    both(3, pass_v)
+    both(2, pass_far)
+    both(3, pass_far)
 
     @pl.loop(1, grid.dp)
     def _(step):
@@ -572,7 +580,7 @@
             for yy in range(2):
                 arrived(grid.flat(level, xx, yy, 1 - core))
                 sent(grid.flat(level, xx, yy, core), sibling, 4)
-        shard, other = grid.flat(level, x, y, core), grid.flat(level, ux, uy, core)
+        shard = grid.flat(level, x, y, core)
 
         @pl.when((level <= z) & has_up)
         def _():
@@ -582,9 +590,11 @@
         def _():
             sent(shard, down, 1)
 
-        sent(shard, u_device, 2)
-        sent(shard, v_device, 3)
-        sent(other, v_device, 3)
+        sent(shard, u_devices, 2)
+        sent(shard, v_devices, 3)
+        for m in range(count):
+            other = grid.flat(level, *u_places[m], core)
+            copy(m, other, v_devices[m], 3, False).wait_send()
 
     for item in local:
         item.wait()
@@ -2033,9 +2043,7 @@
     ids_all = lax.all_gather(ids_flat, "dp", axis=0, tiled=True)
     picked = ids_all - row_base
     inside = (picked >= 0) & (picked < vocab_rows)
-    chosen = lax.optimization_barrier(
-        jnp.take(table, jnp.clip(picked, 0, vocab_rows - 1), axis=0)
-    )
+    chosen = jnp.take(table, jnp.clip(picked, 0, vocab_rows - 1), axis=0)
     return lax.psum_scatter(
         jnp.where(inside[:, None], chosen, 0.0).astype(jnp.bfloat16),
         "dp",
@@ -2126,7 +2134,13 @@
     asked = heard[:, 0, :CAP]
     negatives = heard[:, 1, :pairs_here].reshape(-1).astype(jnp.int32)
     any_spilled = jnp.max(heard[:, 2, 0]) > 0.5
-    embedded = once(any_spilled, lambda _: dense_rows(ids_flat, table, row_base), embedded)
+    embedded = once(
+        any_spilled,
+        lambda rows: dense_rows(
+            ids_flat, table + jnp.minimum(jnp.abs(rows[0, 0]), 0.0), row_base
+        ),
+        embedded,
+    )
 
     mask_col = mask_rows.astype(jnp.float32).reshape(tokens, 1)
     mixed, attended, totals, after, pre, final, pooled, projected = run_forward(

time: 437 us -> 427 us (0.977)
  other arithmetic: 16.1 us -> 8.28 us
  Pallas kernels: 377 us -> 370 us
  local copies, waits for them, and re-layouts: 13.9 us -> 18.5 us
    unnamed x1 -> x0, other arithmetic: 7.78 us -> none
    unnamed x31, local copies, waits for them, and re-layouts: 3.1 us -> 7.7 us
where the time goes in v7:
time: 427 us; the launch traced here: 419 us
  Pallas kernels  370 us (87%)
  local copies, waits for them, and re-layouts  18.5 us (4%)
  between operations  15.9 us (4%)
  other arithmetic  8.28 us (2%)
  matrix products  5.96 us (1%)
    pallas_call x1, Pallas kernels, run_head(): pl.pallas_call(functools.partial(head_kernel, grid), out_shape=[jax.Shape...  91.5 us
    pallas_call x1, Pallas kernels, finish(): pl.pallas_call(functools.partial(finish_kernel, grid, count), out_shape=[...  88.8 us
    pallas_call x1, Pallas kernels, run_attn_back(): pl.pallas_call(functools.partial(attn_back_kernel, grid), grid=(steps,),...  64.1 us
    pallas_call x1, Pallas kernels, run_ffn_back(): pl.pallas_call(ffn_back_kernel, out_shape=[jax.ShapeDtypeStruct((tokens,...  40 us
    pallas_call x1, Pallas kernels, run_update(): pl.pallas_call(functools.partial(update_kernel, fs), grid=(-(-vocab_rows...  38.5 us
    pallas_call x1, Pallas kernels, run_forward(): pl.pallas_call(forward_kernel, grid=(steps,), out_shape=[kept(WIDE, jnp.b...  30.8 us
    pallas_call x1, Pallas kernels, run_loss(): pl.pallas_call(functools.partial(loss_kernel, grid, each // 2), out_shape...  15.9 us

profile of v7, /device:TPU:0, one launch (start us, length us, event | category | flops | bytes accessed | tf_op | source)
XLA Modules:
  0.0 418.9 jit_solution(9353938574091802979)
XLA Ops:
  7.8 1.2 slice.98
  9.0 1.3 fusion.39
  13.0 1.3 reshape.285.gains_ref.refs_6_
  14.4 1.1 copy.91.mask_col_ref.refs_1_
  15.7 1.6 fusion.9
  17.3 1.1 copy.107
  18.5 1.0 copy-done
  19.4 1.0 copy-done.1
  20.4 0.9 copy-done.2
  23.1 91.5 %shard_map.416 = (bf16[32,24,6912]{2,1,0:T(8,128)(2,1)}, bf16[32,96,768]{2,1,0:T(8,128)(2,1)}, f32[32,8,128]{2,1,0:T(8,128)S(1)}, f32[1024,1]{1,0:T(8,128)S(1)}, f32[1024,768]{1,0:T(8,128)}) custom-call(f32[1024,1]{1,0:T(8,128)S(1)} %copy.88.col_ref, f32[1,1024]{1,0:T(1,128)S(1)} %bitcast.79, f32[1,128]{1,0:T(1,128)S(1)} %scatter.10.negative_ref, ...), custom_call_target="tpu_custom_call" | custom-call | tf_op jit(solution)/shard_map/pallas_call | solution.py:613
  117.3 0.9 slice.100
  118.2 0.9 slice_convert_fusion
  120.8 30.8 %shard_map.417 = (bf16[1024,2304]{1,0:T(8,128)(2,1)}, bf16[1024,768]{1,0:T(8,128)(2,1)}, f32[8,12,128]{2,1,0:T(8,128)}, f32[1024,768]{1,0:T(8,128)}, f32[1024,30...) custom-call(f32[1024,768]{1,0:T(8,128)} %get-tuple-element.194.x0_ref.refs_0_, ...), custom_call_target="tpu_custom_call" | custom-call | tf_op jit(solution)/shard_map/pallas_call | solution.py:769
  151.6 15.9 %shard_map.418 = (bf16[8,768]{1,0:T(8,128)(2,1)}, f32[8,128]{1,0:T(8,128)}) custom-call(f32[8,768]{1,0:T(8,128)} %get-tuple-element.197.projected_ref, s32[256,1]{1,0:T(8,128)} %reshape.320.target_ref, f32[1,1]{1,0:T(1,128)} %bitcast.16.scale_ref), custom_call_target="tpu_custom_call" | custom-call | tf_op jit(solution)/shard_map/pallas_call | solution.py:920
  167.5 40.0 %shard_map.419 = (f32[1024,768]{1,0:T(8,128)}, f32[3,768]{1,0:T(4,128)}, bf16[768,3840]{1,0:T(8,128)(2,1)}, bf16[3072,768]{1,0:T(8,128)(2,1)}) custom-call(f32[1024,768]{1,0:T(8,128)} %get-tuple-element.202.final_ref, f32[1024,768]{1,0:T(8,128)} %get-tuple-element.203.after_ref, f32[1024,1]{1,0:T(8,128)} %copy.91.mask_col_ref.refs_1_, ...), custom_call_target="tpu_custom_call" | custom-call | tf_op jit(solution)/shard_map/pallas_call | solution.py:1290
  207.5 1.3 fusion.41
  208.8 64.1 %shard_map.420 = (bf16[1024,768]{1,0:T(8,128)(2,1)S(1)}, f32[1,768]{1,0:T(1,128)}, f32[12,128,128]{2,1,0:T(8,128)}, bf16[768,3072]{1,0:T(8,128)(2,1)}, f32[24,38...) custom-call(f32[1024,768]{1,0:T(8,128)} %get-tuple-element.194.x0_ref.refs_0_, ...), custom_call_target="tpu_custom_call" | custom-call | tf_op jit(solution)/shard_map/pallas_call | solution.py:1464
  273.6 1.2 pad.26
  275.5 1.2 fusion.11
  277.4 3.2 fusion.14
  280.6 88.8 %shard_map.421 = (f32[24,3072]{1,0:T(8,128)}, bf16[4016,768]{1,0:T(8,128)(2,1)}, f32[24,128]{1,0:T(8,128)}, f32[16,128]{1,0:T(8,128)S(1)}) custom-call(bf16[4,2,2,2,24,3072]{5,4,3,2,1,0:T(8,128)(2,1)} %bitcast.91, bf16[8,112,768]{2,1,0:T(8,128)(2,1)} %bitcast.94, f32[4,896]{1,0:T(4,128)} %reshape.292.refs_2_, f32[24,128]{1,0:T(8,128)} %fusion.21.refs_3_, ...), custom_call_target="tpu_custom_call" | custom-call | tf_op jit(solution)/shard_map/pallas_call | solution.py:1752
  370.1 38.5 %shard_map.422 = (f32[8,128]{1,0:T(8,128)}, f32[4016,768]{1,0:T(8,128)}, f32[4016,768]{1,0:T(8,128)}, f32[4016,768]{1,0:T(8,128)}, f32[24,2304]{1,0:T(8,128)}, /...) custom-call(f32[16,128]{1,0:T(8,128)S(1)} %get-tuple-element.219.ref, ...), custom_call_target="tpu_custom_call" | custom-call | tf_op jit(solution)/shard_map/pallas_call | solution.py:1824
  408.7 1.2 slice.103
  410.6 1.3 add_subtract_fusion
  (52 shorter events, 11.8 us)
Async XLA Ops:
  7.2 109.4 %copy-start.8 = (s32[2,4,128]{2,1,0:T(4,128)S(1)}, s32[2,4,128]{2,1,0:T(4,128)}, u32[]{:S(2)}) copy-start(s32[2,4,128]{2,1,0:T(4,128)} %param.37) | copy-start | bytes 12292
  18.4 1.0 copy-start
  19.4 1.0 copy-start.1
  20.4 0.9 copy-start.2
  21.3 0.9 copy-start.3
  22.2 0.9 copy-start.4
  114.6 0.7 copy-start.5
  208.8 64.1 %copy-start.15 = (f32[3,768]{1,0:T(4,128)S(1)}, f32[3,768]{1,0:T(4,128)}, u32[]{:S(2)}) copy-start(f32[3,768]{1,0:T(4,128)} %get-tuple-element.214) | copy-start | bytes 27652
  208.8 66.7 %copy-start.9 = (s32[16384]{0:T(1024)S(1)}, s32[16384]{0:T(1024)}, u32[]{:S(2)}) copy-start(s32[16384]{0:T(1024)} %constant.256.clone) | copy-start | bytes 196612
  208.8 68.6 %copy-start.14 = (f32[896]{0:T(1024)S(1)}, f32[896]{0:T(1024)}, u32[]{:S(2)}) copy-start(f32[896]{0:T(1024)} %iota_convert_fusion) | copy-start | bytes 10756
  369.4 0.7 copy-start.11
  370.1 40.5 %copy-start.10 = (f32[2689]{0:T(1024)S(1)}, f32[2689]{0:T(1024)}, u32[]{:S(2)}) copy-start(f32[2689]{0:T(1024)} %param.58) | copy-start | bytes 32272
  370.1 40.5 %copy-start.12 = (f32[2689]{0:T(1024)S(1)}, f32[2689]{0:T(1024)}, u32[]{:S(2)}) copy-start(f32[2689]{0:T(1024)} %param.60) | copy-start | bytes 32272
  370.1 40.5 %copy-start.13 = (f32[2689]{0:T(1024)S(1)}, f32[2689]{0:T(1024)}, u32[]{:S(2)}) copy-start(f32[2689]{0:T(1024)} %param.59) | copy-start | bytes 32272

commit v8 on v7

--- a/solution.py
+++ b/solution.py
@@ -273,6 +273,11 @@
     answers,
     found,
     messages,
+    in_wide,
+    out_wide,
+    up_wide,
+    proj_wide,
+    down_wide,
     send_sem,
     recv_sem,
     own_sem,
@@ -282,6 +287,7 @@
     note_recv,
     note_on,
     table_sem,
+    wide_sem,
 ):
     srcs, outs = (packed_mine, down_mine), (packed_out, down_out)
     count = 2
@@ -306,12 +312,17 @@
     greet(sibling)
     vocab_rows = table_hbm.shape[0]
     fetch = pltpu.make_async_copy(table_hbm, table.at[pl.ds(0, vocab_rows), :], table_sem)
+    wide = (in_wide, out_wide, up_wide, proj_wide, down_wide)
+    for k, ref in enumerate((in_ref, out_ref, up_ref, proj_ref, down_ref)):
+        pltpu.make_async_copy(ref, wide[k], wide_sem.at[k]).start()
     fetch.start()
     at = 0
-    for ref in (in_ref, out_ref, up_ref, proj_ref):
-        packed_mine[:, at : at + ref.shape[1]] = ref[...].astype(jnp.bfloat16)
-        at += ref.shape[1]
-    down_mine[...] = down_ref[...].astype(jnp.bfloat16)
+    for k, ref in enumerate((in_ref, out_ref, up_ref, proj_ref, down_ref)):
+        pltpu.make_async_copy(ref, wide[k], wide_sem.at[k]).wait()
+        if k < 4:
+            packed_mine[:, at : at + ref.shape[1]] = wide[k][...].astype(jnp.bfloat16)
+            at += ref.shape[1]
+    down_mine[...] = down_wide[...].astype(jnp.bfloat16)
     local = [pltpu.make_async_copy(srcs[m], outs[m].at[me], own_sem.at[m]) for m in range(count)]
     for item in local:
         item.start()
@@ -618,7 +629,7 @@
             jax.ShapeDtypeStruct((tokens, 1), jnp.float32),
             jax.ShapeDtypeStruct((tokens, D), jnp.float32),
         ],
-        in_specs=[inside] * 8 + [anywhere],
+        in_specs=[inside] * 3 + [anywhere] * 6,
         out_specs=[anywhere] * 2 + [inside] * 3,
         scratch_shapes=[pltpu.VMEM(shape, jnp.bfloat16) for shape in shapes]
         + [
@@ -627,6 +638,12 @@
             pltpu.VMEM((grid.dp, CAP, D), jnp.bfloat16),
             pltpu.VMEM((grid.dp, CAP, D), jnp.bfloat16),
             pltpu.VMEM((grid.dp, 8, 128), jnp.float32),
+        ]
+        + [
+            pltpu.VMEM(array.shape, jnp.float32)
+            for array in (attn_in, attn_out, ffn_in, proj_head, ffn_out)
+        ]
+        + [
             dma((5, 2, grid.total)),
             dma((2, grid.total)),
             dma((2,)),
@@ -636,9 +653,10 @@
             everyone,
             dma((2, grid.total)),
             dma,
+            dma((5,)),
         ],
         compiler_params=pltpu.CompilerParams(
-            collective_id=number, has_side_effects=True, vmem_limit_bytes=48 * 1024 * 1024
+            collective_id=number, has_side_effects=True, vmem_limit_bytes=62 * 1024 * 1024
         ),
     )(wide.reshape(tokens, 1), wide.reshape(1, tokens), row, attn_in, attn_out, ffn_in, proj_head, ffn_out, table)
 
@@ -1505,14 +1523,14 @@
 
 
 def finish_kernel(grid, count, *refs):
-    srcs, (sums, ids, small, square_ref) = refs[:count], refs[count : count + 4]
-    refs = refs[count + 4 :]
+    srcs, (grad_rows, slot_ref, ids, small, square_ref) = refs[:count], refs[count : count + 5]
+    refs = refs[count + 5 :]
     outs, (table_out, small_out, square_out) = refs[:count], refs[count : count + 3]
     refs = refs[count + 3 :]
     tree = Tree(grid, srcs, refs[: Tree.size(count)])
     refs = refs[Tree.size(count) :]
-    rows, part_sums, small_stage, small_in, square_stage, square_in = refs[:6]
-    row_own, line_send, on_send, row_recv, small_send, small_recv, square_send, square_recv = refs[6:]
+    sums, rows, part_sums, small_stage, small_in, square_stage, square_in = refs[:7]
+    line_send, on_send, row_recv, small_send, small_recv, square_send, square_recv = refs[7:]
     z, x, y, core = grid.here()
     tall = grid.tall
     d, f = lax.axis_index("dp"), lax.axis_index("fsdp")
@@ -1609,17 +1627,26 @@
     small_stage[0] = small[...]
     small_sends, small_take, small_result = total_of(small_stage, small_in, small_send, small_recv)
     square_sends, square_take, square_result = total_of(square_stage, square_in, square_send, square_recv)
-    own_rows = pltpu.make_async_copy(sums.at[d], rows.at[me], row_own)
-    own_rows.start()
     tree.loads()
     meet(grid.dp + 1)
     small_sends(0)
+    tree.sides()
+    cap = sums.shape[1]
+    lanes = lax.broadcasted_iota(jnp.int32, (1, cap), 1).astype(jnp.float32)
+
+    def sum_of(peer):
+        hot = jnp.where(slot_ref[...] == lanes + (peer * cap).astype(jnp.float32), 1.0, 0.0)
+        return matmul_tn(hot.astype(jnp.bfloat16), grad_rows[...]).astype(jnp.bfloat16)
 
     @pl.loop(1, grid.dp)
     def _(step):
-        line(lax.rem(d + step, grid.dp), me).start()
-
-    tree.sides()
+        peer = lax.rem(d + step, grid.dp)
+        sums[peer] = sum_of(peer)
+        line(peer, me).start()
+
+    own_sum = sum_of(d)
+    sums[d] = own_sum
+    rows[me] = own_sum
     onward(me, False, True).start()
     onward(me, True, True).start()
 
@@ -1685,7 +1712,6 @@
     pass_lines()
     tree.second(0)
     tree.second(1)
-    own_rows.wait()
     rows_in(f_side)
     spread_near()
     tree.third(0)
@@ -1727,23 +1753,22 @@
     square_out[...] = square_result()
 
 
-def finish(srcs, sums, ids, small, squares, vocab_rows, number):
+def finish(srcs, grad_rows, slot, ids, small, squares, vocab_rows, number):
     grid = Grid()
     count = len(srcs)
     tall = grid.tall
     blocks = [src.shape[1:] for src in srcs]
     srcs = [src.reshape((tall, 2, 2, 2) + src.shape[1:]) for src in srcs]
-    cap = sums.shape[1]
     dma = pltpu.SemaphoreType.DMA
     by_device, by_step = dma((grid.total,)), dma((3 + tall,))
     scratch = Tree.scratch(grid, blocks) + [
-        pltpu.VMEM((grid.total, cap, D), jnp.bfloat16),
+        pltpu.VMEM((grid.dp, CAP, D), jnp.bfloat16),
+        pltpu.VMEM((grid.total, CAP, D), jnp.bfloat16),
         pltpu.VMEM((-(-vocab_rows // ROW_BLOCK) * ROW_BLOCK, D), jnp.float32),
         pltpu.VMEM((4,) + small.shape, jnp.float32),
         pltpu.VMEM((3 + tall,) + small.shape, jnp.float32),
         pltpu.VMEM((4, 16, 128), jnp.float32),
         pltpu.VMEM((3 + tall, 16, 128), jnp.float32),
-        dma,
         dma((grid.dp,)),
         dma((2, grid.total)),
         by_device,
@@ -1757,13 +1782,13 @@
             jax.ShapeDtypeStruct(small.shape, jnp.float32),
             jax.ShapeDtypeStruct((16, 128), jnp.float32),
         ],
-        in_specs=[anywhere] * (count + 1) + [inside] * 3,
+        in_specs=[anywhere] * count + [inside] * 5,
         out_specs=[inside] * (count + 3),
         scratch_shapes=scratch + [by_step] * 4,
         compiler_params=pltpu.CompilerParams(
             collective_id=number, has_side_effects=True, vmem_limit_bytes=62 * 1024 * 1024
         ),
-    )(*srcs, sums, ids, small, squares)
+    )(*srcs, grad_rows, slot, ids, small, squares)
     return (results[:count], *results[count:])
 
 
@@ -2169,12 +2194,10 @@
     small_local = jnp.concatenate([grad_gains.reshape(-1), grad_bias_table.reshape(-1)])
     width = -(-small_local.shape[0] // 1024) * 8
     small_local = jnp.pad(small_local, (0, width * 128 - small_local.shape[0]))
-    slots = jnp.arange(dp_count * CAP, dtype=jnp.int32).astype(jnp.float32)
-    slot_hot = (slot == slots[None, :]).astype(jnp.bfloat16)
-    slot_sums = matmul_tn(slot_hot, grad_low).astype(jnp.bfloat16).reshape(dp_count, CAP, D)
     (attn_shard,), table_grad, summed, squares = finish(
         [grad_attn.reshape(total, -1, WIDE + D)],
-        slot_sums,
+        grad_low,
+        slot,
         asked.reshape(dp_count, fsdp_count, CAP).transpose(1, 0, 2).reshape(fsdp_count, -1),
         small_local.reshape(width, 128),
         squares,

time: 427 us -> 423 us (level)
  the two profiles are of different devices: /device:TPU:0 before, /device:TPU:2 now
where the time goes in v8:
time: 423 us; the launch traced here: 415 us
  Pallas kernels  373 us (88%)
  between operations  15.8 us (4%)
  local copies, waits for them, and re-layouts  14.5 us (3%)
  other arithmetic  8.39 us (2%)
    pallas_call x1, Pallas kernels, finish(): pl.pallas_call(functools.partial(finish_kernel, grid, count), out_shape=[...  93 us
    pallas_call x1, Pallas kernels, run_head(): pl.pallas_call(functools.partial(head_kernel, grid), out_shape=[jax.Shape...  91.1 us
    pallas_call x1, Pallas kernels, run_attn_back(): pl.pallas_call(functools.partial(attn_back_kernel, grid), grid=(steps,),...  63.9 us
    pallas_call x1, Pallas kernels, run_ffn_back(): pl.pallas_call(ffn_back_kernel, out_shape=[jax.ShapeDtypeStruct((tokens,...  40.2 us
    pallas_call x1, Pallas kernels, run_update(): pl.pallas_call(functools.partial(update_kernel, fs), grid=(-(-vocab_rows...  38.5 us
    pallas_call x1, Pallas kernels, run_forward(): pl.pallas_call(forward_kernel, grid=(steps,), out_shape=[kept(WIDE, jnp.b...  30.8 us
    pallas_call x1, Pallas kernels, run_loss(): pl.pallas_call(functools.partial(loss_kernel, grid, each // 2), out_shape...  15.8 us

profile of v8, /device:TPU:2, one launch (start us, length us, event | category | flops | bytes accessed | tf_op | source)
XLA Modules:
  0.0 415.2 jit_solution(9351610421278611193)
XLA Ops:
  7.8 1.2 slice.98
  9.0 1.3 fusion.32
  12.9 1.3 reshape.278.gains_ref.refs_6_
  14.4 1.1 copy.91.mask_col_ref.refs_1_
  15.4 1.0 copy.88.col_ref
  16.4 1.6 fusion.7
  18.0 1.1 copy.107
  19.2 91.1 %shard_map.416 = (bf16[32,24,6912]{2,1,0:T(8,128)(2,1)}, bf16[32,96,768]{2,1,0:T(8,128)(2,1)}, f32[32,8,128]{2,1,0:T(8,128)}, f32[1024,1]{1,0:T(8,128)}, f32[1024,768]{1,0:T(8,128)}) custom-call(f32[1024,1]{1,0:T(8,128)} %copy.88.col_ref, f32[1,1024]{1,0:T(1,128)} %bitcast.96, f32[1,128]{1,0:T(1,128)} %scatter.10.negative_ref, f32[24,2304]{1,0:T(8,128)} %refs_7_.1, ...), custom_call_target="tpu_custom_call" | custom-call | tf_op jit(solution)/shard_map/pallas_call | solution.py:624
  110.2 1.5 slice_reduce_fusion
  112.7 0.9 slice.100
  113.6 0.9 slice_convert_fusion
  115.4 0.8 reshape.312.target_ref
  116.2 30.8 %shard_map.417 = (bf16[1024,2304]{1,0:T(8,128)(2,1)}, bf16[1024,768]{1,0:T(8,128)(2,1)}, f32[8,12,128]{2,1,0:T(8,128)}, f32[1024,768]{1,0:T(8,128)}, f32[1024,30...) custom-call(f32[1024,768]{1,0:T(8,128)} %get-tuple-element.194.x0_ref.refs_0_, ...), custom_call_target="tpu_custom_call" | custom-call | tf_op jit(solution)/shard_map/pallas_call | solution.py:787
  147.0 15.8 %shard_map.418 = (bf16[8,768]{1,0:T(8,128)(2,1)}, f32[8,128]{1,0:T(8,128)}) custom-call(f32[8,768]{1,0:T(8,128)} %get-tuple-element.197.projected_ref, s32[256,1]{1,0:T(8,128)} %reshape.312.target_ref, f32[1,1]{1,0:T(1,128)} %bitcast.16.scale_ref), custom_call_target="tpu_custom_call" | custom-call | tf_op jit(solution)/shard_map/pallas_call | solution.py:938
  162.8 40.2 %shard_map.419 = (f32[1024,768]{1,0:T(8,128)}, f32[3,768]{1,0:T(4,128)}, bf16[768,3840]{1,0:T(8,128)(2,1)}, bf16[3072,768]{1,0:T(8,128)(2,1)}) custom-call(f32[1024,768]{1,0:T(8,128)} %get-tuple-element.202.final_ref, f32[1024,768]{1,0:T(8,128)} %get-tuple-element.203.after_ref, f32[1024,1]{1,0:T(8,128)} %copy.91.mask_col_ref.refs_1_, ...), custom_call_target="tpu_custom_call" | custom-call | tf_op jit(solution)/shard_map/pallas_call | solution.py:1308
  203.0 1.3 fusion.34
  204.3 63.9 %shard_map.420 = (bf16[1024,768]{1,0:T(8,128)(2,1)S(1)}, f32[1,768]{1,0:T(1,128)}, f32[12,128,128]{2,1,0:T(8,128)}, bf16[768,3072]{1,0:T(8,128)(2,1)}, f32[24,38...) custom-call(f32[1024,768]{1,0:T(8,128)} %get-tuple-element.194.x0_ref.refs_0_, ...), custom_call_target="tpu_custom_call" | custom-call | tf_op jit(solution)/shard_map/pallas_call | solution.py:1482
  268.2 0.7 pad_maximum_fusion
  268.9 1.2 pad.26
  270.8 1.2 fusion.9
  272.7 93.0 %shard_map.421 = (f32[24,3072]{1,0:T(8,128)}, bf16[4016,768]{1,0:T(8,128)(2,1)}, f32[24,128]{1,0:T(8,128)}, f32[16,128]{1,0:T(8,128)S(1)}) custom-call(bf16[4,2,2,2,24,3072]{5,4,3,2,1,0:T(8,128)(2,1)} %bitcast.87, bf16[1024,768]{1,0:T(8,128)(2,1)S(1)} %get-tuple-element.385.refs_1_, f32[1024,1]{1,0:T(8,128)} %get-tuple-element.212.refs_2_, ...), custom_call_target="tpu_custom_call" | custom-call | tf_op jit(solution)/shard_map/pallas_call | solution.py:1777
  366.4 38.5 %shard_map.422 = (f32[8,128]{1,0:T(8,128)}, f32[4016,768]{1,0:T(8,128)}, f32[4016,768]{1,0:T(8,128)}, f32[4016,768]{1,0:T(8,128)}, f32[24,2304]{1,0:T(8,128)}, /...) custom-call(f32[16,128]{1,0:T(8,128)S(1)} %get-tuple-element.219.ref, ...), custom_call_target="tpu_custom_call" | custom-call | tf_op jit(solution)/shard_map/pallas_call | solution.py:1849
  405.0 1.2 slice.103
  406.9 1.2 add_subtract_fusion
  (37 shorter events, 6.5 us)
Async XLA Ops:
  7.2 105.2 %copy-start.2 = (s32[2,4,128]{2,1,0:T(4,128)S(1)}, s32[2,4,128]{2,1,0:T(4,128)}, u32[]{:S(2)}) copy-start(s32[2,4,128]{2,1,0:T(4,128)} %param.37) | copy-start | bytes 12292
  12.2 6.9 %copy-start.6 = (f32[2,4,128]{2,1,0:T(4,128)}, f32[2,4,128]{2,1,0:T(4,128)S(1)}, u32[]{:S(2)}) copy-start(f32[2,4,128]{2,1,0:T(4,128)S(1)} %convert_element_type.67) | copy-start | bytes 12292
  204.3 63.9 %copy-start.9 = (f32[3,768]{1,0:T(4,128)S(1)}, f32[3,768]{1,0:T(4,128)}, u32[]{:S(2)}) copy-start(f32[3,768]{1,0:T(4,128)} %get-tuple-element.214) | copy-start | bytes 27652
  204.3 66.5 %copy-start.3 = (s32[16384]{0:T(1024)S(1)}, s32[16384]{0:T(1024)}, u32[]{:S(2)}) copy-start(s32[16384]{0:T(1024)} %constant.256.clone) | copy-start | bytes 196612
  365.7 0.7 copy-start.5
  366.4 40.4 %copy-start.4 = (f32[2689]{0:T(1024)S(1)}, f32[2689]{0:T(1024)}, u32[]{:S(2)}) copy-start(f32[2689]{0:T(1024)} %param.58) | copy-start | bytes 32272
  366.4 40.5 %copy-start.7 = (f32[2689]{0:T(1024)S(1)}, f32[2689]{0:T(1024)}, u32[]{:S(2)}) copy-start(f32[2689]{0:T(1024)} %param.60) | copy-start | bytes 32272
  366.4 40.5 %copy-start.8 = (f32[2689]{0:T(1024)S(1)}, f32[2689]{0:T(1024)}, u32[]{:S(2)}) copy-start(f32[2689]{0:T(1024)} %param.59) | copy-start | bytes 32272

commit v9 on v8

--- a/solution.py
+++ b/solution.py
@@ -245,6 +245,7 @@
 
 
 ROW_BLOCK = 512
+UPDATE_BLOCK = 672
 WIDE = 3 * D
 PACKED = WIDE + D + 4 * D + D
 TILE_SEQS = 4
@@ -1628,25 +1629,23 @@
     small_sends, small_take, small_result = total_of(small_stage, small_in, small_send, small_recv)
     square_sends, square_take, square_result = total_of(square_stage, square_in, square_send, square_recv)
     tree.loads()
+    cap = sums.shape[1]
+    lanes = lax.broadcasted_iota(jnp.int32, (1, cap), 1).astype(jnp.float32)
+
+    @pl.loop(0, grid.dp)
+    def _(peer):
+        hot = jnp.where(slot_ref[...] == lanes + (peer * cap).astype(jnp.float32), 1.0, 0.0)
+        sums[peer] = matmul_tn(hot.astype(jnp.bfloat16), grad_rows[...]).astype(jnp.bfloat16)
+
+    rows[me] = sums[d]
     meet(grid.dp + 1)
     small_sends(0)
-    tree.sides()
-    cap = sums.shape[1]
-    lanes = lax.broadcasted_iota(jnp.int32, (1, cap), 1).astype(jnp.float32)
-
-    def sum_of(peer):
-        hot = jnp.where(slot_ref[...] == lanes + (peer * cap).astype(jnp.float32), 1.0, 0.0)
-        return matmul_tn(hot.astype(jnp.bfloat16), grad_rows[...]).astype(jnp.bfloat16)
 
     @pl.loop(1, grid.dp)
     def _(step):
-        peer = lax.rem(d + step, grid.dp)
-        sums[peer] = sum_of(peer)
-        line(peer, me).start()
-
-    own_sum = sum_of(d)
-    sums[d] = own_sum
-    rows[me] = own_sum
+        line(lax.rem(d + step, grid.dp), me).start()
+
+    tree.sides()
     onward(me, False, True).start()
     onward(me, True, True).start()
 
@@ -1838,7 +1837,7 @@
 
 def run_update(fs, squares, summed, scale_grad, table_arrays, table_grad, rest, shards):
     vocab_rows = table_grad.shape[0]
-    blocks = pl.BlockSpec((ROW_BLOCK, D), lambda i: (i, 0))
+    blocks = pl.BlockSpec((UPDATE_BLOCK, D), lambda i: (i, 0))
 
     def whole(array):
         return pl.BlockSpec(
@@ -1848,7 +1847,7 @@
     norm = jax.ShapeDtypeStruct((8, 128), jnp.float32)
     return pl.pallas_call(
         functools.partial(update_kernel, fs),
-        grid=(-(-vocab_rows // ROW_BLOCK),),
+        grid=(-(-vocab_rows // UPDATE_BLOCK),),
         out_shape=[norm]
         + [jax.ShapeDtypeStruct(table_grad.shape, jnp.float32)] * 3
         + [jax.ShapeDtypeStruct(array.shape, jnp.float32) for array in rest],

time: 423 us -> 423 us (level)
  the two profiles are of different devices: /device:TPU:2 before, /device:TPU:0 now
where the time goes in v9:
time: 423 us; the launch traced here: 414 us
  Pallas kernels  373 us (88%)
  between operations  15.8 us (4%)
  local copies, waits for them, and re-layouts  14.5 us (3%)
  other arithmetic  8.39 us (2%)
    pallas_call x1, Pallas kernels, run_head(): pl.pallas_call(functools.partial(head_kernel, grid), out_shape=[jax.Shape...  92.9 us
    pallas_call x1, Pallas kernels, finish(): pl.pallas_call(functools.partial(finish_kernel, grid, count), out_shape=[...  90.8 us
    pallas_call x1, Pallas kernels, run_attn_back(): pl.pallas_call(functools.partial(attn_back_kernel, grid), grid=(steps,),...  64.3 us
    pallas_call x1, Pallas kernels, run_ffn_back(): pl.pallas_call(ffn_back_kernel, out_shape=[jax.ShapeDtypeStruct((tokens,...  40.2 us
    pallas_call x1, Pallas kernels, run_update(): pl.pallas_call(functools.partial(update_kernel, fs), grid=(-(-vocab_rows...  37.9 us
    pallas_call x1, Pallas kernels, run_forward(): pl.pallas_call(forward_kernel, grid=(steps,), out_shape=[kept(WIDE, jnp.b...  30.8 us
    pallas_call x1, Pallas kernels, run_loss(): pl.pallas_call(functools.partial(loss_kernel, grid, each // 2), out_shape...  15.7 us

profile of v9, /device:TPU:0, one launch (start us, length us, event | category | flops | bytes accessed | tf_op | source)
XLA Modules:
  0.0 414.5 jit_solution(3061126835514826881)
XLA Ops:
  7.8 1.2 slice.98
  9.0 1.3 fusion.32
  12.9 1.3 reshape.278.gains_ref.refs_6_
  14.4 1.1 copy.91.mask_col_ref.refs_1_
  15.4 1.0 copy.88.col_ref
  16.4 1.6 fusion.7
  18.0 1.1 copy.107
  19.2 92.9 %shard_map.416 = (bf16[32,24,6912]{2,1,0:T(8,128)(2,1)}, bf16[32,96,768]{2,1,0:T(8,128)(2,1)}, f32[32,8,128]{2,1,0:T(8,128)}, f32[1024,1]{1,0:T(8,128)}, f32[1024,768]{1,0:T(8,128)}) custom-call(f32[1024,1]{1,0:T(8,128)} %copy.88.col_ref, f32[1,1024]{1,0:T(1,128)} %bitcast.96, f32[1,128]{1,0:T(1,128)} %scatter.10.negative_ref, f32[24,2304]{1,0:T(8,128)} %refs_7_.1, ...), custom_call_target="tpu_custom_call" | custom-call | tf_op jit(solution)/shard_map/pallas_call | solution.py:625
  112.0 1.5 slice_reduce_fusion
  114.5 0.9 slice.100
  115.4 0.9 slice_convert_fusion
  117.2 0.8 reshape.312.target_ref
  118.0 30.8 %shard_map.417 = (bf16[1024,2304]{1,0:T(8,128)(2,1)}, bf16[1024,768]{1,0:T(8,128)(2,1)}, f32[8,12,128]{2,1,0:T(8,128)}, f32[1024,768]{1,0:T(8,128)}, f32[1024,30...) custom-call(f32[1024,768]{1,0:T(8,128)} %get-tuple-element.194.x0_ref.refs_0_, ...), custom_call_target="tpu_custom_call" | custom-call | tf_op jit(solution)/shard_map/pallas_call | solution.py:788
  148.8 15.7 %shard_map.418 = (bf16[8,768]{1,0:T(8,128)(2,1)}, f32[8,128]{1,0:T(8,128)}) custom-call(f32[8,768]{1,0:T(8,128)} %get-tuple-element.197.projected_ref, s32[256,1]{1,0:T(8,128)} %reshape.312.target_ref, f32[1,1]{1,0:T(1,128)} %bitcast.16.scale_ref), custom_call_target="tpu_custom_call" | custom-call | tf_op jit(solution)/shard_map/pallas_call | solution.py:939
  164.5 40.2 %shard_map.419 = (f32[1024,768]{1,0:T(8,128)}, f32[3,768]{1,0:T(4,128)}, bf16[768,3840]{1,0:T(8,128)(2,1)}, bf16[3072,768]{1,0:T(8,128)(2,1)}) custom-call(f32[1024,768]{1,0:T(8,128)} %get-tuple-element.202.final_ref, f32[1024,768]{1,0:T(8,128)} %get-tuple-element.203.after_ref, f32[1024,1]{1,0:T(8,128)} %copy.91.mask_col_ref.refs_1_, ...), custom_call_target="tpu_custom_call" | custom-call | tf_op jit(solution)/shard_map/pallas_call | solution.py:1309
  204.7 1.3 fusion.34
  206.0 64.3 %shard_map.420 = (bf16[1024,768]{1,0:T(8,128)(2,1)S(1)}, f32[1,768]{1,0:T(1,128)}, f32[12,128,128]{2,1,0:T(8,128)}, bf16[768,3072]{1,0:T(8,128)(2,1)}, f32[24,38...) custom-call(f32[1024,768]{1,0:T(8,128)} %get-tuple-element.194.x0_ref.refs_0_, ...), custom_call_target="tpu_custom_call" | custom-call | tf_op jit(solution)/shard_map/pallas_call | solution.py:1483
  270.4 0.7 pad_maximum_fusion
  271.1 1.2 pad.26
  272.9 1.2 fusion.9
  274.9 90.8 %shard_map.421 = (f32[24,3072]{1,0:T(8,128)}, bf16[4016,768]{1,0:T(8,128)(2,1)}, f32[24,128]{1,0:T(8,128)}, f32[16,128]{1,0:T(8,128)S(1)}) custom-call(bf16[4,2,2,2,24,3072]{5,4,3,2,1,0:T(8,128)(2,1)} %bitcast.87, bf16[1024,768]{1,0:T(8,128)(2,1)S(1)} %get-tuple-element.385.refs_1_, f32[1024,1]{1,0:T(8,128)} %get-tuple-element.212.refs_2_, ...), custom_call_target="tpu_custom_call" | custom-call | tf_op jit(solution)/shard_map/pallas_call | solution.py:1776
  366.4 37.9 %shard_map.422 = (f32[8,128]{1,0:T(8,128)}, f32[4016,768]{1,0:T(8,128)}, f32[4016,768]{1,0:T(8,128)}, f32[4016,768]{1,0:T(8,128)}, f32[24,2304]{1,0:T(8,128)}, /...) custom-call(f32[16,128]{1,0:T(8,128)S(1)} %get-tuple-element.219.ref, ...), custom_call_target="tpu_custom_call" | custom-call | tf_op jit(solution)/shard_map/pallas_call | solution.py:1848
  404.2 1.2 slice.103
  406.2 1.2 add_subtract_fusion
  (37 shorter events, 6.5 us)
Async XLA Ops:
  7.2 107.0 %copy-start.2 = (s32[2,4,128]{2,1,0:T(4,128)S(1)}, s32[2,4,128]{2,1,0:T(4,128)}, u32[]{:S(2)}) copy-start(s32[2,4,128]{2,1,0:T(4,128)} %param.37) | copy-start | bytes 12292
  12.2 6.9 %copy-start.6 = (f32[2,4,128]{2,1,0:T(4,128)}, f32[2,4,128]{2,1,0:T(4,128)S(1)}, u32[]{:S(2)}) copy-start(f32[2,4,128]{2,1,0:T(4,128)S(1)} %convert_element_type.67) | copy-start | bytes 12292
  206.0 64.3 %copy-start.9 = (f32[3,768]{1,0:T(4,128)S(1)}, f32[3,768]{1,0:T(4,128)}, u32[]{:S(2)}) copy-start(f32[3,768]{1,0:T(4,128)} %get-tuple-element.214) | copy-start | bytes 27652
  206.0 66.9 %copy-start.3 = (s32[16384]{0:T(1024)S(1)}, s32[16384]{0:T(1024)}, u32[]{:S(2)}) copy-start(s32[16384]{0:T(1024)} %constant.256.clone) | copy-start | bytes 196612
  365.7 0.7 copy-start.5
  366.4 39.8 %copy-start.4 = (f32[2689]{0:T(1024)S(1)}, f32[2689]{0:T(1024)}, u32[]{:S(2)}) copy-start(f32[2689]{0:T(1024)} %param.58) | copy-start | bytes 32272
  366.4 39.8 %copy-start.7 = (f32[2689]{0:T(1024)S(1)}, f32[2689]{0:T(1024)}, u32[]{:S(2)}) copy-start(f32[2689]{0:T(1024)} %param.60) | copy-start | bytes 32272
  366.4 39.8 %copy-start.8 = (f32[2689]{0:T(1024)S(1)}, f32[2689]{0:T(1024)}, u32[]{:S(2)}) copy-start(f32[2689]{0:T(1024)} %param.59) | copy-start | bytes 32272
